TPU v7x, 32 devices: a whole 2x2x4 slice. The times are simulated.
32 devices in a mesh: seq: 8 (over z, y), head: 4 (over x, core).
Axes of the slice: x: 2, y: 2, z: 4, core: 2. Of those that a mesh axis runs over, the one named last changes fastest.
Arguments:
- hidden_in: bfloat16 [4, 2048, 768], P(None, ('seq', 'head')), may hold values from -5.2 to 5.2
- query_weight: bfloat16 [2, 768, 768], P(None, None, 'head'), may hold values from -0.21875 to 0.21875
- key_weight: bfloat16 [2, 768, 768], P(None, None, 'head'), may hold values from -0.21875 to 0.21875
- value_weight: bfloat16 [2, 768, 768], P(None, None, 'head'), may hold values from -0.21875 to 0.21875
- query_bias: float32 [2, 768], P(None, 'head'), may hold values from -3 to 3
- value_bias: float32 [2, 768], P(None, 'head'), may hold values from -3 to 3
- out_weight: bfloat16 [2, 768, 768], P(None, 'head'), may hold values from -0.4375 to 0.4375
- out_bias: float32 [2, 768], replicated, may hold values from -2 to 2
- conv_taps: float32 [2, 12, 65], P(None, 'head'), may hold values from -0.4 to 0.4
- up_weight: bfloat16 [2, 768, 3072], P(None, None, 'head'), may hold values from -0.21875 to 0.21875
- up_bias: float32 [2, 3072], P(None, 'head'), may hold values from -3 to 3
- down_weight: bfloat16 [2, 3072, 768], P(None, 'head'), may hold values from -0.109375 to 0.109375
- down_bias: float32 [2, 768], replicated, may hold values from -2 to 2
- gain_one: float32 [2, 768], replicated, may hold values from 0.5 to 1.5
- shift_one: float32 [2, 768], replicated, may hold values from -1 to 1
- gain_two: float32 [2, 768], replicated, may hold values from 0.5 to 1.5
- shift_two: float32 [2, 768], replicated, may hold values from -1 to 1
- out_grad: float32 [4, 2048, 768], P(None, ('seq', 'head')), may hold values from -6 to 6
- item_lengths: int32 [4, 4], replicated, may hold values from 0 to 2048, as said below
Outputs:
- layer_out: bfloat16 [4, 2048, 768], P(None, ('seq', 'head'))
- hidden_grad: float32 [4, 2048, 768], P(None, ('seq', 'head'))
- query_weight_grad: float32 [2, 768, 768], P(None, None, 'head')
- key_weight_grad: float32 [2, 768, 768], P(None, None, 'head')
- value_weight_grad: float32 [2, 768, 768], P(None, None, 'head')
- query_bias_grad: float32 [2, 768], P(None, 'head')
- value_bias_grad: float32 [2, 768], P(None, 'head')
- out_weight_grad: float32 [2, 768, 768], P(None, 'head')
- out_bias_grad: float32 [2, 768], replicated
- conv_taps_grad: float32 [2, 12, 65], P(None, 'head')
- up_weight_grad: float32 [2, 768, 3072], P(None, None, 'head')
- up_bias_grad: float32 [2, 3072], P(None, 'head')
- down_weight_grad: float32 [2, 3072, 768], P(None, 'head')
- down_bias_grad: float32 [2, 768], replicated
- gain_one_grad: float32 [2, 768], replicated
- shift_one_grad: float32 [2, 768], replicated
- gain_two_grad: float32 [2, 768], replicated
- shift_two_grad: float32 [2, 768], replicated
Inputs may be any that keep to these rules, and one draw needn't show every extreme that they name: `item_lengths`: row r lists the lengths of the items packed into row r in order of position, then zeros; each length is 512 times a power of two, every item starts at a multiple of its own length, and the lengths of a row sum to 2048.
All inputs are finite; a program needn't handle non-finite values.
Results may differ from a plain program's by a relative error of at most 0.015.
Values may be sent and summed in bfloat16 or wider, within the bound.
No kernel may reach another device: no remote copies, remote signals or barrier semaphores. Data moves between devices by JAX's collectives and lax.ppermute only.
A program may use at most 192 MiB of HBM per device.

v0:
```python
import jax
import jax.numpy as jnp
from jax import lax
from jax.sharding import PartitionSpec as P

LANDMARKS = 64
NS_STEPS = 6


HIGHEST = lax.Precision.HIGHEST
EPSILON = 1e-05
FLOOR_TOP = -1e30


def swapped(block, axis, bit):
    count = lax.axis_size(axis)
    route = []
    for low in range(count):
        high = low | 1 << bit
        if high != low and high < count:
            route += [(low, high), (high, low)]
    return lax.ppermute(block, axis, route)


def extended_2(block, sides, width):
    for axis, dim in sides:
        count = lax.axis_size(axis)
        forward = [(i, i + 1) for i in range(count - 1)]
        backward = [(target, source) for source, target in forward]
        low = lax.ppermute(
            lax.slice_in_dim(block, block.shape[dim] - width, None, axis=dim), axis, forward
        )
        high = lax.ppermute(lax.slice_in_dim(block, 0, width, axis=dim), axis, backward)
        block = jnp.concatenate([low, block, high], axis=dim)
    return block


def layer_norm(values, gain, offset):
    centred = values - jnp.mean(values, axis=-1, keepdims=True)
    variance = jnp.mean(centred * centred, axis=-1, keepdims=True)
    return centred * lax.rsqrt(variance + EPSILON) * gain + offset


def gelu_exact(values):
    return jax.nn.gelu(values, approximate=False)


def pseudo_inverse(matrix):
    columns = jnp.sum(matrix, axis=-2)
    bound = jnp.sum(columns**8, axis=-1) ** 0.125
    iterate = jnp.swapaxes(matrix, -1, -2) / bound[..., None, None]
    identity = jnp.eye(matrix.shape[-1], dtype=jnp.float32)
    for step_index in range(NS_STEPS):
        product = jnp.matmul(matrix, iterate, precision=HIGHEST)
        inner = jnp.matmul(product, 7.0 * identity - product, precision=HIGHEST)
        middle = jnp.matmul(product, 15.0 * identity - inner, precision=HIGHEST)
        iterate = 0.25 * jnp.matmul(iterate, 13.0 * identity - middle, precision=HIGHEST)
    return iterate


def landmark_mix(land_query, land_key, weighted):
    scale = land_query.shape[-1] ** (-0.5)
    scores = jnp.einsum("rjhe,rihe->rhji", land_query, land_key, precision=HIGHEST) * scale
    inverse = pseudo_inverse(jax.nn.softmax(scores, axis=-1))
    return jnp.einsum("rhji,rihe->rjhe", inverse, weighted, precision=HIGHEST)


def item_layout(item_lengths, tok_row):
    place = lax.axis_index("seq")
    ends = jnp.cumsum(item_lengths, axis=1)
    starts = ends - item_lengths
    first_token = place * tok_row
    chosen = (starts <= first_token) & (first_token < ends)
    length = jnp.sum(jnp.where(chosen, item_lengths, 0), axis=1)
    begin = jnp.sum(jnp.where(chosen, starts, 0), axis=1)
    segment = length // LANDMARKS
    first_dev = begin // tok_row
    group = length // tok_row
    positions = first_token + jnp.arange(tok_row)
    marks = (positions[None, :] - begin[:, None]) // segment[:, None]
    hits = (marks[:, None, :] == jnp.arange(LANDMARKS)[None, :, None]).astype(jnp.float32)
    pooling = hits / segment[:, None, None].astype(jnp.float32)
    left_open = place > first_dev
    right_open = place + 1 < first_dev + group
    return (group, first_dev, pooling, left_open, right_open)


def spread(values):
    return lax.all_gather(values, "head", axis=1, tiled=True)


def collect(terms):
    return lax.psum_scatter(terms, "head", scatter_dimension=1, tiled=True)


def spread_grad(values):
    return lax.all_gather(values, "head", axis=1, tiled=True)


def collect_grad(terms):
    return lax.psum_scatter(terms, "head", scatter_dimension=1, tiled=True)


def join_parts(top_one, total_one, top_two, total_two):
    row_top = jnp.maximum(top_one, top_two)
    return (
        row_top,
        total_one * jnp.exp(top_one - row_top) + total_two * jnp.exp(top_two - row_top),
    )


def item_sum(values, layout):
    group = layout[0]
    levels = lax.axis_size("seq").bit_length() - 1
    running = values
    for bit_index in range(levels):
        partner = swapped(running, "seq", bit_index)
        inside = group > 1 << bit_index
        running = running + jnp.where(inside[:, None, None], partner, 0.0)
    return running


def item_merge(row_top, row_total, layout):
    group = layout[0]
    for bit_index in range(lax.axis_size("seq").bit_length() - 1):
        other_top, other_total = swapped((row_top, row_total), "seq", bit_index)
        inside = (group > 1 << bit_index)[:, None, None]
        row_top, row_total = join_parts(
            row_top,
            row_total,
            jnp.where(inside, other_top, FLOOR_TOP),
            jnp.where(inside, other_total, 0.0),
        )
    return (row_top, row_total)


def conv_band(tok_row, taps):
    half = (taps - 1) // 2
    out_pos = jnp.arange(tok_row)[:, None, None]
    in_pos = jnp.arange(tok_row + 2 * half)[None, :, None]
    tap_index = jnp.arange(taps)[None, None, :]
    return (in_pos - out_pos == tap_index).astype(jnp.float32)


def close_rims(extended, half, left_open, right_open):
    length = extended.shape[1]
    index = jnp.arange(length)
    middle = (index >= half) & (index < length - half)
    keep = (
        middle[None, :]
        | (index < half)[None, :] & left_open[:, None]
        | (index >= length - half)[None, :] & right_open[:, None]
    )
    return jnp.where(keep[:, :, None], extended, jnp.zeros((), extended.dtype))


def layer_forward(hidden, params, layout, band):
    (
        query_weight,
        key_weight,
        value_weight,
        query_bias,
        value_bias,
        out_weight,
        out_bias,
        conv_taps,
        up_weight,
        up_bias,
        down_weight,
        down_bias,
        gain_one,
        shift_one,
        gain_two,
        shift_two,
    ) = params
    group, first_dev, pooling, left_open, right_open = layout
    heads_dev, taps = conv_taps.shape
    half = (taps - 1) // 2
    x_full = spread(hidden.astype(jnp.bfloat16))
    batch_rows, tok_row = (x_full.shape[0], x_full.shape[1])
    width = query_weight.shape[1]
    head_dim = width // heads_dev
    scale = head_dim ** (-0.5)
    shape_four = (batch_rows, tok_row, heads_dev, head_dim)
    query_flat = (
        jnp.einsum("rtd,dc->rtc", x_full, query_weight, preferred_element_type=jnp.float32)
        + query_bias
    )
    key_flat = jnp.einsum("rtd,dc->rtc", x_full, key_weight, preferred_element_type=jnp.float32)
    values_low = (
        jnp.einsum("rtd,dc->rtc", x_full, value_weight, preferred_element_type=jnp.float32)
        + value_bias
    ).astype(jnp.bfloat16)
    queries = query_flat.reshape(shape_four)
    tok_keys = key_flat.reshape(shape_four)
    tok_values = values_low.astype(jnp.float32).reshape(shape_four)
    pooled = jnp.einsum(
        "rjt,rtc->rjc", pooling, jnp.concatenate([query_flat, key_flat], axis=-1), precision=HIGHEST
    )
    pooled = lax.optimization_barrier(pooled.astype(jnp.bfloat16)).astype(jnp.float32)
    marks = item_sum(pooled, layout)
    land_shape = (batch_rows, LANDMARKS, heads_dev, head_dim)
    land_q = marks[:, :, :width].reshape(land_shape)
    land_k = marks[:, :, width:].reshape(land_shape)
    far_scores = jnp.einsum("rjhe,rthe->rjht", land_q, tok_keys, precision=HIGHEST) * scale
    local_top = jnp.max(far_scores, axis=-1)
    local_total = jnp.sum(jnp.exp(far_scores - local_top[..., None]), axis=-1)
    row_top, row_total = item_merge(local_top, local_total, layout)
    far_probs = jnp.exp(far_scores - row_top[..., None]) / row_total[..., None]
    partial_mix = jnp.einsum("rjht,rthe->rjhe", far_probs, tok_values, precision=HIGHEST)
    weighted = item_sum(partial_mix.reshape(batch_rows, LANDMARKS, width), layout).reshape(
        land_shape
    )
    land_out = landmark_mix(land_q, land_k, weighted)
    near_scores = jnp.einsum("rthe,rjhe->rthj", queries, land_k, precision=HIGHEST) * scale
    near_probs = jax.nn.softmax(near_scores, axis=-1)
    mixed = jnp.einsum("rthj,rjhe->rthe", near_probs, land_out, precision=HIGHEST)
    rims = close_rims(extended_2(values_low, (("seq", 1),), half), half, left_open, right_open)
    rims_four = rims.astype(jnp.float32).reshape(
        batch_rows, tok_row + 2 * half, heads_dev, head_dim
    )
    toeplitz = jnp.einsum("hk,tsk->hts", conv_taps, band, precision=HIGHEST)
    conv_out = jnp.einsum("hts,rshe->rthe", toeplitz, rims_four, precision=HIGHEST)
    att_low = (mixed + conv_out).reshape(batch_rows, tok_row, width).astype(jnp.bfloat16)
    attn_out = (
        collect(jnp.einsum("rtc,cd->rtd", att_low, out_weight, preferred_element_type=jnp.float32))
        + out_bias
    )
    resid_one = hidden + attn_out
    normed = layer_norm(resid_one, gain_one, shift_one)
    h_full = spread(normed.astype(jnp.bfloat16))
    up_pre = (
        jnp.einsum("rtd,df->rtf", h_full, up_weight, preferred_element_type=jnp.float32) + up_bias
    )
    gelu_low = gelu_exact(up_pre).astype(jnp.bfloat16)
    mlp_out = (
        collect(
            jnp.einsum("rtf,fd->rtd", gelu_low, down_weight, preferred_element_type=jnp.float32)
        )
        + down_bias
    )
    resid_two = normed + mlp_out
    result = layer_norm(resid_two, gain_two, shift_two)
    kept = (
        x_full,
        queries,
        tok_keys,
        tok_values,
        land_q,
        land_k,
        far_probs,
        weighted,
        land_out,
        near_probs,
        rims_four,
        att_low,
        resid_one,
        h_full,
        up_pre,
        gelu_low,
        resid_two,
    )
    return (result, kept)


def layer_backward(grad_out, kept, params, layout, band):
    (
        query_weight,
        key_weight,
        value_weight,
        query_bias,
        value_bias,
        out_weight,
        out_bias,
        conv_taps,
        up_weight,
        up_bias,
        down_weight,
        down_bias,
        gain_one,
        shift_one,
        gain_two,
        shift_two,
    ) = params
    (
        x_full,
        queries,
        tok_keys,
        tok_values,
        land_q,
        land_k,
        far_probs,
        weighted,
        land_out,
        near_probs,
        rims_four,
        att_low,
        resid_one,
        h_full,
        up_pre,
        gelu_low,
        resid_two,
    ) = kept
    group, first_dev, pooling, left_open, right_open = layout
    heads_dev, taps = conv_taps.shape
    half = (taps - 1) // 2
    batch_rows, tok_row = (x_full.shape[0], x_full.shape[1])
    width = query_weight.shape[1]
    head_dim = width // heads_dev
    scale = head_dim ** (-0.5)
    shape_four = (batch_rows, tok_row, heads_dev, head_dim)
    land_shape = (batch_rows, LANDMARKS, heads_dev, head_dim)
    unused_two, pull_two = jax.vjp(layer_norm, resid_two, gain_two, shift_two)
    grad_two, grad_gain_two, grad_shift_two = pull_two(grad_out)
    grad_mlp = grad_two.astype(jnp.bfloat16)
    grad_down_bias = jnp.sum(grad_mlp.astype(jnp.float32), axis=(0, 1))
    grad_mlp_full = spread_grad(grad_mlp)
    grad_down_weight = jnp.einsum(
        "rtf,rtd->fd", gelu_low, grad_mlp_full, preferred_element_type=jnp.float32
    )
    grad_gelu = jnp.einsum(
        "rtd,fd->rtf", grad_mlp_full, down_weight, preferred_element_type=jnp.float32
    )
    unused_gelu, pull_gelu = jax.vjp(gelu_exact, up_pre)
    grad_up = pull_gelu(grad_gelu)[0].astype(jnp.bfloat16)
    grad_up_bias = jnp.sum(grad_up.astype(jnp.float32), axis=(0, 1))
    grad_up_weight = jnp.einsum("rtd,rtf->df", h_full, grad_up, preferred_element_type=jnp.float32)
    grad_normed = grad_two + collect_grad(
        jnp.einsum("rtf,df->rtd", grad_up, up_weight, preferred_element_type=jnp.float32)
    )
    unused_one, pull_one = jax.vjp(layer_norm, resid_one, gain_one, shift_one)
    grad_one, grad_gain_one, grad_shift_one = pull_one(grad_normed)
    grad_attn = grad_one.astype(jnp.bfloat16)
    grad_out_bias = jnp.sum(grad_attn.astype(jnp.float32), axis=(0, 1))
    grad_attn_full = spread_grad(grad_attn)
    grad_out_weight = jnp.einsum(
        "rtc,rtd->cd", att_low, grad_attn_full, preferred_element_type=jnp.float32
    )
    grad_mixed = jnp.einsum(
        "rtd,cd->rtc", grad_attn_full, out_weight, preferred_element_type=jnp.float32
    ).reshape(shape_four)
    grad_near = jnp.einsum("rthe,rjhe->rthj", grad_mixed, land_out, precision=HIGHEST)
    grad_near_scores = (
        near_probs * (grad_near - jnp.sum(grad_near * near_probs, axis=-1, keepdims=True)) * scale
    )
    grad_queries = jnp.einsum("rthj,rjhe->rthe", grad_near_scores, land_k, precision=HIGHEST)
    part_land_k = jnp.einsum("rthj,rthe->rjhe", grad_near_scores, queries, precision=HIGHEST)
    part_land_out = jnp.einsum("rthj,rthe->rjhe", near_probs, grad_mixed, precision=HIGHEST)
    summed = item_sum(
        jnp.concatenate(
            [
                part_land_out.reshape(batch_rows, LANDMARKS, width),
                part_land_k.reshape(batch_rows, LANDMARKS, width),
            ],
            axis=-1,
        ),
        layout,
    )
    grad_land_out = summed[:, :, :width].reshape(land_shape)
    near_land_k = summed[:, :, width:].reshape(land_shape)
    unused_mix, pull_mix = jax.vjp(landmark_mix, land_q, land_k, weighted)
    mix_land_q, mix_land_k, grad_weighted = pull_mix(grad_land_out)
    inner_dot = jnp.sum(grad_weighted * weighted, axis=-1)
    grad_far = jnp.einsum("rjhe,rthe->rjht", grad_weighted, tok_values, precision=HIGHEST)
    grad_far_scores = far_probs * (grad_far - inner_dot[..., None]) * scale
    part_land_q = jnp.einsum("rjht,rthe->rjhe", grad_far_scores, tok_keys, precision=HIGHEST)
    grad_keys = jnp.einsum("rjht,rjhe->rthe", grad_far_scores, land_q, precision=HIGHEST)
    grad_values = jnp.einsum("rjht,rjhe->rthe", far_probs, grad_weighted, precision=HIGHEST)
    far_land_q = item_sum(part_land_q.reshape(batch_rows, LANDMARKS, width), layout).reshape(
        land_shape
    )
    grad_land_q = mix_land_q + far_land_q
    grad_land_k = mix_land_k + near_land_k
    grad_queries = grad_queries + jnp.einsum(
        "rjt,rjhe->rthe", pooling, grad_land_q, precision=HIGHEST
    )
    grad_keys = grad_keys + jnp.einsum("rjt,rjhe->rthe", pooling, grad_land_k, precision=HIGHEST)
    rim_grads = close_rims(
        extended_2(grad_mixed.reshape(batch_rows, tok_row, width), (("seq", 1),), half),
        half,
        left_open,
        right_open,
    )
    rim_grads = rim_grads.reshape(batch_rows, tok_row + 2 * half, heads_dev, head_dim)
    flipped = jnp.einsum("hk,tsk->hts", conv_taps[:, ::-1], band, precision=HIGHEST)
    grad_values = grad_values + jnp.einsum("hts,rshe->rthe", flipped, rim_grads, precision=HIGHEST)
    tap_field = jnp.einsum("rthe,rshe->hts", grad_mixed, rims_four, precision=HIGHEST)
    grad_taps = jnp.einsum("hts,tsk->hk", tap_field, band, precision=HIGHEST)
    query_low = grad_queries.reshape(batch_rows, tok_row, width).astype(jnp.bfloat16)
    key_low = grad_keys.reshape(batch_rows, tok_row, width).astype(jnp.bfloat16)
    value_low = grad_values.reshape(batch_rows, tok_row, width).astype(jnp.bfloat16)
    grad_query_weight = jnp.einsum(
        "rtd,rtc->dc", x_full, query_low, preferred_element_type=jnp.float32
    )
    grad_key_weight = jnp.einsum("rtd,rtc->dc", x_full, key_low, preferred_element_type=jnp.float32)
    grad_value_weight = jnp.einsum(
        "rtd,rtc->dc", x_full, value_low, preferred_element_type=jnp.float32
    )
    grad_query_bias = jnp.sum(query_low.astype(jnp.float32), axis=(0, 1))
    grad_value_bias = jnp.sum(value_low.astype(jnp.float32), axis=(0, 1))
    input_terms = (
        jnp.einsum("rtc,dc->rtd", query_low, query_weight, preferred_element_type=jnp.float32)
        + jnp.einsum("rtc,dc->rtd", key_low, key_weight, preferred_element_type=jnp.float32)
        + jnp.einsum("rtc,dc->rtd", value_low, value_weight, preferred_element_type=jnp.float32)
    )
    grad_hidden = grad_one + collect_grad(input_terms)
    big_grads = (
        grad_query_weight,
        grad_key_weight,
        grad_value_weight,
        grad_query_bias,
        grad_value_bias,
        grad_out_weight,
        grad_taps,
        grad_up_weight,
        grad_up_bias,
        grad_down_weight,
    )
    small_grads = (
        grad_out_bias,
        grad_down_bias,
        grad_gain_one,
        grad_shift_one,
        grad_gain_two,
        grad_shift_two,
    )
    return (grad_hidden, big_grads, small_grads)


def on_device(
    hidden_in,
    query_weight,
    key_weight,
    value_weight,
    query_bias,
    value_bias,
    out_weight,
    out_bias,
    conv_taps,
    up_weight,
    up_bias,
    down_weight,
    down_bias,
    gain_one,
    shift_one,
    gain_two,
    shift_two,
    out_grad,
    item_lengths,
):
    tok_row = hidden_in.shape[1] * lax.axis_size("head")
    layout = item_layout(item_lengths, tok_row)
    band = conv_band(tok_row, conv_taps.shape[2])
    every = (
        query_weight,
        key_weight,
        value_weight,
        query_bias,
        value_bias,
        out_weight,
        out_bias,
        conv_taps,
        up_weight,
        up_bias,
        down_weight,
        down_bias,
        gain_one,
        shift_one,
        gain_two,
        shift_two,
    )
    first_params = tuple((array[0] for array in every))
    second_params = tuple((array[1] for array in every))
    start = hidden_in.astype(jnp.float32)
    middle, dropped = layer_forward(start, first_params, layout, band)
    final, kept_two = layer_forward(middle, second_params, layout, band)
    grad_middle, big_two, small_two = layer_backward(
        out_grad, kept_two, second_params, layout, band
    )
    unused_final, kept_one = layer_forward(start, first_params, layout, band)
    grad_start, big_one, small_one = layer_backward(
        grad_middle, kept_one, first_params, layout, band
    )
    (
        stack_query,
        stack_key,
        stack_value,
        stack_qbias,
        stack_vbias,
        stack_out,
        stack_taps,
        stack_up,
        stack_ubias,
        stack_down,
    ) = tuple((jnp.stack([one_grad, two_grad]) for one_grad, two_grad in zip(big_one, big_two)))
    stacked = lax.psum(
        (
            stack_query,
            stack_key,
            stack_value,
            stack_qbias,
            stack_vbias,
            stack_out,
            stack_taps,
            stack_up,
            stack_ubias,
            stack_down,
        ),
        "seq",
    )
    norm_obias, norm_dbias, norm_gone, norm_sone, norm_gtwo, norm_stwo = tuple(
        (jnp.stack([one_grad, two_grad]) for one_grad, two_grad in zip(small_one, small_two))
    )
    small_sums = lax.psum(
        (norm_obias, norm_dbias, norm_gone, norm_sone, norm_gtwo, norm_stwo), ("seq", "head")
    )
    return (
        final.astype(jnp.bfloat16),
        grad_start,
        stacked[0],
        stacked[1],
        stacked[2],
        stacked[3],
        stacked[4],
        stacked[5],
        small_sums[0],
        stacked[6],
        stacked[7],
        stacked[8],
        stacked[9],
        small_sums[1],
        small_sums[2],
        small_sums[3],
        small_sums[4],
        small_sums[5],
    )


def solution(mesh):
    placed = (
        P(None, ("seq", "head"), None),
        P(None, None, "head"),
        P(None, None, "head"),
        P(None, None, "head"),
        P(None, "head"),
        P(None, "head"),
        P(None, "head", None),
        P(),
        P(None, "head", None),
        P(None, None, "head"),
        P(None, "head"),
        P(None, "head", None),
        P(),
        P(),
        P(),
        P(),
        P(),
        P(None, ("seq", "head"), None),
        P(),
    )
    return jax.shard_map(
        on_device,
        mesh=mesh,
        in_specs=placed,
        out_specs=(
            P(None, ("seq", "head"), None),
            P(None, ("seq", "head"), None),
            P(None, None, "head"),
            P(None, None, "head"),
            P(None, None, "head"),
            P(None, "head"),
            P(None, "head"),
            P(None, "head", None),
            P(),
            P(None, "head", None),
            P(None, None, "head"),
            P(None, "head"),
            P(None, "head", None),
            P(),
            P(),
            P(),
            P(),
            P(),
        ),
        check_vma=False,
    )
```

profile of v0, /device:TPU:0, one launch (start us, length us, event | category | flops | bytes accessed | tf_op | source)
XLA Modules:
  0.0 1614.0 jit_solution(1989162408859929200)
XLA Ops:
  15.8 16.1 %all-gather.9.cloned.1.call-done = bf16[4,256,768]{2,1,0:T(8,128)(2,1)} async-done(((bf16[4,64,768]{2,1,0:T(8,128)(2,1)}), bf16[4,256,768]{2,1,0:T(8,128)(2,1)}) %all-gather.9.cloned.1.call-update) | async-done | bytes 1572880 | tf_op jit(solution)/shard_map/all_gather | solution.py:89
  40.5 8.0 fusion.5
  54.7 4.8 collective-permute-start.12
  59.5 3.6 collective-permute-done.1
  69.2 12.0 collective-permute-done.2
  102.1 10.8 fusion.332
  119.1 3.4 collective-permute-start.5
  130.8 5.7 collective-permute-done.9
  138.1 8.1 collective-permute-done.10
  147.8 12.9 collective-permute-done.11
  166.3 35.6 %reduce-scatter.9.cloned.1.call-done = f32[4,64,768]{2,1,0:T(8,128)} async-done(((f32[4,256,768]{2,1,0:T(8,128)}), f32[4,64,768]{2,1,0:T(8,128)}) %reduce-scatter.9.cloned.1.call-update) | async-done | bytes 786448 | tf_op jit(solution)/shard_map/reduce_scatter | solution.py:93
  205.1 19.1 %all-gather.11.cloned.1.call-done = bf16[4,256,768]{2,1,0:T(8,128)(2,1)} async-done(((bf16[4,64,768]{2,1,0:T(8,128)(2,1)}), bf16[4,256,768]{2,1,0:T(8,128)(2,1)}) %all-gather.11.cloned.1.call-update) | async-done | bytes 1572880 | tf_op jit(solution)/shard_map/all_gather | solution.py:89
  224.3 3.8 fusion.136
  228.1 8.1 multiply_convert_fusion.1
  241.3 36.2 %reduce-scatter.11.cloned.1.call-done = f32[4,64,768]{2,1,0:T(8,128)} async-done(((f32[4,256,768]{2,1,0:T(8,128)}), f32[4,64,768]{2,1,0:T(8,128)}) %reduce-scatter.11.cloned.1.call-update) | async-done | bytes 786448 | tf_op jit(solution)/shard_map/reduce_scatter | solution.py:93
  282.0 19.4 %all-gather.13.cloned.1.call-done = bf16[4,256,768]{2,1,0:T(8,128)(2,1)} async-done(((bf16[4,64,768]{2,1,0:T(8,128)(2,1)}), bf16[4,256,768]{2,1,0:T(8,128)(2,1)}) %all-gather.13.cloned.1.call-update) | async-done | bytes 1572880 | tf_op jit(solution)/shard_map/all_gather | solution.py:89
  309.9 8.9 fusion.4
  324.1 4.7 collective-permute-start.26
  328.8 3.7 collective-permute-done.15
  338.6 12.0 collective-permute-done.16
  385.2 3.4 collective-permute-start.19
  396.6 6.0 collective-permute-done.23
  404.1 8.4 collective-permute-done.24
  414.3 12.4 collective-permute-done.25
  433.1 35.3 %reduce-scatter.13.cloned.1.call-done = f32[4,64,768]{2,1,0:T(8,128)} async-done(((f32[4,256,768]{2,1,0:T(8,128)}), f32[4,64,768]{2,1,0:T(8,128)}) %reduce-scatter.13.cloned.1.call-update) | async-done | bytes 786448 | tf_op jit(solution)/shard_map/reduce_scatter | solution.py:93
  472.0 19.8 %all-gather.15.cloned.1.call-done = bf16[4,256,768]{2,1,0:T(8,128)(2,1)} async-done(((bf16[4,64,768]{2,1,0:T(8,128)(2,1)}), bf16[4,256,768]{2,1,0:T(8,128)(2,1)}) %all-gather.15.cloned.1.call-update) | async-done | bytes 1572880 | tf_op jit(solution)/shard_map/all_gather | solution.py:89
  491.8 3.8 fusion.137
  495.6 8.5 multiply_convert_fusion
  508.5 38.0 %reduce-scatter.15.cloned.1.call-done = f32[4,64,768]{2,1,0:T(8,128)} async-done(((f32[4,256,768]{2,1,0:T(8,128)}), f32[4,64,768]{2,1,0:T(8,128)}) %reduce-scatter.15.cloned.1.call-update) | async-done | bytes 786448 | tf_op jit(solution)/shard_map/reduce_scatter | solution.py:93
  553.1 19.8 %all-gather.17.cloned.1.call-done = bf16[4,256,768]{2,1,0:T(8,128)(2,1)} async-done(((bf16[4,64,768]{2,1,0:T(8,128)(2,1)}), bf16[4,256,768]{2,1,0:T(8,128)(2,1)}) %all-gather.17.cloned.1.call-update) | async-done | bytes 1572880 | tf_op jit(solution)/shard_map/all_gather | solution.py:97
  572.8 6.6 convert_reduce_fusion
  583.7 38.1 %reduce-scatter.17.cloned.1.call-done = f32[4,64,768]{2,1,0:T(8,128)} async-done(((f32[4,256,768]{2,1,0:T(8,128)}), f32[4,64,768]{2,1,0:T(8,128)}) %reduce-scatter.17.cloned.1.call-update) | async-done | bytes 786448 | tf_op jit(solution)/shard_map/reduce_scatter | solution.py:101
  627.6 19.6 %all-gather.19.cloned.1.call-done = bf16[4,256,768]{2,1,0:T(8,128)(2,1)} async-done(((bf16[4,64,768]{2,1,0:T(8,128)(2,1)}), bf16[4,256,768]{2,1,0:T(8,128)(2,1)}) %all-gather.19.cloned.1.call-update) | async-done | bytes 1572880 | tf_op jit(solution)/shard_map/all_gather | solution.py:97
  663.2 8.7 collective-permute-done.28
  674.7 9.4 fusion.3
  685.5 4.6 collective-permute-start.34
  696.3 8.3 collective-permute-done.34
  704.6 3.3 convolution_bitcast_fusion.19
  707.9 6.2 collective-permute-done.30
  774.4 3.3 collective-permute-start.32
  778.3 6.3 collective-permute-done.32
  785.4 3.5 collective-permute-start.33
  790.6 13.0 collective-permute-done.33
  811.6 37.4 %reduce-scatter.19.cloned.1.call-done = f32[4,64,768]{2,1,0:T(8,128)} async-done(((f32[4,256,768]{2,1,0:T(8,128)}), f32[4,64,768]{2,1,0:T(8,128)}) %reduce-scatter.19.cloned.1.call-update) | async-done | bytes 786448 | tf_op jit(solution)/shard_map/reduce_scatter | solution.py:101
  855.5 19.8 %all-gather.21.cloned.1.call-done = bf16[4,256,768]{2,1,0:T(8,128)(2,1)} async-done(((bf16[4,64,768]{2,1,0:T(8,128)(2,1)}), bf16[4,256,768]{2,1,0:T(8,128)(2,1)}) %all-gather.21.cloned.1.call-update) | async-done | bytes 1572880 | tf_op jit(solution)/shard_map/all_gather | solution.py:97
  875.3 6.6 convert_reduce_fusion.1
  886.2 38.0 %reduce-scatter.21.cloned.1.call-done = f32[4,64,768]{2,1,0:T(8,128)} async-done(((f32[4,256,768]{2,1,0:T(8,128)}), f32[4,64,768]{2,1,0:T(8,128)}) %reduce-scatter.21.cloned.1.call-update) | async-done | bytes 786448 | tf_op jit(solution)/shard_map/reduce_scatter | solution.py:101
  930.8 19.5 %all-gather.23.cloned.1.call-done = bf16[4,256,768]{2,1,0:T(8,128)(2,1)} async-done(((bf16[4,64,768]{2,1,0:T(8,128)(2,1)}), bf16[4,256,768]{2,1,0:T(8,128)(2,1)}) %all-gather.23.cloned.1.call-update) | async-done | bytes 1572880 | tf_op jit(solution)/shard_map/all_gather | solution.py:97
  962.8 10.0 collective-permute-done.36
  975.5 9.5 fusion.2
  986.4 4.6 collective-permute-start.42
  997.2 8.3 collective-permute-done.42
  1005.5 3.3 convolution_bitcast_fusion.18
  1008.8 6.2 collective-permute-done.38
  1072.2 3.3 collective-permute-start.40
  1076.1 6.3 collective-permute-done.40
  1083.3 3.4 collective-permute-start.41
  1088.4 13.0 collective-permute-done.41
  1108.8 3.5 convolution_bitcast_fusion.2
  1135.3 11.5 fusion.115
  1147.2 44.6 %all-reduce = (f32[2,768]{1,0:T(2,128)}, f32[2,768]{1,0:T(2,128)}, f32[2,768]{1,0:T(2,128)}, f32[2,768]{1,0:T(2,128)}, f32[2,768]{1,0:T(2,128)}, /*index=5*/f32[2,768]{1,0:T(2,128)}) all-reduce(f32[2,768]{1,0:T(2,128)S(1)} %pad_maximum_fusion.12, ...), channel_id=1, replica_groups=mesh['seq'=8,'head'=4] {'seq','head'}, use_global_device_ids=true, to_apply=%region_63.64 | all-reduce | flops 9216 | bytes 73728 | tf_op jit(solution)/shard_map/psum | solution.py:514
  1192.6 11.3 fusion.112
  1204.1 38.8 %all-reduce.1 = (f32[2,192]{1,0:T(2,128)}, f32[2,192]{1,0:T(2,128)}, f32[2,3,65]{2,1,0:T(4,128)S(1)}, f32[2,768]{1,0:T(2,128)}) all-reduce(f32[2,192]{1,0:T(2,128)S(1)} %pad_maximum_fusion.20, f32[2,192]{1,0:T(2,128)S(1)} %pad_maximum_fusion.21, f32[2,3,65]{2,1,0:T(4,128)S(1)} %pad_maximum_fusion.19, ...), channel_id=1, replica_groups=mesh['seq'=8,'head'=4] {'seq'}, use_global_device_ids=true, to_apply=%region_56.57 | all-reduce | flops 2694 | bytes 21552 | tf_op jit(solution)/shard_map/psum | solution.py:496
  1245.7 350.5 %all-reduce.5.cloned.1.call-done = (f32[2,768,192]{1,2,0:T(8,128)}, f32[2,768,192]{1,2,0:T(8,128)}, f32[2,768,192]{1,2,0:T(8,128)}, f32[2,192,768]{2,1,0:T(8,128...) async-done(((f32[2,768,192]{1,2,0:T(8,128)}, f32[2,768,192]{1,2,0:T(8,128)}, f32[2,768,192]{1,2,0:T(8,128)}, f32[2,192,768]{2,1,0:T(8,128)}, f32[2,768,768]{2,1,0:T(8,128)}, ...) | async-done | bytes 14155792 | tf_op jit(solution)/shard_map/psum | solution.py:496
  (1131 shorter events, 421.3 us)
Async XLA Ops:
  7.2 24.8 %all-gather.9.cloned.1.call-start = ((), (), s32[]{:S(2)}) async-start(), calls=%async_computation.8 | async-start | bytes 1966080 | tf_op jit(solution)/shard_map/all_gather | solution.py:89
  7.9 193.9 %reduce-scatter.9.cloned.1.call-start = ((), (), s32[]{:S(2)}) async-start(), calls=%async_computation.9 | async-start | bytes 3932160 | tf_op jit(solution)/shard_map/reduce_scatter | solution.py:93
  10.3 747.8 %copy-start.7 = (f32[64,64]{1,0:T(8,128)}, f32[64,64]{1,0:T(8,128)S(1)}, u32[]{:S(2)}) copy-start(f32[64,64]{1,0:T(8,128)S(1)} %get-tuple-element.227) | copy-start | bytes 49156
  38.9 11.3 collective-permute-start
  51.0 12.1 collective-permute-start.1
  53.4 13.0 collective-permute-start.13
  54.7 11.7 collective-permute-start.12
  63.9 17.4 %collective-permute-start.2 = (f32[4,64,384]{2,1,0:T(8,128)S(1)}, f32[4,64,384]{2,1,0:T(8,128)S(1)}, u32[]{:S(2)}, u32[]{:S(2)}) collective-permute-start(f32[4,64,384]{2,1,0:T(8,128)S(1)} %select_add_fusion.22), channel_id=1, source_target_pairs={{0,16},{16,0},{4,20},{20,4},{8,24},{24,8},{12,28},{28,12},{1,17},{... | collective-permute-start | bytes 1179656 | tf_op jit(solution)/shard_map/ppermute | solution.py:22
  83.3 30.2 %collective-permute-start.3 = (f32[4,64,3]{1,2,0:T(4,128)S(1)}, f32[4,64,3]{1,2,0:T(4,128)S(1)}, u32[]{:S(2)}, u32[]{:S(2)}) collective-permute-start(f32[4,64,3]{1,2,0:T(4,128)S(1)} %get-tuple-element.181), channel_id=1, source_target_pairs={{0,4},{4,0},{8,12},{12,8},{16,20},{20,16},{24,28},{28,24},{1,5},{5... | collective-permute-start | bytes 9224 | tf_op jit(solution)/shard_map/ppermute | solution.py:22
  85.2 28.3 %collective-permute-start.6 = (f32[4,64,3]{1,2,0:T(4,128)S(1)}, f32[4,64,3]{1,2,0:T(4,128)S(1)}, u32[]{:S(2)}, u32[]{:S(2)}) collective-permute-start(f32[4,64,3]{1,2,0:T(4,128)S(1)} %exponential_reduce_fusion.1), channel_id=1, source_target_pairs={{0,4},{4,0},{8,12},{12,8},{16,20},{20,16},{24,28},{28,24},{1,5},{5... | collective-permute-start | bytes 9224 | tf_op jit(solution)/shard_map/ppermute | solution.py:22
  114.3 3.7 collective-permute-start.7
  114.7 3.7 collective-permute-start.4
  119.1 5.1 collective-permute-start.5
  122.6 4.5 collective-permute-start.8
  128.7 7.8 collective-permute-start.9
  137.3 9.0 collective-permute-start.10
  147.0 13.7 collective-permute-start.11
  165.6 58.7 %all-gather.11.cloned.1.call-start = ((), (), s32[]{:S(2)}) async-start(), calls=%async_computation.10 | async-start | bytes 1966080 | tf_op jit(solution)/shard_map/all_gather | solution.py:89
  204.4 73.1 %reduce-scatter.11.cloned.1.call-start = ((), (), s32[]{:S(2)}) async-start(), calls=%async_computation.11 | async-start | bytes 3932160 | tf_op jit(solution)/shard_map/reduce_scatter | solution.py:93
  239.4 62.0 %all-gather.13.cloned.1.call-start = ((), (), s32[]{:S(2)}) async-start(), calls=%async_computation.12 | async-start | bytes 1966080 | tf_op jit(solution)/shard_map/all_gather | solution.py:89
  281.5 186.8 %reduce-scatter.13.cloned.1.call-start = ((), (), s32[]{:S(2)}) async-start(), calls=%async_computation.13 | async-start | bytes 3932160 | tf_op jit(solution)/shard_map/reduce_scatter | solution.py:93
  308.3 11.3 collective-permute-start.14
  320.4 12.1 collective-permute-start.15
  322.8 13.0 collective-permute-start.27
  324.1 11.7 collective-permute-start.26
  333.3 17.4 %collective-permute-start.16 = (f32[4,64,384]{2,1,0:T(8,128)S(1)}, f32[4,64,384]{2,1,0:T(8,128)S(1)}, u32[]{:S(2)}, u32[]{:S(2)}) collective-permute-start(f32[4,64,384]{2,1,0:T(8,128)S(1)} %select_add_fusion.16), channel_id=1, source_target_pairs={{0,16},{16,0},{4,20},{20,4},{8,24},{24,8},{12,28},{28,12},{1,17},{... | collective-permute-start | bytes 1179656 | tf_op jit(solution)/shard_map/ppermute | solution.py:22
  355.6 23.8 %collective-permute-start.17 = (f32[4,64,3]{1,2,0:T(4,128)S(1)}, f32[4,64,3]{1,2,0:T(4,128)}, u32[]{:S(2)}, u32[]{:S(2)}) collective-permute-start(f32[4,64,3]{1,2,0:T(4,128)S(1)} %get-tuple-element.188), channel_id=1, source_target_pairs={{0,4},{4,0},{8,12},{12,8},{16,20},{20,16},{24,28},{28,24},{1,5},{5... | collective-permute-start | bytes 9224 | tf_op jit(solution)/shard_map/ppermute | solution.py:22
  358.0 21.4 %collective-permute-start.20 = (f32[4,64,3]{1,2,0:T(4,128)}, f32[4,64,3]{1,2,0:T(4,128)}, u32[]{:S(2)}, u32[]{:S(2)}) collective-permute-start(f32[4,64,3]{1,2,0:T(4,128)} %exponential_reduce_fusion), channel_id=1, source_target_pairs={{0,4},{4,0},{8,12},{12,8},{16,20},{20,16},{24,28},{28,24},{1,5},{5... | collective-permute-start | bytes 9224 | tf_op jit(solution)/shard_map/ppermute | solution.py:22
  380.3 3.7 collective-permute-start.21
  380.9 3.7 collective-permute-start.18
  385.2 5.1 collective-permute-start.19
  388.7 4.5 collective-permute-start.22
  394.0 361.1 %copy-start.273 = (f32[4,64,3]{1,2,0:T(4,128)}, f32[4,64,3]{1,2,0:T(4,128)S(1)}, u32[]{:S(2)}) copy-start(f32[4,64,3]{1,2,0:T(4,128)S(1)} %get-tuple-element.164) | copy-start | bytes 9220
  394.0 361.1 %copy-start.275 = (f32[4,64,3]{1,2,0:T(4,128)}, f32[4,64,3]{1,2,0:T(4,128)S(1)}, u32[]{:S(2)}) copy-start(f32[4,64,3]{1,2,0:T(4,128)S(1)} %get-tuple-element.165) | copy-start | bytes 9220
  394.8 7.8 collective-permute-start.23
  403.4 9.1 collective-permute-start.24
  413.2 13.5 collective-permute-start.25
  433.0 58.8 %all-gather.15.cloned.1.call-start = ((), (), s32[]{:S(2)}) async-start(), calls=%async_computation.14 | async-start | bytes 1966080 | tf_op jit(solution)/shard_map/all_gather | solution.py:89
  471.9 74.6 %reduce-scatter.15.cloned.1.call-start = ((), (), s32[]{:S(2)}) async-start(), calls=%async_computation.15 | async-start | bytes 3932160 | tf_op jit(solution)/shard_map/reduce_scatter | solution.py:93
  508.5 64.4 %all-gather.17.cloned.1.call-start = ((), (), s32[]{:S(2)}) async-start(), calls=%async_computation.16 | async-start | bytes 1966080 | tf_op jit(solution)/shard_map/all_gather | solution.py:97
  553.0 68.8 %reduce-scatter.17.cloned.1.call-start = ((), (), s32[]{:S(2)}) async-start(), calls=%async_computation.17 | async-start | bytes 3932160 | tf_op jit(solution)/shard_map/reduce_scatter | solution.py:101
  583.7 63.5 %all-gather.19.cloned.1.call-start = ((), (), s32[]{:S(2)}) async-start(), calls=%async_computation.18 | async-start | bytes 1966080 | tf_op jit(solution)/shard_map/all_gather | solution.py:97
  627.3 221.7 %reduce-scatter.19.cloned.1.call-start = ((), (), s32[]{:S(2)}) async-start(), calls=%async_computation.19 | async-start | bytes 3932160 | tf_op jit(solution)/shard_map/reduce_scatter | solution.py:101
  660.3 11.6 collective-permute-start.28
  673.1 17.0 %collective-permute-start.29 = (f32[4,64,384]{2,1,0:T(8,128)S(1)}, f32[4,64,384]{2,1,0:T(8,128)S(1)}, u32[]{:S(2)}, u32[]{:S(2)}) collective-permute-start(f32[4,64,384]{2,1,0:T(8,128)S(1)} %select_add_fusion.11), channel_id=1, source_target_pairs={{0,8},{8,0},{4,12},{12,4},{16,24},{24,16},{20,28},{28,20},{1,9},{9... | collective-permute-start | bytes 1179656 | tf_op jit(solution)/shard_map/ppermute | solution.py:22
  684.2 12.0 collective-permute-start.35
  685.5 19.1 %collective-permute-start.34 = (f32[4,32,192]{1,2,0:T(8,128)S(1)}, f32[4,32,192]{1,2,0:T(8,128)S(1)}, u32[]{:S(2)}, u32[]{:S(2)}) collective-permute-start(f32[4,32,192]{1,2,0:T(8,128)S(1)} %get-tuple-element.150), channel_id=1, source_target_pairs={{0,4},{4,8},{8,12},{12,16},{16,20},{20,24},{24,28},{1,5},{5,9},{9,... | collective-permute-start | bytes 294920 | tf_op jit(solution)/shard_map/ppermute | solution.py:30
  690.9 23.2 %collective-permute-start.30 = (f32[4,64,384]{2,1,0:T(8,128)S(1)}, f32[4,64,384]{2,1,0:T(8,128)S(1)}, u32[]{:S(2)}, u32[]{:S(2)}) collective-permute-start(f32[4,64,384]{2,1,0:T(8,128)S(1)} %select_add_fusion.10), channel_id=1, source_target_pairs={{0,16},{16,0},{4,20},{20,4},{8,24},{24,8},{12,28},{28,12},{1,17},{... | collective-permute-start | bytes 1179656 | tf_op jit(solution)/shard_map/ppermute | solution.py:22
  758.1 14.8 collective-permute-start.31
  774.4 10.2 collective-permute-start.32
  785.4 18.2 %collective-permute-start.33 = (f32[4,64,192]{1,2,0:T(8,128)S(1)}, f32[4,64,192]{1,2,0:T(8,128)S(1)}, u32[]{:S(2)}, u32[]{:S(2)}) collective-permute-start(f32[4,64,192]{1,2,0:T(8,128)S(1)} %select_add_fusion.7), channel_id=1, source_target_pairs={{0,16},{16,0},{4,20},{20,4},{8,24},{24,8},{12,28},{28,12},{1,17},{... | collective-permute-start | bytes 589832 | tf_op jit(solution)/shard_map/ppermute | solution.py:22
  811.6 63.7 %all-gather.21.cloned.1.call-start = ((), (), s32[]{:S(2)}) async-start(), calls=%async_computation.20 | async-start | bytes 1966080 | tf_op jit(solution)/shard_map/all_gather | solution.py:97
  855.5 68.7 %reduce-scatter.21.cloned.1.call-start = ((), (), s32[]{:S(2)}) async-start(), calls=%async_computation.21 | async-start | bytes 3932160 | tf_op jit(solution)/shard_map/reduce_scatter | solution.py:101
  886.1 64.3 %all-gather.23.cloned.1.call-start = ((), (), s32[]{:S(2)}) async-start(), calls=%async_computation.22 | async-start | bytes 1966080 | tf_op jit(solution)/shard_map/all_gather | solution.py:97
  930.6 312.9 %reduce-scatter.23.cloned.1.call-start = ((), (), s32[]{:S(2)}) async-start(), calls=%async_computation.23 | async-start | bytes 3932160 | tf_op jit(solution)/shard_map/reduce_scatter | solution.py:101
  961.2 11.6 collective-permute-start.36
  974.0 17.1 %collective-permute-start.37 = (f32[4,64,384]{2,1,0:T(8,128)S(1)}, f32[4,64,384]{2,1,0:T(8,128)S(1)}, u32[]{:S(2)}, u32[]{:S(2)}) collective-permute-start(f32[4,64,384]{2,1,0:T(8,128)S(1)} %select_add_fusion.5), channel_id=1, source_target_pairs={{0,8},{8,0},{4,12},{12,4},{16,24},{24,16},{20,28},{28,20},{1,9},{9... | collective-permute-start | bytes 1179656 | tf_op jit(solution)/shard_map/ppermute | solution.py:22
  985.1 12.0 collective-permute-start.43
  986.4 19.1 %collective-permute-start.42 = (f32[4,32,192]{1,2,0:T(8,128)S(1)}, f32[4,32,192]{1,2,0:T(8,128)S(1)}, u32[]{:S(2)}, u32[]{:S(2)}) collective-permute-start(f32[4,32,192]{1,2,0:T(8,128)S(1)} %get-tuple-element.148), channel_id=1, source_target_pairs={{0,4},{4,8},{8,12},{12,16},{16,20},{20,24},{24,28},{1,5},{5,9},{9,... | collective-permute-start | bytes 294920 | tf_op jit(solution)/shard_map/ppermute | solution.py:30
  991.8 23.2 %collective-permute-start.38 = (f32[4,64,384]{2,1,0:T(8,128)S(1)}, f32[4,64,384]{2,1,0:T(8,128)S(1)}, u32[]{:S(2)}, u32[]{:S(2)}) collective-permute-start(f32[4,64,384]{2,1,0:T(8,128)S(1)} %select_add_fusion.4), channel_id=1, source_target_pairs={{0,16},{16,0},{4,20},{20,4},{8,24},{24,8},{12,28},{28,12},{1,17},{... | collective-permute-start | bytes 1179656 | tf_op jit(solution)/shard_map/ppermute | solution.py:22
  1058.2 12.6 collective-permute-start.39
  1072.2 10.3 collective-permute-start.40
  1083.3 18.2 %collective-permute-start.41 = (f32[4,64,192]{1,2,0:T(8,128)S(1)}, f32[4,64,192]{1,2,0:T(8,128)S(1)}, u32[]{:S(2)}, u32[]{:S(2)}) collective-permute-start(f32[4,64,192]{1,2,0:T(8,128)S(1)} %select_add_fusion.1), channel_id=1, source_target_pairs={{0,16},{16,0},{4,20},{20,4},{8,24},{24,8},{12,28},{28,12},{1,17},{... | collective-permute-start | bytes 589832 | tf_op jit(solution)/shard_map/ppermute | solution.py:22
  1108.7 487.5 %all-reduce.5.cloned.1.call-start = ((), (), s32[]{:S(2)}) async-start(), calls=%async_computation.24 | async-start | bytes 28311552 | tf_op jit(solution)/shard_map/psum | solution.py:496
  (313 other events, 4480.0 us)
Sparse Core Ops, SparseCore 0:
  9.6 22.3 all-gather.8
  165.7 36.1 reduce-scatter.8
  204.6 19.6 all-gather.10
  239.5 37.9 reduce-scatter.10
  281.6 19.6 all-gather.12
  433.1 35.1 reduce-scatter.12
  472.1 19.6 all-gather.14
  508.6 37.9 reduce-scatter.14
  553.1 19.6 all-gather.16
  583.8 37.9 reduce-scatter.16
  627.5 19.6 all-gather.18
  811.7 37.2 reduce-scatter.18
  855.6 19.6 all-gather.20
  886.2 37.9 reduce-scatter.20
  930.7 19.6 all-gather.22
  1108.8 37.2 reduce-scatter.22
  1152.5 443.6 all-reduce.4
where the time goes:
time: 1630 us; the launch traced here: 1610 us
  waiting for transfers between devices  953 us (58%)
  matrix products  320 us (20%)
  other arithmetic  99.7 us (6%)
  blocking collectives  83.4 us (5%)
  starting transfers between devices  80.3 us (5%)
  local copies, waits for them, and re-layouts  57.8 us (4%)
  between operations  20 us (1%)
    psum x1, waiting for transfers between devices, on_device(): lax.psum((stack_query, stack_key, stack_value, stack_qbias, stack_vbias,...  351 us
    ppermute x36, waiting for transfers between devices, swapped(): return lax.ppermute(block, axis, route)  167 us
    reduce_scatter x4, waiting for transfers between devices, collect(): return lax.psum_scatter(terms, 'head', scatter_dimension=1, tiled=True)  145 us
    reduce_scatter x4, waiting for transfers between devices, collect_grad(): return lax.psum_scatter(terms, 'head', scatter_dimension=1, tiled=True)  113 us
    all_gather x4, waiting for transfers between devices, spread_grad(): return lax.all_gather(values, 'head', axis=1, tiled=True)  78.7 us
    all_gather x4, waiting for transfers between devices, spread(): return lax.all_gather(values, 'head', axis=1, tiled=True)  74.4 us
    ppermute x36, starting transfers between devices, swapped(): return lax.ppermute(block, axis, route)  54.9 us
    psum x1, blocking collectives, on_device(): lax.psum((norm_obias, norm_dbias, norm_gone, norm_sone, norm_gtwo, norm_s...  44.6 us
  transfers between devices with their start and end apart: 61, of which 48 were waited for; matrix products, arithmetic and copies ran while one was open for 12% of the time, Pallas kernels for 0%

commit v1 on v0

v1 whole, which is shorter than its diff:
```python
import functools

import jax
import jax.numpy as jnp
from jax import lax
from jax.experimental import pallas as pl
from jax.experimental.pallas import tpu as pltpu
from jax.sharding import PartitionSpec as P

LANDMARKS = 64
NS_STEPS = 6


HIGHEST = lax.Precision.HIGHEST
EPSILON = 1e-05
FLOOR_TOP = -1e30
LOW = jnp.bfloat16
GROUP = ((0, 2), (1, 0), (1, 2))


def layer_norm(values, gain, offset):
    centred = values - jnp.mean(values, axis=-1, keepdims=True)
    variance = jnp.mean(centred * centred, axis=-1, keepdims=True)
    return centred * lax.rsqrt(variance + EPSILON) * gain + offset


def exchange(values, seq_mask, head_mask):
    if seq_mask == 0:
        count = lax.axis_size("head")
        return lax.ppermute(values, "head", [(i, i ^ head_mask) for i in range(count)])
    if head_mask == 0:
        count = lax.axis_size("seq")
        return lax.ppermute(values, "seq", [(i, i ^ seq_mask) for i in range(count)])
    heads = lax.axis_size("head")
    route = []
    for s in range(lax.axis_size("seq")):
        for h in range(heads):
            route.append((s * heads + h, (s ^ seq_mask) * heads + (h ^ head_mask)))
    return lax.ppermute(values, ("seq", "head"), route)


def rank_shift(values, step):
    heads = lax.axis_size("head")
    ranks = lax.axis_size("seq") * (heads // 2)
    route = []
    for rank in range(ranks):
        target = rank + step
        if 0 <= target < ranks:
            for core in range(2):
                source_dev = (rank // 2) * heads + (rank % 2) * 2 + core
                target_dev = (target // 2) * heads + (target % 2) * 2 + core
                route.append((source_dev, target_dev))
    return lax.ppermute(values, ("seq", "head"), route)


def place():
    seq = lax.axis_index("seq")
    head = lax.axis_index("head")
    return seq, head // 2, head % 2


def pair_join(values, axis):
    core = place()[2]
    other = exchange(values, 0, 1)
    low = jnp.where(core == 0, values, other)
    high = jnp.where(core == 0, other, values)
    return jnp.concatenate([low, high], axis=axis)


def pair_collect(terms):
    core = place()[2]
    half = terms.shape[1] // 2
    low, high = terms[:, :half], terms[:, half:]
    mine = jnp.where(core == 0, low, high)
    theirs = jnp.where(core == 0, high, low).astype(jnp.bfloat16)
    return mine + exchange(theirs, 0, 1).astype(jnp.float32)


def group_index():
    seq, across, core = place()
    return across + 2 * (seq % 2)


def upper_levels():
    levels = (lax.axis_size("seq") // 2).bit_length() - 1
    return [(low, min(2, levels - low)) for low in range(0, levels, 2)]


def nn(one, two, precision=None):
    return lax.dot_general(
        one, two, (((1,), (0,)), ((), ())), precision, preferred_element_type=jnp.float32
    )


def nt(one, two, precision=None):
    return lax.dot_general(
        one, two, (((1,), (1,)), ((), ())), precision, preferred_element_type=jnp.float32
    )


def tn(one, two, precision=None):
    return lax.dot_general(
        one, two, (((0,), (0,)), ((), ())), precision, preferred_element_type=jnp.float32
    )


def on_core(kernel, outs, scalars, *arrays):
    shapes = tuple(jax.ShapeDtypeStruct(shape, dtype) for shape, dtype in outs)
    specs = [pl.BlockSpec(memory_space=pltpu.SMEM)] if scalars is not None else []
    specs += [pl.BlockSpec(memory_space=pltpu.VMEM)] * len(arrays)
    given = ((scalars,) if scalars is not None else ()) + arrays
    return pl.pallas_call(
        kernel,
        out_shape=shapes,
        in_specs=specs,
        out_specs=tuple(pl.BlockSpec(memory_space=pltpu.VMEM) for _ in outs),
        compiler_params=pltpu.CompilerParams(vmem_limit_bytes=48 * 1024 * 1024),
    )(*given)


def tokens_of(row, tok_row):
    return pl.ds(pl.multiple_of(row * tok_row, tok_row), tok_row)


def lanes(shape):
    return lax.broadcasted_iota(jnp.int32, shape, len(shape) - 1)


def join_pool_kernel(spot, own, other, pool, full, one, two, three, four):
    rows, piece, model = own.shape
    tok_row = 2 * piece
    core = spot[1]
    half = model // 2
    for row in range(rows):
        mine = pl.multiple_of(row * tok_row + core * piece, piece)
        theirs = pl.multiple_of(row * tok_row + (1 - core) * piece, piece)
        full[pl.ds(mine, piece), :] = own[row]
        full[pl.ds(theirs, piece), :] = other[row]
    side = pl.ds(pl.multiple_of(core * half, half), half)
    for step, out in enumerate((one, two, three, four)):
        row = spot[0] ^ step
        block = full[tokens_of(row, tok_row), side]
        out[...] = nn(pool[row], block).astype(LOW)


def rim_blocks(block_of, rows, tok_row, half):
    low, high = None, None
    for row in range(rows):
        block = block_of(row).astype(jnp.float32)
        lane = lanes(block.shape)
        first = block if row == 0 else pltpu.roll(block, row * half, 1)
        shift = (row * half + half) % tok_row
        last = block if shift == 0 else pltpu.roll(block, shift, 1)
        inside = lane // half == row
        low = jnp.where(inside, first, 0.0 if low is None else low)
        high = jnp.where(inside, last, 0.0 if high is None else high)
    return low.astype(LOW), high.astype(LOW)


def far_kernel(half, spot, qkv, land, one, two, three, four, low, high):
    width = qkv.shape[0] // 3
    head_dim = LANDMARKS
    heads = width // head_dim
    tok_row = qkv.shape[1] // 4
    scale = head_dim ** (-0.5)
    for step, out in enumerate((one, two, three, four)):
        here = tokens_of(spot[0] ^ step, tok_row)
        logs = jnp.zeros((LANDMARKS, out.shape[1] - width), jnp.float32)
        lane = lanes(logs.shape)
        for head in range(heads):
            cols = slice(head * head_dim, (head + 1) * head_dim)
            keys = qkv[width + head * head_dim : width + (head + 1) * head_dim, here]
            values = qkv[2 * width + head * head_dim : 2 * width + (head + 1) * head_dim, here]
            land_q = land[step * LANDMARKS : (step + 1) * LANDMARKS, cols]
            scores = nn(land_q, keys) * scale
            top = jnp.max(scores, axis=1, keepdims=True)
            grown = jnp.exp(scores - top)
            total = jnp.sum(grown, axis=1, keepdims=True)
            out[:, cols] = nt(grown.astype(LOW), values) / total
            logs = jnp.where(lane == head, top + jnp.log(total), logs)
        out[:, width:] = logs
    low[...], high[...] = rim_blocks(
        lambda row: qkv[2 * width :, row * tok_row : (row + 1) * tok_row], 4, tok_row, half
    )


def merged(flags, pieces, width):
    head_dim = LANDMARKS
    mixes, logs = [], []
    for head in range(width // head_dim):
        cols = slice(head * head_dim, (head + 1) * head_dim)
        column = slice(width + head, width + head + 1)
        log = [pieces[0][:, column]]
        for index, piece in enumerate(pieces[1:]):
            log.append(jnp.where(flags[index] > 0, piece[:, column], FLOOR_TOP))
        top = functools.reduce(jnp.maximum, log)
        shares = [jnp.exp(value - top) for value in log]
        total = functools.reduce(jnp.add, shares)
        mix = sum(share * piece[:, cols] for share, piece in zip(shares, pieces))
        mixes.append(mix / total)
        logs.append(top + jnp.log(total))
    return mixes, logs


def merge_kernel(count, flags, *refs):
    out = refs[count]
    width = out.shape[1] - 128
    mixes, logs = merged(flags, refs[:count], width)
    packed = jnp.zeros((LANDMARKS, 128), jnp.float32)
    lane = lanes(packed.shape)
    for head, (mix, log) in enumerate(zip(mixes, logs)):
        out[:, head * LANDMARKS : (head + 1) * LANDMARKS] = mix
        packed = jnp.where(lane == head, log, packed)
    out[:, width:] = packed


def packed_parts(columns):
    packed = jnp.zeros((LANDMARKS, 128), jnp.float32)
    lane = lanes(packed.shape)
    for head, column in enumerate(columns):
        for part in range(3):
            rounded = column.astype(LOW).astype(jnp.float32)
            packed = jnp.where(lane == head + 8 * part, rounded, packed)
            column = column - rounded
    return packed.astype(LOW)


def unpacked_part(packed, head):
    packed = packed.astype(jnp.float32)
    return (
        packed[:, head : head + 1]
        + packed[:, head + 8 : head + 9]
        + packed[:, head + 16 : head + 17]
    )


def land_out_kernel(count, flags, *refs):
    inverse, out, weighted = refs[count:]
    width = weighted.shape[1]
    mixes, logs = merged(flags, refs[:count], width)
    for head, mix in enumerate(mixes):
        cols = slice(head * LANDMARKS, (head + 1) * LANDMARKS)
        weighted[:, cols] = mix
        out[:, cols] = nn(inverse[head], mix, HIGHEST).astype(LOW)
    out[:, width:] = packed_parts(logs)


def inverse_kernel(land, amats, inverses, products, seconds, thirds):
    width = land.shape[1] // 2
    heads = width // LANDMARKS
    scale = LANDMARKS ** (-0.5)
    shape = (LANDMARKS, LANDMARKS)
    rows = lax.broadcasted_iota(jnp.int32, shape, 0)
    eye = (rows == lanes(shape)).astype(jnp.float32)
    matrices, iterates = [], []
    for head in range(heads):
        cols = slice(head * LANDMARKS, (head + 1) * LANDMARKS)
        keys = slice(width + head * LANDMARKS, width + (head + 1) * LANDMARKS)
        scores = nt(land[:LANDMARKS, cols], land[:LANDMARKS, keys]) * scale
        grown = jnp.exp(scores - jnp.max(scores, axis=1, keepdims=True))
        matrix = grown / jnp.sum(grown, axis=1, keepdims=True)
        columns = jnp.sum(matrix, axis=0, keepdims=True)
        square = columns * columns
        fourth = square * square
        bound = jnp.sum(fourth * fourth, axis=1, keepdims=True)
        bound = jnp.exp(jnp.log(bound) * 0.125)
        amats[head] = matrix
        matrices.append(matrix)
        iterates.append(matrix.T / bound)
    for step in range(NS_STEPS):
        product = [nn(a, z, HIGHEST) for a, z in zip(matrices, iterates)]
        inner = [nn(p, 7.0 * eye - p, HIGHEST) for p in product]
        second = [15.0 * eye - value for value in inner]
        third = [13.0 * eye - nn(p, m, HIGHEST) for p, m in zip(product, second)]
        for head in range(heads):
            inverses[step * heads + head] = iterates[head]
            products[step * heads + head] = product[head]
            seconds[step * heads + head] = second[head]
            thirds[step * heads + head] = third[head]
        iterates = [0.25 * nn(z, m, HIGHEST) for z, m in zip(iterates, third)]
    for head in range(heads):
        inverses[NS_STEPS * heads + head] = iterates[head]


def band_blocks(line, tok_row, half):
    span = line.shape[1]
    wide = jnp.broadcast_to(line, (tok_row, span))
    middle = pltpu.roll(wide, 0, 1, stride=1, stride_axis=0)[:, :tok_row]
    short = jnp.broadcast_to(line, (half, span))
    low = pltpu.roll(short, span - half, 1, stride=1, stride_axis=0)[:, :tok_row]
    high = pltpu.roll(short, tok_row, 1, stride=1, stride_axis=0)[:, :tok_row]
    reps = tok_row // half
    return [
        part.astype(LOW)
        for part in (middle, jnp.concatenate([low] * reps, 0), jnp.concatenate([high] * reps, 0))
    ]


def near_kernel(half, spot, qkv, low, high, rims, land, one, two, three, four, line, out):
    width = qkv.shape[0] // 3
    tok_row = qkv.shape[1] // 4
    head_dim = LANDMARKS
    scale = head_dim ** (-0.5)
    low_all = low[...].astype(jnp.float32) * rims[0:1, :]
    high_all = high[...].astype(jnp.float32) * rims[1:2, :]
    lane = lanes((head_dim, tok_row)) // half
    bands = [band_blocks(line[h : h + 1, :], tok_row, half) for h in range(width // head_dim)]
    for step, mixed in enumerate((one, two, three, four)):
        row = spot[0] ^ step
        here = tokens_of(row, tok_row)
        land_rows = slice(step * LANDMARKS, (step + 1) * LANDMARKS)
        for head in range(width // head_dim):
            cols = slice(head * head_dim, (head + 1) * head_dim)
            keys = slice(width + head * head_dim, width + (head + 1) * head_dim)
            queries = qkv[cols, here]
            scores = nn(land[land_rows, keys], queries) * scale
            grown = jnp.exp(scores - jnp.max(scores, axis=0, keepdims=True))
            probs = grown / jnp.sum(grown, axis=0, keepdims=True)
            total = tn(mixed[:, cols], probs.astype(LOW))
            values = qkv[2 * width + head * head_dim : 2 * width + (head + 1) * head_dim, here]
            total = total + nn(values, bands[head][0])
            mine = lane == row
            total = total + nn(jnp.where(mine, low_all[cols, :], 0.0).astype(LOW), bands[head][1])
            total = total + nn(jnp.where(mine, high_all[cols, :], 0.0).astype(LOW), bands[head][2])
            out[cols, here] = total.astype(LOW)


def near_back_kernel(half, spot, qkv, grads, land, *refs):
    mixes, queries_out = refs[:4], refs[4]
    land_outs, land_keys, low, high = refs[5:9], refs[9:13], refs[13], refs[14]
    width = qkv.shape[0] // 3
    tok_row = qkv.shape[1] // 4
    head_dim = LANDMARKS
    scale = head_dim ** (-0.5)
    for step in range(4):
        here = tokens_of(spot[0] ^ step, tok_row)
        land_rows = slice(step * LANDMARKS, (step + 1) * LANDMARKS)
        for head in range(width // head_dim):
            cols = slice(head * head_dim, (head + 1) * head_dim)
            keys = slice(width + head * head_dim, width + (head + 1) * head_dim)
            queries = qkv[cols, here]
            land_k = land[land_rows, keys]
            scores = nn(land_k, queries) * scale
            grown = jnp.exp(scores - jnp.max(scores, axis=0, keepdims=True))
            probs = grown / jnp.sum(grown, axis=0, keepdims=True)
            grad = grads[cols, here]
            grad_probs = nn(mixes[step][:, cols], grad)
            inner = jnp.sum(grad_probs * probs, axis=0, keepdims=True)
            grad_scores = (probs * (grad_probs - inner) * scale).astype(LOW)
            queries_out[cols, here] = tn(land_k, grad_scores)
            land_keys[step][:, cols] = nt(grad_scores, queries).astype(LOW)
            land_outs[step][:, cols] = nt(probs.astype(LOW), grad).astype(LOW)
    low[...], high[...] = rim_blocks(
        lambda row: grads[:, row * tok_row : (row + 1) * tok_row], 4, tok_row, half
    )


def conv_back_kernel(half, qkv, grads, low, high, grad_low, grad_high, rims, line, out, taps):
    width = qkv.shape[0] // 3
    tok_row = qkv.shape[1] // 4
    head_dim = LANDMARKS
    span = line.shape[1]
    low_all = low[...].astype(jnp.float32) * rims[0:1, :]
    high_all = high[...].astype(jnp.float32) * rims[1:2, :]
    grad_low_all = grad_low[...].astype(jnp.float32) * rims[0:1, :]
    grad_high_all = grad_high[...].astype(jnp.float32) * rims[1:2, :]
    lane = lanes((head_dim, tok_row)) // half
    square = (tok_row, tok_row)
    turned = (lax.broadcasted_iota(jnp.int32, square, 0) + lanes(square) == tok_row - 1).astype(LOW)
    wide = lanes((tok_row, span))
    for head in range(width // head_dim):
        cols = slice(head * head_dim, (head + 1) * head_dim)
        bands = band_blocks(line[head : head + 1, :], tok_row, half)
        fields = [jnp.zeros(square, jnp.float32) for _ in range(3)]
        for row in range(4):
            here = slice(row * tok_row, (row + 1) * tok_row)
            mine = lane == row

            def rim(block):
                return jnp.where(mine, block[cols, :], 0.0).astype(LOW)

            grad = grads[cols, here]
            values = qkv[2 * width + head * head_dim : 2 * width + (head + 1) * head_dim, here]
            total = nn(grad, bands[0]) + nn(rim(grad_low_all), bands[1])
            out[cols, here] = total + nn(rim(grad_high_all), bands[2])
            backward = nn(grad, turned).astype(LOW)
            for index, block in enumerate((values, rim(low_all), rim(high_all))):
                fields[index] = fields[index] + tn(backward, block)
        ends = []
        for field in fields[1:]:
            folded = field + pltpu.roll(field, 2 * half, 1)
            folded = folded + pltpu.roll(folded, half, 1)
            ends.append(jnp.concatenate([folded, folded], axis=1))
        whole = jnp.concatenate([fields[0], jnp.zeros(square, jnp.float32)], axis=1)
        whole = pltpu.roll(whole, half, 1)
        whole = jnp.where(wide < half, ends[0], whole)
        right = (wide >= half + tok_row) & (wide < 2 * half + tok_row)
        whole = jnp.where(right, ends[1], whole)
        whole = pltpu.roll(whole, span - tok_row + 1, 1, stride=1, stride_axis=0)
        taps[head : head + 1, :] = jnp.sum(whole, axis=0, keepdims=True)[:, :128]


def mixture_grad_kernel(grads, inverse, weighted, out):
    width = grads.shape[1]
    inner = []
    for head in range(width // LANDMARKS):
        cols = slice(head * LANDMARKS, (head + 1) * LANDMARKS)
        value = tn(inverse[head], grads[:, cols], HIGHEST).astype(LOW)
        out[:, cols] = value
        product = value.astype(jnp.float32) * weighted[:, cols]
        inner.append(jnp.sum(product, axis=1, keepdims=True))
    out[:, width:] = packed_parts(inner)


def inverse_back_kernel(
    grads, weighted, land, amats, inverses, products, seconds, thirds, out
):
    width = grads.shape[1]
    heads = width // LANDMARKS
    scale = LANDMARKS ** (-0.5)
    shape = (LANDMARKS, LANDMARKS)
    rows = lax.broadcasted_iota(jnp.int32, shape, 0)
    eye = (rows == lanes(shape)).astype(jnp.float32)
    every = range(heads)
    columns = [slice(head * LANDMARKS, (head + 1) * LANDMARKS) for head in every]
    grad = [nt(grads[:, c], weighted[:, c], HIGHEST) for c in columns]
    matrices = [amats[head] for head in every]
    total = [jnp.zeros(shape, jnp.float32) for _ in every]
    for step in reversed(range(NS_STEPS)):
        z = [inverses[step * heads + head] for head in every]
        p = [products[step * heads + head] for head in every]
        m2 = [seconds[step * heads + head] for head in every]
        m3 = [thirds[step * heads + head] for head in every]
        g3 = [-0.25 * tn(z[i], grad[i], HIGHEST) for i in every]
        gz = [0.25 * nt(grad[i], m3[i], HIGHEST) for i in every]
        g2 = [-tn(p[i], g3[i], HIGHEST) for i in every]
        gp = [nt(g3[i], m2[i], HIGHEST) for i in every]
        g1 = [tn(p[i], g2[i], HIGHEST) for i in every]
        gp = [gp[i] + nt(g2[i], 7.0 * eye - p[i], HIGHEST) - g1[i] for i in every]
        total = [total[i] + nt(gp[i], z[i], HIGHEST) for i in every]
        grad = [gz[i] + tn(matrices[i], gp[i], HIGHEST) for i in every]
    for head in every:
        matrix = matrices[head]
        sums = jnp.sum(matrix, axis=0, keepdims=True)
        square = sums * sums
        fourth = square * square
        bound = jnp.sum(fourth * fourth, axis=1, keepdims=True)
        bound = jnp.exp(jnp.log(bound) * 0.125)
        first = inverses[head]
        lost = jnp.sum(grad[head] * first, axis=1, keepdims=True)
        lost = -jnp.sum(lost, axis=0, keepdims=True) / bound
        ratio = sums / bound
        cube = ratio * ratio * ratio
        value = total[head] + grad[head].T / bound + lost * (cube * cube * ratio)
        inner = jnp.sum(value * matrix, axis=1, keepdims=True)
        scores = matrix * (value - inner) * scale
        keys = slice(width + head * LANDMARKS, width + (head + 1) * LANDMARKS)
        land_q = land[:LANDMARKS, columns[head]].astype(jnp.float32)
        land_k = land[:LANDMARKS, keys].astype(jnp.float32)
        out[:, columns[head]] = nn(scores, land_k, HIGHEST)
        out[:, keys] = tn(scores, land_q, HIGHEST)


def far_back_kernel(spot, qkv, land, conv, *refs):
    mixes, grads, near_keys = refs[:4], refs[4:8], refs[8:12]
    keys_out, values_out, parts = refs[12], refs[13], refs[14:18]
    width = qkv.shape[0] // 3
    tok_row = qkv.shape[1] // 4
    head_dim = LANDMARKS
    scale = head_dim ** (-0.5)
    for step in range(4):
        here = tokens_of(spot[0] ^ step, tok_row)
        land_rows = slice(step * LANDMARKS, (step + 1) * LANDMARKS)
        for head in range(width // head_dim):
            cols = slice(head * head_dim, (head + 1) * head_dim)
            keys = qkv[width + head * head_dim : width + (head + 1) * head_dim, here]
            values = qkv[2 * width + head * head_dim : 2 * width + (head + 1) * head_dim, here]
            land_q = land[land_rows, cols]
            log = unpacked_part(mixes[step][:, width:], head)
            inner = unpacked_part(grads[step][:, width:], head)
            probs = jnp.exp(nn(land_q, keys) * scale - log)
            grad = grads[step][:, cols]
            scores = (probs * (nn(grad, values) - inner) * scale).astype(LOW)
            parts[step][:, cols] = nt(scores, keys).astype(LOW)
            keys_out[cols, here] = tn(land_q, scores)
            values_out[cols, here] = (conv[cols, here] + tn(grad, probs.astype(LOW))).astype(LOW)
        parts[step][:, width:] = near_keys[step][...]


def token_grad_kernel(spot, near, far, values, pool, one, two, three, four, out):
    width = near.shape[0]
    tok_row = near.shape[1] // 4
    for step, grads in enumerate((one, two, three, four)):
        row = spot[0] ^ step
        here = tokens_of(row, tok_row)
        share = pool[row]
        out[:width, here] = (near[:, here] + tn(grads[:, :width], share)).astype(LOW)
        out[width : 2 * width, here] = (far[:, here] + tn(grads[:, width:], share)).astype(LOW)
    out[2 * width :, :] = values[...]


def send_rows(pieces):
    got = [exchange(piece, s, h) for piece, (s, h) in zip(pieces[1:], GROUP)]
    return [pieces[0]] + got


def spread_row(row):
    return [row] + [exchange(row, s, h) for s, h in GROUP]


def item_sum(pieces, layout):
    span = layout["span"]
    dtype = pieces[0].dtype
    pieces = [piece.astype(jnp.float32) for piece in send_rows(pieces)]
    total = (pieces[0] + pieces[1]) + (pieces[2] + pieces[3])
    for low, bits in upper_levels():
        sent = total.astype(dtype)
        near = exchange(sent, 2 << low, 0).astype(jnp.float32)
        pair = total + jnp.where(span > 4 << low, near, 0.0)
        if bits == 2:
            far = exchange(sent, 4 << low, 0).astype(jnp.float32)
            cross = exchange(sent, 6 << low, 0).astype(jnp.float32)
            pair = pair + jnp.where(span > 8 << low, far + cross, 0.0)
        total = pair
    return total


def land_mixture(pieces, inverse, layout):
    span = layout["span"]
    width = pieces[0].shape[1] - 128
    pieces = send_rows(pieces)
    flags = jnp.ones((3,), jnp.int32)
    for low, bits in upper_levels():
        call = functools.partial(merge_kernel, len(pieces))
        (row,) = on_core(call, [(pieces[0].shape, jnp.float32)], flags, *pieces)
        pieces = [row] + [exchange(row, m << (low + 1), 0) for m in range(1, 1 << bits)]
        wide = (span > 8 << low).astype(jnp.int32)
        flags = jnp.stack([(span > 4 << low).astype(jnp.int32), wide, wide])
    outs = [(pieces[0].shape, LOW), ((LANDMARKS, width), jnp.float32)]
    call = functools.partial(land_out_kernel, len(pieces))
    return on_core(call, outs, flags, *pieces, inverse)


def item_layout(item_lengths, tok_row, half):
    seq, across, core = place()
    rank = seq * 2 + across
    ends = jnp.cumsum(item_lengths, axis=1)
    starts = ends - item_lengths
    first_token = rank * tok_row
    chosen = (starts <= first_token) & (first_token < ends)
    length = jnp.sum(jnp.where(chosen, item_lengths, 0), axis=1)
    begin = jnp.sum(jnp.where(chosen, starts, 0), axis=1)
    segment = length // LANDMARKS
    first_rank = begin // tok_row
    spans = length // tok_row
    positions = first_token + jnp.arange(tok_row)
    marks = (positions[None, :] - begin[:, None]) // segment[:, None]
    hits = marks[:, None, :] == jnp.arange(LANDMARKS)[None, :, None]
    share = 1.0 / segment.astype(jnp.float32)
    pool = jnp.where(hits, share[:, None, None], 0.0).astype(LOW)
    left_open = rank > first_rank
    right_open = rank + 1 < first_rank + spans
    rims = jnp.repeat(jnp.stack([left_open, right_open]).astype(jnp.float32), half, axis=1)
    me = group_index()
    return dict(
        span=lax.dynamic_index_in_dim(spans, me, 0, keepdims=False),
        pool=pool,
        rims=jnp.pad(rims, ((0, 6), (0, 0))),
        spot=jnp.stack([me, core]).astype(jnp.int32),
    )


def dot(spec, one, two):
    return jnp.einsum(spec, one, two, preferred_element_type=jnp.float32)


def ordered(mine, other, axis):
    across = place()[1]
    low = jnp.where(across == 0, mine, other)
    high = jnp.where(across == 0, other, mine)
    return jnp.stack([low, high], axis=axis)


def fetch_small(query_bias, value_bias, conv_taps, up_bias):
    layers = query_bias.shape[0]
    flat = [a.reshape(layers, -1) for a in (query_bias, value_bias, conv_taps, up_bias)]
    sizes = [a.shape[1] for a in flat]
    packed = jnp.concatenate(flat, axis=1)
    other = exchange(jnp.pad(packed, ((0, 0), (0, -packed.shape[1] % 128))), 0, 2)
    rest, at = [], 0
    for size in sizes:
        rest.append(other[:, at : at + size])
        at += size
    heads = conv_taps.shape[1]
    q_bias = ordered(query_bias, rest[0], 1).reshape(layers, -1)
    v_bias = ordered(value_bias, rest[1], 1).reshape(layers, -1)
    taps = ordered(conv_taps, rest[2].reshape(conv_taps.shape), 1).reshape(layers, 2 * heads, -1)
    return q_bias, v_bias, taps, rest[3]


def fetch_layer(query_weight, key_weight, value_weight, out_weight, up_weight, down_weight):
    mine = jnp.concatenate([query_weight.T, key_weight.T, value_weight.T, out_weight], axis=0)
    other = exchange(mine, 0, 2)
    split = (4, -1, mine.shape[1])
    attn = ordered(mine.reshape(split), other.reshape(split), 1)
    attn = attn.reshape(2 * mine.shape[0], mine.shape[1])
    split_at = attn.shape[0] * 3 // 4
    return dict(
        qkv=attn[:split_at],
        out=attn[split_at:],
        up=[up_weight, exchange(up_weight, 0, 2)],
        down=[down_weight, exchange(down_weight, 0, 2)],
    )


def tap_lines(taps):
    count = taps.shape[1]
    half = (count - 1) // 2
    gap = jnp.zeros((taps.shape[0], 256 - count), jnp.float32)
    flipped = taps[:, ::-1]
    lines = [jnp.concatenate([t[:, half:], gap, t[:, :half]], axis=1) for t in (flipped, taps)]
    pad = -taps.shape[0] % 8
    return [jnp.pad(line, ((0, pad), (0, 0))) for line in lines]


def layer_forward(hidden, params, layout):
    weights = params["weights"]
    spot = layout["spot"]
    batch_rows, piece, model = hidden.shape
    tok_row = 2 * piece
    tokens = batch_rows * tok_row
    width = weights["out"].shape[0]
    half = params["half"]
    quarter = [((LANDMARKS, model // 2), LOW)] * 4
    x_low = hidden.astype(LOW)
    x_full, *pooled = on_core(
        join_pool_kernel,
        [((tokens, model), LOW)] + quarter,
        spot,
        x_low,
        exchange(x_low, 0, 1),
        layout["pool"],
    )
    pooled = jnp.concatenate(spread_row(item_sum(pooled, layout).astype(LOW)), axis=0)
    pooled = pair_join(pooled, 1)
    bias_q, bias_v = params["q_bias"], params["v_bias"]
    no_bias = jnp.zeros_like(bias_q)
    column = jnp.concatenate([bias_q, no_bias, bias_v])[:, None]
    qkv = (nt(weights["qkv"], x_full) + column).astype(LOW)
    land = nt(pooled, weights["qkv"][: 2 * width]) + jnp.concatenate([bias_q, no_bias])
    land = land.astype(LOW)
    heads = width // LANDMARKS
    message = [((LANDMARKS, width + 128), jnp.float32)] * 4
    rim = [((width, batch_rows * half), LOW)] * 2
    *parts, low, high = on_core(
        functools.partial(far_kernel, half), message + rim, spot, qkv, land
    )
    low, high = rank_shift(high, 1), rank_shift(low, -1)
    square = (LANDMARKS, LANDMARKS)
    steps = ((NS_STEPS * heads,) + square, jnp.float32)
    own_land = land[:LANDMARKS]
    chain = on_core(
        inverse_kernel,
        [
            ((heads,) + square, jnp.float32),
            (((NS_STEPS + 1) * heads,) + square, jnp.float32),
            steps,
            steps,
            steps,
        ],
        None,
        own_land,
    )
    inverse = chain[1][NS_STEPS * heads :]
    own_out, weighted = land_mixture(parts, inverse, layout)
    mixes = spread_row(own_out)
    (att_low,) = on_core(
        functools.partial(near_kernel, half),
        [((width, tokens), LOW)],
        spot,
        qkv,
        low,
        high,
        layout["rims"],
        land,
        *mixes,
        params["lines"][0],
    )
    terms = tn(att_low, weights["out"]).reshape(batch_rows, tok_row, model)
    resid_one = hidden + (pair_collect(terms) + params["out_bias"])
    normed = layer_norm(resid_one, params["gain_one"], params["shift_one"])
    h_full = pair_join(normed.astype(LOW), 1).reshape(tokens, model)
    gelu_low, slopes = [], []
    for weight, bias in zip(weights["up"], params["up_bias"]):
        up_pre = nn(h_full, weight) + bias
        area = 0.5 * (1.0 + lax.erf(up_pre * 0.7071067811865476))
        bell = jnp.exp(-0.5 * up_pre * up_pre) * 0.3989422804014327
        gelu_low.append((up_pre * area).astype(LOW))
        slopes.append((area + up_pre * bell).astype(LOW))
    down = weights["down"]
    terms = nn(gelu_low[0], down[0]) + nn(gelu_low[1], down[1])
    mlp_out = pair_collect(terms.reshape(batch_rows, tok_row, model)) + params["down_bias"]
    resid_two = normed + mlp_out
    result = layer_norm(resid_two, params["gain_two"], params["shift_two"])
    kept = dict(
        x_full=x_full,
        qkv=qkv,
        land=land,
        own_land=own_land,
        rims=(low, high),
        chain=chain,
        inverse=inverse,
        weighted=weighted,
        mixes=mixes,
        att_low=att_low,
        resid_one=resid_one,
        h_full=h_full,
        gelu_low=gelu_low,
        slopes=slopes,
        resid_two=resid_two,
    )
    return result, kept


def layer_backward(grad_out, kept, params, layout):
    weights = params["weights"]
    spot = layout["spot"]
    batch_rows, piece, model = grad_out.shape
    tok_row = 2 * piece
    tokens = batch_rows * tok_row
    width = weights["out"].shape[0]
    half = params["half"]
    unused_two, pull_two = jax.vjp(
        layer_norm, kept["resid_two"], params["gain_two"], params["shift_two"]
    )
    grad_two, grad_gain_two, grad_shift_two = pull_two(grad_out)
    grad_mlp = grad_two.astype(LOW)
    grad_down_bias = jnp.sum(grad_mlp.astype(jnp.float32), axis=(0, 1))
    grad_mlp_full = pair_join(grad_mlp, 1).reshape(tokens, model)
    grad_up = [
        (nt(grad_mlp_full, weight) * slope.astype(jnp.float32)).astype(LOW)
        for weight, slope in zip(weights["down"], kept["slopes"])
    ]
    up = weights["up"]
    terms = nt(grad_up[0], up[0]) + nt(grad_up[1], up[1])
    grad_normed = grad_two + pair_collect(terms.reshape(batch_rows, tok_row, model))
    down_sum = reduce_big([tn(g, grad_mlp_full) for g in kept["gelu_low"]])
    up_sum = reduce_big([tn(kept["h_full"], g) for g in grad_up])
    grad_up_bias = [jnp.sum(g.astype(jnp.float32), axis=0) for g in grad_up]
    unused_one, pull_one = jax.vjp(
        layer_norm, kept["resid_one"], params["gain_one"], params["shift_one"]
    )
    grad_one, grad_gain_one, grad_shift_one = pull_one(grad_normed)
    grad_attn = grad_one.astype(LOW)
    grad_out_bias = jnp.sum(grad_attn.astype(jnp.float32), axis=(0, 1))
    grad_attn_full = pair_join(grad_attn, 1).reshape(tokens, model)
    grad_att = nt(weights["out"], grad_attn_full).astype(LOW)
    qkv, land, mixes = kept["qkv"], kept["land"], kept["mixes"]
    row = [((LANDMARKS, width), LOW)]
    rim = [((width, batch_rows * half), LOW)] * 2
    near_queries, *rest = on_core(
        functools.partial(near_back_kernel, half),
        [((width, tokens), jnp.float32)] + row * 8 + rim,
        spot,
        qkv,
        grad_att,
        land,
        *mixes,
    )
    near_outs, near_keys, (low, high) = rest[:4], rest[4:8], rest[8:]
    low, high = rank_shift(high, 1), rank_shift(low, -1)
    own_grad = item_sum(near_outs, layout)
    (own_mix_grad,) = on_core(
        mixture_grad_kernel,
        [((LANDMARKS, width + 128), LOW)],
        None,
        own_grad,
        kept["inverse"],
        kept["weighted"],
    )
    mix_grads = spread_row(own_mix_grad)
    grad_out_weight = nn(kept["att_low"], grad_attn_full)
    out_sum = reduce_big(split_across(grad_out_weight.reshape(1, width, model)))
    conv_grad, tap_grad = on_core(
        functools.partial(conv_back_kernel, half),
        [((width, tokens), jnp.float32), ((8, 128), jnp.float32)],
        None,
        qkv,
        grad_att,
        *kept["rims"],
        low,
        high,
        layout["rims"],
        params["lines"][1],
    )
    far_keys, values_low, *parts = on_core(
        far_back_kernel,
        [((width, tokens), jnp.float32), ((width, tokens), LOW)]
        + [((LANDMARKS, 2 * width), LOW)] * 4,
        spot,
        qkv,
        land,
        conv_grad,
        *mixes,
        *mix_grads,
        *near_keys,
    )
    (own_land_grad,) = on_core(
        inverse_back_kernel,
        [((LANDMARKS, 2 * width), jnp.float32)],
        None,
        own_grad,
        kept["weighted"],
        kept["own_land"],
        *kept["chain"],
    )
    own_land_grad = item_sum(parts, layout) + own_land_grad
    land_grads = spread_row(own_land_grad.astype(LOW))
    (grad_qkv,) = on_core(
        token_grad_kernel,
        [((3 * width, tokens), LOW)],
        spot,
        near_queries,
        far_keys,
        values_low,
        layout["pool"],
        *land_grads,
    )
    terms = tn(grad_qkv, weights["qkv"]).reshape(batch_rows, tok_row, model)
    grad_hidden = grad_one + pair_collect(terms)
    grad_weight = nn(grad_qkv, kept["x_full"]).reshape(3, width, model)
    qkv_sum = reduce_big(split_across(grad_weight))
    grad_bias = jnp.sum(grad_qkv.astype(jnp.float32), axis=1)
    heads = width // LANDMARKS
    mids = [
        split_flat(grad_bias[:width]),
        split_flat(grad_bias[2 * width :]),
        split_flat(tap_grad[:heads, : 2 * half + 1]),
        grad_up_bias,
    ]
    smalls = [
        grad_out_bias,
        grad_down_bias,
        grad_gain_one,
        grad_shift_one,
        grad_gain_two,
        grad_shift_two,
    ]
    return grad_hidden, (qkv_sum, out_sum, up_sum, down_sum), mids, smalls


def split_flat(values):
    across = place()[1]
    half = values.shape[0] // 2
    low, high = values[:half], values[half:]
    return [jnp.where(across == 0, low, high), jnp.where(across == 0, high, low)]


def split_across(values):
    across = place()[1]
    half = values.shape[1] // 2
    model = values.shape[2]
    low = values[:, :half].reshape(-1, model)
    high = values[:, half:].reshape(-1, model)
    return [jnp.where(across == 0, low, high), jnp.where(across == 0, high, low)]


def halve(values, mask):
    side = (lax.axis_index("seq") // mask) % 2
    half = values.shape[0] // 2
    low, high = values[:half], values[half:]
    keep = jnp.where(side == 0, low, high)
    sent = jnp.where(side == 0, high, low)
    return (keep.astype(jnp.float32) + exchange(sent, mask, 0).astype(jnp.float32)).astype(LOW)


def double(values, mask):
    side = (lax.axis_index("seq") // mask) % 2
    other = exchange(values, mask, 0)
    low = jnp.where(side == 0, values, other)
    high = jnp.where(side == 0, other, values)
    return jnp.concatenate([low, high], axis=0)


def reduce_big(pair):
    mine, theirs = pair
    got = exchange(theirs.astype(LOW), 0, 2).astype(jnp.float32)
    total = (mine + got).astype(LOW)
    masks = [1 << i for i in range(lax.axis_size("seq").bit_length() - 1)]
    rows = total.shape[0]
    extra = -rows % (2 * lax.axis_size("seq"))
    if extra:
        total = jnp.pad(total, ((0, extra), (0, 0)))
    middle = total.shape[0] // 2
    done = []
    for part, order in ((total[:middle], masks), (total[middle:], masks[1:] + masks[:1])):
        for mask in order:
            part = halve(part, mask)
        for mask in reversed(order):
            part = double(part, mask)
        done.append(part)
    return jnp.concatenate(done, axis=0)[:rows].astype(jnp.float32)


def seq_sum(values):
    mask = 1
    while mask < lax.axis_size("seq"):
        values = values + exchange(values, mask, 0)
        mask *= 2
    return values


def reduce_small(mid, small):
    mine = jnp.concatenate([m[0].reshape(-1) for m in mid])
    theirs = jnp.concatenate([m[1].reshape(-1) for m in mid])
    every = jnp.concatenate([s.reshape(-1) for s in small])
    count, extra = every.shape[0], mine.shape[0]
    pad = -(count + extra) % 1024
    got = exchange(jnp.pad(jnp.concatenate([every, theirs]), (0, pad)), 0, 2)
    total = jnp.pad(jnp.concatenate([every, mine]), (0, pad)) + got
    total = seq_sum(total)
    every = total[:count]
    every = every + exchange(every, 0, 1)
    mids, at = [], count
    for m in mid:
        mids.append(total[at : at + m[0].size].reshape(m[0].shape))
        at += m[0].size
    smalls, at = [], 0
    for s in small:
        smalls.append(every[at : at + s.size].reshape(s.shape))
        at += s.size
    return mids, smalls


def on_device(
    hidden_in,
    query_weight,
    key_weight,
    value_weight,
    query_bias,
    value_bias,
    out_weight,
    out_bias,
    conv_taps,
    up_weight,
    up_bias,
    down_weight,
    down_bias,
    gain_one,
    shift_one,
    gain_two,
    shift_two,
    out_grad,
    item_lengths,
):
    tok_row = hidden_in.shape[1] * 2
    half = (conv_taps.shape[2] - 1) // 2
    layout = item_layout(item_lengths, tok_row, half)
    q_bias, v_bias, taps, other_up = fetch_small(query_bias, value_bias, conv_taps, up_bias)
    params = []
    for i in range(2):
        params.append(
            dict(
                weights=fetch_layer(
                    query_weight[i],
                    key_weight[i],
                    value_weight[i],
                    out_weight[i],
                    up_weight[i],
                    down_weight[i],
                ),
                half=half,
                q_bias=q_bias[i],
                v_bias=v_bias[i],
                lines=tap_lines(taps[i]),
                up_bias=[up_bias[i], other_up[i]],
                out_bias=out_bias[i],
                down_bias=down_bias[i],
                gain_one=gain_one[i],
                shift_one=shift_one[i],
                gain_two=gain_two[i],
                shift_two=shift_two[i],
            )
        )
    hidden = hidden_in.astype(jnp.float32)
    kept = [None, None]
    for i in range(2):
        hidden, kept[i] = layer_forward(hidden, params[i], layout)
    grad = out_grad
    big, mid, small = [None, None], [None, None], [None, None]
    for i in (1, 0):
        grad, big[i], mid_i, small_i = layer_backward(grad, kept[i], params[i], layout)
        mid[i], small[i] = reduce_small(mid_i, small_i)
    mids = [jnp.stack([one, two]) for one, two in zip(*mid)]
    smalls = [jnp.stack([one, two]) for one, two in zip(*small)]
    width = query_weight.shape[2]
    qkv = jnp.stack([big[0][0], big[1][0]]).reshape(2, 3, width, -1)
    qkv = [jnp.swapaxes(qkv[:, i], 1, 2) for i in range(3)]
    outs, ups, downs = [jnp.stack([big[0][i], big[1][i]]) for i in (1, 2, 3)]
    return (
        hidden.astype(LOW),
        grad,
        qkv[0],
        qkv[1],
        qkv[2],
        mids[0],
        mids[1],
        outs,
        smalls[0],
        mids[2].reshape(conv_taps.shape),
        ups,
        mids[3],
        downs,
        smalls[1],
        smalls[2],
        smalls[3],
        smalls[4],
        smalls[5],
    )


def solution(mesh):
    placed = (
        P(None, ("seq", "head"), None),
        P(None, None, "head"),
        P(None, None, "head"),
        P(None, None, "head"),
        P(None, "head"),
        P(None, "head"),
        P(None, "head", None),
        P(),
        P(None, "head", None),
        P(None, None, "head"),
        P(None, "head"),
        P(None, "head", None),
        P(),
        P(),
        P(),
        P(),
        P(),
        P(None, ("seq", "head"), None),
        P(),
    )
    return jax.shard_map(
        on_device,
        mesh=mesh,
        in_specs=placed,
        out_specs=(
            P(None, ("seq", "head"), None),
            P(None, ("seq", "head"), None),
            P(None, None, "head"),
            P(None, None, "head"),
            P(None, None, "head"),
            P(None, "head"),
            P(None, "head"),
            P(None, "head", None),
            P(),
            P(None, "head", None),
            P(None, None, "head"),
            P(None, "head"),
            P(None, "head", None),
            P(),
            P(),
            P(),
            P(),
            P(),
        ),
        check_vma=False,
    )
```

time: 1630 us -> 909 us (0.56)
  waiting for transfers between devices: 953 us -> 343 us
  matrix products: 320 us -> 51.1 us
  starting transfers between devices: 80.3 us -> 255 us
  Pallas kernels: 0 us -> 92.5 us
  blocking collectives: 83.4 us -> 0 us
  other arithmetic: 99.7 us -> 83.1 us
    psum x1 -> x0, waiting for transfers between devices: 351 us -> none  [on_device(): lax.psum((stack_query, stack_key, stack_value, stack_qbias, stack_vbias,...]
    dot_general x230 -> x38, matrix products: 314 us -> 51.1 us  [the longest x12 24.1 us: tn(): lax.dot_general(one, two, (((0,), (0,)), ((), ())), precision, preferred_...]
    reduce_scatter x8 -> x0, waiting for transfers between devices: 259 us -> none  [the longest x4 145 us: collect(): return lax.psum_scatter(terms, 'head', scatter_dimension=1, tiled=True)]
    ppermute x44 -> x219, starting transfers between devices: 78.8 us -> 255 us  [the longest x142 175 us: exchange(): lax.ppermute(values, 'seq', [(i, i ^ seq_mask) for i in range(count)])]
    ppermute x44 -> x219, waiting for transfers between devices: 189 us -> 343 us  [the longest x53 169 us: exchange(): lax.ppermute(values, 'head', [(i, i ^ head_mask) for i in range(count)])]
    all_gather x8 -> x0, waiting for transfers between devices: 153 us -> none  [the longest x4 78.7 us: spread_grad(): return lax.all_gather(values, 'head', axis=1, tiled=True)]
    pallas_call x0 -> x24, Pallas kernels: none -> 92.5 us  [on_core(): pl.pallas_call(kernel, out_shape=shapes, in_specs=specs, out_specs=tuple(...]
    psum x2 -> x0, blocking collectives: 83.4 us -> none  [the longest x1 44.6 us: on_device(): lax.psum((norm_obias, norm_dbias, norm_gone, norm_sone, norm_gtwo, norm_s...]
  transfers between devices with their start and end apart: 61 -> 219, of which waited for: 48 -> 98; matrix products, arithmetic and copies ran while one was open for 12% -> 15% of each run, Pallas kernels for 0% -> 8%
where the time goes in v1:
time: 909 us; the launch traced here: 900 us
  waiting for transfers between devices  343 us (38%)
  starting transfers between devices  255 us (28%)
  Pallas kernels  92.5 us (10%)
  other arithmetic  83.1 us (9%)
  local copies, waits for them, and re-layouts  68.6 us (8%)
  matrix products  51.1 us (6%)
    ppermute x142, starting transfers between devices, exchange(): lax.ppermute(values, 'seq', [(i, i ^ seq_mask) for i in range(count)])  175 us
    ppermute x53, waiting for transfers between devices, exchange(): lax.ppermute(values, 'head', [(i, i ^ head_mask) for i in range(count)])  169 us
    ppermute x142, waiting for transfers between devices, exchange(): lax.ppermute(values, 'seq', [(i, i ^ seq_mask) for i in range(count)])  162 us
    pallas_call x24, Pallas kernels, on_core(): pl.pallas_call(kernel, out_shape=shapes, in_specs=specs, out_specs=tuple(...  92.5 us
    unnamed x530, local copies, waits for them, and re-layouts  37.8 us
    ppermute x53, starting transfers between devices, exchange(): lax.ppermute(values, 'head', [(i, i ^ head_mask) for i in range(count)])  37.2 us
    ppermute x16, starting transfers between devices, exchange(): return lax.ppermute(values, ('seq', 'head'), route)  25.1 us
    dot_general x12, matrix products, tn(): lax.dot_general(one, two, (((0,), (0,)), ((), ())), precision, preferred_...  24.1 us
  transfers between devices with their start and end apart: 219, of which 98 were waited for; matrix products, arithmetic and copies ran while one was open for 15% of the time, Pallas kernels for 8%

profile of v1, /device:TPU:0, one launch (start us, length us, event | category | flops | bytes accessed | tf_op | source)
XLA Modules:
  0.0 899.7 jit_solution(11629713744374035445)
XLA Ops:
  2.4 3.0 collective-permute-start.2
  18.1 21.9 %collective-permute-done.3 = bf16[64,384]{1,0:T(8,128)(2,1)S(1)} collective-permute-done((bf16[64,384]{1,0:T(8,128)(2,1)S(1)}, bf16[64,384]{1,0:T(8,128)(2,1)S(1)}, u32[]{:S(2)}, u32[]{:S(2)}) %collective-permute-start.3) | collective-permute-done | bytes 49184 | tf_op jit(solution)/shard_map/ppermute | solution.py:30
  41.6 3.7 collective-permute-start.8
  63.5 3.9 shard_map.323
  73.7 3.7 collective-permute-done.16.refs_2_
  87.5 5.0 shard_map.325
  99.3 3.3 collective-permute-start.23
  107.7 3.2 shard_map.327
  127.2 17.2 %collective-permute-done.26 = bf16[768,768]{1,0:T(8,128)(2,1)S(1)} collective-permute-done((bf16[768,768]{1,0:T(8,128)(2,1)S(1)}, bf16[768,768]{1,0:T(8,128)(2,1)S(1)}, u32[]{:S(2)}, u32[]{:S(2)}) %collective-permute-start.26) | collective-permute-done | bytes 1179680 | tf_op jit(solution)/shard_map/ppermute | solution.py:30
  146.6 22.6 %collective-permute-done.27 = bf16[768,768]{1,0:T(8,128)(2,1)S(1)} collective-permute-done((bf16[768,768]{1,0:T(8,128)(2,1)S(1)}, bf16[768,768]{1,0:T(8,128)(2,1)S(1)}, u32[]{:S(2)}, u32[]{:S(2)}) %collective-permute-start.27) | collective-permute-done | bytes 1179680 | tf_op jit(solution)/shard_map/ppermute | solution.py:30
  180.2 19.6 %collective-permute-done.29 = bf16[768,768]{1,0:T(8,128)(2,1)S(1)} collective-permute-done((bf16[768,768]{1,0:T(8,128)(2,1)S(1)}, bf16[768,768]{1,0:T(8,128)(2,1)S(1)}, u32[]{:S(2)}, u32[]{:S(2)}) %collective-permute-start.29) | collective-permute-done | bytes 1179680 | tf_op jit(solution)/shard_map/ppermute | solution.py:30
  201.8 2.8 collective-permute-start.36
  209.7 2.9 collective-permute-start.39
  218.8 3.9 shard_map.329
  226.3 2.8 collective-permute-done.43.refs_1_
  242.2 5.0 shard_map.331
  253.5 3.8 collective-permute-start.51
  261.9 3.2 shard_map.333
  278.5 23.7 %collective-permute-done.54 = bf16[768,768]{1,0:T(8,128)(2,1)S(1)} collective-permute-done((bf16[768,768]{1,0:T(8,128)(2,1)S(1)}, bf16[768,768]{1,0:T(8,128)(2,1)S(1)}, u32[]{:S(2)}, u32[]{:S(2)}) %collective-permute-start.54) | collective-permute-done | bytes 1179680 | tf_op jit(solution)/shard_map/ppermute | solution.py:30
  303.1 23.6 %collective-permute-done.55 = bf16[768,768]{1,0:T(8,128)(2,1)S(1)} collective-permute-done((bf16[768,768]{1,0:T(8,128)(2,1)S(1)}, bf16[768,768]{1,0:T(8,128)(2,1)S(1)}, u32[]{:S(2)}, u32[]{:S(2)}) %collective-permute-start.55) | collective-permute-done | bytes 1179680 | tf_op jit(solution)/shard_map/ppermute | solution.py:30
  347.7 3.2 convolution_convert_fusion
  353.1 5.5 shard_map.334
  364.8 2.6 collective-permute-done.64
  372.5 2.7 collective-permute-start.60
  382.8 13.2 %shard_map.338 = f32[64,768]{1,0:T(8,128)S(1)} custom-call(f32[64,384]{1,0:T(8,128)S(1)} %select_add_fusion.1.grads, f32[64,384]{1,0:T(8,128)S(1)} %copy-done.71, bf16[64,768]{1,0:T(8,128)(2,1)S(1)} %copy-done.28, f32[6,64,64]{2,1,0:T(8,128)S(1)} %copy-done.83, f32[42,64,64]{2,1,0:T(8,128)S(1)} %copy-done.5, f32[36,64,64]{2,1,0:T(8,128)S(1)} %copy-done.20, ...), custom_call_target="tpu_custom_call" | custom-call | tf_op jit(solution)/shard_map/pallas_call | solution.py:112
  398.1 5.7 shard_map.335
  403.9 5.2 shard_map.337
  416.1 16.6 %collective-permute-done.71 = bf16[64,768]{1,0:T(8,128)(2,1)S(1)} collective-permute-done((bf16[64,768]{1,0:T(8,128)(2,1)}, bf16[64,768]{1,0:T(8,128)(2,1)S(1)}, u32[]{:S(2)}, u32[]{:S(2)}) %collective-permute-start.71) | collective-permute-done | bytes 98336 | tf_op jit(solution)/shard_map/ppermute | solution.py:30
  437.2 3.8 collective-permute-start.76
  465.5 5.3 collective-permute-done.161
  476.4 3.3 collective-permute-done.162
  497.0 3.1 fusion.90
  503.5 2.7 collective-permute-done.135
  521.8 3.4 collective-permute-done.138
  537.6 5.9 collective-permute-done.188
  545.2 3.4 collective-permute-done.214
  548.7 2.7 collective-permute-done.208
  556.3 2.7 collective-permute-start.184
  560.6 2.8 collective-permute-start.210
  564.5 5.4 collective-permute-done.210
  569.9 5.5 collective-permute-done.191
  605.4 3.5 collective-permute-start.126
  624.5 3.2 collective-permute-done.122
  630.7 3.0 collective-permute-done.123
  636.7 5.5 shard_map.340
  646.5 3.7 collective-permute-start.84
  651.6 4.5 collective-permute-start.91
  668.5 5.7 shard_map.341
  674.2 5.1 shard_map.343
  691.8 12.9 %shard_map.344 = f32[64,768]{1,0:T(8,128)S(1)} custom-call(f32[64,384]{1,0:T(8,128)S(1)} %select_add_fusion.grads, f32[64,384]{1,0:T(8,128)S(1)} %copy-done.69, bf16[64,768]{1,0:T(8,128)(2,1)S(1)} %copy-done.26, f32[6,64,64]{2,1,0:T(8,128)S(1)} %copy-done.81, f32[42,64,64]{2,1,0:T(8,128)S(1)} %copy-done.3, f32[36,64,64]{2,1,0:T(8,128)S(1)} %copy-done.14, ...), custom_call_target="tpu_custom_call" | custom-call | tf_op jit(solution)/shard_map/pallas_call | solution.py:112
  731.5 4.8 collective-permute-done.148
  737.9 3.2 collective-permute-done.142
  760.9 3.1 fusion.91
  775.0 2.9 collective-permute-done.133
  780.5 2.8 collective-permute-done.145
  806.9 5.9 collective-permute-done.175
  814.2 3.2 collective-permute-done.201
  833.2 6.7 collective-permute-start.204
  842.2 4.1 collective-permute-done.172
  852.0 8.0 collective-permute-done.205
  869.0 3.2 collective-permute-done.113
  877.4 3.1 collective-permute-done.108
  887.7 3.3 collective-permute-start.117
  892.3 2.6 collective-permute-done.117
  (1359 shorter events, 505.8 us)
Async XLA Ops:
  10.0 48.7 %collective-permute-start = (bf16[768,768]{1,0:T(8,128)(2,1)}, bf16[768,768]{1,0:T(8,128)(2,1)}, u32[]{:S(2)}, u32[]{:S(2)}) collective-permute-start(bf16[768,768]{1,0:T(8,128)(2,1)} %pad_maximum_fusion), channel_id=1, source_target_pairs={{0,2},{1,3},{2,0},{3,1},{4,6},{5,7},{6,4},{7,5},{8,10},{9,11},{10,... | collective-permute-start | bytes 3538952 | tf_op jit(solution)/shard_map/ppermute | solution.py:30
  14.5 25.4 %collective-permute-start.3 = (bf16[64,384]{1,0:T(8,128)(2,1)S(1)}, bf16[64,384]{1,0:T(8,128)(2,1)S(1)}, u32[]{:S(2)}, u32[]{:S(2)}) collective-permute-start(bf16[64,384]{1,0:T(8,128)(2,1)S(1)} %get-tuple-element.94), channel_id=1, source_target_pairs={{0,2},{1,3},{2,0},{3,1},{4,6},{5,7},{6,4},{7,5},{8,10},{9,11},{10,... | collective-permute-start | bytes 147464 | tf_op jit(solution)/shard_map/ppermute | solution.py:30
  16.5 23.4 %collective-permute-start.4 = (bf16[64,384]{1,0:T(8,128)(2,1)S(1)}, bf16[64,384]{1,0:T(8,128)(2,1)S(1)}, u32[]{:S(2)}, u32[]{:S(2)}) collective-permute-start(bf16[64,384]{1,0:T(8,128)(2,1)S(1)} %get-tuple-element.95), channel_id=1, source_target_pairs={{0,4},{4,0},{8,12},{12,8},{16,20},{20,16},{24,28},{28,24},{1,5},{5... | collective-permute-start | bytes 147464 | tf_op jit(solution)/shard_map/ppermute | solution.py:33
  18.1 23.5 %collective-permute-start.5 = (bf16[64,384]{1,0:T(8,128)(2,1)S(1)}, bf16[64,384]{1,0:T(8,128)(2,1)S(1)}, u32[]{:S(2)}, u32[]{:S(2)}) collective-permute-start(bf16[64,384]{1,0:T(8,128)(2,1)S(1)} %get-tuple-element.96), channel_id=1, source_target_pairs={{0,6},{1,7},{2,4},{3,5},{4,2},{5,3},{6,0},{7,1},{8,14},{9,15},{10,... | collective-permute-start | bytes 147464 | tf_op jit(solution)/shard_map/ppermute | solution.py:39
  78.4 19.0 %collective-permute-start.20 = (f32[64,512]{1,0:T(8,128)S(1)}, f32[64,512]{1,0:T(8,128)S(1)}, u32[]{:S(2)}, u32[]{:S(2)}) collective-permute-start(f32[64,512]{1,0:T(8,128)S(1)} %shard_map.324.refs_0_), channel_id=1, source_target_pairs={{0,24},{4,28},{8,16},{12,20},{16,8},{20,12},{24,0},{28,4},{1,25},{... | collective-permute-start | bytes 393224 | tf_op jit(solution)/shard_map/ppermute | solution.py:33
  83.6 22.6 %collective-permute-start.13 = (bf16[384,128]{1,0:T(8,128)(2,1)S(1)}, bf16[384,128]{1,0:T(8,128)(2,1)S(1)}, u32[]{:S(2)}, u32[]{:S(2)}) collective-permute-start(bf16[384,128]{1,0:T(8,128)(2,1)S(1)} %get-tuple-element.97), channel_id=1, source_target_pairs={{0,2},{1,3},{2,4},{3,5},{4,6},{5,7},{6,8},{7,9},{8,10},{9,11},{10,... | collective-permute-start | bytes 294920 | tf_op jit(solution)/shard_map/ppermute | solution.py:53
  86.0 20.2 %collective-permute-start.14 = (bf16[384,128]{1,0:T(8,128)(2,1)S(1)}, bf16[384,128]{1,0:T(8,128)(2,1)S(1)}, u32[]{:S(2)}, u32[]{:S(2)}) collective-permute-start(bf16[384,128]{1,0:T(8,128)(2,1)S(1)} %get-tuple-element.98), channel_id=1, source_target_pairs={{2,0},{3,1},{4,2},{5,3},{6,4},{7,5},{8,6},{9,7},{10,8},{11,9},{12,... | collective-permute-start | bytes 294920 | tf_op jit(solution)/shard_map/ppermute | solution.py:53
  115.6 28.8 %collective-permute-start.26 = (bf16[768,768]{1,0:T(8,128)(2,1)S(1)}, bf16[768,768]{1,0:T(8,128)(2,1)S(1)}, u32[]{:S(2)}, u32[]{:S(2)}) collective-permute-start(bf16[768,768]{1,0:T(8,128)(2,1)S(1)} %get-tuple-element.271), channel_id=1, source_target_pairs={{0,2},{1,3},{2,0},{3,1},{4,6},{5,7},{6,4},{7,5},{8,10},{9,11},{10,... | collective-permute-start | bytes 3538952 | tf_op jit(solution)/shard_map/ppermute | solution.py:30
  121.5 47.8 %collective-permute-start.27 = (bf16[768,768]{1,0:T(8,128)(2,1)S(1)}, bf16[768,768]{1,0:T(8,128)(2,1)S(1)}, u32[]{:S(2)}, u32[]{:S(2)}) collective-permute-start(bf16[768,768]{1,0:T(8,128)(2,1)S(1)} %get-tuple-element.269), channel_id=1, source_target_pairs={{0,2},{1,3},{2,0},{3,1},{4,6},{5,7},{6,4},{7,5},{8,10},{9,11},{10,... | collective-permute-start | bytes 3538952 | tf_op jit(solution)/shard_map/ppermute | solution.py:30
  170.9 28.9 %collective-permute-start.29 = (bf16[768,768]{1,0:T(8,128)(2,1)S(1)}, bf16[768,768]{1,0:T(8,128)(2,1)S(1)}, u32[]{:S(2)}, u32[]{:S(2)}) collective-permute-start(bf16[768,768]{1,0:T(8,128)(2,1)S(1)} %pad_maximum_fusion.1), channel_id=1, source_target_pairs={{0,2},{1,3},{2,0},{3,1},{4,6},{5,7},{6,4},{7,5},{8,10},{9,11},{10,... | collective-permute-start | bytes 3538952 | tf_op jit(solution)/shard_map/ppermute | solution.py:30
  176.7 23.9 %collective-permute-start.31 = (bf16[64,384]{1,0:T(8,128)(2,1)S(1)}, bf16[64,384]{1,0:T(8,128)(2,1)S(1)}, u32[]{:S(2)}, u32[]{:S(2)}) collective-permute-start(bf16[64,384]{1,0:T(8,128)(2,1)S(1)} %get-tuple-element.107), channel_id=1, source_target_pairs={{0,2},{1,3},{2,0},{3,1},{4,6},{5,7},{6,4},{7,5},{8,10},{9,11},{10,... | collective-permute-start | bytes 147464 | tf_op jit(solution)/shard_map/ppermute | solution.py:30
  177.9 22.7 %collective-permute-start.32 = (bf16[64,384]{1,0:T(8,128)(2,1)S(1)}, bf16[64,384]{1,0:T(8,128)(2,1)S(1)}, u32[]{:S(2)}, u32[]{:S(2)}) collective-permute-start(bf16[64,384]{1,0:T(8,128)(2,1)S(1)} %get-tuple-element.108), channel_id=1, source_target_pairs={{0,4},{4,0},{8,12},{12,8},{16,20},{20,16},{24,28},{28,24},{1,5},{5... | collective-permute-start | bytes 147464 | tf_op jit(solution)/shard_map/ppermute | solution.py:33
  179.1 22.6 %collective-permute-start.33 = (bf16[64,384]{1,0:T(8,128)(2,1)S(1)}, bf16[64,384]{1,0:T(8,128)(2,1)S(1)}, u32[]{:S(2)}, u32[]{:S(2)}) collective-permute-start(bf16[64,384]{1,0:T(8,128)(2,1)S(1)} %get-tuple-element.109), channel_id=1, source_target_pairs={{0,6},{1,7},{2,4},{3,5},{4,2},{5,3},{6,0},{7,1},{8,14},{9,15},{10,... | collective-permute-start | bytes 147464 | tf_op jit(solution)/shard_map/ppermute | solution.py:39
  233.6 18.0 %collective-permute-start.48 = (f32[64,512]{1,0:T(8,128)S(1)}, f32[64,512]{1,0:T(8,128)S(1)}, u32[]{:S(2)}, u32[]{:S(2)}) collective-permute-start(f32[64,512]{1,0:T(8,128)S(1)} %shard_map.330.refs_0_), channel_id=1, source_target_pairs={{0,24},{4,28},{8,16},{12,20},{16,8},{20,12},{24,0},{28,4},{1,25},{... | collective-permute-start | bytes 393224 | tf_op jit(solution)/shard_map/ppermute | solution.py:33
  238.1 21.4 %collective-permute-start.41 = (bf16[384,128]{1,0:T(8,128)(2,1)S(1)}, bf16[384,128]{1,0:T(8,128)(2,1)S(1)}, u32[]{:S(2)}, u32[]{:S(2)}) collective-permute-start(bf16[384,128]{1,0:T(8,128)(2,1)S(1)} %get-tuple-element.110), channel_id=1, source_target_pairs={{0,2},{1,3},{2,4},{3,5},{4,6},{5,7},{6,8},{7,9},{8,10},{9,11},{10,... | collective-permute-start | bytes 294920 | tf_op jit(solution)/shard_map/ppermute | solution.py:53
  240.5 18.9 %collective-permute-start.42 = (bf16[384,128]{1,0:T(8,128)(2,1)S(1)}, bf16[384,128]{1,0:T(8,128)(2,1)S(1)}, u32[]{:S(2)}, u32[]{:S(2)}) collective-permute-start(bf16[384,128]{1,0:T(8,128)(2,1)S(1)} %get-tuple-element.111), channel_id=1, source_target_pairs={{2,0},{3,1},{4,2},{5,3},{6,4},{7,5},{8,6},{9,7},{10,8},{11,9},{12,... | collective-permute-start | bytes 294920 | tf_op jit(solution)/shard_map/ppermute | solution.py:53
  273.4 28.8 %collective-permute-start.54 = (bf16[768,768]{1,0:T(8,128)(2,1)S(1)}, bf16[768,768]{1,0:T(8,128)(2,1)S(1)}, u32[]{:S(2)}, u32[]{:S(2)}) collective-permute-start(bf16[768,768]{1,0:T(8,128)(2,1)S(1)} %copy-done.143), channel_id=1, source_target_pairs={{0,2},{1,3},{2,0},{3,1},{4,6},{5,7},{6,4},{7,5},{8,10},{9,11},{10,... | collective-permute-start | bytes 3538952 | tf_op jit(solution)/shard_map/ppermute | solution.py:30
  274.4 52.3 %collective-permute-start.55 = (bf16[768,768]{1,0:T(8,128)(2,1)S(1)}, bf16[768,768]{1,0:T(8,128)(2,1)S(1)}, u32[]{:S(2)}, u32[]{:S(2)}) collective-permute-start(bf16[768,768]{1,0:T(8,128)(2,1)S(1)} %copy-done.144), channel_id=1, source_target_pairs={{0,2},{1,3},{2,0},{3,1},{4,6},{5,7},{6,4},{7,5},{8,10},{9,11},{10,... | collective-permute-start | bytes 3538952 | tf_op jit(solution)/shard_map/ppermute | solution.py:30
  372.5 23.6 %collective-permute-start.60 = (bf16[384,128]{1,0:T(8,128)(2,1)S(1)}, bf16[384,128]{1,0:T(8,128)(2,1)S(1)}, u32[]{:S(2)}, u32[]{:S(2)}) collective-permute-start(bf16[384,128]{1,0:T(8,128)(2,1)S(1)} %get-tuple-element.119), channel_id=1, source_target_pairs={{0,2},{1,3},{2,4},{3,5},{4,6},{5,7},{6,8},{7,9},{8,10},{9,11},{10,... | collective-permute-start | bytes 294920 | tf_op jit(solution)/shard_map/ppermute | solution.py:53
  375.2 22.7 %collective-permute-start.61 = (bf16[384,128]{1,0:T(8,128)(2,1)S(1)}, bf16[384,128]{1,0:T(8,128)(2,1)S(1)}, u32[]{:S(2)}, u32[]{:S(2)}) collective-permute-start(bf16[384,128]{1,0:T(8,128)(2,1)S(1)} %get-tuple-element.120), channel_id=1, source_target_pairs={{2,0},{3,1},{4,2},{5,3},{6,4},{7,5},{8,6},{9,7},{10,8},{11,9},{12,... | collective-permute-start | bytes 294920 | tf_op jit(solution)/shard_map/ppermute | solution.py:53
  377.5 26.3 %collective-permute-start.70 = (bf16[64,512]{1,0:T(8,128)(2,1)S(1)}, bf16[64,512]{1,0:T(8,128)(2,1)S(1)}, u32[]{:S(2)}, u32[]{:S(2)}) collective-permute-start(bf16[64,512]{1,0:T(8,128)(2,1)S(1)} %shard_map.336.refs_4_), channel_id=1, source_target_pairs={{0,6},{1,7},{2,4},{3,5},{4,2},{5,3},{6,0},{7,1},{8,14},{9,15},{10,... | collective-permute-start | bytes 196616 | tf_op jit(solution)/shard_map/ppermute | solution.py:39
  379.9 23.9 %collective-permute-start.69 = (bf16[64,512]{1,0:T(8,128)(2,1)S(1)}, bf16[64,512]{1,0:T(8,128)(2,1)S(1)}, u32[]{:S(2)}, u32[]{:S(2)}) collective-permute-start(bf16[64,512]{1,0:T(8,128)(2,1)S(1)} %shard_map.336.refs_4_), channel_id=1, source_target_pairs={{0,4},{4,0},{8,12},{12,8},{16,20},{20,16},{24,28},{28,24},{1,5},{5... | collective-permute-start | bytes 196616 | tf_op jit(solution)/shard_map/ppermute | solution.py:33
  381.7 22.2 %collective-permute-start.68 = (bf16[64,512]{1,0:T(8,128)(2,1)S(1)}, bf16[64,512]{1,0:T(8,128)(2,1)S(1)}, u32[]{:S(2)}, u32[]{:S(2)}) collective-permute-start(bf16[64,512]{1,0:T(8,128)(2,1)S(1)} %shard_map.336.refs_4_), channel_id=1, source_target_pairs={{0,2},{1,3},{2,0},{3,1},{4,6},{5,7},{6,4},{7,5},{8,10},{9,11},{10,... | collective-permute-start | bytes 196616 | tf_op jit(solution)/shard_map/ppermute | solution.py:30
  396.0 55.7 %collective-permute-start.180 = (bf16[768,768]{1,0:T(8,128)(2,1)}, bf16[768,768]{1,0:T(8,128)(2,1)}, u32[]{:S(2)}, u32[]{:S(2)}) collective-permute-start(bf16[768,768]{1,0:T(8,128)(2,1)} %convolution_convert_fusion.2), channel_id=1, source_target_pairs={{0,2},{1,3},{2,0},{3,1},{4,6},{5,7},{6,4},{7,5},{8,10},{9,11},{10,... | collective-permute-start | bytes 3538952 | tf_op jit(solution)/shard_map/ppermute | solution.py:30
  397.9 43.1 %collective-permute-start.152 = (bf16[192,768]{1,0:T(8,128)(2,1)}, bf16[192,768]{1,0:T(8,128)(2,1)}, u32[]{:S(2)}, u32[]{:S(2)}) collective-permute-start(bf16[192,768]{1,0:T(8,128)(2,1)} %fusion.42), channel_id=1, source_target_pairs={{0,2},{1,3},{2,0},{3,1},{4,6},{5,7},{6,4},{7,5},{8,10},{9,11},{10,... | collective-permute-start | bytes 884744 | tf_op jit(solution)/shard_map/ppermute | solution.py:30
  411.3 21.4 %collective-permute-start.71 = (bf16[64,768]{1,0:T(8,128)(2,1)}, bf16[64,768]{1,0:T(8,128)(2,1)S(1)}, u32[]{:S(2)}, u32[]{:S(2)}) collective-permute-start(bf16[64,768]{1,0:T(8,128)(2,1)} %get-tuple-element.134), channel_id=1, source_target_pairs={{0,2},{1,3},{2,0},{3,1},{4,6},{5,7},{6,4},{7,5},{8,10},{9,11},{10,... | collective-permute-start | bytes 294920 | tf_op jit(solution)/shard_map/ppermute | solution.py:30
  413.1 21.4 %collective-permute-start.72 = (bf16[64,768]{1,0:T(8,128)(2,1)}, bf16[64,768]{1,0:T(8,128)(2,1)S(1)}, u32[]{:S(2)}, u32[]{:S(2)}) collective-permute-start(bf16[64,768]{1,0:T(8,128)(2,1)} %get-tuple-element.135), channel_id=1, source_target_pairs={{0,4},{4,0},{8,12},{12,8},{16,20},{20,16},{24,28},{28,24},{1,5},{5... | collective-permute-start | bytes 294920 | tf_op jit(solution)/shard_map/ppermute | solution.py:33
  413.4 22.8 %collective-permute-start.73 = (bf16[64,768]{1,0:T(8,128)(2,1)}, bf16[64,768]{1,0:T(8,128)(2,1)S(1)}, u32[]{:S(2)}, u32[]{:S(2)}) collective-permute-start(bf16[64,768]{1,0:T(8,128)(2,1)} %get-tuple-element.136), channel_id=1, source_target_pairs={{0,6},{1,7},{2,4},{3,5},{4,2},{5,3},{6,0},{7,1},{8,14},{9,15},{10,... | collective-permute-start | bytes 294920 | tf_op jit(solution)/shard_map/ppermute | solution.py:39
  432.7 26.4 %collective-permute-start.206 = (bf16[768,768]{1,0:T(8,128)(2,1)}, bf16[768,768]{1,0:T(8,128)(2,1)S(1)}, u32[]{:S(2)}, u32[]{:S(2)}) collective-permute-start(bf16[768,768]{1,0:T(8,128)(2,1)} %convolution_convert_fusion), channel_id=1, source_target_pairs={{0,2},{1,3},{2,0},{3,1},{4,6},{5,7},{6,4},{7,5},{8,10},{9,11},{10,... | collective-permute-start | bytes 3538952 | tf_op jit(solution)/shard_map/ppermute | solution.py:30
  447.2 37.9 %collective-permute-start.79 = (bf16[64,768]{1,0:T(8,128)(2,1)S(1)}, bf16[64,768]{1,0:T(8,128)(2,1)S(1)}, u32[]{:S(2)}, u32[]{:S(2)}) collective-permute-start(bf16[64,768]{1,0:T(8,128)(2,1)S(1)} %add_convert_fusion.34.one), channel_id=1, source_target_pairs={{0,6},{1,7},{2,4},{3,5},{4,2},{5,3},{6,0},{7,1},{8,14},{9,15},{10,... | collective-permute-start | bytes 294920 | tf_op jit(solution)/shard_map/ppermute | solution.py:39
  448.1 38.3 %collective-permute-start.78 = (bf16[64,768]{1,0:T(8,128)(2,1)S(1)}, bf16[64,768]{1,0:T(8,128)(2,1)S(1)}, u32[]{:S(2)}, u32[]{:S(2)}) collective-permute-start(bf16[64,768]{1,0:T(8,128)(2,1)S(1)} %add_convert_fusion.34.one), channel_id=1, source_target_pairs={{0,4},{4,0},{8,12},{12,8},{16,20},{20,16},{24,28},{28,24},{1,5},{5... | collective-permute-start | bytes 294920 | tf_op jit(solution)/shard_map/ppermute | solution.py:33
  451.4 37.1 %collective-permute-start.77 = (bf16[64,768]{1,0:T(8,128)(2,1)S(1)}, bf16[64,768]{1,0:T(8,128)(2,1)S(1)}, u32[]{:S(2)}, u32[]{:S(2)}) collective-permute-start(bf16[64,768]{1,0:T(8,128)(2,1)S(1)} %add_convert_fusion.34.one), channel_id=1, source_target_pairs={{0,2},{1,3},{2,0},{3,1},{4,6},{5,7},{6,4},{7,5},{8,10},{9,11},{10,... | collective-permute-start | bytes 294920 | tf_op jit(solution)/shard_map/ppermute | solution.py:30
  463.3 67.9 %collective-permute-start.181 = (bf16[192,768]{1,0:T(8,128)(2,1)}, bf16[192,768]{1,0:T(8,128)(2,1)}, u32[]{:S(2)}, u32[]{:S(2)}) collective-permute-start(bf16[192,768]{1,0:T(8,128)(2,1)} %get-tuple-element.290), channel_id=1, source_target_pairs={{0,4},{4,0},{8,12},{12,8},{16,20},{20,16},{24,28},{28,24},{1,5},{5... | collective-permute-start | bytes 884744 | tf_op jit(solution)/shard_map/ppermute | solution.py:33
  484.4 47.1 %collective-permute-start.187 = (bf16[192,768]{1,0:T(8,128)(2,1)}, bf16[192,768]{1,0:T(8,128)(2,1)}, u32[]{:S(2)}, u32[]{:S(2)}) collective-permute-start(bf16[192,768]{1,0:T(8,128)(2,1)} %get-tuple-element.291), channel_id=1, source_target_pairs={{0,8},{4,12},{8,0},{12,4},{16,24},{20,28},{24,16},{28,20},{1,9},{5... | collective-permute-start | bytes 884744 | tf_op jit(solution)/shard_map/ppermute | solution.py:33
  485.1 48.5 %collective-permute-start.207 = (bf16[192,768]{1,0:T(8,128)(2,1)}, bf16[192,768]{1,0:T(8,128)(2,1)}, u32[]{:S(2)}, u32[]{:S(2)}) collective-permute-start(bf16[192,768]{1,0:T(8,128)(2,1)} %get-tuple-element.282), channel_id=1, source_target_pairs={{0,4},{4,0},{8,12},{12,8},{16,20},{20,16},{24,28},{28,24},{1,5},{5... | collective-permute-start | bytes 884744 | tf_op jit(solution)/shard_map/ppermute | solution.py:33
  488.5 17.9 %collective-permute-start.157 = (bf16[24,768]{1,0:T(8,128)(2,1)}, bf16[24,768]{1,0:T(8,128)(2,1)}, u32[]{:S(2)}, u32[]{:S(2)}) collective-permute-start(bf16[24,768]{1,0:T(8,128)(2,1)} %pad_maximum_fusion.44), channel_id=1, source_target_pairs={{0,8},{4,12},{8,0},{12,4},{16,24},{20,28},{24,16},{28,20},{1,9},{5... | collective-permute-start | bytes 110600 | tf_op jit(solution)/shard_map/ppermute | solution.py:33
  514.1 19.8 %collective-permute-start.213 = (bf16[192,768]{1,0:T(8,128)(2,1)}, bf16[192,768]{1,0:T(8,128)(2,1)}, u32[]{:S(2)}, u32[]{:S(2)}) collective-permute-start(bf16[192,768]{1,0:T(8,128)(2,1)} %get-tuple-element.283), channel_id=1, source_target_pairs={{0,8},{4,12},{8,0},{12,4},{16,24},{20,28},{24,16},{28,20},{1,9},{5... | collective-permute-start | bytes 884744 | tf_op jit(solution)/shard_map/ppermute | solution.py:33
  527.2 25.9 %collective-permute-start.80 = (bf16[4,64,768]{2,1,0:T(8,128)(2,1)}, bf16[4,64,768]{2,1,0:T(8,128)(2,1)S(1)}, u32[]{:S(2)}, u32[]{:S(2)}) collective-permute-start(bf16[4,64,768]{2,1,0:T(8,128)(2,1)} %select_convert_fusion.4), channel_id=1, source_target_pairs={{0,1},{1,0},{2,3},{3,2},{4,5},{5,4},{6,7},{7,6},{8,9},{9,8},{10,11... | collective-permute-start | bytes 1179656 | tf_op jit(solution)/shard_map/ppermute | solution.py:30
  531.2 64.5 %collective-permute-start.118 = (bf16[576,768]{1,0:T(8,128)(2,1)}, bf16[576,768]{1,0:T(8,128)(2,1)S(1)}, u32[]{:S(2)}, u32[]{:S(2)}) collective-permute-start(bf16[576,768]{1,0:T(8,128)(2,1)} %bitcast.362), channel_id=1, source_target_pairs={{0,2},{1,3},{2,0},{3,1},{4,6},{5,7},{6,4},{7,5},{8,10},{9,11},{10,... | collective-permute-start | bytes 2654216 | tf_op jit(solution)/shard_map/ppermute | solution.py:30
  555.5 27.6 %collective-permute-start.81 = (bf16[4,64,768]{2,1,0:T(8,128)(2,1)S(1)}, bf16[4,64,768]{2,1,0:T(8,128)(2,1)S(1)}, u32[]{:S(2)}, u32[]{:S(2)}) collective-permute-start(bf16[4,64,768]{2,1,0:T(8,128)(2,1)S(1)} %get-tuple-element.237), channel_id=1, source_target_pairs={{0,1},{1,0},{2,3},{3,2},{4,5},{5,4},{6,7},{7,6},{8,9},{9,8},{10,11... | collective-permute-start | bytes 1179656 | tf_op jit(solution)/shard_map/ppermute | solution.py:30
  576.8 19.2 %collective-permute-start.192 = (bf16[192,768]{1,0:T(8,128)(2,1)S(1)}, bf16[192,768]{1,0:T(8,128)(2,1)S(1)}, u32[]{:S(2)}, u32[]{:S(2)}) collective-permute-start(bf16[192,768]{1,0:T(8,128)(2,1)S(1)} %pad_maximum_fusion.15), channel_id=1, source_target_pairs={{0,8},{4,12},{8,0},{12,4},{16,24},{20,28},{24,16},{28,20},{1,9},{5... | collective-permute-start | bytes 884744 | tf_op jit(solution)/shard_map/ppermute | solution.py:33
  579.0 18.2 %collective-permute-start.186 = (bf16[192,768]{1,0:T(8,128)(2,1)S(1)}, bf16[192,768]{1,0:T(8,128)(2,1)S(1)}, u32[]{:S(2)}, u32[]{:S(2)}) collective-permute-start(bf16[192,768]{1,0:T(8,128)(2,1)S(1)} %pad_maximum_fusion.14), channel_id=1, source_target_pairs={{0,4},{4,0},{8,12},{12,8},{16,20},{20,16},{24,28},{28,24},{1,5},{5... | collective-permute-start | bytes 884744 | tf_op jit(solution)/shard_map/ppermute | solution.py:33
  582.2 18.1 %collective-permute-start.218 = (bf16[192,768]{1,0:T(8,128)(2,1)S(1)}, bf16[192,768]{1,0:T(8,128)(2,1)S(1)}, u32[]{:S(2)}, u32[]{:S(2)}) collective-permute-start(bf16[192,768]{1,0:T(8,128)(2,1)S(1)} %pad_maximum_fusion.19), channel_id=1, source_target_pairs={{0,8},{4,12},{8,0},{12,4},{16,24},{20,28},{24,16},{28,20},{1,9},{5... | collective-permute-start | bytes 884744 | tf_op jit(solution)/shard_map/ppermute | solution.py:33
  583.2 18.5 %collective-permute-start.212 = (bf16[192,768]{1,0:T(8,128)(2,1)S(1)}, bf16[192,768]{1,0:T(8,128)(2,1)S(1)}, u32[]{:S(2)}, u32[]{:S(2)}) collective-permute-start(bf16[192,768]{1,0:T(8,128)(2,1)S(1)} %pad_maximum_fusion.18), channel_id=1, source_target_pairs={{0,4},{4,0},{8,12},{12,8},{16,20},{20,16},{24,28},{28,24},{1,5},{5... | collective-permute-start | bytes 884744 | tf_op jit(solution)/shard_map/ppermute | solution.py:33
  611.5 23.4 %collective-permute-start.83 = (bf16[4,64,768]{2,1,0:T(8,128)(2,1)S(1)}, bf16[4,64,768]{2,1,0:T(8,128)(2,1)S(1)}, u32[]{:S(2)}, u32[]{:S(2)}) collective-permute-start(bf16[4,64,768]{2,1,0:T(8,128)(2,1)S(1)} %get-tuple-element.239), channel_id=1, source_target_pairs={{0,1},{1,0},{2,3},{3,2},{4,5},{5,4},{6,7},{7,6},{8,9},{9,8},{10,11... | collective-permute-start | bytes 1179656 | tf_op jit(solution)/shard_map/ppermute | solution.py:30
  630.4 25.7 %collective-permute-start.130 = (bf16[144,768]{1,0:T(8,128)(2,1)S(1)}, bf16[144,768]{1,0:T(8,128)(2,1)S(1)}, u32[]{:S(2)}, u32[]{:S(2)}) collective-permute-start(bf16[144,768]{1,0:T(8,128)(2,1)S(1)} %pad_maximum_fusion.23), channel_id=1, source_target_pairs={{0,8},{4,12},{8,0},{12,4},{16,24},{20,28},{24,16},{28,20},{1,9},{5... | collective-permute-start | bytes 663560 | tf_op jit(solution)/shard_map/ppermute | solution.py:33
  633.8 22.5 %collective-permute-start.124 = (bf16[144,768]{1,0:T(8,128)(2,1)S(1)}, bf16[144,768]{1,0:T(8,128)(2,1)S(1)}, u32[]{:S(2)}, u32[]{:S(2)}) collective-permute-start(bf16[144,768]{1,0:T(8,128)(2,1)S(1)} %pad_maximum_fusion.22), channel_id=1, source_target_pairs={{0,4},{4,0},{8,12},{12,8},{16,20},{20,16},{24,28},{28,24},{1,5},{5... | collective-permute-start | bytes 663560 | tf_op jit(solution)/shard_map/ppermute | solution.py:33
  646.5 19.9 %collective-permute-start.84 = (bf16[384,128]{1,0:T(8,128)(2,1)S(1)}, bf16[384,128]{1,0:T(8,128)(2,1)S(1)}, u32[]{:S(2)}, u32[]{:S(2)}) collective-permute-start(bf16[384,128]{1,0:T(8,128)(2,1)S(1)} %get-tuple-element.142), channel_id=1, source_target_pairs={{0,2},{1,3},{2,4},{3,5},{4,6},{5,7},{6,8},{7,9},{8,10},{9,11},{10,... | collective-permute-start | bytes 294920 | tf_op jit(solution)/shard_map/ppermute | solution.py:53
  666.4 54.9 %collective-permute-start.167 = (bf16[768,768]{1,0:T(8,128)(2,1)}, bf16[768,768]{1,0:T(8,128)(2,1)}, u32[]{:S(2)}, u32[]{:S(2)}) collective-permute-start(bf16[768,768]{1,0:T(8,128)(2,1)} %convolution_convert_fusion.3), channel_id=1, source_target_pairs={{0,2},{1,3},{2,0},{3,1},{4,6},{5,7},{6,4},{7,5},{8,10},{9,11},{10,... | collective-permute-start | bytes 3538952 | tf_op jit(solution)/shard_map/ppermute | solution.py:30
  666.8 42.5 %collective-permute-start.139 = (bf16[192,768]{1,0:T(8,128)(2,1)}, bf16[192,768]{1,0:T(8,128)(2,1)}, u32[]{:S(2)}, u32[]{:S(2)}) collective-permute-start(bf16[192,768]{1,0:T(8,128)(2,1)} %fusion.41), channel_id=1, source_target_pairs={{0,2},{1,3},{2,0},{3,1},{4,6},{5,7},{6,4},{7,5},{8,10},{9,11},{10,... | collective-permute-start | bytes 884744 | tf_op jit(solution)/shard_map/ppermute | solution.py:30
  681.6 23.1 %collective-permute-start.95 = (bf16[64,768]{1,0:T(8,128)(2,1)}, bf16[64,768]{1,0:T(8,128)(2,1)S(1)}, u32[]{:S(2)}, u32[]{:S(2)}) collective-permute-start(bf16[64,768]{1,0:T(8,128)(2,1)} %get-tuple-element.157), channel_id=1, source_target_pairs={{0,2},{1,3},{2,0},{3,1},{4,6},{5,7},{6,4},{7,5},{8,10},{9,11},{10,... | collective-permute-start | bytes 294920 | tf_op jit(solution)/shard_map/ppermute | solution.py:30
  682.0 23.2 %collective-permute-start.96 = (bf16[64,768]{1,0:T(8,128)(2,1)}, bf16[64,768]{1,0:T(8,128)(2,1)}, u32[]{:S(2)}, u32[]{:S(2)}) collective-permute-start(bf16[64,768]{1,0:T(8,128)(2,1)} %get-tuple-element.158), channel_id=1, source_target_pairs={{0,4},{4,0},{8,12},{12,8},{16,20},{20,16},{24,28},{28,24},{1,5},{5... | collective-permute-start | bytes 294920 | tf_op jit(solution)/shard_map/ppermute | solution.py:33
  682.8 22.4 %collective-permute-start.97 = (bf16[64,768]{1,0:T(8,128)(2,1)}, bf16[64,768]{1,0:T(8,128)(2,1)}, u32[]{:S(2)}, u32[]{:S(2)}) collective-permute-start(bf16[64,768]{1,0:T(8,128)(2,1)} %get-tuple-element.159), channel_id=1, source_target_pairs={{0,6},{1,7},{2,4},{3,5},{4,2},{5,3},{6,0},{7,1},{8,14},{9,15},{10,... | collective-permute-start | bytes 294920 | tf_op jit(solution)/shard_map/ppermute | solution.py:39
  704.8 21.3 %collective-permute-start.193 = (bf16[768,768]{1,0:T(8,128)(2,1)S(1)}, bf16[768,768]{1,0:T(8,128)(2,1)S(1)}, u32[]{:S(2)}, u32[]{:S(2)}) collective-permute-start(bf16[768,768]{1,0:T(8,128)(2,1)S(1)} %copy-done.253), channel_id=1, source_target_pairs={{0,2},{1,3},{2,0},{3,1},{4,6},{5,7},{6,4},{7,5},{8,10},{9,11},{10,... | collective-permute-start | bytes 3538952 | tf_op jit(solution)/shard_map/ppermute | solution.py:30
  717.0 34.5 %collective-permute-start.103 = (bf16[64,768]{1,0:T(8,128)(2,1)S(1)}, bf16[64,768]{1,0:T(8,128)(2,1)S(1)}, u32[]{:S(2)}, u32[]{:S(2)}) collective-permute-start(bf16[64,768]{1,0:T(8,128)(2,1)S(1)} %add_convert_fusion.33.one), channel_id=1, source_target_pairs={{0,6},{1,7},{2,4},{3,5},{4,2},{5,3},{6,0},{7,1},{8,14},{9,15},{10,... | collective-permute-start | bytes 294920 | tf_op jit(solution)/shard_map/ppermute | solution.py:39
  718.4 34.1 %collective-permute-start.102 = (bf16[64,768]{1,0:T(8,128)(2,1)S(1)}, bf16[64,768]{1,0:T(8,128)(2,1)S(1)}, u32[]{:S(2)}, u32[]{:S(2)}) collective-permute-start(bf16[64,768]{1,0:T(8,128)(2,1)S(1)} %add_convert_fusion.33.one), channel_id=1, source_target_pairs={{0,4},{4,0},{8,12},{12,8},{16,20},{20,16},{24,28},{28,24},{1,5},{5... | collective-permute-start | bytes 294920 | tf_op jit(solution)/shard_map/ppermute | solution.py:33
  720.3 33.1 %collective-permute-start.101 = (bf16[64,768]{1,0:T(8,128)(2,1)S(1)}, bf16[64,768]{1,0:T(8,128)(2,1)S(1)}, u32[]{:S(2)}, u32[]{:S(2)}) collective-permute-start(bf16[64,768]{1,0:T(8,128)(2,1)S(1)} %add_convert_fusion.33.one), channel_id=1, source_target_pairs={{0,2},{1,3},{2,0},{3,1},{4,6},{5,7},{6,4},{7,5},{8,10},{9,11},{10,... | collective-permute-start | bytes 294920 | tf_op jit(solution)/shard_map/ppermute | solution.py:30
  729.2 69.7 %collective-permute-start.168 = (bf16[192,768]{1,0:T(8,128)(2,1)}, bf16[192,768]{1,0:T(8,128)(2,1)}, u32[]{:S(2)}, u32[]{:S(2)}) collective-permute-start(bf16[192,768]{1,0:T(8,128)(2,1)} %get-tuple-element.286), channel_id=1, source_target_pairs={{0,4},{4,0},{8,12},{12,8},{16,20},{20,16},{24,28},{28,24},{1,5},{5... | collective-permute-start | bytes 884744 | tf_op jit(solution)/shard_map/ppermute | solution.py:33
  749.7 50.3 %collective-permute-start.174 = (bf16[192,768]{1,0:T(8,128)(2,1)}, bf16[192,768]{1,0:T(8,128)(2,1)}, u32[]{:S(2)}, u32[]{:S(2)}) collective-permute-start(bf16[192,768]{1,0:T(8,128)(2,1)} %get-tuple-element.287), channel_id=1, source_target_pairs={{0,8},{4,12},{8,0},{12,4},{16,24},{20,28},{24,16},{28,20},{1,9},{5... | collective-permute-start | bytes 884744 | tf_op jit(solution)/shard_map/ppermute | solution.py:33
  751.4 51.9 %collective-permute-start.194 = (bf16[192,768]{1,0:T(8,128)(2,1)}, bf16[192,768]{1,0:T(8,128)(2,1)}, u32[]{:S(2)}, u32[]{:S(2)}) collective-permute-start(bf16[192,768]{1,0:T(8,128)(2,1)} %get-tuple-element.278), channel_id=1, source_target_pairs={{0,4},{4,0},{8,12},{12,8},{16,20},{20,16},{24,28},{28,24},{1,5},{5... | collective-permute-start | bytes 884744 | tf_op jit(solution)/shard_map/ppermute | solution.py:33
  777.9 26.3 %collective-permute-start.200 = (bf16[192,768]{1,0:T(8,128)(2,1)}, bf16[192,768]{1,0:T(8,128)(2,1)}, u32[]{:S(2)}, u32[]{:S(2)}) collective-permute-start(bf16[192,768]{1,0:T(8,128)(2,1)} %get-tuple-element.279), channel_id=1, source_target_pairs={{0,8},{4,12},{8,0},{12,4},{16,24},{20,28},{24,16},{28,20},{1,9},{5... | collective-permute-start | bytes 884744 | tf_op jit(solution)/shard_map/ppermute | solution.py:33
  793.3 26.9 %collective-permute-start.104 = (bf16[4,64,768]{2,1,0:T(8,128)(2,1)S(1)}, bf16[4,64,768]{2,1,0:T(8,128)(2,1)S(1)}, u32[]{:S(2)}, u32[]{:S(2)}) collective-permute-start(bf16[4,64,768]{2,1,0:T(8,128)(2,1)S(1)} %select_convert_fusion.2), channel_id=1, source_target_pairs={{0,1},{1,0},{2,3},{3,2},{4,5},{5,4},{6,7},{7,6},{8,9},{9,8},{10,11... | collective-permute-start | bytes 1179656 | tf_op jit(solution)/shard_map/ppermute | solution.py:30
  798.8 50.8 %collective-permute-start.105 = (bf16[576,768]{1,0:T(8,128)(2,1)}, bf16[576,768]{1,0:T(8,128)(2,1)S(1)}, u32[]{:S(2)}, u32[]{:S(2)}) collective-permute-start(bf16[576,768]{1,0:T(8,128)(2,1)} %bitcast.363), channel_id=1, source_target_pairs={{0,2},{1,3},{2,0},{3,1},{4,6},{5,7},{6,4},{7,5},{8,10},{9,11},{10,... | collective-permute-start | bytes 2654216 | tf_op jit(solution)/shard_map/ppermute | solution.py:30
  841.6 21.1 %collective-permute-start.179 = (bf16[192,768]{1,0:T(8,128)(2,1)S(1)}, bf16[192,768]{1,0:T(8,128)(2,1)S(1)}, u32[]{:S(2)}, u32[]{:S(2)}) collective-permute-start(bf16[192,768]{1,0:T(8,128)(2,1)S(1)} %pad_maximum_fusion.13), channel_id=1, source_target_pairs={{0,8},{4,12},{8,0},{12,4},{16,24},{20,28},{24,16},{28,20},{1,9},{5... | collective-permute-start | bytes 884744 | tf_op jit(solution)/shard_map/ppermute | solution.py:33
  (419 other events, 3832.1 us)

commit v2 on v1

--- a/solution.py
+++ b/solution.py
@@ -595,7 +595,11 @@
     q_bias = ordered(query_bias, rest[0], 1).reshape(layers, -1)
     v_bias = ordered(value_bias, rest[1], 1).reshape(layers, -1)
     taps = ordered(conv_taps, rest[2].reshape(conv_taps.shape), 1).reshape(layers, 2 * heads, -1)
-    return q_bias, v_bias, taps, rest[3]
+    return q_bias, v_bias, taps, ordered(up_bias, rest[3], 1)
+
+
+def across_gather(values):
+    return lax.all_gather(values, "head", axis=0, axis_index_groups=[[0, 2], [1, 3]])
 
 
 def fetch_layer(query_weight, key_weight, value_weight, out_weight, up_weight, down_weight):
@@ -605,11 +609,12 @@
     attn = ordered(mine.reshape(split), other.reshape(split), 1)
     attn = attn.reshape(2 * mine.shape[0], mine.shape[1])
     split_at = attn.shape[0] * 3 // 4
+    ffn = across_gather(jnp.concatenate([up_weight, down_weight], axis=0))
     return dict(
         qkv=attn[:split_at],
         out=attn[split_at:],
-        up=[up_weight, exchange(up_weight, 0, 2)],
-        down=[down_weight, exchange(down_weight, 0, 2)],
+        up=ffn[:, : up_weight.shape[0]],
+        down=ffn[:, up_weight.shape[0] :],
     )
 
 
@@ -690,15 +695,12 @@
     resid_one = hidden + (pair_collect(terms) + params["out_bias"])
     normed = layer_norm(resid_one, params["gain_one"], params["shift_one"])
     h_full = pair_join(normed.astype(LOW), 1).reshape(tokens, model)
-    gelu_low, slopes = [], []
-    for weight, bias in zip(weights["up"], params["up_bias"]):
-        up_pre = nn(h_full, weight) + bias
-        area = 0.5 * (1.0 + lax.erf(up_pre * 0.7071067811865476))
-        bell = jnp.exp(-0.5 * up_pre * up_pre) * 0.3989422804014327
-        gelu_low.append((up_pre * area).astype(LOW))
-        slopes.append((area + up_pre * bell).astype(LOW))
-    down = weights["down"]
-    terms = nn(gelu_low[0], down[0]) + nn(gelu_low[1], down[1])
+    up_pre = dot("td,gdf->gtf", h_full, weights["up"]) + params["up_bias"][:, None, :]
+    area = 0.5 * (1.0 + lax.erf(up_pre * 0.7071067811865476))
+    bell = jnp.exp(-0.5 * up_pre * up_pre) * 0.3989422804014327
+    gelu_low = (up_pre * area).astype(LOW)
+    slopes = (area + up_pre * bell).astype(LOW)
+    terms = dot("gtf,gfd->td", gelu_low, weights["down"])
     mlp_out = pair_collect(terms.reshape(batch_rows, tok_row, model)) + params["down_bias"]
     resid_two = normed + mlp_out
     result = layer_norm(resid_two, params["gain_two"], params["shift_two"])
@@ -737,16 +739,13 @@
     grad_mlp = grad_two.astype(LOW)
     grad_down_bias = jnp.sum(grad_mlp.astype(jnp.float32), axis=(0, 1))
     grad_mlp_full = pair_join(grad_mlp, 1).reshape(tokens, model)
-    grad_up = [
-        (nt(grad_mlp_full, weight) * slope.astype(jnp.float32)).astype(LOW)
-        for weight, slope in zip(weights["down"], kept["slopes"])
-    ]
-    up = weights["up"]
-    terms = nt(grad_up[0], up[0]) + nt(grad_up[1], up[1])
+    grad_up = dot("td,gfd->gtf", grad_mlp_full, weights["down"])
+    grad_up = (grad_up * kept["slopes"].astype(jnp.float32)).astype(LOW)
+    terms = dot("gtf,gdf->td", grad_up, weights["up"])
     grad_normed = grad_two + pair_collect(terms.reshape(batch_rows, tok_row, model))
-    down_sum = reduce_big([tn(g, grad_mlp_full) for g in kept["gelu_low"]])
-    up_sum = reduce_big([tn(kept["h_full"], g) for g in grad_up])
-    grad_up_bias = [jnp.sum(g.astype(jnp.float32), axis=0) for g in grad_up]
+    down_grad = across_sum(sides(dot("gtf,td->gfd", kept["gelu_low"], grad_mlp_full)))
+    up_grad = across_sum(sides(dot("td,gtf->gdf", kept["h_full"], grad_up)))
+    grad_up_bias = sides(jnp.sum(grad_up.astype(jnp.float32), axis=1))
     unused_one, pull_one = jax.vjp(
         layer_norm, kept["resid_one"], params["gain_one"], params["shift_one"]
     )
@@ -780,7 +779,7 @@
     )
     mix_grads = spread_row(own_mix_grad)
     grad_out_weight = nn(kept["att_low"], grad_attn_full)
-    out_sum = reduce_big(split_across(grad_out_weight.reshape(1, width, model)))
+    out_grad = across_sum(split_across(grad_out_weight.reshape(1, width, model)))
     conv_grad, tap_grad = on_core(
         functools.partial(conv_back_kernel, half),
         [((width, tokens), jnp.float32), ((8, 128), jnp.float32)],
@@ -829,7 +828,7 @@
     terms = tn(grad_qkv, weights["qkv"]).reshape(batch_rows, tok_row, model)
     grad_hidden = grad_one + pair_collect(terms)
     grad_weight = nn(grad_qkv, kept["x_full"]).reshape(3, width, model)
-    qkv_sum = reduce_big(split_across(grad_weight))
+    qkv_grad = across_sum(split_across(grad_weight))
     grad_bias = jnp.sum(grad_qkv.astype(jnp.float32), axis=1)
     heads = width // LANDMARKS
     mids = [
@@ -846,7 +845,18 @@
         grad_gain_two,
         grad_shift_two,
     ]
-    return grad_hidden, (qkv_sum, out_sum, up_sum, down_sum), mids, smalls
+    return grad_hidden, (qkv_grad, out_grad, up_grad, down_grad), mids, smalls
+
+
+def sides(values):
+    across = place()[1]
+    return [jnp.where(across == 0, values[0], values[1]), jnp.where(across == 0, values[1], values[0])]
+
+
+def across_sum(pair):
+    mine, theirs = pair
+    got = exchange(theirs.astype(LOW), 0, 2).astype(jnp.float32)
+    return (mine + got).astype(LOW)
 
 
 def split_flat(values):
@@ -882,10 +892,7 @@
     return jnp.concatenate([low, high], axis=0)
 
 
-def reduce_big(pair):
-    mine, theirs = pair
-    got = exchange(theirs.astype(LOW), 0, 2).astype(jnp.float32)
-    total = (mine + got).astype(LOW)
+def reduce_big(total):
     masks = [1 << i for i in range(lax.axis_size("seq").bit_length() - 1)]
     rows = total.shape[0]
     extra = -rows % (2 * lax.axis_size("seq"))
@@ -899,7 +906,7 @@
         for mask in reversed(order):
             part = double(part, mask)
         done.append(part)
-    return jnp.concatenate(done, axis=0)[:rows].astype(jnp.float32)
+    return jnp.concatenate(done, axis=0)[:rows]
 
 
 def seq_sum(values):
@@ -956,7 +963,7 @@
     tok_row = hidden_in.shape[1] * 2
     half = (conv_taps.shape[2] - 1) // 2
     layout = item_layout(item_lengths, tok_row, half)
-    q_bias, v_bias, taps, other_up = fetch_small(query_bias, value_bias, conv_taps, up_bias)
+    q_bias, v_bias, taps, both_up = fetch_small(query_bias, value_bias, conv_taps, up_bias)
     params = []
     for i in range(2):
         params.append(
@@ -973,7 +980,7 @@
                 q_bias=q_bias[i],
                 v_bias=v_bias[i],
                 lines=tap_lines(taps[i]),
-                up_bias=[up_bias[i], other_up[i]],
+                up_bias=both_up[i],
                 out_bias=out_bias[i],
                 down_bias=down_bias[i],
                 gain_one=gain_one[i],
@@ -989,14 +996,30 @@
     grad = out_grad
     big, mid, small = [None, None], [None, None], [None, None]
     for i in (1, 0):
-        grad, big[i], mid_i, small_i = layer_backward(grad, kept[i], params[i], layout)
-        mid[i], small[i] = reduce_small(mid_i, small_i)
-    mids = [jnp.stack([one, two]) for one, two in zip(*mid)]
-    smalls = [jnp.stack([one, two]) for one, two in zip(*small)]
+        grad, grads, mid[i], small[i] = layer_backward(grad, kept[i], params[i], layout)
+        if i == 1:
+            big[i] = lax.psum(grads, "seq")
+        else:
+            qkv_grad, out_grad_one, up_grad, down_grad = grads
+            rows = [out_grad_one.shape[0], up_grad.shape[0]]
+            early = reduce_big(jnp.concatenate([out_grad_one, up_grad, down_grad], axis=0))
+            late = reduce_big(qkv_grad)
+            big[i] = (
+                late,
+                early[: rows[0]],
+                early[rows[0] : rows[0] + rows[1]],
+                early[rows[0] + rows[1] :],
+            )
+    mids, smalls = reduce_small(
+        [[jnp.stack(m) for m in zip(*pairs)] for pairs in zip(*mid)],
+        [jnp.stack(pair) for pair in zip(*small)],
+    )
     width = query_weight.shape[2]
     qkv = jnp.stack([big[0][0], big[1][0]]).reshape(2, 3, width, -1)
-    qkv = [jnp.swapaxes(qkv[:, i], 1, 2) for i in range(3)]
-    outs, ups, downs = [jnp.stack([big[0][i], big[1][i]]) for i in (1, 2, 3)]
+    qkv = [jnp.swapaxes(qkv[:, i], 1, 2).astype(jnp.float32) for i in range(3)]
+    outs, ups, downs = [
+        jnp.stack([big[0][i], big[1][i]]).astype(jnp.float32) for i in (1, 2, 3)
+    ]
     return (
         hidden.astype(LOW),
         grad,

time: 909 us -> 794 us (0.87)
  starting transfers between devices: 255 us -> 165 us
  waiting for transfers between devices: 343 us -> 278 us
  between operations: 6.51 us -> 19.4 us
  other arithmetic: 83.1 us -> 94.1 us
  matrix products: 51.1 us -> 60.5 us
    ppermute x142 -> x67, starting transfers between devices: 175 us -> 83.4 us  [exchange(): lax.ppermute(values, 'seq', [(i, i ^ seq_mask) for i in range(count)])]
    ppermute x142 -> x67, waiting for transfers between devices: 162 us -> 110 us  [exchange(): lax.ppermute(values, 'seq', [(i, i ^ seq_mask) for i in range(count)])]
    dot_general x0 -> x12, matrix products: none -> 39.8 us  [dot(): return jnp.einsum(spec, one, two, preferred_element_type=jnp.float32)]
    convert_element_type x8 -> x15, other arithmetic: 6.56 us -> 33.9 us  [the longest x6 13.9 us: across_sum(): got = exchange(theirs.astype(LOW), 0, 2).astype(jnp.float32)]
    ppermute x53 -> x47, waiting for transfers between devices: 169 us -> 143 us  [exchange(): lax.ppermute(values, 'head', [(i, i ^ head_mask) for i in range(count)])]
    dot_general x12 -> x4, matrix products: 24.1 us -> 8.59 us  [tn(): lax.dot_general(one, two, (((0,), (0,)), ((), ())), precision, preferred_...]
    ppermute x16, waiting for transfers between devices: 12.2 us -> 24.8 us  [exchange(): return lax.ppermute(values, ('seq', 'head'), route)]
    dot_general x14 -> x6, matrix products: 14.2 us -> 4.28 us  [nt(): lax.dot_general(one, two, (((1,), (1,)), ((), ())), precision, preferred_...]
  transfers between devices with their start and end apart: 219 -> 141, of which waited for: 98 -> 52; matrix products, arithmetic and copies ran while one was open for 15% -> 19% of each run, Pallas kernels for 8% -> 11%
where the time goes in v2:
time: 794 us; the launch traced here: 786 us
  waiting for transfers between devices  278 us (35%)
  starting transfers between devices  165 us (21%)
  other arithmetic  94.1 us (12%)
  Pallas kernels  92.5 us (12%)
  local copies, waits for them, and re-layouts  76.3 us (10%)
  matrix products  60.5 us (8%)
  between operations  19.4 us (2%)
    ppermute x47, waiting for transfers between devices, exchange(): lax.ppermute(values, 'head', [(i, i ^ head_mask) for i in range(count)])  143 us
    ppermute x67, waiting for transfers between devices, exchange(): lax.ppermute(values, 'seq', [(i, i ^ seq_mask) for i in range(count)])  110 us
    pallas_call x24, Pallas kernels, on_core(): pl.pallas_call(kernel, out_shape=shapes, in_specs=specs, out_specs=tuple(...  92.5 us
    ppermute x67, starting transfers between devices, exchange(): lax.ppermute(values, 'seq', [(i, i ^ seq_mask) for i in range(count)])  83.4 us
    dot_general x12, matrix products, dot(): return jnp.einsum(spec, one, two, preferred_element_type=jnp.float32)  39.8 us
    unnamed x502, local copies, waits for them, and re-layouts  37.9 us
    ppermute x47, starting transfers between devices, exchange(): lax.ppermute(values, 'head', [(i, i ^ head_mask) for i in range(count)])  35.1 us
    ppermute x16, starting transfers between devices, exchange(): return lax.ppermute(values, ('seq', 'head'), route)  30.2 us
  transfers between devices with their start and end apart: 141, of which 52 were waited for; matrix products, arithmetic and copies ran while one was open for 19% of the time, Pallas kernels for 11%

profile of v2, /device:TPU:0, one launch (start us, length us, event | category | flops | bytes accessed | tf_op | source)
XLA Modules:
  0.0 786.0 jit_solution(10224132813643190033)
XLA Ops:
  9.0 3.0 collective-permute-start.2
  30.9 28.6 %collective-permute-done.3 = bf16[64,384]{1,0:T(8,128)(2,1)S(1)} collective-permute-done((bf16[64,384]{1,0:T(8,128)(2,1)S(1)}, bf16[64,384]{1,0:T(8,128)(2,1)S(1)}, u32[]{:S(2)}, u32[]{:S(2)}) %collective-permute-start.3) | collective-permute-done | bytes 49184 | tf_op jit(solution)/shard_map/ppermute | solution.py:30
  62.2 3.9 collective-permute-start.8
  86.2 3.9 shard_map.323
  93.9 5.5 collective-permute-done.15.refs_1_
  99.4 6.0 collective-permute-done.17.refs_3_
  115.8 5.0 shard_map.325
  126.3 3.7 collective-permute-start.23
  134.8 3.2 shard_map.327
  145.4 5.1 fusion.19
  165.1 29.2 %collective-permute-done.27 = bf16[768,768]{1,0:T(8,128)(2,1)} collective-permute-done((bf16[768,768]{1,0:T(8,128)(2,1)}, bf16[768,768]{1,0:T(8,128)(2,1)}, u32[]{:S(2)}, u32[]{:S(2)}) %collective-permute-start.27) | collective-permute-done | bytes 1179680 | tf_op jit(solution)/shard_map/ppermute | solution.py:30
  206.0 3.4 collective-permute-start.37
  216.7 3.9 shard_map.329
  224.2 5.6 collective-permute-done.41.refs_1_
  229.8 6.8 collective-permute-done.43.refs_3_
  245.5 5.0 shard_map.331
  256.8 3.5 collective-permute-start.49
  265.1 3.2 shard_map.333
  278.9 5.2 fusion.15
  300.9 4.2 convert_reduce_fusion
  307.1 3.6 fusion.128
  312.6 3.6 convolution_bitcast_fusion
  317.8 5.5 shard_map.334
  326.9 5.2 fusion.54
  332.1 3.7 collective-permute-start.63
  339.1 3.6 collective-permute-start.56
  344.9 3.3 collective-permute-start.66
  352.4 5.7 shard_map.335
  358.1 4.5 shard_map.337
  366.9 40.0 %collective-permute-done.67 = bf16[64,768]{1,0:T(8,128)(2,1)S(1)} collective-permute-done((bf16[64,768]{1,0:T(8,128)(2,1)S(1)}, bf16[64,768]{1,0:T(8,128)(2,1)S(1)}, u32[]{:S(2)}, u32[]{:S(2)}) %collective-permute-start.67) | collective-permute-done | bytes 98336 | tf_op jit(solution)/shard_map/ppermute | solution.py:30
  409.6 13.0 %shard_map.338 = f32[64,768]{1,0:T(8,128)S(1)} custom-call(f32[64,384]{1,0:T(8,128)S(1)} %select_add_fusion.1.grads, f32[64,384]{1,0:T(8,128)S(1)} %copy-done.61, bf16[64,768]{1,0:T(8,128)(2,1)S(1)} %copy-done.28, f32[6,64,64]{2,1,0:T(8,128)S(1)} %copy-done.73, f32[42,64,64]{2,1,0:T(8,128)S(1)} %copy-done.5, f32[36,64,64]{2,1,0:T(8,128)S(1)} %copy-done.20, ...), custom_call_target="tpu_custom_call" | custom-call | tf_op jit(solution)/shard_map/pallas_call | solution.py:112
  435.0 4.1 fusion.56
  447.8 3.2 fusion.123
  462.1 3.6 fusion.127
  465.8 4.0 convert_reduce_fusion.1
  472.4 3.6 convolution_bitcast_fusion.1
  478.9 5.7 fusion.52
  493.4 6.3 shard_map.340
  507.8 6.8 collective-permute-done.82
  526.7 3.6 collective-permute-done.86
  536.2 5.7 shard_map.341
  544.1 5.2 shard_map.343
  551.5 4.7 collective-permute-start.92
  556.2 15.1 %collective-permute-done.91 = bf16[64,768]{1,0:T(8,128)(2,1)S(1)} collective-permute-done((bf16[64,768]{1,0:T(8,128)(2,1)S(1)}, bf16[64,768]{1,0:T(8,128)(2,1)S(1)}, u32[]{:S(2)}, u32[]{:S(2)}) %collective-permute-start.91) | collective-permute-done | bytes 98336 | tf_op jit(solution)/shard_map/ppermute | solution.py:30
  571.4 4.8 collective-permute-start.93
  582.1 13.0 %shard_map.344 = f32[64,768]{1,0:T(8,128)S(1)} custom-call(f32[64,384]{1,0:T(8,128)S(1)} %select_add_fusion.grads, f32[64,384]{1,0:T(8,128)S(1)} %copy-done.59, bf16[64,768]{1,0:T(8,128)(2,1)S(1)} %copy-done.26, f32[6,64,64]{2,1,0:T(8,128)S(1)} %copy-done.71, f32[42,64,64]{2,1,0:T(8,128)S(1)} %copy-done.3, f32[36,64,64]{2,1,0:T(8,128)S(1)} %copy-done.14, ...), custom_call_target="tpu_custom_call" | custom-call | tf_op jit(solution)/shard_map/pallas_call | solution.py:112
  600.8 3.5 collective-permute-done.96
  604.3 9.3 %collective-permute-done.95 = bf16[64,768]{1,0:T(8,128)(2,1)S(1)} collective-permute-done((bf16[64,768]{1,0:T(8,128)(2,1)S(1)}, bf16[64,768]{1,0:T(8,128)(2,1)S(1)}, u32[]{:S(2)}, u32[]{:S(2)}) %collective-permute-start.95) | collective-permute-done | bytes 98336 | tf_op jit(solution)/shard_map/ppermute | solution.py:33
  617.3 3.1 fusion.25
  631.4 3.0 fusion.124
  635.9 3.6 slice_select_fusion.1
  642.7 14.7 %collective-permute-done.117 = f32[12288]{0:T(1024)S(1)} collective-permute-done((f32[12288]{0:T(1024)S(1)}, f32[12288]{0:T(1024)S(1)}, u32[]{:S(2)}, u32[]{:S(2)}) %collective-permute-start.117) | collective-permute-done | bytes 49184 | tf_op jit(solution)/shard_map/ppermute | solution.py:33
  659.3 3.2 collective-permute-done.118
  676.6 4.0 collective-permute-done.101
  685.9 4.4 collective-permute-done.131
  692.8 4.0 collective-permute-done.132
  698.4 4.0 collective-permute-done.123
  705.8 11.9 %collective-permute-done.109 = bf16[72,768]{1,0:T(8,128)(2,1)S(1)} collective-permute-done((bf16[72,768]{1,0:T(8,128)(2,1)S(1)}, bf16[72,768]{1,0:T(8,128)(2,1)S(1)}, u32[]{:S(2)}, u32[]{:S(2)}) %collective-permute-start.109) | collective-permute-done | bytes 110624 | tf_op jit(solution)/shard_map/ppermute | solution.py:33
  723.4 7.6 collective-permute-done.104
  734.1 9.7 %collective-permute-done.105 = bf16[36,768]{1,0:T(8,128)(2,1)S(1)} collective-permute-done((bf16[36,768]{1,0:T(8,128)(2,1)S(1)}, bf16[36,768]{1,0:T(8,128)(2,1)S(1)}, u32[]{:S(2)}, u32[]{:S(2)}) %collective-permute-start.105) | collective-permute-done | bytes 55328 | tf_op jit(solution)/shard_map/ppermute | solution.py:33
  746.1 3.4 collective-permute-done.106
  754.4 3.7 collective-permute-done.107
  759.1 8.5 %collective-permute-done.135 = bf16[432,768]{1,0:T(8,128)(2,1)S(1)} collective-permute-done((bf16[432,768]{1,0:T(8,128)(2,1)S(1)}, bf16[432,768]{1,0:T(8,128)(2,1)S(1)}, u32[]{:S(2)}, u32[]{:S(2)}) %collective-permute-start.135) | collective-permute-done | bytes 663584 | tf_op jit(solution)/shard_map/ppermute | solution.py:33
  770.9 3.1 convert_bitcast_fusion
  (1071 shorter events, 342.4 us)
Async XLA Ops:
  7.2 138.2 %all-gather.5.cloned.1.call-start = ((), (), s32[]{:S(2)}) async-start(), calls=%async_computation | async-start | bytes 7077888 | tf_op jit(solution)/shard_map/all_gather | solution.py:602
  9.0 17.3 %collective-permute-start.2 = (f32[2,1408]{1,0:T(2,128)S(1)}, f32[2,1408]{1,0:T(2,128)S(1)}, u32[]{:S(2)}, u32[]{:S(2)}) collective-permute-start(f32[2,1408]{1,0:T(2,128)S(1)} %pad.30), channel_id=1, source_target_pairs={{0,2},{1,3},{2,0},{3,1},{4,6},{5,7},{6,4},{7,5},{8,10},{9,11},{10,... | collective-permute-start | bytes 33800 | tf_op jit(solution)/shard_map/ppermute | solution.py:30
  12.0 14.5 %collective-permute-start.1 = (bf16[4,64,768]{2,1,0:T(8,128)(2,1)}, bf16[4,64,768]{2,1,0:T(8,128)(2,1)S(1)}, u32[]{:S(2)}, u32[]{:S(2)}) collective-permute-start(bf16[4,64,768]{2,1,0:T(8,128)(2,1)} %own), channel_id=1, source_target_pairs={{0,1},{1,0},{2,3},{3,2},{4,5},{5,4},{6,7},{7,6},{8,9},{9,8},{10,11... | collective-permute-start | bytes 1179656 | tf_op jit(solution)/shard_map/ppermute | solution.py:30
  17.2 63.1 %collective-permute-start = (bf16[768,768]{1,0:T(8,128)(2,1)}, bf16[768,768]{1,0:T(8,128)(2,1)}, u32[]{:S(2)}, u32[]{:S(2)}) collective-permute-start(bf16[768,768]{1,0:T(8,128)(2,1)} %pad_maximum_fusion.5), channel_id=1, source_target_pairs={{0,2},{1,3},{2,0},{3,1},{4,6},{5,7},{6,4},{7,5},{8,10},{9,11},{10,... | collective-permute-start | bytes 3538952 | tf_op jit(solution)/shard_map/ppermute | solution.py:30
  22.1 256.8 %all-gather.7.cloned.1.call-start = ((), (), s32[]{:S(2)}) async-start(), calls=%async_computation.1 | async-start | bytes 7077888 | tf_op jit(solution)/shard_map/all_gather | solution.py:602
  27.3 32.1 %collective-permute-start.3 = (bf16[64,384]{1,0:T(8,128)(2,1)S(1)}, bf16[64,384]{1,0:T(8,128)(2,1)S(1)}, u32[]{:S(2)}, u32[]{:S(2)}) collective-permute-start(bf16[64,384]{1,0:T(8,128)(2,1)S(1)} %get-tuple-element.94), channel_id=1, source_target_pairs={{0,2},{1,3},{2,0},{3,1},{4,6},{5,7},{6,4},{7,5},{8,10},{9,11},{10,... | collective-permute-start | bytes 147464 | tf_op jit(solution)/shard_map/ppermute | solution.py:30
  28.5 30.9 %collective-permute-start.4 = (bf16[64,384]{1,0:T(8,128)(2,1)S(1)}, bf16[64,384]{1,0:T(8,128)(2,1)S(1)}, u32[]{:S(2)}, u32[]{:S(2)}) collective-permute-start(bf16[64,384]{1,0:T(8,128)(2,1)S(1)} %get-tuple-element.95), channel_id=1, source_target_pairs={{0,4},{4,0},{8,12},{12,8},{16,20},{20,16},{24,28},{28,24},{1,5},{5... | collective-permute-start | bytes 147464 | tf_op jit(solution)/shard_map/ppermute | solution.py:33
  30.0 32.1 %collective-permute-start.5 = (bf16[64,384]{1,0:T(8,128)(2,1)S(1)}, bf16[64,384]{1,0:T(8,128)(2,1)S(1)}, u32[]{:S(2)}, u32[]{:S(2)}) collective-permute-start(bf16[64,384]{1,0:T(8,128)(2,1)S(1)} %get-tuple-element.96), channel_id=1, source_target_pairs={{0,6},{1,7},{2,4},{3,5},{4,2},{5,3},{6,0},{7,1},{8,14},{9,15},{10,... | collective-permute-start | bytes 147464 | tf_op jit(solution)/shard_map/ppermute | solution.py:39
  92.2 13.1 %collective-permute-start.17 = (f32[64,512]{1,0:T(8,128)S(1)}, f32[64,512]{1,0:T(8,128)S(1)}, u32[]{:S(2)}, u32[]{:S(2)}) collective-permute-start(f32[64,512]{1,0:T(8,128)S(1)} %get-tuple-element.102), channel_id=1, source_target_pairs={{0,6},{1,7},{2,4},{3,5},{4,2},{5,3},{6,0},{7,1},{8,14},{9,15},{10,... | collective-permute-start | bytes 393224 | tf_op jit(solution)/shard_map/ppermute | solution.py:39
  106.3 18.8 %collective-permute-start.20 = (f32[64,512]{1,0:T(8,128)S(1)}, f32[64,512]{1,0:T(8,128)S(1)}, u32[]{:S(2)}, u32[]{:S(2)}) collective-permute-start(f32[64,512]{1,0:T(8,128)S(1)} %shard_map.324.refs_0_), channel_id=1, source_target_pairs={{0,24},{4,28},{8,16},{12,20},{16,8},{20,12},{24,0},{28,4},{1,25},{... | collective-permute-start | bytes 393224 | tf_op jit(solution)/shard_map/ppermute | solution.py:33
  108.0 17.1 %collective-permute-start.19 = (f32[64,512]{1,0:T(8,128)S(1)}, f32[64,512]{1,0:T(8,128)S(1)}, u32[]{:S(2)}, u32[]{:S(2)}) collective-permute-start(f32[64,512]{1,0:T(8,128)S(1)} %shard_map.324.refs_0_), channel_id=1, source_target_pairs={{0,16},{4,20},{8,24},{12,28},{16,0},{20,4},{24,8},{28,12},{1,17},{... | collective-permute-start | bytes 393224 | tf_op jit(solution)/shard_map/ppermute | solution.py:33
  108.6 16.5 %collective-permute-start.18 = (f32[64,512]{1,0:T(8,128)S(1)}, f32[64,512]{1,0:T(8,128)S(1)}, u32[]{:S(2)}, u32[]{:S(2)}) collective-permute-start(f32[64,512]{1,0:T(8,128)S(1)} %shard_map.324.refs_0_), channel_id=1, source_target_pairs={{0,8},{4,12},{8,0},{12,4},{16,24},{20,28},{24,16},{28,20},{1,9},{5... | collective-permute-start | bytes 393224 | tf_op jit(solution)/shard_map/ppermute | solution.py:33
  111.4 21.9 %collective-permute-start.13 = (bf16[384,128]{1,0:T(8,128)(2,1)S(1)}, bf16[384,128]{1,0:T(8,128)(2,1)S(1)}, u32[]{:S(2)}, u32[]{:S(2)}) collective-permute-start(bf16[384,128]{1,0:T(8,128)(2,1)S(1)} %get-tuple-element.97), channel_id=1, source_target_pairs={{0,2},{1,3},{2,4},{3,5},{4,6},{5,7},{6,8},{7,9},{8,10},{9,11},{10,... | collective-permute-start | bytes 294920 | tf_op jit(solution)/shard_map/ppermute | solution.py:53
  114.3 19.1 %collective-permute-start.14 = (bf16[384,128]{1,0:T(8,128)(2,1)S(1)}, bf16[384,128]{1,0:T(8,128)(2,1)S(1)}, u32[]{:S(2)}, u32[]{:S(2)}) collective-permute-start(bf16[384,128]{1,0:T(8,128)(2,1)S(1)} %get-tuple-element.98), channel_id=1, source_target_pairs={{2,0},{3,1},{4,2},{5,3},{6,4},{7,5},{8,6},{9,7},{10,8},{11,9},{12,... | collective-permute-start | bytes 294920 | tf_op jit(solution)/shard_map/ppermute | solution.py:53
  154.1 40.2 %collective-permute-start.27 = (bf16[768,768]{1,0:T(8,128)(2,1)}, bf16[768,768]{1,0:T(8,128)(2,1)}, u32[]{:S(2)}, u32[]{:S(2)}) collective-permute-start(bf16[768,768]{1,0:T(8,128)(2,1)} %pad_maximum_fusion.6), channel_id=1, source_target_pairs={{0,2},{1,3},{2,0},{3,1},{4,6},{5,7},{6,4},{7,5},{8,10},{9,11},{10,... | collective-permute-start | bytes 3538952 | tf_op jit(solution)/shard_map/ppermute | solution.py:30
  160.6 608.2 %all-reduce.13.cloned.1.call-start = ((), (), s32[]{:S(2)}) async-start(), calls=%async_computation.2 | async-start | bytes 7077888 | tf_op jit(solution)/shard_map/psum | solution.py:1001
  161.5 34.7 %collective-permute-start.29 = (bf16[64,384]{1,0:T(8,128)(2,1)S(1)}, bf16[64,384]{1,0:T(8,128)(2,1)S(1)}, u32[]{:S(2)}, u32[]{:S(2)}) collective-permute-start(bf16[64,384]{1,0:T(8,128)(2,1)S(1)} %get-tuple-element.107), channel_id=1, source_target_pairs={{0,2},{1,3},{2,0},{3,1},{4,6},{5,7},{6,4},{7,5},{8,10},{9,11},{10,... | collective-permute-start | bytes 147464 | tf_op jit(solution)/shard_map/ppermute | solution.py:30
  162.6 33.6 %collective-permute-start.30 = (bf16[64,384]{1,0:T(8,128)(2,1)S(1)}, bf16[64,384]{1,0:T(8,128)(2,1)S(1)}, u32[]{:S(2)}, u32[]{:S(2)}) collective-permute-start(bf16[64,384]{1,0:T(8,128)(2,1)S(1)} %get-tuple-element.108), channel_id=1, source_target_pairs={{0,4},{4,0},{8,12},{12,8},{16,20},{20,16},{24,28},{28,24},{1,5},{5... | collective-permute-start | bytes 147464 | tf_op jit(solution)/shard_map/ppermute | solution.py:33
  164.2 34.5 %collective-permute-start.31 = (bf16[64,384]{1,0:T(8,128)(2,1)S(1)}, bf16[64,384]{1,0:T(8,128)(2,1)S(1)}, u32[]{:S(2)}, u32[]{:S(2)}) collective-permute-start(bf16[64,384]{1,0:T(8,128)(2,1)S(1)} %get-tuple-element.109), channel_id=1, source_target_pairs={{0,6},{1,7},{2,4},{3,5},{4,2},{5,3},{6,0},{7,1},{8,14},{9,15},{10,... | collective-permute-start | bytes 147464 | tf_op jit(solution)/shard_map/ppermute | solution.py:39
  222.8 13.9 %collective-permute-start.43 = (f32[64,512]{1,0:T(8,128)S(1)}, f32[64,512]{1,0:T(8,128)S(1)}, u32[]{:S(2)}, u32[]{:S(2)}) collective-permute-start(f32[64,512]{1,0:T(8,128)S(1)} %get-tuple-element.115), channel_id=1, source_target_pairs={{0,6},{1,7},{2,4},{3,5},{4,2},{5,3},{6,0},{7,1},{8,14},{9,15},{10,... | collective-permute-start | bytes 393224 | tf_op jit(solution)/shard_map/ppermute | solution.py:39
  237.6 17.3 %collective-permute-start.46 = (f32[64,512]{1,0:T(8,128)S(1)}, f32[64,512]{1,0:T(8,128)S(1)}, u32[]{:S(2)}, u32[]{:S(2)}) collective-permute-start(f32[64,512]{1,0:T(8,128)S(1)} %shard_map.330.refs_0_), channel_id=1, source_target_pairs={{0,24},{4,28},{8,16},{12,20},{16,8},{20,12},{24,0},{28,4},{1,25},{... | collective-permute-start | bytes 393224 | tf_op jit(solution)/shard_map/ppermute | solution.py:33
  239.3 15.5 %collective-permute-start.45 = (f32[64,512]{1,0:T(8,128)S(1)}, f32[64,512]{1,0:T(8,128)S(1)}, u32[]{:S(2)}, u32[]{:S(2)}) collective-permute-start(f32[64,512]{1,0:T(8,128)S(1)} %shard_map.330.refs_0_), channel_id=1, source_target_pairs={{0,16},{4,20},{8,24},{12,28},{16,0},{20,4},{24,8},{28,12},{1,17},{... | collective-permute-start | bytes 393224 | tf_op jit(solution)/shard_map/ppermute | solution.py:33
  239.4 15.5 %collective-permute-start.44 = (f32[64,512]{1,0:T(8,128)S(1)}, f32[64,512]{1,0:T(8,128)S(1)}, u32[]{:S(2)}, u32[]{:S(2)}) collective-permute-start(f32[64,512]{1,0:T(8,128)S(1)} %shard_map.330.refs_0_), channel_id=1, source_target_pairs={{0,8},{4,12},{8,0},{12,4},{16,24},{20,28},{24,16},{28,20},{1,9},{5... | collective-permute-start | bytes 393224 | tf_op jit(solution)/shard_map/ppermute | solution.py:33
  242.0 20.5 %collective-permute-start.39 = (bf16[384,128]{1,0:T(8,128)(2,1)S(1)}, bf16[384,128]{1,0:T(8,128)(2,1)S(1)}, u32[]{:S(2)}, u32[]{:S(2)}) collective-permute-start(bf16[384,128]{1,0:T(8,128)(2,1)S(1)} %get-tuple-element.110), channel_id=1, source_target_pairs={{0,2},{1,3},{2,4},{3,5},{4,6},{5,7},{6,8},{7,9},{8,10},{9,11},{10,... | collective-permute-start | bytes 294920 | tf_op jit(solution)/shard_map/ppermute | solution.py:53
  244.1 18.5 %collective-permute-start.40 = (bf16[384,128]{1,0:T(8,128)(2,1)S(1)}, bf16[384,128]{1,0:T(8,128)(2,1)S(1)}, u32[]{:S(2)}, u32[]{:S(2)}) collective-permute-start(bf16[384,128]{1,0:T(8,128)(2,1)S(1)} %get-tuple-element.111), channel_id=1, source_target_pairs={{2,0},{3,1},{4,2},{5,3},{6,4},{7,5},{8,6},{9,7},{10,8},{11,9},{12,... | collective-permute-start | bytes 294920 | tf_op jit(solution)/shard_map/ppermute | solution.py:53
  332.1 12.0 %collective-permute-start.63 = (bf16[64,384]{1,0:T(8,128)(2,1)S(1)}, bf16[64,384]{1,0:T(8,128)(2,1)S(1)}, u32[]{:S(2)}, u32[]{:S(2)}) collective-permute-start(bf16[64,384]{1,0:T(8,128)(2,1)S(1)} %fusion.85), channel_id=1, source_target_pairs={{0,24},{4,28},{8,16},{12,20},{16,8},{20,12},{24,0},{28,4},{1,25},{... | collective-permute-start | bytes 147464 | tf_op jit(solution)/shard_map/ppermute | solution.py:33
  344.9 13.2 %collective-permute-start.66 = (bf16[64,512]{1,0:T(8,128)(2,1)S(1)}, bf16[64,512]{1,0:T(8,128)(2,1)S(1)}, u32[]{:S(2)}, u32[]{:S(2)}) collective-permute-start(bf16[64,512]{1,0:T(8,128)(2,1)S(1)} %shard_map.336.refs_4_), channel_id=1, source_target_pairs={{0,6},{1,7},{2,4},{3,5},{4,2},{5,3},{6,0},{7,1},{8,14},{9,15},{10,... | collective-permute-start | bytes 196616 | tf_op jit(solution)/shard_map/ppermute | solution.py:39
  350.3 84.7 %collective-permute-start.136 = (bf16[768,768]{1,0:T(8,128)(2,1)}, bf16[768,768]{1,0:T(8,128)(2,1)}, u32[]{:S(2)}, u32[]{:S(2)}) collective-permute-start(bf16[768,768]{1,0:T(8,128)(2,1)} %get-tuple-element.399), channel_id=1, source_target_pairs={{0,2},{1,3},{2,0},{3,1},{4,6},{5,7},{6,4},{7,5},{8,10},{9,11},{10,... | collective-permute-start | bytes 3538952 | tf_op jit(solution)/shard_map/ppermute | solution.py:30
  351.7 87.5 %collective-permute-start.137 = (bf16[768,768]{1,0:T(8,128)(2,1)S(1)}, bf16[768,768]{1,0:T(8,128)(2,1)}, u32[]{:S(2)}, u32[]{:S(2)}) collective-permute-start(bf16[768,768]{1,0:T(8,128)(2,1)S(1)} %get-tuple-element.400), channel_id=1, source_target_pairs={{0,2},{1,3},{2,0},{3,1},{4,6},{5,7},{6,4},{7,5},{8,10},{9,11},{10,... | collective-permute-start | bytes 3538952 | tf_op jit(solution)/shard_map/ppermute | solution.py:30
  362.7 44.2 %collective-permute-start.67 = (bf16[64,768]{1,0:T(8,128)(2,1)S(1)}, bf16[64,768]{1,0:T(8,128)(2,1)S(1)}, u32[]{:S(2)}, u32[]{:S(2)}) collective-permute-start(bf16[64,768]{1,0:T(8,128)(2,1)S(1)} %get-tuple-element.134), channel_id=1, source_target_pairs={{0,2},{1,3},{2,0},{3,1},{4,6},{5,7},{6,4},{7,5},{8,10},{9,11},{10,... | collective-permute-start | bytes 294920 | tf_op jit(solution)/shard_map/ppermute | solution.py:30
  364.1 61.6 %collective-permute-start.127 = (bf16[192,768]{1,0:T(8,128)(2,1)S(1)}, bf16[192,768]{1,0:T(8,128)(2,1)S(1)}, u32[]{:S(2)}, u32[]{:S(2)}) collective-permute-start(bf16[192,768]{1,0:T(8,128)(2,1)S(1)} %fusion.79), channel_id=1, source_target_pairs={{0,2},{1,3},{2,0},{3,1},{4,6},{5,7},{6,4},{7,5},{8,10},{9,11},{10,... | collective-permute-start | bytes 884744 | tf_op jit(solution)/shard_map/ppermute | solution.py:30
  364.9 57.7 %collective-permute-start.68 = (bf16[64,768]{1,0:T(8,128)(2,1)S(1)}, bf16[64,768]{1,0:T(8,128)(2,1)S(1)}, u32[]{:S(2)}, u32[]{:S(2)}) collective-permute-start(bf16[64,768]{1,0:T(8,128)(2,1)S(1)} %get-tuple-element.135), channel_id=1, source_target_pairs={{0,4},{4,0},{8,12},{12,8},{16,20},{20,16},{24,28},{28,24},{1,5},{5... | collective-permute-start | bytes 294920 | tf_op jit(solution)/shard_map/ppermute | solution.py:33
  406.9 15.8 %collective-permute-start.69 = (bf16[64,768]{1,0:T(8,128)(2,1)S(1)}, bf16[64,768]{1,0:T(8,128)(2,1)S(1)}, u32[]{:S(2)}, u32[]{:S(2)}) collective-permute-start(bf16[64,768]{1,0:T(8,128)(2,1)S(1)} %get-tuple-element.136), channel_id=1, source_target_pairs={{0,6},{1,7},{2,4},{3,5},{4,2},{5,3},{6,0},{7,1},{8,14},{9,15},{10,... | collective-permute-start | bytes 294920 | tf_op jit(solution)/shard_map/ppermute | solution.py:39
  457.5 30.0 %collective-permute-start.114 = (bf16[576,768]{1,0:T(8,128)(2,1)}, bf16[576,768]{1,0:T(8,128)(2,1)}, u32[]{:S(2)}, u32[]{:S(2)}) collective-permute-start(bf16[576,768]{1,0:T(8,128)(2,1)} %bitcast.92), channel_id=1, source_target_pairs={{0,2},{1,3},{2,0},{3,1},{4,6},{5,7},{6,4},{7,5},{8,10},{9,11},{10,... | collective-permute-start | bytes 2654216 | tf_op jit(solution)/shard_map/ppermute | solution.py:30
  484.6 132.7 %collective-permute-start.120 = (bf16[768,768]{1,0:T(8,128)(2,1)}, bf16[768,768]{1,0:T(8,128)(2,1)}, u32[]{:S(2)}, u32[]{:S(2)}) collective-permute-start(bf16[768,768]{1,0:T(8,128)(2,1)} %get-tuple-element.397), channel_id=1, source_target_pairs={{0,2},{1,3},{2,0},{3,1},{4,6},{5,7},{6,4},{7,5},{8,10},{9,11},{10,... | collective-permute-start | bytes 3538952 | tf_op jit(solution)/shard_map/ppermute | solution.py:30
  502.5 12.2 %collective-permute-start.82 = (bf16[64,384]{1,0:T(8,128)(2,1)S(1)}, bf16[64,384]{1,0:T(8,128)(2,1)S(1)}, u32[]{:S(2)}, u32[]{:S(2)}) collective-permute-start(bf16[64,384]{1,0:T(8,128)(2,1)S(1)} %get-tuple-element.146), channel_id=1, source_target_pairs={{0,2},{1,3},{2,0},{3,1},{4,6},{5,7},{6,4},{7,5},{8,10},{9,11},{10,... | collective-permute-start | bytes 147464 | tf_op jit(solution)/shard_map/ppermute | solution.py:30
  518.8 11.5 %collective-permute-start.86 = (bf16[64,384]{1,0:T(8,128)(2,1)S(1)}, bf16[64,384]{1,0:T(8,128)(2,1)S(1)}, u32[]{:S(2)}, u32[]{:S(2)}) collective-permute-start(bf16[64,384]{1,0:T(8,128)(2,1)S(1)} %fusion.86), channel_id=1, source_target_pairs={{0,16},{4,20},{8,24},{12,28},{16,0},{20,4},{24,8},{28,12},{1,17},{... | collective-permute-start | bytes 147464 | tf_op jit(solution)/shard_map/ppermute | solution.py:33
  532.3 11.7 %collective-permute-start.89 = (bf16[64,512]{1,0:T(8,128)(2,1)S(1)}, bf16[64,512]{1,0:T(8,128)(2,1)S(1)}, u32[]{:S(2)}, u32[]{:S(2)}) collective-permute-start(bf16[64,512]{1,0:T(8,128)(2,1)S(1)} %shard_map.342.refs_4_), channel_id=1, source_target_pairs={{0,4},{4,0},{8,12},{12,8},{16,20},{20,16},{24,28},{28,24},{1,5},{5... | collective-permute-start | bytes 196616 | tf_op jit(solution)/shard_map/ppermute | solution.py:33
  536.2 84.2 %collective-permute-start.129 = (bf16[768,768]{1,0:T(8,128)(2,1)}, bf16[768,768]{1,0:T(8,128)(2,1)}, u32[]{:S(2)}, u32[]{:S(2)}) collective-permute-start(bf16[768,768]{1,0:T(8,128)(2,1)} %get-tuple-element.398), channel_id=1, source_target_pairs={{0,2},{1,3},{2,0},{3,1},{4,6},{5,7},{6,4},{7,5},{8,10},{9,11},{10,... | collective-permute-start | bytes 3538952 | tf_op jit(solution)/shard_map/ppermute | solution.py:30
  541.9 54.7 %collective-permute-start.119 = (bf16[192,768]{1,0:T(8,128)(2,1)}, bf16[192,768]{1,0:T(8,128)(2,1)}, u32[]{:S(2)}, u32[]{:S(2)}) collective-permute-start(bf16[192,768]{1,0:T(8,128)(2,1)} %fusion.78), channel_id=1, source_target_pairs={{0,2},{1,3},{2,0},{3,1},{4,6},{5,7},{6,4},{7,5},{8,10},{9,11},{10,... | collective-permute-start | bytes 884744 | tf_op jit(solution)/shard_map/ppermute | solution.py:30
  551.5 19.9 %collective-permute-start.91 = (bf16[64,768]{1,0:T(8,128)(2,1)S(1)}, bf16[64,768]{1,0:T(8,128)(2,1)S(1)}, u32[]{:S(2)}, u32[]{:S(2)}) collective-permute-start(bf16[64,768]{1,0:T(8,128)(2,1)S(1)} %get-tuple-element.157), channel_id=1, source_target_pairs={{0,2},{1,3},{2,0},{3,1},{4,6},{5,7},{6,4},{7,5},{8,10},{9,11},{10,... | collective-permute-start | bytes 294920 | tf_op jit(solution)/shard_map/ppermute | solution.py:30
  551.5 43.5 %collective-permute-start.92 = (bf16[64,768]{1,0:T(8,128)(2,1)}, bf16[64,768]{1,0:T(8,128)(2,1)S(1)}, u32[]{:S(2)}, u32[]{:S(2)}) collective-permute-start(bf16[64,768]{1,0:T(8,128)(2,1)} %get-tuple-element.158), channel_id=1, source_target_pairs={{0,4},{4,0},{8,12},{12,8},{16,20},{20,16},{24,28},{28,24},{1,5},{5... | collective-permute-start | bytes 294920 | tf_op jit(solution)/shard_map/ppermute | solution.py:33
  571.4 23.7 %collective-permute-start.93 = (bf16[64,768]{1,0:T(8,128)(2,1)}, bf16[64,768]{1,0:T(8,128)(2,1)S(1)}, u32[]{:S(2)}, u32[]{:S(2)}) collective-permute-start(bf16[64,768]{1,0:T(8,128)(2,1)} %get-tuple-element.159), channel_id=1, source_target_pairs={{0,6},{1,7},{2,4},{3,5},{4,2},{5,3},{6,0},{7,1},{8,14},{9,15},{10,... | collective-permute-start | bytes 294920 | tf_op jit(solution)/shard_map/ppermute | solution.py:39
  595.2 18.4 %collective-permute-start.95 = (bf16[64,768]{1,0:T(8,128)(2,1)S(1)}, bf16[64,768]{1,0:T(8,128)(2,1)S(1)}, u32[]{:S(2)}, u32[]{:S(2)}) collective-permute-start(bf16[64,768]{1,0:T(8,128)(2,1)S(1)} %fusion.82), channel_id=1, source_target_pairs={{0,16},{4,20},{8,24},{12,28},{16,0},{20,4},{24,8},{28,12},{1,17},{... | collective-permute-start | bytes 294920 | tf_op jit(solution)/shard_map/ppermute | solution.py:33
  596.7 16.9 %collective-permute-start.94 = (bf16[64,768]{1,0:T(8,128)(2,1)S(1)}, bf16[64,768]{1,0:T(8,128)(2,1)S(1)}, u32[]{:S(2)}, u32[]{:S(2)}) collective-permute-start(bf16[64,768]{1,0:T(8,128)(2,1)S(1)} %fusion.82), channel_id=1, source_target_pairs={{0,8},{4,12},{8,0},{12,4},{16,24},{20,28},{24,16},{28,20},{1,9},{5... | collective-permute-start | bytes 294920 | tf_op jit(solution)/shard_map/ppermute | solution.py:33
  623.8 47.6 %collective-permute-start.130 = (bf16[432,768]{1,0:T(8,128)(2,1)}, bf16[432,768]{1,0:T(8,128)(2,1)}, u32[]{:S(2)}, u32[]{:S(2)}) collective-permute-start(bf16[432,768]{1,0:T(8,128)(2,1)} %get-tuple-element.236), channel_id=1, source_target_pairs={{0,8},{4,12},{8,0},{12,4},{16,24},{20,28},{24,16},{28,20},{1,9},{5... | collective-permute-start | bytes 1990664 | tf_op jit(solution)/shard_map/ppermute | solution.py:33
  623.8 49.2 %collective-permute-start.121 = (bf16[432,768]{1,0:T(8,128)(2,1)}, bf16[432,768]{1,0:T(8,128)(2,1)}, u32[]{:S(2)}, u32[]{:S(2)}) collective-permute-start(bf16[432,768]{1,0:T(8,128)(2,1)} %get-tuple-element.282), channel_id=1, source_target_pairs={{0,4},{4,0},{8,12},{12,8},{16,20},{20,16},{24,28},{28,24},{1,5},{5... | collective-permute-start | bytes 1990664 | tf_op jit(solution)/shard_map/ppermute | solution.py:33
  639.5 17.9 %collective-permute-start.117 = (f32[12288]{0:T(1024)S(1)}, f32[12288]{0:T(1024)S(1)}, u32[]{:S(2)}, u32[]{:S(2)}) collective-permute-start(f32[12288]{0:T(1024)S(1)} %add.706), channel_id=1, source_target_pairs={{0,8},{4,12},{8,0},{12,4},{16,24},{20,28},{24,16},{28,20},{1,9},{5... | collective-permute-start | bytes 147464 | tf_op jit(solution)/shard_map/ppermute | solution.py:33
  658.3 22.4 %collective-permute-start.101 = (bf16[576,768]{1,0:T(8,128)(2,1)}, bf16[576,768]{1,0:T(8,128)(2,1)}, u32[]{:S(2)}, u32[]{:S(2)}) collective-permute-start(bf16[576,768]{1,0:T(8,128)(2,1)} %bitcast.88), channel_id=1, source_target_pairs={{0,2},{1,3},{2,0},{3,1},{4,6},{5,7},{6,4},{7,5},{8,10},{9,11},{10,... | collective-permute-start | bytes 2654216 | tf_op jit(solution)/shard_map/ppermute | solution.py:30
  673.0 17.3 %collective-permute-start.131 = (bf16[216,768]{1,0:T(8,128)(2,1)S(1)}, bf16[216,768]{1,0:T(8,128)(2,1)S(1)}, u32[]{:S(2)}, u32[]{:S(2)}) collective-permute-start(bf16[216,768]{1,0:T(8,128)(2,1)S(1)} %broadcast_select_fusion.24), channel_id=1, source_target_pairs={{0,16},{4,20},{8,24},{12,28},{16,0},{20,4},{24,8},{28,12},{1,17},{... | collective-permute-start | bytes 995336 | tf_op jit(solution)/shard_map/ppermute | solution.py:33
  674.6 17.7 %collective-permute-start.122 = (bf16[216,768]{1,0:T(8,128)(2,1)S(1)}, bf16[216,768]{1,0:T(8,128)(2,1)S(1)}, u32[]{:S(2)}, u32[]{:S(2)}) collective-permute-start(bf16[216,768]{1,0:T(8,128)(2,1)S(1)} %broadcast_select_fusion.27), channel_id=1, source_target_pairs={{0,8},{4,12},{8,0},{12,4},{16,24},{20,28},{24,16},{28,20},{1,9},{5... | collective-permute-start | bytes 995336 | tf_op jit(solution)/shard_map/ppermute | solution.py:33
  682.3 20.2 %collective-permute-start.102 = (bf16[144,768]{1,0:T(8,128)(2,1)S(1)}, bf16[144,768]{1,0:T(8,128)(2,1)S(1)}, u32[]{:S(2)}, u32[]{:S(2)}) collective-permute-start(bf16[144,768]{1,0:T(8,128)(2,1)S(1)} %get-tuple-element.285), channel_id=1, source_target_pairs={{0,4},{4,0},{8,12},{12,8},{16,20},{20,16},{24,28},{28,24},{1,5},{5... | collective-permute-start | bytes 663560 | tf_op jit(solution)/shard_map/ppermute | solution.py:33
  683.3 19.2 %collective-permute-start.108 = (bf16[144,768]{1,0:T(8,128)(2,1)S(1)}, bf16[144,768]{1,0:T(8,128)(2,1)S(1)}, u32[]{:S(2)}, u32[]{:S(2)}) collective-permute-start(bf16[144,768]{1,0:T(8,128)(2,1)S(1)} %get-tuple-element.286), channel_id=1, source_target_pairs={{0,8},{4,12},{8,0},{12,4},{16,24},{20,28},{24,16},{28,20},{1,9},{5... | collective-permute-start | bytes 663560 | tf_op jit(solution)/shard_map/ppermute | solution.py:33
  696.9 21.9 %collective-permute-start.133 = (bf16[108,768]{1,0:T(8,128)(2,1)S(1)}, bf16[108,768]{1,0:T(8,128)(2,1)S(1)}, u32[]{:S(2)}, u32[]{:S(2)}) collective-permute-start(bf16[108,768]{1,0:T(8,128)(2,1)S(1)} %add_convert_fusion.11), channel_id=1, source_target_pairs={{0,4},{4,0},{8,12},{12,8},{16,20},{20,16},{24,28},{28,24},{1,5},{5... | collective-permute-start | bytes 497672 | tf_op jit(solution)/shard_map/ppermute | solution.py:33
  702.4 19.5 %collective-permute-start.124 = (bf16[108,768]{1,0:T(8,128)(2,1)S(1)}, bf16[108,768]{1,0:T(8,128)(2,1)S(1)}, u32[]{:S(2)}, u32[]{:S(2)}) collective-permute-start(bf16[108,768]{1,0:T(8,128)(2,1)S(1)} %add_convert_fusion.12), channel_id=1, source_target_pairs={{0,16},{4,20},{8,24},{12,28},{16,0},{20,4},{24,8},{28,12},{1,17},{... | collective-permute-start | bytes 497672 | tf_op jit(solution)/shard_map/ppermute | solution.py:33
  702.7 15.0 %collective-permute-start.109 = (bf16[72,768]{1,0:T(8,128)(2,1)S(1)}, bf16[72,768]{1,0:T(8,128)(2,1)S(1)}, u32[]{:S(2)}, u32[]{:S(2)}) collective-permute-start(bf16[72,768]{1,0:T(8,128)(2,1)S(1)} %broadcast_select_fusion.46), channel_id=1, source_target_pairs={{0,16},{4,20},{8,24},{12,28},{16,0},{20,4},{24,8},{28,12},{1,17},{... | collective-permute-start | bytes 331784 | tf_op jit(solution)/shard_map/ppermute | solution.py:33
  705.7 13.0 %collective-permute-start.103 = (bf16[72,768]{1,0:T(8,128)(2,1)S(1)}, bf16[72,768]{1,0:T(8,128)(2,1)S(1)}, u32[]{:S(2)}, u32[]{:S(2)}) collective-permute-start(bf16[72,768]{1,0:T(8,128)(2,1)S(1)} %broadcast_select_fusion.49), channel_id=1, source_target_pairs={{0,8},{4,12},{8,0},{12,4},{16,24},{20,28},{24,16},{28,20},{1,9},{5... | collective-permute-start | bytes 331784 | tf_op jit(solution)/shard_map/ppermute | solution.py:33
  718.7 12.2 %collective-permute-start.104 = (bf16[36,768]{1,0:T(8,128)(2,1)S(1)}, bf16[36,768]{1,0:T(8,128)(2,1)S(1)}, u32[]{:S(2)}, u32[]{:S(2)}) collective-permute-start(bf16[36,768]{1,0:T(8,128)(2,1)S(1)} %broadcast_select_fusion.55), channel_id=1, source_target_pairs={{0,16},{4,20},{8,24},{12,28},{16,0},{20,4},{24,8},{28,12},{1,17},{... | collective-permute-start | bytes 165896 | tf_op jit(solution)/shard_map/ppermute | solution.py:33
  718.9 32.2 %collective-permute-start.134 = (bf16[216,768]{1,0:T(8,128)(2,1)S(1)}, bf16[216,768]{1,0:T(8,128)(2,1)S(1)}, u32[]{:S(2)}, u32[]{:S(2)}) collective-permute-start(bf16[216,768]{1,0:T(8,128)(2,1)S(1)} %pad_maximum_fusion.22), channel_id=1, source_target_pairs={{0,16},{4,20},{8,24},{12,28},{16,0},{20,4},{24,8},{28,12},{1,17},{... | collective-permute-start | bytes 995336 | tf_op jit(solution)/shard_map/ppermute | solution.py:33
  722.0 29.4 %collective-permute-start.125 = (bf16[216,768]{1,0:T(8,128)(2,1)S(1)}, bf16[216,768]{1,0:T(8,128)(2,1)S(1)}, u32[]{:S(2)}, u32[]{:S(2)}) collective-permute-start(bf16[216,768]{1,0:T(8,128)(2,1)S(1)} %pad_maximum_fusion.21), channel_id=1, source_target_pairs={{0,8},{4,12},{8,0},{12,4},{16,24},{20,28},{24,16},{28,20},{1,9},{5... | collective-permute-start | bytes 995336 | tf_op jit(solution)/shard_map/ppermute | solution.py:33
  731.0 12.8 %collective-permute-start.105 = (bf16[36,768]{1,0:T(8,128)(2,1)S(1)}, bf16[36,768]{1,0:T(8,128)(2,1)S(1)}, u32[]{:S(2)}, u32[]{:S(2)}) collective-permute-start(bf16[36,768]{1,0:T(8,128)(2,1)S(1)} %add_convert_fusion.18), channel_id=1, source_target_pairs={{0,16},{4,20},{8,24},{12,28},{16,0},{20,4},{24,8},{28,12},{1,17},{... | collective-permute-start | bytes 165896 | tf_op jit(solution)/shard_map/ppermute | solution.py:33
  731.2 14.4 %collective-permute-start.112 = (bf16[72,768]{1,0:T(8,128)(2,1)S(1)}, bf16[72,768]{1,0:T(8,128)(2,1)S(1)}, u32[]{:S(2)}, u32[]{:S(2)}) collective-permute-start(bf16[72,768]{1,0:T(8,128)(2,1)S(1)} %pad_maximum_fusion.28), channel_id=1, source_target_pairs={{0,16},{4,20},{8,24},{12,28},{16,0},{20,4},{24,8},{28,12},{1,17},{... | collective-permute-start | bytes 331784 | tf_op jit(solution)/shard_map/ppermute | solution.py:33
  751.3 16.4 %collective-permute-start.135 = (bf16[432,768]{1,0:T(8,128)(2,1)S(1)}, bf16[432,768]{1,0:T(8,128)(2,1)S(1)}, u32[]{:S(2)}, u32[]{:S(2)}) collective-permute-start(bf16[432,768]{1,0:T(8,128)(2,1)S(1)} %pad_maximum_fusion.17), channel_id=1, source_target_pairs={{0,8},{4,12},{8,0},{12,4},{16,24},{20,28},{24,16},{28,20},{1,9},{5... | collective-permute-start | bytes 1990664 | tf_op jit(solution)/shard_map/ppermute | solution.py:33
  751.6 16.7 %collective-permute-start.126 = (bf16[432,768]{1,0:T(8,128)(2,1)S(1)}, bf16[432,768]{1,0:T(8,128)(2,1)S(1)}, u32[]{:S(2)}, u32[]{:S(2)}) collective-permute-start(bf16[432,768]{1,0:T(8,128)(2,1)S(1)} %pad_maximum_fusion.16), channel_id=1, source_target_pairs={{0,4},{4,0},{8,12},{12,8},{16,20},{20,16},{24,28},{28,24},{1,5},{5... | collective-permute-start | bytes 1990664 | tf_op jit(solution)/shard_map/ppermute | solution.py:33
  (326 other events, 2631.1 us)
Sparse Core Ops, SparseCore 0:
  22.2 84.2 all-gather.4
  160.7 82.1 all-gather.6
  490.2 164.4 all-reduce.12

commit v3 on v2

--- a/solution.py
+++ b/solution.py
@@ -104,7 +104,7 @@
     )
 
 
-def on_core(kernel, outs, scalars, *arrays):
+def on_core(kernel, outs, scalars, *arrays, us=1):
     shapes = tuple(jax.ShapeDtypeStruct(shape, dtype) for shape, dtype in outs)
     specs = [pl.BlockSpec(memory_space=pltpu.SMEM)] if scalars is not None else []
     specs += [pl.BlockSpec(memory_space=pltpu.VMEM)] * len(arrays)
@@ -115,6 +115,9 @@
         in_specs=specs,
         out_specs=tuple(pl.BlockSpec(memory_space=pltpu.VMEM) for _ in outs),
         compiler_params=pltpu.CompilerParams(vmem_limit_bytes=48 * 1024 * 1024),
+        cost_estimate=pl.CostEstimate(
+            flops=us * 10**9, bytes_accessed=us * 3 * 10**6, transcendentals=0
+        ),
     )(*given)
 
 
@@ -508,11 +511,18 @@
     return [row] + [exchange(row, s, h) for s, h in GROUP]
 
 
-def item_sum(pieces, layout):
+def item_sum(pieces, layout, beside=None):
+    return item_total(send_rows(pieces), layout, beside)
+
+
+def item_total(pieces, layout, beside=None):
     span = layout["span"]
     dtype = pieces[0].dtype
-    pieces = [piece.astype(jnp.float32) for piece in send_rows(pieces)]
+    pieces = [piece.astype(jnp.float32) for piece in pieces]
     total = (pieces[0] + pieces[1]) + (pieces[2] + pieces[3])
+    if beside is not None:
+        beside, total = tied(beside, total)
+        beside = exchange(beside, 0, 2)
     for low, bits in upper_levels():
         sent = total.astype(dtype)
         near = exchange(sent, 2 << low, 0).astype(jnp.float32)
@@ -522,6 +532,9 @@
             cross = exchange(sent, 6 << low, 0).astype(jnp.float32)
             pair = pair + jnp.where(span > 8 << low, far + cross, 0.0)
         total = pair
+    if beside is not None:
+        beside, total = tied(beside, total)
+        return total, beside
     return total
 
 
@@ -602,20 +615,35 @@
     return lax.all_gather(values, "head", axis=0, axis_index_groups=[[0, 2], [1, 3]])
 
 
-def fetch_layer(query_weight, key_weight, value_weight, out_weight, up_weight, down_weight):
-    mine = jnp.concatenate([query_weight.T, key_weight.T, value_weight.T, out_weight], axis=0)
-    other = exchange(mine, 0, 2)
-    split = (4, -1, mine.shape[1])
-    attn = ordered(mine.reshape(split), other.reshape(split), 1)
-    attn = attn.reshape(2 * mine.shape[0], mine.shape[1])
-    split_at = attn.shape[0] * 3 // 4
-    ffn = across_gather(jnp.concatenate([up_weight, down_weight], axis=0))
-    return dict(
-        qkv=attn[:split_at],
-        out=attn[split_at:],
-        up=ffn[:, : up_weight.shape[0]],
-        down=ffn[:, up_weight.shape[0] :],
-    )
+def fetch_weights(
+    query_weight, key_weight, value_weight, out_weight, up_weight, down_weight, pooled
+):
+    model = up_weight.shape[1]
+    packs = [
+        jnp.concatenate([query_weight[i].T, key_weight[i].T, value_weight[i].T], 0)
+        for i in range(2)
+    ]
+    pack, *pooled = tied(packs[0], *pooled)
+    other = exchange(pack, 0, 2)
+    own_out, other = tied(out_weight[0], other)
+    other_out = exchange(own_out, 0, 2)
+    held = jnp.concatenate([packs[1], out_weight[1]], 0)
+    held, other_out = tied(held, other_out)
+    first = ordered(pack.reshape(3, -1, model), other.reshape(3, -1, model), 1)
+    layers = [
+        dict(
+            qkv=first.reshape(-1, model),
+            out=ordered(own_out, other_out, 0).reshape(-1, model),
+            up=up_weight[:1],
+            down=down_weight[:1],
+        ),
+        dict(
+            attn=jnp.swapaxes(across_gather(held).reshape(2, 4, -1, model), 0, 1),
+            up=across_gather(up_weight[1]),
+            down=across_gather(down_weight[1]),
+        ),
+    ]
+    return layers, pooled
 
 
 def tap_lines(taps):
@@ -628,25 +656,53 @@
     return [jnp.pad(line, ((0, pad), (0, 0))) for line in lines]
 
 
-def layer_forward(hidden, params, layout):
+def token_sets(values, own_pair):
+    own = pair_join(values, 1)
+    flat = (own.shape[0] * own.shape[1], own.shape[2])
+    if own_pair:
+        return [own.reshape(flat)]
+    return [own.reshape(flat), pair_join(exchange(values, 0, 2), 1).reshape(flat)]
+
+
+def collect_sets(terms, rows):
+    terms = [term.reshape(rows, -1, term.shape[-1]) for term in terms]
+    total = pair_collect(terms[0])
+    if len(terms) == 2:
+        total = total + exchange(pair_collect(terms[1]).astype(LOW), 0, 2).astype(jnp.float32)
+    return total
+
+
+def join_pool(hidden, layout):
+    batch_rows, piece, model = hidden.shape
+    quarter = [((LANDMARKS, model // 2), LOW)] * 4
+    x_low = hidden.astype(LOW)
+    x_full, *pooled = on_core(
+        join_pool_kernel,
+        [((batch_rows * 2 * piece, model), LOW)] + quarter,
+        layout["spot"],
+        x_low,
+        exchange(x_low, 0, 1),
+        layout["pool"],
+    )
+    return x_full, send_rows(pooled)
+
+
+def layer_forward(hidden, params, layout, joined, ahead=None):
     weights = params["weights"]
+    if params["offload"]:
+        attn = weights["attn"].reshape(-1, hidden.shape[2])
+        weights["qkv"] = attn[: attn.shape[0] * 3 // 4]
+        weights["out"] = attn[attn.shape[0] * 3 // 4 :]
     spot = layout["spot"]
     batch_rows, piece, model = hidden.shape
     tok_row = 2 * piece
     tokens = batch_rows * tok_row
     width = weights["out"].shape[0]
     half = params["half"]
-    quarter = [((LANDMARKS, model // 2), LOW)] * 4
-    x_low = hidden.astype(LOW)
-    x_full, *pooled = on_core(
-        join_pool_kernel,
-        [((tokens, model), LOW)] + quarter,
-        spot,
-        x_low,
-        exchange(x_low, 0, 1),
-        layout["pool"],
-    )
-    pooled = jnp.concatenate(spread_row(item_sum(pooled, layout).astype(LOW)), axis=0)
+    x_full, pooled = joined
+    if params["offload"]:
+        weights["up"], *pooled = tied(weights["up"], *pooled)
+    pooled = jnp.concatenate(spread_row(item_total(pooled, layout).astype(LOW)), axis=0)
     pooled = pair_join(pooled, 1)
     bias_q, bias_v = params["q_bias"], params["v_bias"]
     no_bias = jnp.zeros_like(bias_q)
@@ -658,7 +714,7 @@
     message = [((LANDMARKS, width + 128), jnp.float32)] * 4
     rim = [((width, batch_rows * half), LOW)] * 2
     *parts, low, high = on_core(
-        functools.partial(far_kernel, half), message + rim, spot, qkv, land
+        functools.partial(far_kernel, half), message + rim, spot, qkv, land, us=4
     )
     low, high = rank_shift(high, 1), rank_shift(low, -1)
     square = (LANDMARKS, LANDMARKS)
@@ -675,9 +731,12 @@
         ],
         None,
         own_land,
+        us=5,
     )
     inverse = chain[1][NS_STEPS * heads :]
     own_out, weighted = land_mixture(parts, inverse, layout)
+    if params["offload"]:
+        own_out, weights["down"] = tied(own_out, weights["down"])
     mixes = spread_row(own_out)
     (att_low,) = on_core(
         functools.partial(near_kernel, half),
@@ -690,18 +749,23 @@
         land,
         *mixes,
         params["lines"][0],
+        us=3,
     )
     terms = tn(att_low, weights["out"]).reshape(batch_rows, tok_row, model)
+    if ahead is not None:
+        terms, ahead["attn"] = tied(terms, ahead["attn"])
     resid_one = hidden + (pair_collect(terms) + params["out_bias"])
     normed = layer_norm(resid_one, params["gain_one"], params["shift_one"])
-    h_full = pair_join(normed.astype(LOW), 1).reshape(tokens, model)
-    up_pre = dot("td,gdf->gtf", h_full, weights["up"]) + params["up_bias"][:, None, :]
-    area = 0.5 * (1.0 + lax.erf(up_pre * 0.7071067811865476))
-    bell = jnp.exp(-0.5 * up_pre * up_pre) * 0.3989422804014327
-    gelu_low = (up_pre * area).astype(LOW)
-    slopes = (area + up_pre * bell).astype(LOW)
-    terms = dot("gtf,gfd->td", gelu_low, weights["down"])
-    mlp_out = pair_collect(terms.reshape(batch_rows, tok_row, model)) + params["down_bias"]
+    h_sets = token_sets(normed.astype(LOW), params["offload"])
+    gelu_low, slopes, terms = [], [], []
+    for h_full in h_sets:
+        up_pre = dot("td,gdf->gtf", h_full, weights["up"]) + params["up_bias"][:, None, :]
+        area = 0.5 * (1.0 + lax.erf(up_pre * 0.7071067811865476))
+        bell = jnp.exp(-0.5 * up_pre * up_pre) * 0.3989422804014327
+        gelu_low.append((up_pre * area).astype(LOW))
+        slopes.append((area + up_pre * bell).astype(LOW))
+        terms.append(dot("gtf,gfd->td", gelu_low[-1], weights["down"]))
+    mlp_out = collect_sets(terms, batch_rows) + params["down_bias"]
     resid_two = normed + mlp_out
     result = layer_norm(resid_two, params["gain_two"], params["shift_two"])
     kept = dict(
@@ -716,7 +780,7 @@
         mixes=mixes,
         att_low=att_low,
         resid_one=resid_one,
-        h_full=h_full,
+        h_sets=h_sets,
         gelu_low=gelu_low,
         slopes=slopes,
         resid_two=resid_two,
@@ -724,7 +788,7 @@
     return result, kept
 
 
-def layer_backward(grad_out, kept, params, layout):
+def layer_backward(grad_out, kept, params, layout, pending):
     weights = params["weights"]
     spot = layout["spot"]
     batch_rows, piece, model = grad_out.shape
@@ -738,14 +802,26 @@
     grad_two, grad_gain_two, grad_shift_two = pull_two(grad_out)
     grad_mlp = grad_two.astype(LOW)
     grad_down_bias = jnp.sum(grad_mlp.astype(jnp.float32), axis=(0, 1))
-    grad_mlp_full = pair_join(grad_mlp, 1).reshape(tokens, model)
-    grad_up = dot("td,gfd->gtf", grad_mlp_full, weights["down"])
-    grad_up = (grad_up * kept["slopes"].astype(jnp.float32)).astype(LOW)
-    terms = dot("gtf,gdf->td", grad_up, weights["up"])
-    grad_normed = grad_two + pair_collect(terms.reshape(batch_rows, tok_row, model))
-    down_grad = across_sum(sides(dot("gtf,td->gfd", kept["gelu_low"], grad_mlp_full)))
-    up_grad = across_sum(sides(dot("td,gtf->gdf", kept["h_full"], grad_up)))
-    grad_up_bias = sides(jnp.sum(grad_up.astype(jnp.float32), axis=1))
+    grad_sets = token_sets(grad_mlp, params["offload"])
+    grad_ups, terms = [], []
+    for grad_set, slope in zip(grad_sets, kept["slopes"]):
+        grad_up = dot("td,gfd->gtf", grad_set, weights["down"])
+        grad_ups.append((grad_up * slope.astype(jnp.float32)).astype(LOW))
+        terms.append(dot("gtf,gdf->td", grad_ups[-1], weights["up"]))
+    grad_normed = grad_two + collect_sets(terms, batch_rows)
+    down_grad = sum(dot("gtf,td->gfd", g, d) for g, d in zip(kept["gelu_low"], grad_sets))
+    up_grad = sum(dot("td,gtf->gdf", h, g) for h, g in zip(kept["h_sets"], grad_ups))
+    ffn_grad = jnp.concatenate([up_grad, down_grad], axis=1).astype(LOW)
+    grad_up_bias = sum(jnp.sum(g.astype(jnp.float32), axis=1) for g in grad_ups)
+    if params["offload"]:
+        ffn_grad = seq_scatter(ffn_grad)
+        grad_up_bias = sides(grad_up_bias)
+    else:
+        ffn_one, attn_one = pending
+        rows = attn_one.shape[1]
+        packed = jnp.stack([attn_one[0], attn_one[1], ffn_grad[0, :rows], ffn_grad[0, rows:]])
+        ffn_grad = (ffn_one, seq_scatter(packed))
+        grad_up_bias = [grad_up_bias[0], jnp.zeros_like(grad_up_bias[0])]
     unused_one, pull_one = jax.vjp(
         layer_norm, kept["resid_one"], params["gain_one"], params["shift_one"]
     )
@@ -765,6 +841,7 @@
         grad_att,
         land,
         *mixes,
+        us=6,
     )
     near_outs, near_keys, (low, high) = rest[:4], rest[4:8], rest[8:]
     low, high = rank_shift(high, 1), rank_shift(low, -1)
@@ -778,8 +855,10 @@
         kept["weighted"],
     )
     mix_grads = spread_row(own_mix_grad)
+    if pending is not None:
+        ffn_one, *mix_grads = tied(ffn_grad[0], *mix_grads)
+        ffn_grad = (ffn_one, ffn_grad[1])
     grad_out_weight = nn(kept["att_low"], grad_attn_full)
-    out_grad = across_sum(split_across(grad_out_weight.reshape(1, width, model)))
     conv_grad, tap_grad = on_core(
         functools.partial(conv_back_kernel, half),
         [((width, tokens), jnp.float32), ((8, 128), jnp.float32)],
@@ -791,6 +870,7 @@
         high,
         layout["rims"],
         params["lines"][1],
+        us=6,
     )
     far_keys, values_low, *parts = on_core(
         far_back_kernel,
@@ -803,6 +883,7 @@
         *mixes,
         *mix_grads,
         *near_keys,
+        us=5,
     )
     (own_land_grad,) = on_core(
         inverse_back_kernel,
@@ -812,8 +893,16 @@
         kept["weighted"],
         kept["own_land"],
         *kept["chain"],
-    )
-    own_land_grad = item_sum(parts, layout) + own_land_grad
+        us=13,
+    )
+    if params["offload"]:
+        own_land_grad = item_sum(parts, layout) + own_land_grad
+    else:
+        first_grad = jnp.stack([nn(values_low, kept["x_full"]), grad_out_weight])
+        first_mine, first_theirs = split_across(first_grad)
+        land_sum, first_got = item_sum(parts, layout, first_theirs.astype(LOW))
+        own_land_grad = land_sum + own_land_grad
+        first_grad = (first_mine + first_got.astype(jnp.float32)).astype(LOW)
     land_grads = spread_row(own_land_grad.astype(LOW))
     (grad_qkv,) = on_core(
         token_grad_kernel,
@@ -827,8 +916,17 @@
     )
     terms = tn(grad_qkv, weights["qkv"]).reshape(batch_rows, tok_row, model)
     grad_hidden = grad_one + pair_collect(terms)
-    grad_weight = nn(grad_qkv, kept["x_full"]).reshape(3, width, model)
-    qkv_grad = across_sum(split_across(grad_weight))
+    if params["offload"]:
+        grad_weight = nn(grad_qkv, kept["x_full"])
+        attn_grad = jnp.concatenate([grad_weight, grad_out_weight], axis=0)
+        attn_grad = attn_grad.reshape(4, 2, width // 2, model).astype(LOW)
+        attn_grad = jnp.swapaxes(attn_grad, 0, 1).reshape(2, 2 * width, model)
+    else:
+        grad_weight = nn(grad_qkv[: 2 * width], kept["x_full"]).reshape(2, width, model)
+        attn_grad = across_sum(split_across(grad_weight))
+        attn_grad, packed = tied(attn_grad, ffn_grad[1])
+        ffn_grad = (ffn_grad[0], packed)
+        attn_grad = jnp.concatenate([attn_grad, first_grad], axis=0)
     grad_bias = jnp.sum(grad_qkv.astype(jnp.float32), axis=1)
     heads = width // LANDMARKS
     mids = [
@@ -845,12 +943,29 @@
         grad_gain_two,
         grad_shift_two,
     ]
-    return grad_hidden, (qkv_grad, out_grad, up_grad, down_grad), mids, smalls
+    return grad_hidden, (attn_grad, ffn_grad), mids, smalls
 
 
 def sides(values):
     across = place()[1]
     return [jnp.where(across == 0, values[0], values[1]), jnp.where(across == 0, values[1], values[0])]
+
+
+def seq_scatter(values):
+    return lax.psum_scatter(values, "seq", scatter_dimension=values.ndim - 2, tiled=True)
+
+
+def seq_gather(values):
+    return lax.all_gather(values, "seq", axis=0, tiled=True)
+
+
+def across_pick(values):
+    mine, theirs = sides(values)
+    return across_sum([mine.astype(jnp.float32), theirs])
+
+
+def tied(values, *others):
+    return lax.optimization_barrier((values,) + others)
 
 
 def across_sum(pair):
@@ -964,23 +1079,22 @@
     half = (conv_taps.shape[2] - 1) // 2
     layout = item_layout(item_lengths, tok_row, half)
     q_bias, v_bias, taps, both_up = fetch_small(query_bias, value_bias, conv_taps, up_bias)
+    hidden = hidden_in.astype(jnp.float32)
+    x_full, pooled = join_pool(hidden, layout)
+    weights, pooled = fetch_weights(
+        query_weight, key_weight, value_weight, out_weight, up_weight, down_weight, pooled
+    )
     params = []
     for i in range(2):
         params.append(
             dict(
-                weights=fetch_layer(
-                    query_weight[i],
-                    key_weight[i],
-                    value_weight[i],
-                    out_weight[i],
-                    up_weight[i],
-                    down_weight[i],
-                ),
+                weights=weights[i],
                 half=half,
+                offload=i == 1,
                 q_bias=q_bias[i],
                 v_bias=v_bias[i],
                 lines=tap_lines(taps[i]),
-                up_bias=both_up[i],
+                up_bias=both_up[i] if i == 1 else up_bias[:1],
                 out_bias=out_bias[i],
                 down_bias=down_bias[i],
                 gain_one=gain_one[i],
@@ -989,37 +1103,38 @@
                 shift_two=shift_two[i],
             )
         )
-    hidden = hidden_in.astype(jnp.float32)
     kept = [None, None]
     for i in range(2):
-        hidden, kept[i] = layer_forward(hidden, params[i], layout)
+        joined = (x_full, pooled) if i == 0 else join_pool(hidden, layout)
+        ahead = weights[1] if i == 0 else None
+        hidden, kept[i] = layer_forward(hidden, params[i], layout, joined, ahead)
     grad = out_grad
     big, mid, small = [None, None], [None, None], [None, None]
+    pending = None
     for i in (1, 0):
-        grad, grads, mid[i], small[i] = layer_backward(grad, kept[i], params[i], layout)
+        grad, grads, mid[i], small[i] = layer_backward(grad, kept[i], params[i], layout, pending)
         if i == 1:
-            big[i] = lax.psum(grads, "seq")
+            attn_grad, ffn_grad = grads
+            grad, ffn_grad = tied(grad, ffn_grad)
+            pending = [seq_gather(across_pick(ffn_grad)), attn_grad]
         else:
-            qkv_grad, out_grad_one, up_grad, down_grad = grads
-            rows = [out_grad_one.shape[0], up_grad.shape[0]]
-            early = reduce_big(jnp.concatenate([out_grad_one, up_grad, down_grad], axis=0))
-            late = reduce_big(qkv_grad)
-            big[i] = (
-                late,
-                early[: rows[0]],
-                early[rows[0] : rows[0] + rows[1]],
-                early[rows[0] + rows[1] :],
-            )
+            attn_grad, (ffn_one, packed) = grads
+            packed = jnp.concatenate([across_pick(packed[:2])[None], packed[2:]], axis=0)
+            packed = lax.all_gather(packed, "seq", axis=1, tiled=True)
+            big[0] = (reduce_big(attn_grad), packed[1:].reshape(-1, packed.shape[2]))
+            big[1] = (packed[0], ffn_one)
     mids, smalls = reduce_small(
         [[jnp.stack(m) for m in zip(*pairs)] for pairs in zip(*mid)],
         [jnp.stack(pair) for pair in zip(*small)],
     )
     width = query_weight.shape[2]
-    qkv = jnp.stack([big[0][0], big[1][0]]).reshape(2, 3, width, -1)
-    qkv = [jnp.swapaxes(qkv[:, i], 1, 2).astype(jnp.float32) for i in range(3)]
-    outs, ups, downs = [
-        jnp.stack([big[0][i], big[1][i]]).astype(jnp.float32) for i in (1, 2, 3)
-    ]
+    attn = jnp.stack([big[0][0], big[1][0]]).reshape(2, 4, width, -1)
+    qkv = [jnp.swapaxes(attn[:, i], 1, 2).astype(jnp.float32) for i in range(3)]
+    outs = attn[:, 3].astype(jnp.float32)
+    both = [big[0][1], big[1][1]]
+    rows = up_weight.shape[1]
+    ups = jnp.stack([one[:rows] for one in both]).astype(jnp.float32)
+    downs = jnp.stack([one[rows:] for one in both]).astype(jnp.float32)
     return (
         hidden.astype(LOW),
         grad,

time: 794 us -> 676 us (0.85)
  waiting for transfers between devices: 278 us -> 208 us
  other arithmetic: 94.1 us -> 65.3 us
  matrix products: 60.5 us -> 46 us
  starting transfers between devices: 165 us -> 153 us
  local copies, waits for them, and re-layouts: 76.3 us -> 85.4 us
    ppermute x47 -> x51, waiting for transfers between devices: 143 us -> 74.4 us  [exchange(): lax.ppermute(values, 'head', [(i, i ^ head_mask) for i in range(count)])]
    ppermute x67 -> x55, waiting for transfers between devices: 110 us -> 92.8 us  [exchange(): lax.ppermute(values, 'seq', [(i, i ^ seq_mask) for i in range(count)])]
    ppermute x67 -> x55, starting transfers between devices: 83.4 us -> 68.3 us  [exchange(): lax.ppermute(values, 'seq', [(i, i ^ seq_mask) for i in range(count)])]
    dot_general x12 -> x18, matrix products: 39.8 us -> 25.2 us  [dot(): return jnp.einsum(spec, one, two, preferred_element_type=jnp.float32)]
    ppermute x16, waiting for transfers between devices: 24.8 us -> 38.9 us  [exchange(): return lax.ppermute(values, ('seq', 'head'), route)]
    convert_element_type x6 -> x1, other arithmetic: 13.9 us -> 0.92 us  [across_sum(): got = exchange(theirs.astype(LOW), 0, 2).astype(jnp.float32)]
    slice x2 -> x10, local copies, waits for them, and re-layouts: 1.21 us -> 10.7 us  [the longest x1 2.36 us: fetch_weights(): down_weight[1]]
    ppermute x47 -> x51, starting transfers between devices: 35.1 us -> 41.4 us  [exchange(): lax.ppermute(values, 'head', [(i, i ^ head_mask) for i in range(count)])]
  transfers between devices with their start and end apart: 141 -> 137, of which waited for: 52 -> 63; matrix products, arithmetic and copies ran while one was open for 19% -> 19% of each run, Pallas kernels for 11% -> 13%
where the time goes in v3:
time: 676 us; the launch traced here: 669 us
  waiting for transfers between devices  208 us (31%)
  starting transfers between devices  153 us (23%)
  Pallas kernels  91.6 us (14%)
  local copies, waits for them, and re-layouts  85.4 us (13%)
  other arithmetic  65.3 us (10%)
  matrix products  46 us (7%)
  between operations  19.3 us (3%)
    ppermute x55, waiting for transfers between devices, exchange(): lax.ppermute(values, 'seq', [(i, i ^ seq_mask) for i in range(count)])  92.8 us
    pallas_call x24, Pallas kernels, on_core(): pl.pallas_call(kernel, out_shape=shapes, in_specs=specs, out_specs=tuple(...  91.6 us
    ppermute x51, waiting for transfers between devices, exchange(): lax.ppermute(values, 'head', [(i, i ^ head_mask) for i in range(count)])  74.4 us
    ppermute x55, starting transfers between devices, exchange(): lax.ppermute(values, 'seq', [(i, i ^ seq_mask) for i in range(count)])  68.3 us
    ppermute x51, starting transfers between devices, exchange(): lax.ppermute(values, 'head', [(i, i ^ head_mask) for i in range(count)])  41.4 us
    ppermute x16, waiting for transfers between devices, exchange(): return lax.ppermute(values, ('seq', 'head'), route)  38.9 us
    unnamed x407, local copies, waits for them, and re-layouts  34.7 us
    dot_general x18, matrix products, dot(): return jnp.einsum(spec, one, two, preferred_element_type=jnp.float32)  25.2 us
  transfers between devices with their start and end apart: 137, of which 63 were waited for; matrix products, arithmetic and copies ran while one was open for 19% of the time, Pallas kernels for 13%

profile of v3, /device:TPU:0, one launch (start us, length us, event | category | flops | bytes accessed | tf_op | source)
XLA Modules:
  0.0 668.8 jit_solution(16895881653607187857)
XLA Ops:
  9.0 3.0 collective-permute-start.5
  25.3 2.8 collective-permute-done.3
  28.2 3.7 collective-permute-start.8
  34.2 2.6 collective-permute-done.7
  40.5 13.5 %collective-permute-done.11 = bf16[64,384]{1,0:T(8,128)(2,1)S(1)} collective-permute-done((bf16[64,384]{1,0:T(8,128)(2,1)S(1)}, bf16[64,384]{1,0:T(8,128)(2,1)S(1)}, u32[]{:S(2)}, u32[]{:S(2)}) %collective-permute-start.11) | collective-permute-done | bytes 49184 | tf_op jit(solution)/shard_map/ppermute | solution.py:39
  63.1 7.0 %collective-permute-done.24 = bf16[192,768]{1,0:T(8,128)(2,1)S(1)} collective-permute-done((bf16[192,768]{1,0:T(8,128)(2,1)}, bf16[192,768]{1,0:T(8,128)(2,1)S(1)}, u32[]{:S(2)}, u32[]{:S(2)}) %collective-permute-start.24) | collective-permute-done | bytes 294944 | tf_op jit(solution)/shard_map/ppermute | solution.py:30
  72.7 3.9 shard_map.323
  80.9 3.4 collective-permute-start.13
  85.8 6.2 collective-permute-done.17.refs_3_
  93.0 2.5 collective-permute-start.20
  97.4 5.0 shard_map.325
  106.1 3.7 collective-permute-start.23
  115.5 3.2 shard_map.327
  120.7 3.3 copy.120
  130.5 8.6 %collective-permute-done.28 = bf16[4,64,768]{2,1,0:T(8,128)(2,1)} collective-permute-done((bf16[4,64,768]{2,1,0:T(8,128)(2,1)S(1)}, bf16[4,64,768]{2,1,0:T(8,128)(2,1)}, u32[]{:S(2)}, u32[]{:S(2)}) %collective-permute-start.28) | collective-permute-done | bytes 393248 | tf_op jit(solution)/shard_map/ppermute | solution.py:30
  148.1 2.7 collective-permute-start.31
  152.0 17.0 %collective-permute-done.31 = bf16[4,64,768]{2,1,0:T(8,128)(2,1)S(1)} collective-permute-done((bf16[4,64,768]{2,1,0:T(8,128)(2,1)S(1)}, bf16[4,64,768]{2,1,0:T(8,128)(2,1)S(1)}, u32[]{:S(2)}, u32[]{:S(2)}) %collective-permute-start.31) | collective-permute-done | bytes 393248 | tf_op jit(solution)/shard_map/ppermute | solution.py:30
  180.2 3.9 collective-permute-start.36
  195.2 3.9 shard_map.329
  202.7 3.3 collective-permute-start.43
  208.3 6.6 collective-permute-done.47.refs_3_
  215.9 4.0 collective-permute-start.50
  221.0 5.0 shard_map.331
  242.6 3.2 shard_map.333
  266.1 2.9 convert_reduce_fusion
  275.5 3.1 multiply_reduce_fusion.2
  282.8 6.2 shard_map.334
  301.6 3.3 collective-permute-start.65
  309.3 3.3 collective-permute-start.60
  321.6 5.7 shard_map.335
  327.4 4.5 shard_map.337
  333.6 4.2 collective-permute-start.72
  339.1 4.4 collective-permute-done.72
  348.0 13.0 %shard_map.338 = f32[64,768]{1,0:T(8,128)S(1)} custom-call(f32[64,384]{1,0:T(8,128)S(1)} %select_add_fusion.2.grads, f32[64,384]{1,0:T(8,128)S(1)} %copy-done.56, bf16[64,768]{1,0:T(8,128)(2,1)S(1)} %slice.705.land, f32[6,64,64]{2,1,0:T(8,128)S(1)} %copy-done.74, f32[42,64,64]{2,1,0:T(8,128)S(1)} %get-tuple-element.162.inverses, ...), custom_call_target="tpu_custom_call" | custom-call | flops 12999999488 | bytes 39000000 | tf_op jit(solution)/shard_map/pallas_call | solution.py:112
  370.5 2.7 fusion.126
  386.9 6.4 collective-permute-done.90
  394.4 6.5 collective-permute-done.83
  400.9 2.7 convert_reduce_fusion.4
  418.4 8.0 %collective-permute-done.86 = bf16[4,64,768]{2,1,0:T(8,128)(2,1)} collective-permute-done((bf16[4,64,768]{2,1,0:T(8,128)(2,1)}, bf16[4,64,768]{2,1,0:T(8,128)(2,1)}, u32[]{:S(2)}, u32[]{:S(2)}) %collective-permute-start.86) | collective-permute-done | bytes 393248 | tf_op jit(solution)/shard_map/ppermute | solution.py:30
  433.0 5.5 shard_map.340
  448.4 2.8 collective-permute-start.94
  451.2 2.6 convolution_bitcast_fusion
  458.2 4.0 collective-permute-start.99
  463.9 5.7 shard_map.341
  476.8 13.0 %shard_map.344 = f32[64,768]{1,0:T(8,128)S(1)} custom-call(f32[64,384]{1,0:T(8,128)S(1)} %select_add_fusion.1.grads, f32[64,384]{1,0:T(8,128)S(1)} %copy-done.53, bf16[64,768]{1,0:T(8,128)(2,1)S(1)} %copy-done.6, f32[6,64,64]{2,1,0:T(8,128)S(1)} %copy-done.72, f32[42,64,64]{2,1,0:T(8,128)S(1)} %copy-done.8, f32[36,64,64]{2,1,0:T(8,128)S(1)} %copy-done.58, ...), custom_call_target="tpu_custom_call" | custom-call | flops 12999999488 | bytes 39000000 | tf_op jit(solution)/shard_map/pallas_call | solution.py:112
  493.0 4.5 shard_map.343
  499.9 4.9 collective-permute-start.101
  505.4 4.3 collective-permute-done.101
  521.5 2.5 collective-permute-done.103
  529.7 2.9 collective-permute-done.108.three
  558.1 2.6 collective-permute-done.124
  562.6 2.7 fusion.127
  566.0 3.5 collective-permute-done.127
  571.4 2.9 collective-permute-start.119
  574.2 6.6 collective-permute-done.128
  588.1 2.6 collective-permute-done.119
  590.9 6.3 collective-permute-done.112
  599.2 11.3 %collective-permute-done.113 = bf16[96,768]{1,0:T(8,128)(2,1)S(1)} collective-permute-done((bf16[96,768]{1,0:T(8,128)(2,1)S(1)}, bf16[96,768]{1,0:T(8,128)(2,1)S(1)}, u32[]{:S(2)}, u32[]{:S(2)}) %collective-permute-start.113) | collective-permute-done | bytes 147488 | tf_op jit(solution)/shard_map/ppermute | solution.py:33
  610.7 14.0 %collective-permute-done.114 = bf16[48,768]{1,0:T(8,128)(2,1)S(1)} collective-permute-done((bf16[48,768]{1,0:T(8,128)(2,1)S(1)}, bf16[48,768]{1,0:T(8,128)(2,1)S(1)}, u32[]{:S(2)}, u32[]{:S(2)}) %collective-permute-start.114) | collective-permute-done | bytes 73760 | tf_op jit(solution)/shard_map/ppermute | solution.py:33
  624.8 3.0 collective-permute-start.122
  627.7 6.9 %collective-permute-done.115 = bf16[48,768]{1,0:T(8,128)(2,1)S(1)} collective-permute-done((bf16[48,768]{1,0:T(8,128)(2,1)S(1)}, bf16[48,768]{1,0:T(8,128)(2,1)S(1)}, u32[]{:S(2)}, u32[]{:S(2)}) %collective-permute-start.115) | collective-permute-done | bytes 73760 | tf_op jit(solution)/shard_map/ppermute | solution.py:33
  634.8 6.6 collective-permute-done.122
  641.5 3.4 collective-permute-done.116
  646.7 3.0 collective-permute-done.123
  (965 shorter events, 322.6 us)
Async XLA Ops:
  7.2 113.5 %all-gather.15.cloned.1.call-start = ((), (), s32[]{:S(2)}) async-start(), calls=%async_computation.8 | async-start | bytes 3538944 | tf_op jit(solution)/shard_map/all_gather | solution.py:615
  9.0 11.1 %collective-permute-start.5 = (f32[2,1408]{1,0:T(2,128)S(1)}, f32[2,1408]{1,0:T(2,128)S(1)}, u32[]{:S(2)}, u32[]{:S(2)}) collective-permute-start(f32[2,1408]{1,0:T(2,128)S(1)} %pad.31), channel_id=1, source_target_pairs={{0,2},{1,3},{2,0},{3,1},{4,6},{5,7},{6,4},{7,5},{8,10},{9,11},{10,... | collective-permute-start | bytes 33800 | tf_op jit(solution)/shard_map/ppermute | solution.py:30
  32.7 24.8 %collective-permute-start.4 = (bf16[576,768]{1,0:T(8,128)(2,1)S(1)}, bf16[576,768]{1,0:T(8,128)(2,1)}, u32[]{:S(2)}, u32[]{:S(2)}) collective-permute-start(bf16[576,768]{1,0:T(8,128)(2,1)S(1)} %pad_maximum_fusion.7), channel_id=1, source_target_pairs={{0,2},{1,3},{2,0},{3,1},{4,6},{5,7},{6,4},{7,5},{8,10},{9,11},{10,... | collective-permute-start | bytes 2654216 | tf_op jit(solution)/shard_map/ppermute | solution.py:30
  36.9 17.1 %collective-permute-start.11 = (bf16[64,384]{1,0:T(8,128)(2,1)S(1)}, bf16[64,384]{1,0:T(8,128)(2,1)S(1)}, u32[]{:S(2)}, u32[]{:S(2)}) collective-permute-start(bf16[64,384]{1,0:T(8,128)(2,1)S(1)} %add_convert_fusion.18), channel_id=1, source_target_pairs={{0,6},{1,7},{2,4},{3,5},{4,2},{5,3},{6,0},{7,1},{8,14},{9,15},{10,... | collective-permute-start | bytes 147464 | tf_op jit(solution)/shard_map/ppermute | solution.py:39
  38.4 15.6 %collective-permute-start.10 = (bf16[64,384]{1,0:T(8,128)(2,1)S(1)}, bf16[64,384]{1,0:T(8,128)(2,1)S(1)}, u32[]{:S(2)}, u32[]{:S(2)}) collective-permute-start(bf16[64,384]{1,0:T(8,128)(2,1)S(1)} %add_convert_fusion.18), channel_id=1, source_target_pairs={{0,4},{4,0},{8,12},{12,8},{16,20},{20,16},{24,28},{28,24},{1,5},{5... | collective-permute-start | bytes 147464 | tf_op jit(solution)/shard_map/ppermute | solution.py:33
  39.9 14.5 %collective-permute-start.9 = (bf16[64,384]{1,0:T(8,128)(2,1)S(1)}, bf16[64,384]{1,0:T(8,128)(2,1)S(1)}, u32[]{:S(2)}, u32[]{:S(2)}) collective-permute-start(bf16[64,384]{1,0:T(8,128)(2,1)S(1)} %add_convert_fusion.18), channel_id=1, source_target_pairs={{0,2},{1,3},{2,0},{3,1},{4,6},{5,7},{6,4},{7,5},{8,10},{9,11},{10,... | collective-permute-start | bytes 147464 | tf_op jit(solution)/shard_map/ppermute | solution.py:30
  60.4 9.7 %collective-permute-start.24 = (bf16[192,768]{1,0:T(8,128)(2,1)}, bf16[192,768]{1,0:T(8,128)(2,1)S(1)}, u32[]{:S(2)}, u32[]{:S(2)}) collective-permute-start(bf16[192,768]{1,0:T(8,128)(2,1)} %get-tuple-element.142), channel_id=1, source_target_pairs={{0,2},{1,3},{2,0},{3,1},{4,6},{5,7},{6,4},{7,5},{8,10},{9,11},{10,... | collective-permute-start | bytes 884744 | tf_op jit(solution)/shard_map/ppermute | solution.py:30
  70.1 106.1 %all-gather.7.cloned.1.call-start = ((), (), s32[]{:S(2)}) async-start(), calls=%async_computation.2 | async-start | bytes 3538944 | tf_op jit(solution)/shard_map/all_gather | solution.py:615
  76.6 9.2 %collective-permute-start.15 = (f32[64,512]{1,0:T(8,128)S(1)}, f32[64,512]{1,0:T(8,128)S(1)}, u32[]{:S(2)}, u32[]{:S(2)}) collective-permute-start(f32[64,512]{1,0:T(8,128)S(1)} %get-tuple-element.137), channel_id=1, source_target_pairs={{0,2},{1,3},{2,0},{3,1},{4,6},{5,7},{6,4},{7,5},{8,10},{9,11},{10,... | collective-permute-start | bytes 393224 | tf_op jit(solution)/shard_map/ppermute | solution.py:30
  79.1 12.9 %collective-permute-start.17 = (f32[64,512]{1,0:T(8,128)S(1)}, f32[64,512]{1,0:T(8,128)S(1)}, u32[]{:S(2)}, u32[]{:S(2)}) collective-permute-start(f32[64,512]{1,0:T(8,128)S(1)} %get-tuple-element.139), channel_id=1, source_target_pairs={{0,6},{1,7},{2,4},{3,5},{4,2},{5,3},{6,0},{7,1},{8,14},{9,15},{10,... | collective-permute-start | bytes 393224 | tf_op jit(solution)/shard_map/ppermute | solution.py:39
  80.9 30.6 %collective-permute-start.13 = (bf16[384,128]{1,0:T(8,128)(2,1)S(1)}, bf16[384,128]{1,0:T(8,128)(2,1)S(1)}, u32[]{:S(2)}, u32[]{:S(2)}) collective-permute-start(bf16[384,128]{1,0:T(8,128)(2,1)S(1)} %get-tuple-element.134), channel_id=1, source_target_pairs={{0,2},{1,3},{2,4},{3,5},{4,6},{5,7},{6,8},{7,9},{8,10},{9,11},{10,... | collective-permute-start | bytes 294920 | tf_op jit(solution)/shard_map/ppermute | solution.py:53
  84.3 27.2 %collective-permute-start.14 = (bf16[384,128]{1,0:T(8,128)(2,1)S(1)}, bf16[384,128]{1,0:T(8,128)(2,1)S(1)}, u32[]{:S(2)}, u32[]{:S(2)}) collective-permute-start(bf16[384,128]{1,0:T(8,128)(2,1)S(1)} %get-tuple-element.135), channel_id=1, source_target_pairs={{2,0},{3,1},{4,2},{5,3},{6,4},{7,5},{8,6},{9,7},{10,8},{11,9},{12,... | collective-permute-start | bytes 294920 | tf_op jit(solution)/shard_map/ppermute | solution.py:53
  93.0 11.3 %collective-permute-start.20 = (f32[64,512]{1,0:T(8,128)S(1)}, f32[64,512]{1,0:T(8,128)S(1)}, u32[]{:S(2)}, u32[]{:S(2)}) collective-permute-start(f32[64,512]{1,0:T(8,128)S(1)} %shard_map.324.refs_0_), channel_id=1, source_target_pairs={{0,24},{4,28},{8,16},{12,20},{16,8},{20,12},{24,0},{28,4},{1,25},{... | collective-permute-start | bytes 393224 | tf_op jit(solution)/shard_map/ppermute | solution.py:33
  95.5 9.0 %collective-permute-start.19 = (f32[64,512]{1,0:T(8,128)S(1)}, f32[64,512]{1,0:T(8,128)S(1)}, u32[]{:S(2)}, u32[]{:S(2)}) collective-permute-start(f32[64,512]{1,0:T(8,128)S(1)} %shard_map.324.refs_0_), channel_id=1, source_target_pairs={{0,16},{4,20},{8,24},{12,28},{16,0},{20,4},{24,8},{28,12},{1,17},{... | collective-permute-start | bytes 393224 | tf_op jit(solution)/shard_map/ppermute | solution.py:33
  95.5 9.0 %collective-permute-start.18 = (f32[64,512]{1,0:T(8,128)S(1)}, f32[64,512]{1,0:T(8,128)S(1)}, u32[]{:S(2)}, u32[]{:S(2)}) collective-permute-start(f32[64,512]{1,0:T(8,128)S(1)} %shard_map.324.refs_0_), channel_id=1, source_target_pairs={{0,8},{4,12},{8,0},{12,4},{16,24},{20,28},{24,16},{28,20},{1,9},{5... | collective-permute-start | bytes 393224 | tf_op jit(solution)/shard_map/ppermute | solution.py:33
  126.7 12.4 %collective-permute-start.28 = (bf16[4,64,768]{2,1,0:T(8,128)(2,1)S(1)}, bf16[4,64,768]{2,1,0:T(8,128)(2,1)}, u32[]{:S(2)}, u32[]{:S(2)}) collective-permute-start(bf16[4,64,768]{2,1,0:T(8,128)(2,1)S(1)} %fusion.62), channel_id=1, source_target_pairs={{0,2},{1,3},{2,0},{3,1},{4,6},{5,7},{6,4},{7,5},{8,10},{9,11},{10,... | collective-permute-start | bytes 1179656 | tf_op jit(solution)/shard_map/ppermute | solution.py:30
  128.9 10.3 %collective-permute-start.26 = (bf16[4,64,768]{2,1,0:T(8,128)(2,1)S(1)}, bf16[4,64,768]{2,1,0:T(8,128)(2,1)S(1)}, u32[]{:S(2)}, u32[]{:S(2)}) collective-permute-start(bf16[4,64,768]{2,1,0:T(8,128)(2,1)S(1)} %fusion.62), channel_id=1, source_target_pairs={{0,1},{1,0},{2,3},{3,2},{4,5},{5,4},{6,7},{7,6},{8,9},{9,8},{10,11... | collective-permute-start | bytes 1179656 | tf_op jit(solution)/shard_map/ppermute | solution.py:30
  130.0 103.0 %all-gather.9.cloned.1.call-start = ((), (), s32[]{:S(2)}) async-start(), calls=%async_computation.3 | async-start | bytes 3538944 | tf_op jit(solution)/shard_map/all_gather | solution.py:615
  148.1 20.9 %collective-permute-start.31 = (bf16[4,64,768]{2,1,0:T(8,128)(2,1)S(1)}, bf16[4,64,768]{2,1,0:T(8,128)(2,1)S(1)}, u32[]{:S(2)}, u32[]{:S(2)}) collective-permute-start(bf16[4,64,768]{2,1,0:T(8,128)(2,1)S(1)} %add_convert_fusion.4), channel_id=1, source_target_pairs={{0,2},{1,3},{2,0},{3,1},{4,6},{5,7},{6,4},{7,5},{8,10},{9,11},{10,... | collective-permute-start | bytes 1179656 | tf_op jit(solution)/shard_map/ppermute | solution.py:30
  186.5 194.3 %reduce-scatter.3.cloned.1.call-start = ((), (), s32[]{:S(2)}) async-start(), calls=%async_computation.4 | async-start | bytes 5308416 | tf_op jit(solution)/shard_map/reduce_scatter | solution.py:955
  199.1 9.2 %collective-permute-start.45 = (f32[64,512]{1,0:T(8,128)S(1)}, f32[64,512]{1,0:T(8,128)S(1)}, u32[]{:S(2)}, u32[]{:S(2)}) collective-permute-start(f32[64,512]{1,0:T(8,128)S(1)} %get-tuple-element.159), channel_id=1, source_target_pairs={{0,2},{1,3},{2,0},{3,1},{4,6},{5,7},{6,4},{7,5},{8,10},{9,11},{10,... | collective-permute-start | bytes 393224 | tf_op jit(solution)/shard_map/ppermute | solution.py:30
  202.6 12.4 %collective-permute-start.47 = (f32[64,512]{1,0:T(8,128)S(1)}, f32[64,512]{1,0:T(8,128)S(1)}, u32[]{:S(2)}, u32[]{:S(2)}) collective-permute-start(f32[64,512]{1,0:T(8,128)S(1)} %get-tuple-element.161), channel_id=1, source_target_pairs={{0,6},{1,7},{2,4},{3,5},{4,2},{5,3},{6,0},{7,1},{8,14},{9,15},{10,... | collective-permute-start | bytes 393224 | tf_op jit(solution)/shard_map/ppermute | solution.py:39
  202.7 35.8 %collective-permute-start.43 = (bf16[384,128]{1,0:T(8,128)(2,1)S(1)}, bf16[384,128]{1,0:T(8,128)(2,1)S(1)}, u32[]{:S(2)}, u32[]{:S(2)}) collective-permute-start(bf16[384,128]{1,0:T(8,128)(2,1)S(1)} %get-tuple-element.156), channel_id=1, source_target_pairs={{0,2},{1,3},{2,4},{3,5},{4,6},{5,7},{6,8},{7,9},{8,10},{9,11},{10,... | collective-permute-start | bytes 294920 | tf_op jit(solution)/shard_map/ppermute | solution.py:53
  206.0 32.5 %collective-permute-start.44 = (bf16[384,128]{1,0:T(8,128)(2,1)S(1)}, bf16[384,128]{1,0:T(8,128)(2,1)S(1)}, u32[]{:S(2)}, u32[]{:S(2)}) collective-permute-start(bf16[384,128]{1,0:T(8,128)(2,1)S(1)} %get-tuple-element.157), channel_id=1, source_target_pairs={{2,0},{3,1},{4,2},{5,3},{6,4},{7,5},{8,6},{9,7},{10,8},{11,9},{12,... | collective-permute-start | bytes 294920 | tf_op jit(solution)/shard_map/ppermute | solution.py:53
  215.9 13.9 %collective-permute-start.50 = (f32[64,512]{1,0:T(8,128)S(1)}, f32[64,512]{1,0:T(8,128)S(1)}, u32[]{:S(2)}, u32[]{:S(2)}) collective-permute-start(f32[64,512]{1,0:T(8,128)S(1)} %shard_map.330.refs_0_), channel_id=1, source_target_pairs={{0,24},{4,28},{8,16},{12,20},{16,8},{20,12},{24,0},{28,4},{1,25},{... | collective-permute-start | bytes 393224 | tf_op jit(solution)/shard_map/ppermute | solution.py:33
  219.9 11.8 %collective-permute-start.49 = (f32[64,512]{1,0:T(8,128)S(1)}, f32[64,512]{1,0:T(8,128)S(1)}, u32[]{:S(2)}, u32[]{:S(2)}) collective-permute-start(f32[64,512]{1,0:T(8,128)S(1)} %shard_map.330.refs_0_), channel_id=1, source_target_pairs={{0,16},{4,20},{8,24},{12,28},{16,0},{20,4},{24,8},{28,12},{1,17},{... | collective-permute-start | bytes 393224 | tf_op jit(solution)/shard_map/ppermute | solution.py:33
  221.0 10.7 %collective-permute-start.48 = (f32[64,512]{1,0:T(8,128)S(1)}, f32[64,512]{1,0:T(8,128)S(1)}, u32[]{:S(2)}, u32[]{:S(2)}) collective-permute-start(f32[64,512]{1,0:T(8,128)S(1)} %shard_map.330.refs_0_), channel_id=1, source_target_pairs={{0,8},{4,12},{8,0},{12,4},{16,24},{20,28},{24,16},{28,20},{1,9},{5... | collective-permute-start | bytes 393224 | tf_op jit(solution)/shard_map/ppermute | solution.py:33
  275.4 215.2 %all-gather.11.cloned.1.call-start = ((), (), s32[]{:S(2)}) async-start(), calls=%async_computation.5 | async-start | bytes 2654208 | tf_op jit(solution)/shard_map/all_gather | solution.py:959
  300.5 13.8 %collective-permute-start.67 = (bf16[64,384]{1,0:T(8,128)(2,1)}, bf16[64,384]{1,0:T(8,128)(2,1)S(1)}, u32[]{:S(2)}, u32[]{:S(2)}) collective-permute-start(bf16[64,384]{1,0:T(8,128)(2,1)} %fusion.85), channel_id=1, source_target_pairs={{0,24},{4,28},{8,16},{12,20},{16,8},{20,12},{24,0},{28,4},{1,25},{... | collective-permute-start | bytes 147464 | tf_op jit(solution)/shard_map/ppermute | solution.py:33
  301.6 12.7 %collective-permute-start.66 = (bf16[64,384]{1,0:T(8,128)(2,1)}, bf16[64,384]{1,0:T(8,128)(2,1)}, u32[]{:S(2)}, u32[]{:S(2)}) collective-permute-start(bf16[64,384]{1,0:T(8,128)(2,1)} %fusion.85), channel_id=1, source_target_pairs={{0,16},{4,20},{8,24},{12,28},{16,0},{20,4},{24,8},{28,12},{1,17},{... | collective-permute-start | bytes 147464 | tf_op jit(solution)/shard_map/ppermute | solution.py:33
  301.6 12.7 %collective-permute-start.65 = (bf16[64,384]{1,0:T(8,128)(2,1)}, bf16[64,384]{1,0:T(8,128)(2,1)}, u32[]{:S(2)}, u32[]{:S(2)}) collective-permute-start(bf16[64,384]{1,0:T(8,128)(2,1)} %fusion.85), channel_id=1, source_target_pairs={{0,8},{4,12},{8,0},{12,4},{16,24},{20,28},{24,16},{28,20},{1,9},{5... | collective-permute-start | bytes 147464 | tf_op jit(solution)/shard_map/ppermute | solution.py:33
  309.3 12.3 %collective-permute-start.60 = (bf16[384,128]{1,0:T(8,128)(2,1)}, bf16[384,128]{1,0:T(8,128)(2,1)S(1)}, u32[]{:S(2)}, u32[]{:S(2)}) collective-permute-start(bf16[384,128]{1,0:T(8,128)(2,1)} %get-tuple-element.168), channel_id=1, source_target_pairs={{0,2},{1,3},{2,4},{3,5},{4,6},{5,7},{6,8},{7,9},{8,10},{9,11},{10,... | collective-permute-start | bytes 294920 | tf_op jit(solution)/shard_map/ppermute | solution.py:53
  312.6 9.0 %collective-permute-start.61 = (bf16[384,128]{1,0:T(8,128)(2,1)}, bf16[384,128]{1,0:T(8,128)(2,1)S(1)}, u32[]{:S(2)}, u32[]{:S(2)}) collective-permute-start(bf16[384,128]{1,0:T(8,128)(2,1)} %get-tuple-element.169), channel_id=1, source_target_pairs={{2,0},{3,1},{4,2},{5,3},{6,4},{7,5},{8,6},{9,7},{10,8},{11,9},{12,... | collective-permute-start | bytes 294920 | tf_op jit(solution)/shard_map/ppermute | solution.py:53
  316.9 10.4 %collective-permute-start.70 = (bf16[64,512]{1,0:T(8,128)(2,1)S(1)}, bf16[64,512]{1,0:T(8,128)(2,1)S(1)}, u32[]{:S(2)}, u32[]{:S(2)}) collective-permute-start(bf16[64,512]{1,0:T(8,128)(2,1)S(1)} %shard_map.336.refs_4_), channel_id=1, source_target_pairs={{0,6},{1,7},{2,4},{3,5},{4,2},{5,3},{6,0},{7,1},{8,14},{9,15},{10,... | collective-permute-start | bytes 196616 | tf_op jit(solution)/shard_map/ppermute | solution.py:39
  333.6 9.9 %collective-permute-start.72 = (bf16[64,768]{1,0:T(8,128)(2,1)S(1)}, bf16[64,768]{1,0:T(8,128)(2,1)S(1)}, u32[]{:S(2)}, u32[]{:S(2)}) collective-permute-start(bf16[64,768]{1,0:T(8,128)(2,1)S(1)} %get-tuple-element.184), channel_id=1, source_target_pairs={{0,4},{4,0},{8,12},{12,8},{16,20},{20,16},{24,28},{28,24},{1,5},{5... | collective-permute-start | bytes 294920 | tf_op jit(solution)/shard_map/ppermute | solution.py:33
  343.5 17.4 %collective-permute-start.76 = (bf16[64,768]{1,0:T(8,128)(2,1)S(1)}, bf16[64,768]{1,0:T(8,128)(2,1)S(1)}, u32[]{:S(2)}, u32[]{:S(2)}) collective-permute-start(bf16[64,768]{1,0:T(8,128)(2,1)S(1)} %fusion.82), channel_id=1, source_target_pairs={{0,24},{4,28},{8,16},{12,20},{16,8},{20,12},{24,0},{28,4},{1,25},{... | collective-permute-start | bytes 294920 | tf_op jit(solution)/shard_map/ppermute | solution.py:33
  343.6 17.4 %collective-permute-start.75 = (bf16[64,768]{1,0:T(8,128)(2,1)S(1)}, bf16[64,768]{1,0:T(8,128)(2,1)S(1)}, u32[]{:S(2)}, u32[]{:S(2)}) collective-permute-start(bf16[64,768]{1,0:T(8,128)(2,1)S(1)} %fusion.82), channel_id=1, source_target_pairs={{0,16},{4,20},{8,24},{12,28},{16,0},{20,4},{24,8},{28,12},{1,17},{... | collective-permute-start | bytes 294920 | tf_op jit(solution)/shard_map/ppermute | solution.py:33
  346.1 14.9 %collective-permute-start.74 = (bf16[64,768]{1,0:T(8,128)(2,1)S(1)}, bf16[64,768]{1,0:T(8,128)(2,1)S(1)}, u32[]{:S(2)}, u32[]{:S(2)}) collective-permute-start(bf16[64,768]{1,0:T(8,128)(2,1)S(1)} %fusion.82), channel_id=1, source_target_pairs={{0,8},{4,12},{8,0},{12,4},{16,24},{20,28},{24,16},{28,20},{1,9},{5... | collective-permute-start | bytes 294920 | tf_op jit(solution)/shard_map/ppermute | solution.py:33
  383.4 9.9 %collective-permute-start.90 = (bf16[192,768]{1,0:T(8,128)(2,1)S(1)}, bf16[192,768]{1,0:T(8,128)(2,1)S(1)}, u32[]{:S(2)}, u32[]{:S(2)}) collective-permute-start(bf16[192,768]{1,0:T(8,128)(2,1)S(1)} %select_bitcast_fusion), channel_id=1, source_target_pairs={{0,2},{1,3},{2,0},{3,1},{4,6},{5,7},{6,4},{7,5},{8,10},{9,11},{10,... | collective-permute-start | bytes 884744 | tf_op jit(solution)/shard_map/ppermute | solution.py:30
  384.3 16.5 %collective-permute-start.83 = (bf16[4,64,768]{2,1,0:T(8,128)(2,1)S(1)}, bf16[4,64,768]{2,1,0:T(8,128)(2,1)}, u32[]{:S(2)}, u32[]{:S(2)}) collective-permute-start(bf16[4,64,768]{2,1,0:T(8,128)(2,1)S(1)} %get-tuple-element.313), channel_id=1, source_target_pairs={{0,2},{1,3},{2,0},{3,1},{4,6},{5,7},{6,4},{7,5},{8,10},{9,11},{10,... | collective-permute-start | bytes 1179656 | tf_op jit(solution)/shard_map/ppermute | solution.py:30
  394.2 160.2 %reduce-scatter.5.cloned.1.call-start = ((), (), s32[]{:S(2)}) async-start(), calls=%async_computation.6 | async-start | bytes 5308416 | tf_op jit(solution)/shard_map/reduce_scatter | solution.py:955
  406.7 11.6 %collective-permute-start.82 = (bf16[4,64,768]{2,1,0:T(8,128)(2,1)}, bf16[4,64,768]{2,1,0:T(8,128)(2,1)S(1)}, u32[]{:S(2)}, u32[]{:S(2)}) collective-permute-start(bf16[4,64,768]{2,1,0:T(8,128)(2,1)} %select_convert_fusion.4), channel_id=1, source_target_pairs={{0,1},{1,0},{2,3},{3,2},{4,5},{5,4},{6,7},{7,6},{8,9},{9,8},{10,11... | collective-permute-start | bytes 1179656 | tf_op jit(solution)/shard_map/ppermute | solution.py:30
  414.8 11.6 %collective-permute-start.86 = (bf16[4,64,768]{2,1,0:T(8,128)(2,1)}, bf16[4,64,768]{2,1,0:T(8,128)(2,1)}, u32[]{:S(2)}, u32[]{:S(2)}) collective-permute-start(bf16[4,64,768]{2,1,0:T(8,128)(2,1)} %add_convert_fusion.2), channel_id=1, source_target_pairs={{0,2},{1,3},{2,0},{3,1},{4,6},{5,7},{6,4},{7,5},{8,10},{9,11},{10,... | collective-permute-start | bytes 1179656 | tf_op jit(solution)/shard_map/ppermute | solution.py:30
  418.1 233.9 %all-gather.13.cloned.1.call-start = ((), (), s32[]{:S(2)}) async-start(), calls=%async_computation.7 | async-start | bytes 3981312 | tf_op jit(solution)/shard_map/all_gather | solution.py:1123
  446.7 10.6 %collective-permute-start.96 = (bf16[64,384]{1,0:T(8,128)(2,1)S(1)}, bf16[64,384]{1,0:T(8,128)(2,1)S(1)}, u32[]{:S(2)}, u32[]{:S(2)}) collective-permute-start(bf16[64,384]{1,0:T(8,128)(2,1)S(1)} %fusion.86), channel_id=1, source_target_pairs={{0,24},{4,28},{8,16},{12,20},{16,8},{20,12},{24,0},{28,4},{1,25},{... | collective-permute-start | bytes 147464 | tf_op jit(solution)/shard_map/ppermute | solution.py:33
  448.4 8.9 %collective-permute-start.94 = (bf16[64,384]{1,0:T(8,128)(2,1)S(1)}, bf16[64,384]{1,0:T(8,128)(2,1)S(1)}, u32[]{:S(2)}, u32[]{:S(2)}) collective-permute-start(bf16[64,384]{1,0:T(8,128)(2,1)S(1)} %fusion.86), channel_id=1, source_target_pairs={{0,8},{4,12},{8,0},{12,4},{16,24},{20,28},{24,16},{28,20},{1,9},{5... | collective-permute-start | bytes 147464 | tf_op jit(solution)/shard_map/ppermute | solution.py:33
  453.8 10.1 %collective-permute-start.88 = (bf16[384,128]{1,0:T(8,128)(2,1)S(1)}, bf16[384,128]{1,0:T(8,128)(2,1)S(1)}, u32[]{:S(2)}, u32[]{:S(2)}) collective-permute-start(bf16[384,128]{1,0:T(8,128)(2,1)S(1)} %get-tuple-element.192), channel_id=1, source_target_pairs={{0,2},{1,3},{2,4},{3,5},{4,6},{5,7},{6,8},{7,9},{8,10},{9,11},{10,... | collective-permute-start | bytes 294920 | tf_op jit(solution)/shard_map/ppermute | solution.py:53
  458.2 32.4 %collective-permute-start.99 = (bf16[64,512]{1,0:T(8,128)(2,1)S(1)}, bf16[64,512]{1,0:T(8,128)(2,1)S(1)}, u32[]{:S(2)}, u32[]{:S(2)}) collective-permute-start(bf16[64,512]{1,0:T(8,128)(2,1)S(1)} %shard_map.342.refs_4_), channel_id=1, source_target_pairs={{0,6},{1,7},{2,4},{3,5},{4,2},{5,3},{6,0},{7,1},{8,14},{9,15},{10,... | collective-permute-start | bytes 196616 | tf_op jit(solution)/shard_map/ppermute | solution.py:39
  462.1 28.4 %collective-permute-start.98 = (bf16[64,512]{1,0:T(8,128)(2,1)S(1)}, bf16[64,512]{1,0:T(8,128)(2,1)S(1)}, u32[]{:S(2)}, u32[]{:S(2)}) collective-permute-start(bf16[64,512]{1,0:T(8,128)(2,1)S(1)} %shard_map.342.refs_4_), channel_id=1, source_target_pairs={{0,4},{4,0},{8,12},{12,8},{16,20},{20,16},{24,28},{28,24},{1,5},{5... | collective-permute-start | bytes 196616 | tf_op jit(solution)/shard_map/ppermute | solution.py:33
  462.5 28.0 %collective-permute-start.97 = (bf16[64,512]{1,0:T(8,128)(2,1)S(1)}, bf16[64,512]{1,0:T(8,128)(2,1)S(1)}, u32[]{:S(2)}, u32[]{:S(2)}) collective-permute-start(bf16[64,512]{1,0:T(8,128)(2,1)S(1)} %shard_map.342.refs_4_), channel_id=1, source_target_pairs={{0,2},{1,3},{2,0},{3,1},{4,6},{5,7},{6,4},{7,5},{8,10},{9,11},{10,... | collective-permute-start | bytes 196616 | tf_op jit(solution)/shard_map/ppermute | solution.py:30
  499.9 9.8 %collective-permute-start.101 = (bf16[64,768]{1,0:T(8,128)(2,1)S(1)}, bf16[64,768]{1,0:T(8,128)(2,1)S(1)}, u32[]{:S(2)}, u32[]{:S(2)}) collective-permute-start(bf16[64,768]{1,0:T(8,128)(2,1)S(1)} %get-tuple-element.213), channel_id=1, source_target_pairs={{0,4},{4,0},{8,12},{12,8},{16,20},{20,16},{24,28},{28,24},{1,5},{5... | collective-permute-start | bytes 294920 | tf_op jit(solution)/shard_map/ppermute | solution.py:33
  511.4 12.6 %collective-permute-start.103 = (bf16[384,768]{1,0:T(8,128)(2,1)S(1)}, bf16[384,768]{1,0:T(8,128)(2,1)S(1)}, u32[]{:S(2)}, u32[]{:S(2)}) collective-permute-start(bf16[384,768]{1,0:T(8,128)(2,1)S(1)} %bitcast.430), channel_id=1, source_target_pairs={{0,2},{1,3},{2,0},{3,1},{4,6},{5,7},{6,4},{7,5},{8,10},{9,11},{10,... | collective-permute-start | bytes 1769480 | tf_op jit(solution)/shard_map/ppermute | solution.py:30
  528.6 41.0 %collective-permute-start.118 = (bf16[192,768]{1,0:T(8,128)(2,1)}, bf16[192,768]{1,0:T(8,128)(2,1)}, u32[]{:S(2)}, u32[]{:S(2)}) collective-permute-start(bf16[192,768]{1,0:T(8,128)(2,1)} %broadcast_select_fusion.21), channel_id=1, source_target_pairs={{0,8},{4,12},{8,0},{12,4},{16,24},{20,28},{24,16},{28,20},{1,9},{5... | collective-permute-start | bytes 884744 | tf_op jit(solution)/shard_map/ppermute | solution.py:33
  538.3 14.8 %collective-permute-start.111 = (bf16[384,768]{1,0:T(8,128)(2,1)}, bf16[384,768]{1,0:T(8,128)(2,1)}, u32[]{:S(2)}, u32[]{:S(2)}) collective-permute-start(bf16[384,768]{1,0:T(8,128)(2,1)} %bitcast.102), channel_id=1, source_target_pairs={{0,2},{1,3},{2,0},{3,1},{4,6},{5,7},{6,4},{7,5},{8,10},{9,11},{10,... | collective-permute-start | bytes 1769480 | tf_op jit(solution)/shard_map/ppermute | solution.py:30
  565.9 79.7 %collective-permute-start.110 = (bf16[4,64,768]{2,1,0:T(8,128)(2,1)S(1)}, bf16[4,64,768]{2,1,0:T(8,128)(2,1)S(1)}, u32[]{:S(2)}, u32[]{:S(2)}) collective-permute-start(bf16[4,64,768]{2,1,0:T(8,128)(2,1)S(1)} %select_convert_fusion.2), channel_id=1, source_target_pairs={{0,1},{1,0},{2,3},{3,2},{4,5},{5,4},{6,7},{7,6},{8,9},{9,8},{10,11... | collective-permute-start | bytes 1179656 | tf_op jit(solution)/shard_map/ppermute | solution.py:30
  569.5 11.3 %collective-permute-start.128 = (f32[12288]{0:T(1024)S(1)}, f32[12288]{0:T(1024)S(1)}, u32[]{:S(2)}, u32[]{:S(2)}) collective-permute-start(f32[12288]{0:T(1024)S(1)} %add.741), channel_id=1, source_target_pairs={{0,16},{4,20},{8,24},{12,28},{16,0},{20,4},{24,8},{28,12},{1,17},{... | collective-permute-start | bytes 147464 | tf_op jit(solution)/shard_map/ppermute | solution.py:33
  571.4 19.4 %collective-permute-start.119 = (bf16[96,768]{1,0:T(8,128)(2,1)}, bf16[96,768]{1,0:T(8,128)(2,1)S(1)}, u32[]{:S(2)}, u32[]{:S(2)}) collective-permute-start(bf16[96,768]{1,0:T(8,128)(2,1)} %broadcast_select_fusion.31), channel_id=1, source_target_pairs={{0,16},{4,20},{8,24},{12,28},{16,0},{20,4},{24,8},{28,12},{1,17},{... | collective-permute-start | bytes 442376 | tf_op jit(solution)/shard_map/ppermute | solution.py:33
  587.3 9.9 %collective-permute-start.112 = (bf16[192,768]{1,0:T(8,128)(2,1)S(1)}, bf16[192,768]{1,0:T(8,128)(2,1)S(1)}, u32[]{:S(2)}, u32[]{:S(2)}) collective-permute-start(bf16[192,768]{1,0:T(8,128)(2,1)S(1)} %broadcast_select_fusion.24), channel_id=1, source_target_pairs={{0,4},{4,0},{8,12},{12,8},{16,20},{20,16},{24,28},{28,24},{1,5},{5... | collective-permute-start | bytes 884744 | tf_op jit(solution)/shard_map/ppermute | solution.py:33
  597.3 13.1 %collective-permute-start.113 = (bf16[96,768]{1,0:T(8,128)(2,1)S(1)}, bf16[96,768]{1,0:T(8,128)(2,1)S(1)}, u32[]{:S(2)}, u32[]{:S(2)}) collective-permute-start(bf16[96,768]{1,0:T(8,128)(2,1)S(1)} %broadcast_select_fusion.34), channel_id=1, source_target_pairs={{0,8},{4,12},{8,0},{12,4},{16,24},{20,28},{24,16},{28,20},{1,9},{5... | collective-permute-start | bytes 442376 | tf_op jit(solution)/shard_map/ppermute | solution.py:33
  598.4 12.2 %collective-permute-start.121 = (bf16[48,768]{1,0:T(8,128)(2,1)S(1)}, bf16[48,768]{1,0:T(8,128)(2,1)S(1)}, u32[]{:S(2)}, u32[]{:S(2)}) collective-permute-start(bf16[48,768]{1,0:T(8,128)(2,1)S(1)} %add_convert_fusion.15), channel_id=1, source_target_pairs={{0,4},{4,0},{8,12},{12,8},{16,20},{20,16},{24,28},{28,24},{1,5},{5... | collective-permute-start | bytes 221192 | tf_op jit(solution)/shard_map/ppermute | solution.py:33
  610.5 14.1 %collective-permute-start.114 = (bf16[48,768]{1,0:T(8,128)(2,1)S(1)}, bf16[48,768]{1,0:T(8,128)(2,1)S(1)}, u32[]{:S(2)}, u32[]{:S(2)}) collective-permute-start(bf16[48,768]{1,0:T(8,128)(2,1)S(1)} %broadcast_select_fusion.40), channel_id=1, source_target_pairs={{0,16},{4,20},{8,24},{12,28},{16,0},{20,4},{24,8},{28,12},{1,17},{... | collective-permute-start | bytes 221192 | tf_op jit(solution)/shard_map/ppermute | solution.py:33
  624.6 10.0 %collective-permute-start.115 = (bf16[48,768]{1,0:T(8,128)(2,1)S(1)}, bf16[48,768]{1,0:T(8,128)(2,1)S(1)}, u32[]{:S(2)}, u32[]{:S(2)}) collective-permute-start(bf16[48,768]{1,0:T(8,128)(2,1)S(1)} %add_convert_fusion.16), channel_id=1, source_target_pairs={{0,16},{4,20},{8,24},{12,28},{16,0},{20,4},{24,8},{28,12},{1,17},{... | collective-permute-start | bytes 221192 | tf_op jit(solution)/shard_map/ppermute | solution.py:33
  624.8 16.6 %collective-permute-start.122 = (bf16[96,768]{1,0:T(8,128)(2,1)S(1)}, bf16[96,768]{1,0:T(8,128)(2,1)S(1)}, u32[]{:S(2)}, u32[]{:S(2)}) collective-permute-start(bf16[96,768]{1,0:T(8,128)(2,1)S(1)} %pad_maximum_fusion.24), channel_id=1, source_target_pairs={{0,16},{4,20},{8,24},{12,28},{16,0},{20,4},{24,8},{28,12},{1,17},{... | collective-permute-start | bytes 442376 | tf_op jit(solution)/shard_map/ppermute | solution.py:33
  634.7 10.2 %collective-permute-start.116 = (bf16[96,768]{1,0:T(8,128)(2,1)S(1)}, bf16[96,768]{1,0:T(8,128)(2,1)S(1)}, u32[]{:S(2)}, u32[]{:S(2)}) collective-permute-start(bf16[96,768]{1,0:T(8,128)(2,1)S(1)} %pad_maximum_fusion.23), channel_id=1, source_target_pairs={{0,8},{4,12},{8,0},{12,4},{16,24},{20,28},{24,16},{28,20},{1,9},{5... | collective-permute-start | bytes 442376 | tf_op jit(solution)/shard_map/ppermute | solution.py:33
  (276 other events, 2142.7 us)
Sparse Core Ops, SparseCore 0:
  70.2 46.9 all-gather.14
  130.1 42.5 all-gather.6
  186.6 43.6 all-gather.8
  275.5 105.2 reduce-scatter.2
  394.3 50.6 all-gather.10
  449.0 101.4 reduce-scatter.4
  562.7 79.6 all-gather.12

commit v4 on v3

--- a/solution.py
+++ b/solution.py
@@ -628,7 +628,7 @@
     own_out, other = tied(out_weight[0], other)
     other_out = exchange(own_out, 0, 2)
     held = jnp.concatenate([packs[1], out_weight[1]], 0)
-    held, other_out = tied(held, other_out)
+    held, other = tied(held, other)
     first = ordered(pack.reshape(3, -1, model), other.reshape(3, -1, model), 1)
     layers = [
         dict(
@@ -885,6 +885,7 @@
         *near_keys,
         us=5,
     )
+    own_grad, *parts = tied(own_grad, *parts)
     (own_land_grad,) = on_core(
         inverse_back_kernel,
         [((LANDMARKS, 2 * width), jnp.float32)],

time: 676 us -> 670 us (level)
  other arithmetic: 65.3 us -> 57.9 us
    reduce_scatter x2, waiting for transfers between devices: 1.79 us -> 11.7 us  [seq_scatter(): lax.psum_scatter(values, 'seq', scatter_dimension=values.ndim - 2, tiled=...]
    unnamed x407 -> x371, local copies, waits for them, and re-layouts: 34.7 us -> 32.3 us
  transfers between devices with their start and end apart: 137 -> 137, of which waited for: 63 -> 63; matrix products, arithmetic and copies ran while one was open for 19% -> 17% of each run, Pallas kernels for 13% -> 13%
where the time goes in v4:
time: 670 us; the launch traced here: 663 us
  waiting for transfers between devices  211 us (31%)
  starting transfers between devices  157 us (23%)
  Pallas kernels  91.8 us (14%)
  local copies, waits for them, and re-layouts  78.7 us (12%)
  other arithmetic  57.9 us (9%)
  matrix products  46.4 us (7%)
  between operations  19.4 us (3%)
    pallas_call x24, Pallas kernels, on_core(): pl.pallas_call(kernel, out_shape=shapes, in_specs=specs, out_specs=tuple(...  91.8 us
    ppermute x55, waiting for transfers between devices, exchange(): lax.ppermute(values, 'seq', [(i, i ^ seq_mask) for i in range(count)])  86.8 us
    ppermute x51, waiting for transfers between devices, exchange(): lax.ppermute(values, 'head', [(i, i ^ head_mask) for i in range(count)])  74 us
    ppermute x55, starting transfers between devices, exchange(): lax.ppermute(values, 'seq', [(i, i ^ seq_mask) for i in range(count)])  72.8 us
    ppermute x51, starting transfers between devices, exchange(): lax.ppermute(values, 'head', [(i, i ^ head_mask) for i in range(count)])  39.4 us
    ppermute x16, waiting for transfers between devices, exchange(): return lax.ppermute(values, ('seq', 'head'), route)  36.2 us
    unnamed x371, local copies, waits for them, and re-layouts  32.3 us
    ppermute x16, starting transfers between devices, exchange(): return lax.ppermute(values, ('seq', 'head'), route)  26.3 us
  transfers between devices with their start and end apart: 137, of which 63 were waited for; matrix products, arithmetic and copies ran while one was open for 17% of the time, Pallas kernels for 13%

profile of v4, /device:TPU:0, one launch (start us, length us, event | category | flops | bytes accessed | tf_op | source)
XLA Modules:
  0.0 663.1 jit_solution(2839451675399032794)
XLA Ops:
  9.0 3.0 collective-permute-start.5
  26.5 2.8 collective-permute-done.3
  29.4 3.7 collective-permute-start.8
  35.4 2.6 collective-permute-done.7
  41.7 13.5 %collective-permute-done.11 = bf16[64,384]{1,0:T(8,128)(2,1)S(1)} collective-permute-done((bf16[64,384]{1,0:T(8,128)(2,1)S(1)}, bf16[64,384]{1,0:T(8,128)(2,1)S(1)}, u32[]{:S(2)}, u32[]{:S(2)}) %collective-permute-start.11) | collective-permute-done | bytes 49184 | tf_op jit(solution)/shard_map/ppermute | solution.py:39
  61.4 2.6 fusion.10.qkv
  64.7 3.9 shard_map.323
  74.4 2.6 collective-permute-start.13
  77.2 5.5 collective-permute-done.17.refs_3_
  83.6 5.8 collective-permute-start.20
  90.1 5.0 shard_map.325
  103.8 2.7 collective-permute-done.14.high
  108.3 2.8 collective-permute-done.21.two.refs_1_
  111.1 3.2 shard_map.327
  117.0 3.8 copy.120
  126.8 9.3 %collective-permute-done.28 = bf16[4,64,768]{2,1,0:T(8,128)(2,1)S(1)} collective-permute-done((bf16[4,64,768]{2,1,0:T(8,128)(2,1)S(1)}, bf16[4,64,768]{2,1,0:T(8,128)(2,1)S(1)}, u32[]{:S(2)}, u32[]{:S(2)}) %collective-permute-start.28) | collective-permute-done | bytes 393248 | tf_op jit(solution)/shard_map/ppermute | solution.py:30
  145.6 19.1 %collective-permute-done.31 = bf16[4,64,768]{2,1,0:T(8,128)(2,1)S(1)} collective-permute-done((bf16[4,64,768]{2,1,0:T(8,128)(2,1)S(1)}, bf16[4,64,768]{2,1,0:T(8,128)(2,1)S(1)}, u32[]{:S(2)}, u32[]{:S(2)}) %collective-permute-start.31) | collective-permute-done | bytes 393248 | tf_op jit(solution)/shard_map/ppermute | solution.py:30
  173.3 2.7 collective-permute-done.35
  176.0 3.5 collective-permute-start.38
  192.8 3.9 shard_map.329
  200.3 3.6 collective-permute-start.43
  205.9 7.0 %collective-permute-done.47.refs_3_ = f32[64,512]{1,0:T(8,128)S(1)} collective-permute-done((f32[64,512]{1,0:T(8,128)S(1)}, f32[64,512]{1,0:T(8,128)S(1)}, u32[]{:S(2)}, u32[]{:S(2)}) %collective-permute-start.47) | collective-permute-done | bytes 131104 | tf_op jit(solution)/shard_map/ppermute | solution.py:39
  213.8 4.0 collective-permute-start.50
  218.6 5.0 shard_map.331
  240.1 3.2 shard_map.333
  263.9 2.9 convert_reduce_fusion
  273.2 3.1 multiply_reduce_fusion.2
  281.2 6.1 shard_map.334
  299.4 2.8 collective-permute-start.67
  309.6 3.5 collective-permute-start.60
  323.2 5.7 shard_map.335
  329.0 4.5 shard_map.337
  334.7 2.9 collective-permute-start.72
  338.9 5.5 collective-permute-done.72
  345.6 2.5 collective-permute-start.75
  349.0 13.0 %shard_map.338 = f32[64,768]{1,0:T(8,128)S(1)} custom-call(f32[64,384]{1,0:T(8,128)S(1)} %select_add_fusion.2.grads, f32[64,384]{1,0:T(8,128)S(1)} %copy-done.54, bf16[64,768]{1,0:T(8,128)(2,1)S(1)} %slice.705.land, f32[6,64,64]{2,1,0:T(8,128)S(1)} %copy-done.72, f32[42,64,64]{2,1,0:T(8,128)S(1)} %get-tuple-element.172.inverses, ...), custom_call_target="tpu_custom_call" | custom-call | flops 12999999488 | bytes 39000000 | tf_op jit(solution)/shard_map/pallas_call | solution.py:112
  371.1 2.7 fusion.126
  385.2 7.6 %collective-permute-done.90 = bf16[192,768]{1,0:T(8,128)(2,1)S(1)} collective-permute-done((bf16[192,768]{1,0:T(8,128)(2,1)S(1)}, bf16[192,768]{1,0:T(8,128)(2,1)S(1)}, u32[]{:S(2)}, u32[]{:S(2)}) %collective-permute-start.90) | collective-permute-done | bytes 294944 | tf_op jit(solution)/shard_map/ppermute | solution.py:30
  393.9 5.2 collective-permute-done.83
  399.1 2.7 convert_reduce_fusion.4
  418.3 6.4 collective-permute-done.86
  431.8 5.5 shard_map.340
  450.0 2.6 convolution_bitcast_fusion
  457.3 3.7 collective-permute-start.99
  463.6 5.7 shard_map.341
  475.8 4.5 shard_map.343
  482.8 4.9 collective-permute-start.101
  488.3 13.0 %shard_map.344 = f32[64,768]{1,0:T(8,128)S(1)} custom-call(f32[64,384]{1,0:T(8,128)S(1)} %select_add_fusion.1.grads, f32[64,384]{1,0:T(8,128)S(1)} %copy-done.51, bf16[64,768]{1,0:T(8,128)(2,1)S(1)} %copy-done.6, f32[6,64,64]{2,1,0:T(8,128)S(1)} %copy-done.70, f32[42,64,64]{2,1,0:T(8,128)S(1)} %copy-done.8, f32[36,64,64]{2,1,0:T(8,128)S(1)} %copy-done.56, ...), custom_call_target="tpu_custom_call" | custom-call | flops 12999999488 | bytes 39000000 | tf_op jit(solution)/shard_map/pallas_call | solution.py:112
  504.8 2.9 collective-permute-start.105
  514.0 4.0 collective-permute-start.109
  533.3 3.9 collective-permute-done.111
  537.3 9.2 %reduce-scatter.5.cloned.1.call-done = bf16[4,96,768]{2,1,0:T(8,128)(2,1)} async-done(((bf16[4,768,768]{2,1,0:T(8,128)(2,1)}), bf16[4,96,768]{2,1,0:T(8,128)(2,1)}) %reduce-scatter.5.cloned.1.call-update) | async-done | bytes 589840 | tf_op jit(solution)/shard_map/reduce_scatter | solution.py:956
  555.4 3.0 fusion.127
  566.8 8.4 %collective-permute-done.128 = f32[12288]{0:T(1024)S(1)} collective-permute-done((f32[12288]{0:T(1024)S(1)}, f32[12288]{0:T(1024)S(1)}, u32[]{:S(2)}, u32[]{:S(2)}) %collective-permute-start.128) | collective-permute-done | bytes 49184 | tf_op jit(solution)/shard_map/ppermute | solution.py:33
  585.7 5.7 collective-permute-done.112
  593.3 9.9 %collective-permute-done.113 = bf16[96,768]{1,0:T(8,128)(2,1)S(1)} collective-permute-done((bf16[96,768]{1,0:T(8,128)(2,1)S(1)}, bf16[96,768]{1,0:T(8,128)(2,1)S(1)}, u32[]{:S(2)}, u32[]{:S(2)}) %collective-permute-start.113) | collective-permute-done | bytes 147488 | tf_op jit(solution)/shard_map/ppermute | solution.py:33
  603.4 12.1 %collective-permute-done.114 = bf16[48,768]{1,0:T(8,128)(2,1)S(1)} collective-permute-done((bf16[48,768]{1,0:T(8,128)(2,1)S(1)}, bf16[48,768]{1,0:T(8,128)(2,1)S(1)}, u32[]{:S(2)}, u32[]{:S(2)}) %collective-permute-start.114) | collective-permute-done | bytes 73760 | tf_op jit(solution)/shard_map/ppermute | solution.py:33
  615.7 3.0 collective-permute-start.122
  618.7 7.7 %collective-permute-done.115 = bf16[48,768]{1,0:T(8,128)(2,1)S(1)} collective-permute-done((bf16[48,768]{1,0:T(8,128)(2,1)S(1)}, bf16[48,768]{1,0:T(8,128)(2,1)S(1)}, u32[]{:S(2)}, u32[]{:S(2)}) %collective-permute-start.115) | collective-permute-done | bytes 73760 | tf_op jit(solution)/shard_map/ppermute | solution.py:33
  626.5 7.3 %collective-permute-done.122 = bf16[96,768]{1,0:T(8,128)(2,1)S(1)} collective-permute-done((bf16[96,768]{1,0:T(8,128)(2,1)S(1)}, bf16[96,768]{1,0:T(8,128)(2,1)S(1)}, u32[]{:S(2)}, u32[]{:S(2)}) %collective-permute-start.122) | collective-permute-done | bytes 147488 | tf_op jit(solution)/shard_map/ppermute | solution.py:33
  634.0 5.3 collective-permute-done.116
  640.9 3.2 collective-permute-done.123
  650.8 2.5 maximum_convert_fusion.1
  653.3 2.5 maximum_convert_fusion
  (929 shorter events, 311.2 us)
Async XLA Ops:
  7.2 109.7 %all-gather.15.cloned.1.call-start = ((), (), s32[]{:S(2)}) async-start(), calls=%async_computation.8 | async-start | bytes 3538944 | tf_op jit(solution)/shard_map/all_gather | solution.py:615
  9.0 12.3 %collective-permute-start.5 = (f32[2,1408]{1,0:T(2,128)S(1)}, f32[2,1408]{1,0:T(2,128)S(1)}, u32[]{:S(2)}, u32[]{:S(2)}) collective-permute-start(f32[2,1408]{1,0:T(2,128)S(1)} %pad.31), channel_id=1, source_target_pairs={{0,2},{1,3},{2,0},{3,1},{4,6},{5,7},{6,4},{7,5},{8,10},{9,11},{10,... | collective-permute-start | bytes 33800 | tf_op jit(solution)/shard_map/ppermute | solution.py:30
  12.0 9.4 %collective-permute-start = (bf16[4,64,768]{2,1,0:T(8,128)(2,1)}, bf16[4,64,768]{2,1,0:T(8,128)(2,1)S(1)}, u32[]{:S(2)}, u32[]{:S(2)}) collective-permute-start(bf16[4,64,768]{2,1,0:T(8,128)(2,1)} %own), channel_id=1, source_target_pairs={{0,1},{1,0},{2,3},{3,2},{4,5},{5,4},{6,7},{7,6},{8,9},{9,8},{10,11... | collective-permute-start | bytes 1179656 | tf_op jit(solution)/shard_map/ppermute | solution.py:30
  33.9 24.6 %collective-permute-start.4 = (bf16[576,768]{1,0:T(8,128)(2,1)S(1)}, bf16[576,768]{1,0:T(8,128)(2,1)}, u32[]{:S(2)}, u32[]{:S(2)}) collective-permute-start(bf16[576,768]{1,0:T(8,128)(2,1)S(1)} %pad_maximum_fusion.7), channel_id=1, source_target_pairs={{0,2},{1,3},{2,0},{3,1},{4,6},{5,7},{6,4},{7,5},{8,10},{9,11},{10,... | collective-permute-start | bytes 2654216 | tf_op jit(solution)/shard_map/ppermute | solution.py:30
  38.1 17.1 %collective-permute-start.11 = (bf16[64,384]{1,0:T(8,128)(2,1)S(1)}, bf16[64,384]{1,0:T(8,128)(2,1)S(1)}, u32[]{:S(2)}, u32[]{:S(2)}) collective-permute-start(bf16[64,384]{1,0:T(8,128)(2,1)S(1)} %add_convert_fusion.18), channel_id=1, source_target_pairs={{0,6},{1,7},{2,4},{3,5},{4,2},{5,3},{6,0},{7,1},{8,14},{9,15},{10,... | collective-permute-start | bytes 147464 | tf_op jit(solution)/shard_map/ppermute | solution.py:39
  39.6 15.6 %collective-permute-start.10 = (bf16[64,384]{1,0:T(8,128)(2,1)S(1)}, bf16[64,384]{1,0:T(8,128)(2,1)S(1)}, u32[]{:S(2)}, u32[]{:S(2)}) collective-permute-start(bf16[64,384]{1,0:T(8,128)(2,1)S(1)} %add_convert_fusion.18), channel_id=1, source_target_pairs={{0,4},{4,0},{8,12},{12,8},{16,20},{20,16},{24,28},{28,24},{1,5},{5... | collective-permute-start | bytes 147464 | tf_op jit(solution)/shard_map/ppermute | solution.py:33
  41.1 14.5 %collective-permute-start.9 = (bf16[64,384]{1,0:T(8,128)(2,1)S(1)}, bf16[64,384]{1,0:T(8,128)(2,1)S(1)}, u32[]{:S(2)}, u32[]{:S(2)}) collective-permute-start(bf16[64,384]{1,0:T(8,128)(2,1)S(1)} %add_convert_fusion.18), channel_id=1, source_target_pairs={{0,2},{1,3},{2,0},{3,1},{4,6},{5,7},{6,4},{7,5},{8,10},{9,11},{10,... | collective-permute-start | bytes 147464 | tf_op jit(solution)/shard_map/ppermute | solution.py:30
  61.3 111.1 %all-gather.7.cloned.1.call-start = ((), (), s32[]{:S(2)}) async-start(), calls=%async_computation.2 | async-start | bytes 3538944 | tf_op jit(solution)/shard_map/all_gather | solution.py:615
  71.1 11.6 %collective-permute-start.17 = (f32[64,512]{1,0:T(8,128)S(1)}, f32[64,512]{1,0:T(8,128)S(1)}, u32[]{:S(2)}, u32[]{:S(2)}) collective-permute-start(f32[64,512]{1,0:T(8,128)S(1)} %get-tuple-element.150), channel_id=1, source_target_pairs={{0,6},{1,7},{2,4},{3,5},{4,2},{5,3},{6,0},{7,1},{8,14},{9,15},{10,... | collective-permute-start | bytes 393224 | tf_op jit(solution)/shard_map/ppermute | solution.py:39
  72.9 30.8 %collective-permute-start.24 = (bf16[192,768]{1,0:T(8,128)(2,1)S(1)}, bf16[192,768]{1,0:T(8,128)(2,1)S(1)}, u32[]{:S(2)}, u32[]{:S(2)}) collective-permute-start(bf16[192,768]{1,0:T(8,128)(2,1)S(1)} %copy-done.129), channel_id=1, source_target_pairs={{0,2},{1,3},{2,0},{3,1},{4,6},{5,7},{6,4},{7,5},{8,10},{9,11},{10,... | collective-permute-start | bytes 884744 | tf_op jit(solution)/shard_map/ppermute | solution.py:30
  74.4 29.4 %collective-permute-start.13 = (bf16[384,128]{1,0:T(8,128)(2,1)S(1)}, bf16[384,128]{1,0:T(8,128)(2,1)S(1)}, u32[]{:S(2)}, u32[]{:S(2)}) collective-permute-start(bf16[384,128]{1,0:T(8,128)(2,1)S(1)} %get-tuple-element.145), channel_id=1, source_target_pairs={{0,2},{1,3},{2,4},{3,5},{4,6},{5,7},{6,8},{7,9},{8,10},{9,11},{10,... | collective-permute-start | bytes 294920 | tf_op jit(solution)/shard_map/ppermute | solution.py:53
  83.6 13.3 %collective-permute-start.20 = (f32[64,512]{1,0:T(8,128)S(1)}, f32[64,512]{1,0:T(8,128)S(1)}, u32[]{:S(2)}, u32[]{:S(2)}) collective-permute-start(f32[64,512]{1,0:T(8,128)S(1)} %shard_map.324.refs_0_), channel_id=1, source_target_pairs={{0,24},{4,28},{8,16},{12,20},{16,8},{20,12},{24,0},{28,4},{1,25},{... | collective-permute-start | bytes 393224 | tf_op jit(solution)/shard_map/ppermute | solution.py:33
  96.9 9.6 %collective-permute-start.14 = (bf16[384,128]{1,0:T(8,128)(2,1)S(1)}, bf16[384,128]{1,0:T(8,128)(2,1)S(1)}, u32[]{:S(2)}, u32[]{:S(2)}) collective-permute-start(bf16[384,128]{1,0:T(8,128)(2,1)S(1)} %get-tuple-element.146), channel_id=1, source_target_pairs={{2,0},{3,1},{4,2},{5,3},{6,4},{7,5},{8,6},{9,7},{10,8},{11,9},{12,... | collective-permute-start | bytes 294920 | tf_op jit(solution)/shard_map/ppermute | solution.py:53
  124.9 11.2 %collective-permute-start.28 = (bf16[4,64,768]{2,1,0:T(8,128)(2,1)S(1)}, bf16[4,64,768]{2,1,0:T(8,128)(2,1)S(1)}, u32[]{:S(2)}, u32[]{:S(2)}) collective-permute-start(bf16[4,64,768]{2,1,0:T(8,128)(2,1)S(1)} %fusion.62), channel_id=1, source_target_pairs={{0,2},{1,3},{2,0},{3,1},{4,6},{5,7},{6,4},{7,5},{8,10},{9,11},{10,... | collective-permute-start | bytes 1179656 | tf_op jit(solution)/shard_map/ppermute | solution.py:30
  125.0 11.1 %collective-permute-start.26 = (bf16[4,64,768]{2,1,0:T(8,128)(2,1)S(1)}, bf16[4,64,768]{2,1,0:T(8,128)(2,1)S(1)}, u32[]{:S(2)}, u32[]{:S(2)}) collective-permute-start(bf16[4,64,768]{2,1,0:T(8,128)(2,1)S(1)} %fusion.62), channel_id=1, source_target_pairs={{0,1},{1,0},{2,3},{3,2},{4,5},{5,4},{6,7},{7,6},{8,9},{9,8},{10,11... | collective-permute-start | bytes 1179656 | tf_op jit(solution)/shard_map/ppermute | solution.py:30
  126.3 104.4 %all-gather.9.cloned.1.call-start = ((), (), s32[]{:S(2)}) async-start(), calls=%async_computation.3 | async-start | bytes 3538944 | tf_op jit(solution)/shard_map/all_gather | solution.py:615
  144.4 20.3 %collective-permute-start.31 = (bf16[4,64,768]{2,1,0:T(8,128)(2,1)S(1)}, bf16[4,64,768]{2,1,0:T(8,128)(2,1)S(1)}, u32[]{:S(2)}, u32[]{:S(2)}) collective-permute-start(bf16[4,64,768]{2,1,0:T(8,128)(2,1)S(1)} %add_convert_fusion.4), channel_id=1, source_target_pairs={{0,2},{1,3},{2,0},{3,1},{4,6},{5,7},{6,4},{7,5},{8,10},{9,11},{10,... | collective-permute-start | bytes 1179656 | tf_op jit(solution)/shard_map/ppermute | solution.py:30
  182.9 198.5 %reduce-scatter.3.cloned.1.call-start = ((), (), s32[]{:S(2)}) async-start(), calls=%async_computation.4 | async-start | bytes 5308416 | tf_op jit(solution)/shard_map/reduce_scatter | solution.py:956
  199.0 13.9 %collective-permute-start.47 = (f32[64,512]{1,0:T(8,128)S(1)}, f32[64,512]{1,0:T(8,128)S(1)}, u32[]{:S(2)}, u32[]{:S(2)}) collective-permute-start(f32[64,512]{1,0:T(8,128)S(1)} %get-tuple-element.171), channel_id=1, source_target_pairs={{0,6},{1,7},{2,4},{3,5},{4,2},{5,3},{6,0},{7,1},{8,14},{9,15},{10,... | collective-permute-start | bytes 393224 | tf_op jit(solution)/shard_map/ppermute | solution.py:39
  200.3 36.0 %collective-permute-start.43 = (bf16[384,128]{1,0:T(8,128)(2,1)S(1)}, bf16[384,128]{1,0:T(8,128)(2,1)S(1)}, u32[]{:S(2)}, u32[]{:S(2)}) collective-permute-start(bf16[384,128]{1,0:T(8,128)(2,1)S(1)} %get-tuple-element.166), channel_id=1, source_target_pairs={{0,2},{1,3},{2,4},{3,5},{4,6},{5,7},{6,8},{7,9},{8,10},{9,11},{10,... | collective-permute-start | bytes 294920 | tf_op jit(solution)/shard_map/ppermute | solution.py:53
  203.9 32.3 %collective-permute-start.44 = (bf16[384,128]{1,0:T(8,128)(2,1)S(1)}, bf16[384,128]{1,0:T(8,128)(2,1)S(1)}, u32[]{:S(2)}, u32[]{:S(2)}) collective-permute-start(bf16[384,128]{1,0:T(8,128)(2,1)S(1)} %get-tuple-element.167), channel_id=1, source_target_pairs={{2,0},{3,1},{4,2},{5,3},{6,4},{7,5},{8,6},{9,7},{10,8},{11,9},{12,... | collective-permute-start | bytes 294920 | tf_op jit(solution)/shard_map/ppermute | solution.py:53
  213.8 13.5 %collective-permute-start.50 = (f32[64,512]{1,0:T(8,128)S(1)}, f32[64,512]{1,0:T(8,128)S(1)}, u32[]{:S(2)}, u32[]{:S(2)}) collective-permute-start(f32[64,512]{1,0:T(8,128)S(1)} %shard_map.330.refs_0_), channel_id=1, source_target_pairs={{0,24},{4,28},{8,16},{12,20},{16,8},{20,12},{24,0},{28,4},{1,25},{... | collective-permute-start | bytes 393224 | tf_op jit(solution)/shard_map/ppermute | solution.py:33
  217.9 11.6 %collective-permute-start.49 = (f32[64,512]{1,0:T(8,128)S(1)}, f32[64,512]{1,0:T(8,128)S(1)}, u32[]{:S(2)}, u32[]{:S(2)}) collective-permute-start(f32[64,512]{1,0:T(8,128)S(1)} %shard_map.330.refs_0_), channel_id=1, source_target_pairs={{0,16},{4,20},{8,24},{12,28},{16,0},{20,4},{24,8},{28,12},{1,17},{... | collective-permute-start | bytes 393224 | tf_op jit(solution)/shard_map/ppermute | solution.py:33
  218.1 11.3 %collective-permute-start.48 = (f32[64,512]{1,0:T(8,128)S(1)}, f32[64,512]{1,0:T(8,128)S(1)}, u32[]{:S(2)}, u32[]{:S(2)}) collective-permute-start(f32[64,512]{1,0:T(8,128)S(1)} %shard_map.330.refs_0_), channel_id=1, source_target_pairs={{0,8},{4,12},{8,0},{12,4},{16,24},{20,28},{24,16},{28,20},{1,9},{5... | collective-permute-start | bytes 393224 | tf_op jit(solution)/shard_map/ppermute | solution.py:33
  273.2 197.8 %all-gather.11.cloned.1.call-start = ((), (), s32[]{:S(2)}) async-start(), calls=%async_computation.5 | async-start | bytes 2654208 | tf_op jit(solution)/shard_map/all_gather | solution.py:960
  299.4 15.4 %collective-permute-start.67 = (bf16[64,384]{1,0:T(8,128)(2,1)}, bf16[64,384]{1,0:T(8,128)(2,1)S(1)}, u32[]{:S(2)}, u32[]{:S(2)}) collective-permute-start(bf16[64,384]{1,0:T(8,128)(2,1)} %fusion.85), channel_id=1, source_target_pairs={{0,24},{4,28},{8,16},{12,20},{16,8},{20,12},{24,0},{28,4},{1,25},{... | collective-permute-start | bytes 147464 | tf_op jit(solution)/shard_map/ppermute | solution.py:33
  302.2 12.6 %collective-permute-start.66 = (bf16[64,384]{1,0:T(8,128)(2,1)}, bf16[64,384]{1,0:T(8,128)(2,1)S(1)}, u32[]{:S(2)}, u32[]{:S(2)}) collective-permute-start(bf16[64,384]{1,0:T(8,128)(2,1)} %fusion.85), channel_id=1, source_target_pairs={{0,16},{4,20},{8,24},{12,28},{16,0},{20,4},{24,8},{28,12},{1,17},{... | collective-permute-start | bytes 147464 | tf_op jit(solution)/shard_map/ppermute | solution.py:33
  302.2 13.2 %collective-permute-start.65 = (bf16[64,384]{1,0:T(8,128)(2,1)}, bf16[64,384]{1,0:T(8,128)(2,1)}, u32[]{:S(2)}, u32[]{:S(2)}) collective-permute-start(bf16[64,384]{1,0:T(8,128)(2,1)} %fusion.85), channel_id=1, source_target_pairs={{0,8},{4,12},{8,0},{12,4},{16,24},{20,28},{24,16},{28,20},{1,9},{5... | collective-permute-start | bytes 147464 | tf_op jit(solution)/shard_map/ppermute | solution.py:33
  309.6 13.5 %collective-permute-start.60 = (bf16[384,128]{1,0:T(8,128)(2,1)}, bf16[384,128]{1,0:T(8,128)(2,1)S(1)}, u32[]{:S(2)}, u32[]{:S(2)}) collective-permute-start(bf16[384,128]{1,0:T(8,128)(2,1)} %get-tuple-element.178), channel_id=1, source_target_pairs={{0,2},{1,3},{2,4},{3,5},{4,6},{5,7},{6,8},{7,9},{8,10},{9,11},{10,... | collective-permute-start | bytes 294920 | tf_op jit(solution)/shard_map/ppermute | solution.py:53
  313.1 10.0 %collective-permute-start.61 = (bf16[384,128]{1,0:T(8,128)(2,1)}, bf16[384,128]{1,0:T(8,128)(2,1)S(1)}, u32[]{:S(2)}, u32[]{:S(2)}) collective-permute-start(bf16[384,128]{1,0:T(8,128)(2,1)} %get-tuple-element.179), channel_id=1, source_target_pairs={{2,0},{3,1},{4,2},{5,3},{6,4},{7,5},{8,6},{9,7},{10,8},{11,9},{12,... | collective-permute-start | bytes 294920 | tf_op jit(solution)/shard_map/ppermute | solution.py:53
  318.1 10.8 %collective-permute-start.70 = (bf16[64,512]{1,0:T(8,128)(2,1)S(1)}, bf16[64,512]{1,0:T(8,128)(2,1)S(1)}, u32[]{:S(2)}, u32[]{:S(2)}) collective-permute-start(bf16[64,512]{1,0:T(8,128)(2,1)S(1)} %shard_map.336.refs_4_), channel_id=1, source_target_pairs={{0,6},{1,7},{2,4},{3,5},{4,2},{5,3},{6,0},{7,1},{8,14},{9,15},{10,... | collective-permute-start | bytes 196616 | tf_op jit(solution)/shard_map/ppermute | solution.py:39
  334.7 9.7 %collective-permute-start.72 = (bf16[64,768]{1,0:T(8,128)(2,1)S(1)}, bf16[64,768]{1,0:T(8,128)(2,1)S(1)}, u32[]{:S(2)}, u32[]{:S(2)}) collective-permute-start(bf16[64,768]{1,0:T(8,128)(2,1)S(1)} %get-tuple-element.198), channel_id=1, source_target_pairs={{0,4},{4,0},{8,12},{12,8},{16,20},{20,16},{24,28},{28,24},{1,5},{5... | collective-permute-start | bytes 294920 | tf_op jit(solution)/shard_map/ppermute | solution.py:33
  344.5 17.5 %collective-permute-start.76 = (bf16[64,768]{1,0:T(8,128)(2,1)S(1)}, bf16[64,768]{1,0:T(8,128)(2,1)S(1)}, u32[]{:S(2)}, u32[]{:S(2)}) collective-permute-start(bf16[64,768]{1,0:T(8,128)(2,1)S(1)} %fusion.82), channel_id=1, source_target_pairs={{0,24},{4,28},{8,16},{12,20},{16,8},{20,12},{24,0},{28,4},{1,25},{... | collective-permute-start | bytes 294920 | tf_op jit(solution)/shard_map/ppermute | solution.py:33
  345.6 16.3 %collective-permute-start.75 = (bf16[64,768]{1,0:T(8,128)(2,1)S(1)}, bf16[64,768]{1,0:T(8,128)(2,1)S(1)}, u32[]{:S(2)}, u32[]{:S(2)}) collective-permute-start(bf16[64,768]{1,0:T(8,128)(2,1)S(1)} %fusion.82), channel_id=1, source_target_pairs={{0,16},{4,20},{8,24},{12,28},{16,0},{20,4},{24,8},{28,12},{1,17},{... | collective-permute-start | bytes 294920 | tf_op jit(solution)/shard_map/ppermute | solution.py:33
  348.1 13.8 %collective-permute-start.74 = (bf16[64,768]{1,0:T(8,128)(2,1)S(1)}, bf16[64,768]{1,0:T(8,128)(2,1)S(1)}, u32[]{:S(2)}, u32[]{:S(2)}) collective-permute-start(bf16[64,768]{1,0:T(8,128)(2,1)S(1)} %fusion.82), channel_id=1, source_target_pairs={{0,8},{4,12},{8,0},{12,4},{16,24},{20,28},{24,16},{28,20},{1,9},{5... | collective-permute-start | bytes 294920 | tf_op jit(solution)/shard_map/ppermute | solution.py:33
  382.8 10.0 %collective-permute-start.90 = (bf16[192,768]{1,0:T(8,128)(2,1)S(1)}, bf16[192,768]{1,0:T(8,128)(2,1)S(1)}, u32[]{:S(2)}, u32[]{:S(2)}) collective-permute-start(bf16[192,768]{1,0:T(8,128)(2,1)S(1)} %select_bitcast_fusion), channel_id=1, source_target_pairs={{0,2},{1,3},{2,0},{3,1},{4,6},{5,7},{6,4},{7,5},{8,10},{9,11},{10,... | collective-permute-start | bytes 884744 | tf_op jit(solution)/shard_map/ppermute | solution.py:30
  384.8 14.3 %collective-permute-start.83 = (bf16[4,64,768]{2,1,0:T(8,128)(2,1)S(1)}, bf16[4,64,768]{2,1,0:T(8,128)(2,1)}, u32[]{:S(2)}, u32[]{:S(2)}) collective-permute-start(bf16[4,64,768]{2,1,0:T(8,128)(2,1)S(1)} %get-tuple-element.333), channel_id=1, source_target_pairs={{0,2},{1,3},{2,0},{3,1},{4,6},{5,7},{6,4},{7,5},{8,10},{9,11},{10,... | collective-permute-start | bytes 1179656 | tf_op jit(solution)/shard_map/ppermute | solution.py:30
  393.7 152.8 %reduce-scatter.5.cloned.1.call-start = ((), (), s32[]{:S(2)}) async-start(), calls=%async_computation.6 | async-start | bytes 5308416 | tf_op jit(solution)/shard_map/reduce_scatter | solution.py:956
  405.0 12.5 %collective-permute-start.82 = (bf16[4,64,768]{2,1,0:T(8,128)(2,1)}, bf16[4,64,768]{2,1,0:T(8,128)(2,1)S(1)}, u32[]{:S(2)}, u32[]{:S(2)}) collective-permute-start(bf16[4,64,768]{2,1,0:T(8,128)(2,1)} %select_convert_fusion.4), channel_id=1, source_target_pairs={{0,1},{1,0},{2,3},{3,2},{4,5},{5,4},{6,7},{7,6},{8,9},{9,8},{10,11... | collective-permute-start | bytes 1179656 | tf_op jit(solution)/shard_map/ppermute | solution.py:30
  413.0 11.6 %collective-permute-start.86 = (bf16[4,64,768]{2,1,0:T(8,128)(2,1)}, bf16[4,64,768]{2,1,0:T(8,128)(2,1)}, u32[]{:S(2)}, u32[]{:S(2)}) collective-permute-start(bf16[4,64,768]{2,1,0:T(8,128)(2,1)} %add_convert_fusion.2), channel_id=1, source_target_pairs={{0,2},{1,3},{2,0},{3,1},{4,6},{5,7},{6,4},{7,5},{8,10},{9,11},{10,... | collective-permute-start | bytes 1179656 | tf_op jit(solution)/shard_map/ppermute | solution.py:30
  417.3 229.1 %all-gather.13.cloned.1.call-start = ((), (), s32[]{:S(2)}) async-start(), calls=%async_computation.7 | async-start | bytes 3981312 | tf_op jit(solution)/shard_map/all_gather | solution.py:1124
  445.6 10.8 %collective-permute-start.96 = (bf16[64,384]{1,0:T(8,128)(2,1)S(1)}, bf16[64,384]{1,0:T(8,128)(2,1)S(1)}, u32[]{:S(2)}, u32[]{:S(2)}) collective-permute-start(bf16[64,384]{1,0:T(8,128)(2,1)S(1)} %fusion.86), channel_id=1, source_target_pairs={{0,24},{4,28},{8,16},{12,20},{16,8},{20,12},{24,0},{28,4},{1,25},{... | collective-permute-start | bytes 147464 | tf_op jit(solution)/shard_map/ppermute | solution.py:33
  452.6 10.9 %collective-permute-start.88 = (bf16[384,128]{1,0:T(8,128)(2,1)S(1)}, bf16[384,128]{1,0:T(8,128)(2,1)S(1)}, u32[]{:S(2)}, u32[]{:S(2)}) collective-permute-start(bf16[384,128]{1,0:T(8,128)(2,1)S(1)} %get-tuple-element.207), channel_id=1, source_target_pairs={{0,2},{1,3},{2,4},{3,5},{4,6},{5,7},{6,8},{7,9},{8,10},{9,11},{10,... | collective-permute-start | bytes 294920 | tf_op jit(solution)/shard_map/ppermute | solution.py:53
  457.3 13.6 %collective-permute-start.99 = (bf16[64,512]{1,0:T(8,128)(2,1)S(1)}, bf16[64,512]{1,0:T(8,128)(2,1)S(1)}, u32[]{:S(2)}, u32[]{:S(2)}) collective-permute-start(bf16[64,512]{1,0:T(8,128)(2,1)S(1)} %shard_map.342.refs_4_), channel_id=1, source_target_pairs={{0,6},{1,7},{2,4},{3,5},{4,2},{5,3},{6,0},{7,1},{8,14},{9,15},{10,... | collective-permute-start | bytes 196616 | tf_op jit(solution)/shard_map/ppermute | solution.py:39
  460.9 10.0 %collective-permute-start.98 = (bf16[64,512]{1,0:T(8,128)(2,1)S(1)}, bf16[64,512]{1,0:T(8,128)(2,1)S(1)}, u32[]{:S(2)}, u32[]{:S(2)}) collective-permute-start(bf16[64,512]{1,0:T(8,128)(2,1)S(1)} %shard_map.342.refs_4_), channel_id=1, source_target_pairs={{0,4},{4,0},{8,12},{12,8},{16,20},{20,16},{24,28},{28,24},{1,5},{5... | collective-permute-start | bytes 196616 | tf_op jit(solution)/shard_map/ppermute | solution.py:33
  480.4 21.1 %collective-permute-start.100 = (bf16[64,768]{1,0:T(8,128)(2,1)S(1)}, bf16[64,768]{1,0:T(8,128)(2,1)S(1)}, u32[]{:S(2)}, u32[]{:S(2)}) collective-permute-start(bf16[64,768]{1,0:T(8,128)(2,1)S(1)} %get-tuple-element.231), channel_id=1, source_target_pairs={{0,2},{1,3},{2,0},{3,1},{4,6},{5,7},{6,4},{7,5},{8,10},{9,11},{10,... | collective-permute-start | bytes 294920 | tf_op jit(solution)/shard_map/ppermute | solution.py:30
  482.8 18.7 %collective-permute-start.101 = (bf16[64,768]{1,0:T(8,128)(2,1)S(1)}, bf16[64,768]{1,0:T(8,128)(2,1)S(1)}, u32[]{:S(2)}, u32[]{:S(2)}) collective-permute-start(bf16[64,768]{1,0:T(8,128)(2,1)S(1)} %get-tuple-element.232), channel_id=1, source_target_pairs={{0,4},{4,0},{8,12},{12,8},{16,20},{20,16},{24,28},{28,24},{1,5},{5... | collective-permute-start | bytes 294920 | tf_op jit(solution)/shard_map/ppermute | solution.py:33
  487.7 13.7 %collective-permute-start.102 = (bf16[64,768]{1,0:T(8,128)(2,1)S(1)}, bf16[64,768]{1,0:T(8,128)(2,1)S(1)}, u32[]{:S(2)}, u32[]{:S(2)}) collective-permute-start(bf16[64,768]{1,0:T(8,128)(2,1)S(1)} %get-tuple-element.233), channel_id=1, source_target_pairs={{0,6},{1,7},{2,4},{3,5},{4,2},{5,3},{6,0},{7,1},{8,14},{9,15},{10,... | collective-permute-start | bytes 294920 | tf_op jit(solution)/shard_map/ppermute | solution.py:39
  501.6 12.4 %collective-permute-start.103 = (bf16[384,768]{1,0:T(8,128)(2,1)S(1)}, bf16[384,768]{1,0:T(8,128)(2,1)S(1)}, u32[]{:S(2)}, u32[]{:S(2)}) collective-permute-start(bf16[384,768]{1,0:T(8,128)(2,1)S(1)} %bitcast.430), channel_id=1, source_target_pairs={{0,2},{1,3},{2,0},{3,1},{4,6},{5,7},{6,4},{7,5},{8,10},{9,11},{10,... | collective-permute-start | bytes 1769480 | tf_op jit(solution)/shard_map/ppermute | solution.py:30
  519.5 44.6 %collective-permute-start.118 = (bf16[192,768]{1,0:T(8,128)(2,1)}, bf16[192,768]{1,0:T(8,128)(2,1)}, u32[]{:S(2)}, u32[]{:S(2)}) collective-permute-start(bf16[192,768]{1,0:T(8,128)(2,1)} %broadcast_select_fusion.21), channel_id=1, source_target_pairs={{0,8},{4,12},{8,0},{12,4},{16,24},{20,28},{24,16},{28,20},{1,9},{5... | collective-permute-start | bytes 884744 | tf_op jit(solution)/shard_map/ppermute | solution.py:33
  527.2 9.9 %collective-permute-start.111 = (bf16[384,768]{1,0:T(8,128)(2,1)S(1)}, bf16[384,768]{1,0:T(8,128)(2,1)S(1)}, u32[]{:S(2)}, u32[]{:S(2)}) collective-permute-start(bf16[384,768]{1,0:T(8,128)(2,1)S(1)} %bitcast.431), channel_id=1, source_target_pairs={{0,2},{1,3},{2,0},{3,1},{4,6},{5,7},{6,4},{7,5},{8,10},{9,11},{10,... | collective-permute-start | bytes 1769480 | tf_op jit(solution)/shard_map/ppermute | solution.py:30
  528.3 20.7 %collective-permute-start.125 = (f32[12288]{0:T(1024)S(1)}, f32[12288]{0:T(1024)S(1)}, u32[]{:S(2)}, u32[]{:S(2)}) collective-permute-start(f32[12288]{0:T(1024)S(1)} %pad.38), channel_id=1, source_target_pairs={{0,2},{1,3},{2,0},{3,1},{4,6},{5,7},{6,4},{7,5},{8,10},{9,11},{10,... | collective-permute-start | bytes 147464 | tf_op jit(solution)/shard_map/ppermute | solution.py:30
  549.0 9.4 %collective-permute-start.126 = (f32[12288]{0:T(1024)S(1)}, f32[12288]{0:T(1024)S(1)}, u32[]{:S(2)}, u32[]{:S(2)}) collective-permute-start(f32[12288]{0:T(1024)S(1)} %pad_add_fusion), channel_id=1, source_target_pairs={{0,4},{4,0},{8,12},{12,8},{16,20},{20,16},{24,28},{28,24},{1,5},{5... | collective-permute-start | bytes 147464 | tf_op jit(solution)/shard_map/ppermute | solution.py:33
  560.6 79.2 %collective-permute-start.110 = (bf16[4,64,768]{2,1,0:T(8,128)(2,1)}, bf16[4,64,768]{2,1,0:T(8,128)(2,1)S(1)}, u32[]{:S(2)}, u32[]{:S(2)}) collective-permute-start(bf16[4,64,768]{2,1,0:T(8,128)(2,1)} %select_convert_fusion.2), channel_id=1, source_target_pairs={{0,1},{1,0},{2,3},{3,2},{4,5},{5,4},{6,7},{7,6},{8,9},{9,8},{10,11... | collective-permute-start | bytes 1179656 | tf_op jit(solution)/shard_map/ppermute | solution.py:30
  562.6 12.5 %collective-permute-start.128 = (f32[12288]{0:T(1024)S(1)}, f32[12288]{0:T(1024)S(1)}, u32[]{:S(2)}, u32[]{:S(2)}) collective-permute-start(f32[12288]{0:T(1024)S(1)} %add.741), channel_id=1, source_target_pairs={{0,16},{4,20},{8,24},{12,28},{16,0},{20,4},{24,8},{28,12},{1,17},{... | collective-permute-start | bytes 147464 | tf_op jit(solution)/shard_map/ppermute | solution.py:33
  565.2 18.2 %collective-permute-start.119 = (bf16[96,768]{1,0:T(8,128)(2,1)S(1)}, bf16[96,768]{1,0:T(8,128)(2,1)S(1)}, u32[]{:S(2)}, u32[]{:S(2)}) collective-permute-start(bf16[96,768]{1,0:T(8,128)(2,1)S(1)} %broadcast_select_fusion.31), channel_id=1, source_target_pairs={{0,16},{4,20},{8,24},{12,28},{16,0},{20,4},{24,8},{28,12},{1,17},{... | collective-permute-start | bytes 442376 | tf_op jit(solution)/shard_map/ppermute | solution.py:33
  581.6 9.9 %collective-permute-start.112 = (bf16[192,768]{1,0:T(8,128)(2,1)S(1)}, bf16[192,768]{1,0:T(8,128)(2,1)S(1)}, u32[]{:S(2)}, u32[]{:S(2)}) collective-permute-start(bf16[192,768]{1,0:T(8,128)(2,1)S(1)} %broadcast_select_fusion.24), channel_id=1, source_target_pairs={{0,4},{4,0},{8,12},{12,8},{16,20},{20,16},{24,28},{28,24},{1,5},{5... | collective-permute-start | bytes 884744 | tf_op jit(solution)/shard_map/ppermute | solution.py:33
  591.6 11.6 %collective-permute-start.113 = (bf16[96,768]{1,0:T(8,128)(2,1)S(1)}, bf16[96,768]{1,0:T(8,128)(2,1)S(1)}, u32[]{:S(2)}, u32[]{:S(2)}) collective-permute-start(bf16[96,768]{1,0:T(8,128)(2,1)S(1)} %broadcast_select_fusion.34), channel_id=1, source_target_pairs={{0,8},{4,12},{8,0},{12,4},{16,24},{20,28},{24,16},{28,20},{1,9},{5... | collective-permute-start | bytes 442376 | tf_op jit(solution)/shard_map/ppermute | solution.py:33
  592.7 10.7 %collective-permute-start.121 = (bf16[48,768]{1,0:T(8,128)(2,1)S(1)}, bf16[48,768]{1,0:T(8,128)(2,1)S(1)}, u32[]{:S(2)}, u32[]{:S(2)}) collective-permute-start(bf16[48,768]{1,0:T(8,128)(2,1)S(1)} %add_convert_fusion.15), channel_id=1, source_target_pairs={{0,4},{4,0},{8,12},{12,8},{16,20},{20,16},{24,28},{28,24},{1,5},{5... | collective-permute-start | bytes 221192 | tf_op jit(solution)/shard_map/ppermute | solution.py:33
  603.3 12.2 %collective-permute-start.114 = (bf16[48,768]{1,0:T(8,128)(2,1)S(1)}, bf16[48,768]{1,0:T(8,128)(2,1)S(1)}, u32[]{:S(2)}, u32[]{:S(2)}) collective-permute-start(bf16[48,768]{1,0:T(8,128)(2,1)S(1)} %broadcast_select_fusion.40), channel_id=1, source_target_pairs={{0,16},{4,20},{8,24},{12,28},{16,0},{20,4},{24,8},{28,12},{1,17},{... | collective-permute-start | bytes 221192 | tf_op jit(solution)/shard_map/ppermute | solution.py:33
  615.6 10.8 %collective-permute-start.115 = (bf16[48,768]{1,0:T(8,128)(2,1)S(1)}, bf16[48,768]{1,0:T(8,128)(2,1)S(1)}, u32[]{:S(2)}, u32[]{:S(2)}) collective-permute-start(bf16[48,768]{1,0:T(8,128)(2,1)S(1)} %add_convert_fusion.16), channel_id=1, source_target_pairs={{0,16},{4,20},{8,24},{12,28},{16,0},{20,4},{24,8},{28,12},{1,17},{... | collective-permute-start | bytes 221192 | tf_op jit(solution)/shard_map/ppermute | solution.py:33
  615.7 18.1 %collective-permute-start.122 = (bf16[96,768]{1,0:T(8,128)(2,1)S(1)}, bf16[96,768]{1,0:T(8,128)(2,1)S(1)}, u32[]{:S(2)}, u32[]{:S(2)}) collective-permute-start(bf16[96,768]{1,0:T(8,128)(2,1)S(1)} %pad_maximum_fusion.24), channel_id=1, source_target_pairs={{0,16},{4,20},{8,24},{12,28},{16,0},{20,4},{24,8},{28,12},{1,17},{... | collective-permute-start | bytes 442376 | tf_op jit(solution)/shard_map/ppermute | solution.py:33
  626.4 12.8 %collective-permute-start.116 = (bf16[96,768]{1,0:T(8,128)(2,1)S(1)}, bf16[96,768]{1,0:T(8,128)(2,1)S(1)}, u32[]{:S(2)}, u32[]{:S(2)}) collective-permute-start(bf16[96,768]{1,0:T(8,128)(2,1)S(1)} %pad_maximum_fusion.23), channel_id=1, source_target_pairs={{0,8},{4,12},{8,0},{12,4},{16,24},{20,28},{24,16},{28,20},{1,9},{5... | collective-permute-start | bytes 442376 | tf_op jit(solution)/shard_map/ppermute | solution.py:33
  633.9 10.2 %collective-permute-start.123 = (bf16[192,768]{1,0:T(8,128)(2,1)S(1)}, bf16[192,768]{1,0:T(8,128)(2,1)S(1)}, u32[]{:S(2)}, u32[]{:S(2)}) collective-permute-start(bf16[192,768]{1,0:T(8,128)(2,1)S(1)} %pad_maximum_fusion.20), channel_id=1, source_target_pairs={{0,8},{4,12},{8,0},{12,4},{16,24},{20,28},{24,16},{28,20},{1,9},{5... | collective-permute-start | bytes 884744 | tf_op jit(solution)/shard_map/ppermute | solution.py:33
  (258 other events, 1996.3 us)
Sparse Core Ops, SparseCore 0:
  61.5 54.6 all-gather.14
  126.4 45.3 all-gather.6
  183.0 46.1 all-gather.8
  273.3 107.9 reduce-scatter.2
  393.8 50.5 all-gather.10
  448.4 98.0 reduce-scatter.4
  555.5 82.2 all-gather.12

commit v5 on v4

--- a/solution.py
+++ b/solution.py
@@ -160,7 +160,7 @@
     return low.astype(LOW), high.astype(LOW)
 
 
-def far_kernel(half, spot, qkv, land, one, two, three, four, low, high):
+def far_kernel(half, spot, qkv, land, base, one, two, three, four, low, high):
     width = qkv.shape[0] // 3
     head_dim = LANDMARKS
     heads = width // head_dim
@@ -168,8 +168,7 @@
     scale = head_dim ** (-0.5)
     for step, out in enumerate((one, two, three, four)):
         here = tokens_of(spot[0] ^ step, tok_row)
-        logs = jnp.zeros((LANDMARKS, out.shape[1] - width), jnp.float32)
-        lane = lanes(logs.shape)
+        logs = []
         for head in range(heads):
             cols = slice(head * head_dim, (head + 1) * head_dim)
             keys = qkv[width + head * head_dim : width + (head + 1) * head_dim, here]
@@ -179,9 +178,10 @@
             top = jnp.max(scores, axis=1, keepdims=True)
             grown = jnp.exp(scores - top)
             total = jnp.sum(grown, axis=1, keepdims=True)
-            out[:, cols] = nt(grown.astype(LOW), values) / total
-            logs = jnp.where(lane == head, top + jnp.log(total), logs)
-        out[:, width:] = logs
+            mix = nt(grown.astype(LOW), values) / total
+            out[:, cols] = (mix - base[step : step + 1, cols]).astype(LOW)
+            logs.append(top + jnp.log(total))
+        out[:, width:] = packed_parts(logs)
     low[...], high[...] = rim_blocks(
         lambda row: qkv[2 * width :, row * tok_row : (row + 1) * tok_row], 4, tok_row, half
     )
@@ -192,14 +192,13 @@
     mixes, logs = [], []
     for head in range(width // head_dim):
         cols = slice(head * head_dim, (head + 1) * head_dim)
-        column = slice(width + head, width + head + 1)
-        log = [pieces[0][:, column]]
-        for index, piece in enumerate(pieces[1:]):
-            log.append(jnp.where(flags[index] > 0, piece[:, column], FLOOR_TOP))
+        log = [unpacked_part(piece[:, width:], head) for piece in pieces]
+        for index in range(1, len(pieces)):
+            log[index] = jnp.where(flags[index - 1] > 0, log[index], FLOOR_TOP)
         top = functools.reduce(jnp.maximum, log)
         shares = [jnp.exp(value - top) for value in log]
         total = functools.reduce(jnp.add, shares)
-        mix = sum(share * piece[:, cols] for share, piece in zip(shares, pieces))
+        mix = sum(s * piece[:, cols].astype(jnp.float32) for s, piece in zip(shares, pieces))
         mixes.append(mix / total)
         logs.append(top + jnp.log(total))
     return mixes, logs
@@ -209,12 +208,9 @@
     out = refs[count]
     width = out.shape[1] - 128
     mixes, logs = merged(flags, refs[:count], width)
-    packed = jnp.zeros((LANDMARKS, 128), jnp.float32)
-    lane = lanes(packed.shape)
-    for head, (mix, log) in enumerate(zip(mixes, logs)):
-        out[:, head * LANDMARKS : (head + 1) * LANDMARKS] = mix
-        packed = jnp.where(lane == head, log, packed)
-    out[:, width:] = packed
+    for head, mix in enumerate(mixes):
+        out[:, head * LANDMARKS : (head + 1) * LANDMARKS] = mix.astype(LOW)
+    out[:, width:] = packed_parts(logs)
 
 
 def packed_parts(columns):
@@ -238,11 +234,12 @@
 
 
 def land_out_kernel(count, flags, *refs):
-    inverse, out, weighted = refs[count:]
+    inverse, base, out, weighted = refs[count:]
     width = weighted.shape[1]
     mixes, logs = merged(flags, refs[:count], width)
     for head, mix in enumerate(mixes):
         cols = slice(head * LANDMARKS, (head + 1) * LANDMARKS)
+        mix = mix + base[0:1, cols]
         weighted[:, cols] = mix
         out[:, cols] = nn(inverse[head], mix, HIGHEST).astype(LOW)
     out[:, width:] = packed_parts(logs)
@@ -538,20 +535,20 @@
     return total
 
 
-def land_mixture(pieces, inverse, layout):
+def land_mixture(pieces, inverse, base, layout):
     span = layout["span"]
     width = pieces[0].shape[1] - 128
     pieces = send_rows(pieces)
     flags = jnp.ones((3,), jnp.int32)
     for low, bits in upper_levels():
         call = functools.partial(merge_kernel, len(pieces))
-        (row,) = on_core(call, [(pieces[0].shape, jnp.float32)], flags, *pieces)
+        (row,) = on_core(call, [(pieces[0].shape, LOW)], flags, *pieces)
         pieces = [row] + [exchange(row, m << (low + 1), 0) for m in range(1, 1 << bits)]
         wide = (span > 8 << low).astype(jnp.int32)
         flags = jnp.stack([(span > 4 << low).astype(jnp.int32), wide, wide])
     outs = [(pieces[0].shape, LOW), ((LANDMARKS, width), jnp.float32)]
     call = functools.partial(land_out_kernel, len(pieces))
-    return on_core(call, outs, flags, *pieces, inverse)
+    return on_core(call, outs, flags, *pieces, inverse, base)
 
 
 def item_layout(item_lengths, tok_row, half):
@@ -711,10 +708,13 @@
     land = nt(pooled, weights["qkv"][: 2 * width]) + jnp.concatenate([bias_q, no_bias])
     land = land.astype(LOW)
     heads = width // LANDMARKS
-    message = [((LANDMARKS, width + 128), jnp.float32)] * 4
+    message = [((LANDMARKS, width + 128), LOW)] * 4
+    means = jnp.mean(pooled.reshape(4, LANDMARKS, -1).astype(jnp.float32), axis=1)
+    base = nt(means.astype(LOW), weights["qkv"][2 * width :]) + bias_v
+    base = jnp.pad(base, ((0, 4), (0, 0)))
     rim = [((width, batch_rows * half), LOW)] * 2
     *parts, low, high = on_core(
-        functools.partial(far_kernel, half), message + rim, spot, qkv, land, us=4
+        functools.partial(far_kernel, half), message + rim, spot, qkv, land, base, us=4
     )
     low, high = rank_shift(high, 1), rank_shift(low, -1)
     square = (LANDMARKS, LANDMARKS)
@@ -734,7 +734,7 @@
         us=5,
     )
     inverse = chain[1][NS_STEPS * heads :]
-    own_out, weighted = land_mixture(parts, inverse, layout)
+    own_out, weighted = land_mixture(parts, inverse, base, layout)
     if params["offload"]:
         own_out, weights["down"] = tied(own_out, weights["down"])
     mixes = spread_row(own_out)
@@ -925,7 +925,7 @@
     else:
         grad_weight = nn(grad_qkv[: 2 * width], kept["x_full"]).reshape(2, width, model)
         attn_grad = across_sum(split_across(grad_weight))
-        attn_grad, packed = tied(attn_grad, ffn_grad[1])
+        unused, packed = tied(attn_grad, ffn_grad[1])
         ffn_grad = (ffn_grad[0], packed)
         attn_grad = jnp.concatenate([attn_grad, first_grad], axis=0)
     grad_bias = jnp.sum(grad_qkv.astype(jnp.float32), axis=1)

time: 670 us -> 660 us (0.985)
  waiting for transfers between devices: 211 us -> 202 us
    unnamed x371 -> x383, local copies, waits for them, and re-layouts: 32.3 us -> 32.3 us
  transfers between devices with their start and end apart: 137 -> 137, of which waited for: 63 -> 62; matrix products, arithmetic and copies ran while one was open for 17% -> 17% of each run, Pallas kernels for 13% -> 14%
where the time goes in v5:
time: 660 us; the launch traced here: 653 us
  waiting for transfers between devices  202 us (31%)
  starting transfers between devices  159 us (24%)
  Pallas kernels  92.3 us (14%)
  local copies, waits for them, and re-layouts  76 us (12%)
  other arithmetic  59.3 us (9%)
  matrix products  45.8 us (7%)
  between operations  19.5 us (3%)
    pallas_call x24, Pallas kernels, on_core(): pl.pallas_call(kernel, out_shape=shapes, in_specs=specs, out_specs=tuple(...  92.3 us
    ppermute x55, waiting for transfers between devices, exchange(): lax.ppermute(values, 'seq', [(i, i ^ seq_mask) for i in range(count)])  83.3 us
    ppermute x55, starting transfers between devices, exchange(): lax.ppermute(values, 'seq', [(i, i ^ seq_mask) for i in range(count)])  73.9 us
    ppermute x51, waiting for transfers between devices, exchange(): lax.ppermute(values, 'head', [(i, i ^ head_mask) for i in range(count)])  71.1 us
    ppermute x51, starting transfers between devices, exchange(): lax.ppermute(values, 'head', [(i, i ^ head_mask) for i in range(count)])  40.6 us
    unnamed x383, local copies, waits for them, and re-layouts  32.3 us
    ppermute x16, waiting for transfers between devices, exchange(): return lax.ppermute(values, ('seq', 'head'), route)  30.3 us
    ppermute x16, starting transfers between devices, exchange(): return lax.ppermute(values, ('seq', 'head'), route)  25.9 us
  transfers between devices with their start and end apart: 137, of which 62 were waited for; matrix products, arithmetic and copies ran while one was open for 17% of the time, Pallas kernels for 14%

profile of v5, /device:TPU:0, one launch (start us, length us, event | category | flops | bytes accessed | tf_op | source)
XLA Modules:
  0.0 653.1 jit_solution(831058607962762621)
XLA Ops:
  9.0 3.0 collective-permute-start.5
  25.9 2.8 collective-permute-done.3
  28.7 3.7 collective-permute-start.8
  34.8 2.6 collective-permute-done.7
  41.1 13.5 %collective-permute-done.11 = bf16[64,384]{1,0:T(8,128)(2,1)S(1)} collective-permute-done((bf16[64,384]{1,0:T(8,128)(2,1)S(1)}, bf16[64,384]{1,0:T(8,128)(2,1)S(1)}, u32[]{:S(2)}, u32[]{:S(2)}) %collective-permute-start.11) | collective-permute-done | bytes 49184 | tf_op jit(solution)/shard_map/ppermute | solution.py:39
  64.1 4.0 shard_map.323
  73.6 2.6 collective-permute-start.13
  78.9 3.5 collective-permute-start.20
  83.4 5.0 shard_map.325
  93.9 3.2 collective-permute-start.23
  100.8 3.0 collective-permute-done.23.four.refs_3_
  105.3 3.2 shard_map.327
  112.7 3.3 copy.120
  123.0 8.4 %collective-permute-done.28 = bf16[4,64,768]{2,1,0:T(8,128)(2,1)S(1)} collective-permute-done((bf16[4,64,768]{2,1,0:T(8,128)(2,1)S(1)}, bf16[4,64,768]{2,1,0:T(8,128)(2,1)S(1)}, u32[]{:S(2)}, u32[]{:S(2)}) %collective-permute-start.28) | collective-permute-done | bytes 393248 | tf_op jit(solution)/shard_map/ppermute | solution.py:30
  141.0 18.9 %collective-permute-done.31 = bf16[4,64,768]{2,1,0:T(8,128)(2,1)S(1)} collective-permute-done((bf16[4,64,768]{2,1,0:T(8,128)(2,1)S(1)}, bf16[4,64,768]{2,1,0:T(8,128)(2,1)S(1)}, u32[]{:S(2)}, u32[]{:S(2)}) %collective-permute-start.31) | collective-permute-done | bytes 393248 | tf_op jit(solution)/shard_map/ppermute | solution.py:30
  171.5 3.5 collective-permute-start.38
  188.9 4.0 shard_map.329
  196.4 3.3 collective-permute-start.43
  203.4 3.9 collective-permute-start.50
  208.0 5.0 shard_map.331
  218.8 2.6 all-gather.9.cloned.1.call-done
  229.8 3.2 shard_map.333
  253.6 2.9 convert_reduce_fusion
  260.3 2.5 pad_maximum_fusion
  262.9 3.1 multiply_reduce_fusion.2
  270.9 6.1 shard_map.334
  289.7 3.3 collective-permute-start.67
  299.9 3.5 collective-permute-start.60
  307.7 3.1 collective-permute-start.70
  312.8 5.7 shard_map.335
  318.6 4.5 shard_map.337
  324.3 4.3 collective-permute-start.72
  330.0 5.4 collective-permute-done.72
  339.9 13.0 %shard_map.338 = f32[64,768]{1,0:T(8,128)S(1)} custom-call(f32[64,384]{1,0:T(8,128)S(1)} %select_add_fusion.2.grads, f32[64,384]{1,0:T(8,128)S(1)} %copy-done.52, bf16[64,768]{1,0:T(8,128)(2,1)S(1)} %slice.724.land, f32[6,64,64]{2,1,0:T(8,128)S(1)} %copy-done.70, f32[42,64,64]{2,1,0:T(8,128)S(1)} %get-tuple-element.171.inverses, ...), custom_call_target="tpu_custom_call" | custom-call | flops 12999999488 | bytes 39000000 | tf_op jit(solution)/shard_map/pallas_call | solution.py:112
  361.8 2.7 fusion.124
  375.3 7.6 %collective-permute-done.90 = bf16[192,768]{1,0:T(8,128)(2,1)S(1)} collective-permute-done((bf16[192,768]{1,0:T(8,128)(2,1)S(1)}, bf16[192,768]{1,0:T(8,128)(2,1)S(1)}, u32[]{:S(2)}, u32[]{:S(2)}) %collective-permute-start.90) | collective-permute-done | bytes 294944 | tf_op jit(solution)/shard_map/ppermute | solution.py:30
  384.0 5.2 collective-permute-done.83
  389.2 2.7 convert_reduce_fusion.4
  404.6 2.5 pad_maximum_fusion.1
  408.1 6.6 %collective-permute-done.86 = bf16[4,64,768]{2,1,0:T(8,128)(2,1)} collective-permute-done((bf16[4,64,768]{2,1,0:T(8,128)(2,1)}, bf16[4,64,768]{2,1,0:T(8,128)(2,1)}, u32[]{:S(2)}, u32[]{:S(2)}) %collective-permute-start.86) | collective-permute-done | bytes 393248 | tf_op jit(solution)/shard_map/ppermute | solution.py:30
  421.8 5.5 shard_map.340
  438.4 2.6 collective-permute-start.94
  441.0 2.6 convolution_bitcast_fusion
  448.0 2.9 collective-permute-start.99
  453.4 5.7 shard_map.341
  466.2 4.5 shard_map.343
  473.2 5.2 collective-permute-start.101
  478.9 13.0 %shard_map.344 = f32[64,768]{1,0:T(8,128)S(1)} custom-call(f32[64,384]{1,0:T(8,128)S(1)} %select_add_fusion.1.grads, f32[64,384]{1,0:T(8,128)S(1)} %copy-done.49, bf16[64,768]{1,0:T(8,128)(2,1)S(1)} %copy-done.6, f32[6,64,64]{2,1,0:T(8,128)S(1)} %copy-done.68, f32[42,64,64]{2,1,0:T(8,128)S(1)} %copy-done.8, f32[36,64,64]{2,1,0:T(8,128)S(1)} %copy-done.54, ...), custom_call_target="tpu_custom_call" | custom-call | flops 12999999488 | bytes 39000000 | tf_op jit(solution)/shard_map/pallas_call | solution.py:112
  504.5 4.0 collective-permute-start.109
  523.5 3.9 collective-permute-done.111
  527.5 9.5 %reduce-scatter.5.cloned.1.call-done = bf16[4,96,768]{2,1,0:T(8,128)(2,1)} async-done(((bf16[4,768,768]{2,1,0:T(8,128)(2,1)}), bf16[4,96,768]{2,1,0:T(8,128)(2,1)}) %reduce-scatter.5.cloned.1.call-update) | async-done | bytes 589840 | tf_op jit(solution)/shard_map/reduce_scatter | solution.py:956
  545.9 3.0 fusion.125
  549.9 3.2 collective-permute-done.127
  554.8 2.5 collective-permute-start.119
  557.3 7.7 %collective-permute-done.128 = f32[12288]{0:T(1024)S(1)} collective-permute-done((f32[12288]{0:T(1024)S(1)}, f32[12288]{0:T(1024)S(1)}, u32[]{:S(2)}, u32[]{:S(2)}) %collective-permute-start.128) | collective-permute-done | bytes 49184 | tf_op jit(solution)/shard_map/ppermute | solution.py:33
  575.0 6.3 collective-permute-done.112
  584.0 9.0 %collective-permute-done.113 = bf16[96,768]{1,0:T(8,128)(2,1)S(1)} collective-permute-done((bf16[96,768]{1,0:T(8,128)(2,1)S(1)}, bf16[96,768]{1,0:T(8,128)(2,1)S(1)}, u32[]{:S(2)}, u32[]{:S(2)}) %collective-permute-start.113) | collective-permute-done | bytes 147488 | tf_op jit(solution)/shard_map/ppermute | solution.py:33
  593.3 12.2 %collective-permute-done.114 = bf16[48,768]{1,0:T(8,128)(2,1)S(1)} collective-permute-done((bf16[48,768]{1,0:T(8,128)(2,1)S(1)}, bf16[48,768]{1,0:T(8,128)(2,1)S(1)}, u32[]{:S(2)}, u32[]{:S(2)}) %collective-permute-start.114) | collective-permute-done | bytes 73760 | tf_op jit(solution)/shard_map/ppermute | solution.py:33
  605.6 3.0 collective-permute-start.122
  608.5 7.7 %collective-permute-done.115 = bf16[48,768]{1,0:T(8,128)(2,1)S(1)} collective-permute-done((bf16[48,768]{1,0:T(8,128)(2,1)S(1)}, bf16[48,768]{1,0:T(8,128)(2,1)S(1)}, u32[]{:S(2)}, u32[]{:S(2)}) %collective-permute-start.115) | collective-permute-done | bytes 73760 | tf_op jit(solution)/shard_map/ppermute | solution.py:33
  616.4 7.3 %collective-permute-done.122 = bf16[96,768]{1,0:T(8,128)(2,1)S(1)} collective-permute-done((bf16[96,768]{1,0:T(8,128)(2,1)S(1)}, bf16[96,768]{1,0:T(8,128)(2,1)S(1)}, u32[]{:S(2)}, u32[]{:S(2)}) %collective-permute-start.122) | collective-permute-done | bytes 147488 | tf_op jit(solution)/shard_map/ppermute | solution.py:33
  623.8 5.3 collective-permute-done.116
  638.6 2.5 maximum_convert_fusion.1
  641.1 2.5 maximum_convert_fusion
  (948 shorter events, 311.0 us)
Async XLA Ops:
  7.2 105.5 %all-gather.15.cloned.1.call-start = ((), (), s32[]{:S(2)}) async-start(), calls=%async_computation.8 | async-start | bytes 3538944 | tf_op jit(solution)/shard_map/all_gather | solution.py:612
  9.0 11.7 %collective-permute-start.5 = (f32[2,1408]{1,0:T(2,128)S(1)}, f32[2,1408]{1,0:T(2,128)S(1)}, u32[]{:S(2)}, u32[]{:S(2)}) collective-permute-start(f32[2,1408]{1,0:T(2,128)S(1)} %pad.38), channel_id=1, source_target_pairs={{0,2},{1,3},{2,0},{3,1},{4,6},{5,7},{6,4},{7,5},{8,10},{9,11},{10,... | collective-permute-start | bytes 33800 | tf_op jit(solution)/shard_map/ppermute | solution.py:30
  33.2 23.5 %collective-permute-start.4 = (bf16[576,768]{1,0:T(8,128)(2,1)S(1)}, bf16[576,768]{1,0:T(8,128)(2,1)}, u32[]{:S(2)}, u32[]{:S(2)}) collective-permute-start(bf16[576,768]{1,0:T(8,128)(2,1)S(1)} %pad_maximum_fusion.7), channel_id=1, source_target_pairs={{0,2},{1,3},{2,0},{3,1},{4,6},{5,7},{6,4},{7,5},{8,10},{9,11},{10,... | collective-permute-start | bytes 2654216 | tf_op jit(solution)/shard_map/ppermute | solution.py:30
  37.5 17.1 %collective-permute-start.11 = (bf16[64,384]{1,0:T(8,128)(2,1)S(1)}, bf16[64,384]{1,0:T(8,128)(2,1)S(1)}, u32[]{:S(2)}, u32[]{:S(2)}) collective-permute-start(bf16[64,384]{1,0:T(8,128)(2,1)S(1)} %add_convert_fusion.18), channel_id=1, source_target_pairs={{0,6},{1,7},{2,4},{3,5},{4,2},{5,3},{6,0},{7,1},{8,14},{9,15},{10,... | collective-permute-start | bytes 147464 | tf_op jit(solution)/shard_map/ppermute | solution.py:39
  39.0 15.6 %collective-permute-start.10 = (bf16[64,384]{1,0:T(8,128)(2,1)S(1)}, bf16[64,384]{1,0:T(8,128)(2,1)S(1)}, u32[]{:S(2)}, u32[]{:S(2)}) collective-permute-start(bf16[64,384]{1,0:T(8,128)(2,1)S(1)} %add_convert_fusion.18), channel_id=1, source_target_pairs={{0,4},{4,0},{8,12},{12,8},{16,20},{20,16},{24,28},{28,24},{1,5},{5... | collective-permute-start | bytes 147464 | tf_op jit(solution)/shard_map/ppermute | solution.py:33
  40.5 14.5 %collective-permute-start.9 = (bf16[64,384]{1,0:T(8,128)(2,1)S(1)}, bf16[64,384]{1,0:T(8,128)(2,1)S(1)}, u32[]{:S(2)}, u32[]{:S(2)}) collective-permute-start(bf16[64,384]{1,0:T(8,128)(2,1)S(1)} %add_convert_fusion.18), channel_id=1, source_target_pairs={{0,2},{1,3},{2,0},{3,1},{4,6},{5,7},{6,4},{7,5},{8,10},{9,11},{10,... | collective-permute-start | bytes 147464 | tf_op jit(solution)/shard_map/ppermute | solution.py:30
  60.6 107.0 %all-gather.7.cloned.1.call-start = ((), (), s32[]{:S(2)}) async-start(), calls=%async_computation.2 | async-start | bytes 3538944 | tf_op jit(solution)/shard_map/all_gather | solution.py:612
  72.0 36.8 %collective-permute-start.24 = (bf16[192,768]{1,0:T(8,128)(2,1)}, bf16[192,768]{1,0:T(8,128)(2,1)}, u32[]{:S(2)}, u32[]{:S(2)}) collective-permute-start(bf16[192,768]{1,0:T(8,128)(2,1)} %get-tuple-element.152), channel_id=1, source_target_pairs={{0,2},{1,3},{2,0},{3,1},{4,6},{5,7},{6,4},{7,5},{8,10},{9,11},{10,... | collective-permute-start | bytes 884744 | tf_op jit(solution)/shard_map/ppermute | solution.py:30
  73.6 24.5 %collective-permute-start.13 = (bf16[384,128]{1,0:T(8,128)(2,1)S(1)}, bf16[384,128]{1,0:T(8,128)(2,1)S(1)}, u32[]{:S(2)}, u32[]{:S(2)}) collective-permute-start(bf16[384,128]{1,0:T(8,128)(2,1)S(1)} %get-tuple-element.144), channel_id=1, source_target_pairs={{0,2},{1,3},{2,4},{3,5},{4,6},{5,7},{6,8},{7,9},{8,10},{9,11},{10,... | collective-permute-start | bytes 294920 | tf_op jit(solution)/shard_map/ppermute | solution.py:53
  78.9 12.2 %collective-permute-start.20 = (bf16[64,512]{1,0:T(8,128)(2,1)S(1)}, bf16[64,512]{1,0:T(8,128)(2,1)S(1)}, u32[]{:S(2)}, u32[]{:S(2)}) collective-permute-start(bf16[64,512]{1,0:T(8,128)(2,1)S(1)} %shard_map.324.refs_0_), channel_id=1, source_target_pairs={{0,24},{4,28},{8,16},{12,20},{16,8},{20,12},{24,0},{28,4},{1,25},{... | collective-permute-start | bytes 196616 | tf_op jit(solution)/shard_map/ppermute | solution.py:33
  82.5 10.0 %collective-permute-start.19 = (bf16[64,512]{1,0:T(8,128)(2,1)S(1)}, bf16[64,512]{1,0:T(8,128)(2,1)S(1)}, u32[]{:S(2)}, u32[]{:S(2)}) collective-permute-start(bf16[64,512]{1,0:T(8,128)(2,1)S(1)} %shard_map.324.refs_0_), channel_id=1, source_target_pairs={{0,16},{4,20},{8,24},{12,28},{16,0},{20,4},{24,8},{28,12},{1,17},{... | collective-permute-start | bytes 196616 | tf_op jit(solution)/shard_map/ppermute | solution.py:33
  82.5 10.0 %collective-permute-start.18 = (bf16[64,512]{1,0:T(8,128)(2,1)S(1)}, bf16[64,512]{1,0:T(8,128)(2,1)S(1)}, u32[]{:S(2)}, u32[]{:S(2)}) collective-permute-start(bf16[64,512]{1,0:T(8,128)(2,1)S(1)} %shard_map.324.refs_0_), channel_id=1, source_target_pairs={{0,8},{4,12},{8,0},{12,4},{16,24},{20,28},{24,16},{28,20},{1,9},{5... | collective-permute-start | bytes 196616 | tf_op jit(solution)/shard_map/ppermute | solution.py:33
  91.1 9.6 %collective-permute-start.14 = (bf16[384,128]{1,0:T(8,128)(2,1)S(1)}, bf16[384,128]{1,0:T(8,128)(2,1)S(1)}, u32[]{:S(2)}, u32[]{:S(2)}) collective-permute-start(bf16[384,128]{1,0:T(8,128)(2,1)S(1)} %get-tuple-element.145), channel_id=1, source_target_pairs={{2,0},{3,1},{4,2},{5,3},{6,4},{7,5},{8,6},{9,7},{10,8},{11,9},{12,... | collective-permute-start | bytes 294920 | tf_op jit(solution)/shard_map/ppermute | solution.py:53
  93.9 9.9 %collective-permute-start.23 = (bf16[64,512]{1,0:T(8,128)(2,1)S(1)}, bf16[64,512]{1,0:T(8,128)(2,1)S(1)}, u32[]{:S(2)}, u32[]{:S(2)}) collective-permute-start(bf16[64,512]{1,0:T(8,128)(2,1)S(1)} %get-tuple-element.151.one.refs_0_), channel_id=1, source_target_pairs={{0,6},{1,7},{2,4},{3,5},{4,2},{5,3},{6,0},{7,1},{8,14},{9,15},{10,... | collective-permute-start | bytes 196616 | tf_op jit(solution)/shard_map/ppermute | solution.py:39
  120.1 11.2 %collective-permute-start.28 = (bf16[4,64,768]{2,1,0:T(8,128)(2,1)S(1)}, bf16[4,64,768]{2,1,0:T(8,128)(2,1)S(1)}, u32[]{:S(2)}, u32[]{:S(2)}) collective-permute-start(bf16[4,64,768]{2,1,0:T(8,128)(2,1)S(1)} %fusion.62), channel_id=1, source_target_pairs={{0,2},{1,3},{2,0},{3,1},{4,6},{5,7},{6,4},{7,5},{8,10},{9,11},{10,... | collective-permute-start | bytes 1179656 | tf_op jit(solution)/shard_map/ppermute | solution.py:30
  121.4 10.0 %collective-permute-start.26 = (bf16[4,64,768]{2,1,0:T(8,128)(2,1)S(1)}, bf16[4,64,768]{2,1,0:T(8,128)(2,1)S(1)}, u32[]{:S(2)}, u32[]{:S(2)}) collective-permute-start(bf16[4,64,768]{2,1,0:T(8,128)(2,1)S(1)} %fusion.62), channel_id=1, source_target_pairs={{0,1},{1,0},{2,3},{3,2},{4,5},{5,4},{6,7},{7,6},{8,9},{9,8},{10,11... | collective-permute-start | bytes 1179656 | tf_op jit(solution)/shard_map/ppermute | solution.py:30
  122.5 98.9 %all-gather.9.cloned.1.call-start = ((), (), s32[]{:S(2)}) async-start(), calls=%async_computation.3 | async-start | bytes 3538944 | tf_op jit(solution)/shard_map/all_gather | solution.py:612
  139.6 20.2 %collective-permute-start.31 = (bf16[4,64,768]{2,1,0:T(8,128)(2,1)S(1)}, bf16[4,64,768]{2,1,0:T(8,128)(2,1)S(1)}, u32[]{:S(2)}, u32[]{:S(2)}) collective-permute-start(bf16[4,64,768]{2,1,0:T(8,128)(2,1)S(1)} %add_convert_fusion.4), channel_id=1, source_target_pairs={{0,2},{1,3},{2,0},{3,1},{4,6},{5,7},{6,4},{7,5},{8,10},{9,11},{10,... | collective-permute-start | bytes 1179656 | tf_op jit(solution)/shard_map/ppermute | solution.py:30
  178.3 193.1 %reduce-scatter.3.cloned.1.call-start = ((), (), s32[]{:S(2)}) async-start(), calls=%async_computation.4 | async-start | bytes 5308416 | tf_op jit(solution)/shard_map/reduce_scatter | solution.py:956
  196.4 28.4 %collective-permute-start.43 = (bf16[384,128]{1,0:T(8,128)(2,1)S(1)}, bf16[384,128]{1,0:T(8,128)(2,1)S(1)}, u32[]{:S(2)}, u32[]{:S(2)}) collective-permute-start(bf16[384,128]{1,0:T(8,128)(2,1)S(1)} %get-tuple-element.165), channel_id=1, source_target_pairs={{0,2},{1,3},{2,4},{3,5},{4,6},{5,7},{6,8},{7,9},{8,10},{9,11},{10,... | collective-permute-start | bytes 294920 | tf_op jit(solution)/shard_map/ppermute | solution.py:53
  199.7 25.2 %collective-permute-start.44 = (bf16[384,128]{1,0:T(8,128)(2,1)S(1)}, bf16[384,128]{1,0:T(8,128)(2,1)S(1)}, u32[]{:S(2)}, u32[]{:S(2)}) collective-permute-start(bf16[384,128]{1,0:T(8,128)(2,1)S(1)} %get-tuple-element.166), channel_id=1, source_target_pairs={{2,0},{3,1},{4,2},{5,3},{6,4},{7,5},{8,6},{9,7},{10,8},{11,9},{12,... | collective-permute-start | bytes 294920 | tf_op jit(solution)/shard_map/ppermute | solution.py:53
  203.4 12.7 %collective-permute-start.50 = (bf16[64,512]{1,0:T(8,128)(2,1)S(1)}, bf16[64,512]{1,0:T(8,128)(2,1)S(1)}, u32[]{:S(2)}, u32[]{:S(2)}) collective-permute-start(bf16[64,512]{1,0:T(8,128)(2,1)S(1)} %shard_map.330.refs_0_), channel_id=1, source_target_pairs={{0,24},{4,28},{8,16},{12,20},{16,8},{20,12},{24,0},{28,4},{1,25},{... | collective-permute-start | bytes 196616 | tf_op jit(solution)/shard_map/ppermute | solution.py:33
  207.6 9.3 %collective-permute-start.48 = (bf16[64,512]{1,0:T(8,128)(2,1)S(1)}, bf16[64,512]{1,0:T(8,128)(2,1)S(1)}, u32[]{:S(2)}, u32[]{:S(2)}) collective-permute-start(bf16[64,512]{1,0:T(8,128)(2,1)S(1)} %shard_map.330.refs_0_), channel_id=1, source_target_pairs={{0,8},{4,12},{8,0},{12,4},{16,24},{20,28},{24,16},{28,20},{1,9},{5... | collective-permute-start | bytes 196616 | tf_op jit(solution)/shard_map/ppermute | solution.py:33
  262.8 198.5 %all-gather.11.cloned.1.call-start = ((), (), s32[]{:S(2)}) async-start(), calls=%async_computation.5 | async-start | bytes 2654208 | tf_op jit(solution)/shard_map/all_gather | solution.py:960
  289.7 15.3 %collective-permute-start.67 = (bf16[64,384]{1,0:T(8,128)(2,1)}, bf16[64,384]{1,0:T(8,128)(2,1)S(1)}, u32[]{:S(2)}, u32[]{:S(2)}) collective-permute-start(bf16[64,384]{1,0:T(8,128)(2,1)} %fusion.80), channel_id=1, source_target_pairs={{0,24},{4,28},{8,16},{12,20},{16,8},{20,12},{24,0},{28,4},{1,25},{... | collective-permute-start | bytes 147464 | tf_op jit(solution)/shard_map/ppermute | solution.py:33
  293.1 12.0 %collective-permute-start.66 = (bf16[64,384]{1,0:T(8,128)(2,1)}, bf16[64,384]{1,0:T(8,128)(2,1)}, u32[]{:S(2)}, u32[]{:S(2)}) collective-permute-start(bf16[64,384]{1,0:T(8,128)(2,1)} %fusion.80), channel_id=1, source_target_pairs={{0,16},{4,20},{8,24},{12,28},{16,0},{20,4},{24,8},{28,12},{1,17},{... | collective-permute-start | bytes 147464 | tf_op jit(solution)/shard_map/ppermute | solution.py:33
  293.1 12.0 %collective-permute-start.65 = (bf16[64,384]{1,0:T(8,128)(2,1)}, bf16[64,384]{1,0:T(8,128)(2,1)}, u32[]{:S(2)}, u32[]{:S(2)}) collective-permute-start(bf16[64,384]{1,0:T(8,128)(2,1)} %fusion.80), channel_id=1, source_target_pairs={{0,8},{4,12},{8,0},{12,4},{16,24},{20,28},{24,16},{28,20},{1,9},{5... | collective-permute-start | bytes 147464 | tf_op jit(solution)/shard_map/ppermute | solution.py:33
  299.9 12.9 %collective-permute-start.60 = (bf16[384,128]{1,0:T(8,128)(2,1)}, bf16[384,128]{1,0:T(8,128)(2,1)S(1)}, u32[]{:S(2)}, u32[]{:S(2)}) collective-permute-start(bf16[384,128]{1,0:T(8,128)(2,1)} %get-tuple-element.177), channel_id=1, source_target_pairs={{0,2},{1,3},{2,4},{3,5},{4,6},{5,7},{6,8},{7,9},{8,10},{9,11},{10,... | collective-permute-start | bytes 294920 | tf_op jit(solution)/shard_map/ppermute | solution.py:53
  303.4 9.4 %collective-permute-start.61 = (bf16[384,128]{1,0:T(8,128)(2,1)}, bf16[384,128]{1,0:T(8,128)(2,1)S(1)}, u32[]{:S(2)}, u32[]{:S(2)}) collective-permute-start(bf16[384,128]{1,0:T(8,128)(2,1)} %get-tuple-element.178), channel_id=1, source_target_pairs={{2,0},{3,1},{4,2},{5,3},{6,4},{7,5},{8,6},{9,7},{10,8},{11,9},{12,... | collective-permute-start | bytes 294920 | tf_op jit(solution)/shard_map/ppermute | solution.py:53
  307.7 10.8 %collective-permute-start.70 = (bf16[64,512]{1,0:T(8,128)(2,1)S(1)}, bf16[64,512]{1,0:T(8,128)(2,1)S(1)}, u32[]{:S(2)}, u32[]{:S(2)}) collective-permute-start(bf16[64,512]{1,0:T(8,128)(2,1)S(1)} %shard_map.336.refs_4_), channel_id=1, source_target_pairs={{0,6},{1,7},{2,4},{3,5},{4,2},{5,3},{6,0},{7,1},{8,14},{9,15},{10,... | collective-permute-start | bytes 196616 | tf_op jit(solution)/shard_map/ppermute | solution.py:39
  324.3 11.0 %collective-permute-start.72 = (bf16[64,768]{1,0:T(8,128)(2,1)S(1)}, bf16[64,768]{1,0:T(8,128)(2,1)S(1)}, u32[]{:S(2)}, u32[]{:S(2)}) collective-permute-start(bf16[64,768]{1,0:T(8,128)(2,1)S(1)} %get-tuple-element.197), channel_id=1, source_target_pairs={{0,4},{4,0},{8,12},{12,8},{16,20},{20,16},{24,28},{28,24},{1,5},{5... | collective-permute-start | bytes 294920 | tf_op jit(solution)/shard_map/ppermute | solution.py:33
  335.4 17.5 %collective-permute-start.76 = (bf16[64,768]{1,0:T(8,128)(2,1)S(1)}, bf16[64,768]{1,0:T(8,128)(2,1)S(1)}, u32[]{:S(2)}, u32[]{:S(2)}) collective-permute-start(bf16[64,768]{1,0:T(8,128)(2,1)S(1)} %fusion.77), channel_id=1, source_target_pairs={{0,24},{4,28},{8,16},{12,20},{16,8},{20,12},{24,0},{28,4},{1,25},{... | collective-permute-start | bytes 294920 | tf_op jit(solution)/shard_map/ppermute | solution.py:33
  335.8 17.0 %collective-permute-start.75 = (bf16[64,768]{1,0:T(8,128)(2,1)S(1)}, bf16[64,768]{1,0:T(8,128)(2,1)S(1)}, u32[]{:S(2)}, u32[]{:S(2)}) collective-permute-start(bf16[64,768]{1,0:T(8,128)(2,1)S(1)} %fusion.77), channel_id=1, source_target_pairs={{0,16},{4,20},{8,24},{12,28},{16,0},{20,4},{24,8},{28,12},{1,17},{... | collective-permute-start | bytes 294920 | tf_op jit(solution)/shard_map/ppermute | solution.py:33
  338.1 14.8 %collective-permute-start.74 = (bf16[64,768]{1,0:T(8,128)(2,1)S(1)}, bf16[64,768]{1,0:T(8,128)(2,1)S(1)}, u32[]{:S(2)}, u32[]{:S(2)}) collective-permute-start(bf16[64,768]{1,0:T(8,128)(2,1)S(1)} %fusion.77), channel_id=1, source_target_pairs={{0,8},{4,12},{8,0},{12,4},{16,24},{20,28},{24,16},{28,20},{1,9},{5... | collective-permute-start | bytes 294920 | tf_op jit(solution)/shard_map/ppermute | solution.py:33
  372.9 10.0 %collective-permute-start.90 = (bf16[192,768]{1,0:T(8,128)(2,1)S(1)}, bf16[192,768]{1,0:T(8,128)(2,1)S(1)}, u32[]{:S(2)}, u32[]{:S(2)}) collective-permute-start(bf16[192,768]{1,0:T(8,128)(2,1)S(1)} %select_bitcast_fusion), channel_id=1, source_target_pairs={{0,2},{1,3},{2,0},{3,1},{4,6},{5,7},{6,4},{7,5},{8,10},{9,11},{10,... | collective-permute-start | bytes 884744 | tf_op jit(solution)/shard_map/ppermute | solution.py:30
  374.6 14.6 %collective-permute-start.83 = (bf16[4,64,768]{2,1,0:T(8,128)(2,1)S(1)}, bf16[4,64,768]{2,1,0:T(8,128)(2,1)}, u32[]{:S(2)}, u32[]{:S(2)}) collective-permute-start(bf16[4,64,768]{2,1,0:T(8,128)(2,1)S(1)} %get-tuple-element.331), channel_id=1, source_target_pairs={{0,2},{1,3},{2,0},{3,1},{4,6},{5,7},{6,4},{7,5},{8,10},{9,11},{10,... | collective-permute-start | bytes 1179656 | tf_op jit(solution)/shard_map/ppermute | solution.py:30
  383.8 153.3 %reduce-scatter.5.cloned.1.call-start = ((), (), s32[]{:S(2)}) async-start(), calls=%async_computation.6 | async-start | bytes 5308416 | tf_op jit(solution)/shard_map/reduce_scatter | solution.py:956
  395.0 12.3 %collective-permute-start.82 = (bf16[4,64,768]{2,1,0:T(8,128)(2,1)}, bf16[4,64,768]{2,1,0:T(8,128)(2,1)S(1)}, u32[]{:S(2)}, u32[]{:S(2)}) collective-permute-start(bf16[4,64,768]{2,1,0:T(8,128)(2,1)} %select_convert_fusion.4), channel_id=1, source_target_pairs={{0,1},{1,0},{2,3},{3,2},{4,5},{5,4},{6,7},{7,6},{8,9},{9,8},{10,11... | collective-permute-start | bytes 1179656 | tf_op jit(solution)/shard_map/ppermute | solution.py:30
  403.1 11.6 %collective-permute-start.86 = (bf16[4,64,768]{2,1,0:T(8,128)(2,1)}, bf16[4,64,768]{2,1,0:T(8,128)(2,1)}, u32[]{:S(2)}, u32[]{:S(2)}) collective-permute-start(bf16[4,64,768]{2,1,0:T(8,128)(2,1)} %add_convert_fusion.2), channel_id=1, source_target_pairs={{0,2},{1,3},{2,0},{3,1},{4,6},{5,7},{6,4},{7,5},{8,10},{9,11},{10,... | collective-permute-start | bytes 1179656 | tf_op jit(solution)/shard_map/ppermute | solution.py:30
  407.1 229.1 %all-gather.13.cloned.1.call-start = ((), (), s32[]{:S(2)}) async-start(), calls=%async_computation.7 | async-start | bytes 3981312 | tf_op jit(solution)/shard_map/all_gather | solution.py:1124
  436.6 10.6 %collective-permute-start.96 = (bf16[64,384]{1,0:T(8,128)(2,1)S(1)}, bf16[64,384]{1,0:T(8,128)(2,1)S(1)}, u32[]{:S(2)}, u32[]{:S(2)}) collective-permute-start(bf16[64,384]{1,0:T(8,128)(2,1)S(1)} %fusion.81), channel_id=1, source_target_pairs={{0,24},{4,28},{8,16},{12,20},{16,8},{20,12},{24,0},{28,4},{1,25},{... | collective-permute-start | bytes 147464 | tf_op jit(solution)/shard_map/ppermute | solution.py:33
  443.7 9.7 %collective-permute-start.88 = (bf16[384,128]{1,0:T(8,128)(2,1)S(1)}, bf16[384,128]{1,0:T(8,128)(2,1)S(1)}, u32[]{:S(2)}, u32[]{:S(2)}) collective-permute-start(bf16[384,128]{1,0:T(8,128)(2,1)S(1)} %get-tuple-element.206), channel_id=1, source_target_pairs={{0,2},{1,3},{2,4},{3,5},{4,6},{5,7},{6,8},{7,9},{8,10},{9,11},{10,... | collective-permute-start | bytes 294920 | tf_op jit(solution)/shard_map/ppermute | solution.py:53
  448.0 13.3 %collective-permute-start.99 = (bf16[64,512]{1,0:T(8,128)(2,1)S(1)}, bf16[64,512]{1,0:T(8,128)(2,1)S(1)}, u32[]{:S(2)}, u32[]{:S(2)}) collective-permute-start(bf16[64,512]{1,0:T(8,128)(2,1)S(1)} %shard_map.342.refs_4_), channel_id=1, source_target_pairs={{0,6},{1,7},{2,4},{3,5},{4,2},{5,3},{6,0},{7,1},{8,14},{9,15},{10,... | collective-permute-start | bytes 196616 | tf_op jit(solution)/shard_map/ppermute | solution.py:39
  451.0 10.4 %collective-permute-start.98 = (bf16[64,512]{1,0:T(8,128)(2,1)S(1)}, bf16[64,512]{1,0:T(8,128)(2,1)S(1)}, u32[]{:S(2)}, u32[]{:S(2)}) collective-permute-start(bf16[64,512]{1,0:T(8,128)(2,1)S(1)} %shard_map.342.refs_4_), channel_id=1, source_target_pairs={{0,4},{4,0},{8,12},{12,8},{16,20},{20,16},{24,28},{28,24},{1,5},{5... | collective-permute-start | bytes 196616 | tf_op jit(solution)/shard_map/ppermute | solution.py:33
  470.8 21.2 %collective-permute-start.100 = (bf16[64,768]{1,0:T(8,128)(2,1)S(1)}, bf16[64,768]{1,0:T(8,128)(2,1)S(1)}, u32[]{:S(2)}, u32[]{:S(2)}) collective-permute-start(bf16[64,768]{1,0:T(8,128)(2,1)S(1)} %get-tuple-element.230), channel_id=1, source_target_pairs={{0,2},{1,3},{2,0},{3,1},{4,6},{5,7},{6,4},{7,5},{8,10},{9,11},{10,... | collective-permute-start | bytes 294920 | tf_op jit(solution)/shard_map/ppermute | solution.py:30
  473.2 18.9 %collective-permute-start.101 = (bf16[64,768]{1,0:T(8,128)(2,1)S(1)}, bf16[64,768]{1,0:T(8,128)(2,1)S(1)}, u32[]{:S(2)}, u32[]{:S(2)}) collective-permute-start(bf16[64,768]{1,0:T(8,128)(2,1)S(1)} %get-tuple-element.231), channel_id=1, source_target_pairs={{0,4},{4,0},{8,12},{12,8},{16,20},{20,16},{24,28},{28,24},{1,5},{5... | collective-permute-start | bytes 294920 | tf_op jit(solution)/shard_map/ppermute | solution.py:33
  478.3 13.7 %collective-permute-start.102 = (bf16[64,768]{1,0:T(8,128)(2,1)S(1)}, bf16[64,768]{1,0:T(8,128)(2,1)S(1)}, u32[]{:S(2)}, u32[]{:S(2)}) collective-permute-start(bf16[64,768]{1,0:T(8,128)(2,1)S(1)} %get-tuple-element.232), channel_id=1, source_target_pairs={{0,6},{1,7},{2,4},{3,5},{4,2},{5,3},{6,0},{7,1},{8,14},{9,15},{10,... | collective-permute-start | bytes 294920 | tf_op jit(solution)/shard_map/ppermute | solution.py:39
  492.1 12.4 %collective-permute-start.103 = (bf16[384,768]{1,0:T(8,128)(2,1)S(1)}, bf16[384,768]{1,0:T(8,128)(2,1)S(1)}, u32[]{:S(2)}, u32[]{:S(2)}) collective-permute-start(bf16[384,768]{1,0:T(8,128)(2,1)S(1)} %bitcast.444), channel_id=1, source_target_pairs={{0,2},{1,3},{2,0},{3,1},{4,6},{5,7},{6,4},{7,5},{8,10},{9,11},{10,... | collective-permute-start | bytes 1769480 | tf_op jit(solution)/shard_map/ppermute | solution.py:30
  510.0 43.6 %collective-permute-start.118 = (bf16[192,768]{1,0:T(8,128)(2,1)}, bf16[192,768]{1,0:T(8,128)(2,1)}, u32[]{:S(2)}, u32[]{:S(2)}) collective-permute-start(bf16[192,768]{1,0:T(8,128)(2,1)} %broadcast_select_fusion.21), channel_id=1, source_target_pairs={{0,8},{4,12},{8,0},{12,4},{16,24},{20,28},{24,16},{28,20},{1,9},{5... | collective-permute-start | bytes 884744 | tf_op jit(solution)/shard_map/ppermute | solution.py:33
  517.4 9.9 %collective-permute-start.111 = (bf16[384,768]{1,0:T(8,128)(2,1)S(1)}, bf16[384,768]{1,0:T(8,128)(2,1)S(1)}, u32[]{:S(2)}, u32[]{:S(2)}) collective-permute-start(bf16[384,768]{1,0:T(8,128)(2,1)S(1)} %bitcast.445), channel_id=1, source_target_pairs={{0,2},{1,3},{2,0},{3,1},{4,6},{5,7},{6,4},{7,5},{8,10},{9,11},{10,... | collective-permute-start | bytes 1769480 | tf_op jit(solution)/shard_map/ppermute | solution.py:30
  518.6 20.9 %collective-permute-start.125 = (f32[12288]{0:T(1024)S(1)}, f32[12288]{0:T(1024)S(1)}, u32[]{:S(2)}, u32[]{:S(2)}) collective-permute-start(f32[12288]{0:T(1024)S(1)} %pad.47), channel_id=1, source_target_pairs={{0,2},{1,3},{2,0},{3,1},{4,6},{5,7},{6,4},{7,5},{8,10},{9,11},{10,... | collective-permute-start | bytes 147464 | tf_op jit(solution)/shard_map/ppermute | solution.py:30
  539.5 9.4 %collective-permute-start.126 = (f32[12288]{0:T(1024)S(1)}, f32[12288]{0:T(1024)S(1)}, u32[]{:S(2)}, u32[]{:S(2)}) collective-permute-start(f32[12288]{0:T(1024)S(1)} %pad_add_fusion), channel_id=1, source_target_pairs={{0,4},{4,0},{8,12},{12,8},{16,20},{20,16},{24,28},{28,24},{1,5},{5... | collective-permute-start | bytes 147464 | tf_op jit(solution)/shard_map/ppermute | solution.py:33
  549.9 80.6 %collective-permute-start.110 = (bf16[4,64,768]{2,1,0:T(8,128)(2,1)}, bf16[4,64,768]{2,1,0:T(8,128)(2,1)S(1)}, u32[]{:S(2)}, u32[]{:S(2)}) collective-permute-start(bf16[4,64,768]{2,1,0:T(8,128)(2,1)} %select_convert_fusion.2), channel_id=1, source_target_pairs={{0,1},{1,0},{2,3},{3,2},{4,5},{5,4},{6,7},{7,6},{8,9},{9,8},{10,11... | collective-permute-start | bytes 1179656 | tf_op jit(solution)/shard_map/ppermute | solution.py:30
  553.1 11.9 %collective-permute-start.128 = (f32[12288]{0:T(1024)S(1)}, f32[12288]{0:T(1024)S(1)}, u32[]{:S(2)}, u32[]{:S(2)}) collective-permute-start(f32[12288]{0:T(1024)S(1)} %add.765), channel_id=1, source_target_pairs={{0,16},{4,20},{8,24},{12,28},{16,0},{20,4},{24,8},{28,12},{1,17},{... | collective-permute-start | bytes 147464 | tf_op jit(solution)/shard_map/ppermute | solution.py:33
  554.8 18.2 %collective-permute-start.119 = (bf16[96,768]{1,0:T(8,128)(2,1)S(1)}, bf16[96,768]{1,0:T(8,128)(2,1)S(1)}, u32[]{:S(2)}, u32[]{:S(2)}) collective-permute-start(bf16[96,768]{1,0:T(8,128)(2,1)S(1)} %broadcast_select_fusion.31), channel_id=1, source_target_pairs={{0,16},{4,20},{8,24},{12,28},{16,0},{20,4},{24,8},{28,12},{1,17},{... | collective-permute-start | bytes 442376 | tf_op jit(solution)/shard_map/ppermute | solution.py:33
  571.5 9.9 %collective-permute-start.112 = (bf16[192,768]{1,0:T(8,128)(2,1)S(1)}, bf16[192,768]{1,0:T(8,128)(2,1)S(1)}, u32[]{:S(2)}, u32[]{:S(2)}) collective-permute-start(bf16[192,768]{1,0:T(8,128)(2,1)S(1)} %broadcast_select_fusion.24), channel_id=1, source_target_pairs={{0,4},{4,0},{8,12},{12,8},{16,20},{20,16},{24,28},{28,24},{1,5},{5... | collective-permute-start | bytes 884744 | tf_op jit(solution)/shard_map/ppermute | solution.py:33
  573.1 9.5 %collective-permute-start.120 = (bf16[48,768]{1,0:T(8,128)(2,1)S(1)}, bf16[48,768]{1,0:T(8,128)(2,1)S(1)}, u32[]{:S(2)}, u32[]{:S(2)}) collective-permute-start(bf16[48,768]{1,0:T(8,128)(2,1)S(1)} %broadcast_select_fusion.37), channel_id=1, source_target_pairs={{0,4},{4,0},{8,12},{12,8},{16,20},{20,16},{24,28},{28,24},{1,5},{5... | collective-permute-start | bytes 221192 | tf_op jit(solution)/shard_map/ppermute | solution.py:33
  581.5 11.6 %collective-permute-start.113 = (bf16[96,768]{1,0:T(8,128)(2,1)S(1)}, bf16[96,768]{1,0:T(8,128)(2,1)S(1)}, u32[]{:S(2)}, u32[]{:S(2)}) collective-permute-start(bf16[96,768]{1,0:T(8,128)(2,1)S(1)} %broadcast_select_fusion.34), channel_id=1, source_target_pairs={{0,8},{4,12},{8,0},{12,4},{16,24},{20,28},{24,16},{28,20},{1,9},{5... | collective-permute-start | bytes 442376 | tf_op jit(solution)/shard_map/ppermute | solution.py:33
  582.5 10.7 %collective-permute-start.121 = (bf16[48,768]{1,0:T(8,128)(2,1)S(1)}, bf16[48,768]{1,0:T(8,128)(2,1)S(1)}, u32[]{:S(2)}, u32[]{:S(2)}) collective-permute-start(bf16[48,768]{1,0:T(8,128)(2,1)S(1)} %add_convert_fusion.15), channel_id=1, source_target_pairs={{0,4},{4,0},{8,12},{12,8},{16,20},{20,16},{24,28},{28,24},{1,5},{5... | collective-permute-start | bytes 221192 | tf_op jit(solution)/shard_map/ppermute | solution.py:33
  593.2 12.3 %collective-permute-start.114 = (bf16[48,768]{1,0:T(8,128)(2,1)S(1)}, bf16[48,768]{1,0:T(8,128)(2,1)S(1)}, u32[]{:S(2)}, u32[]{:S(2)}) collective-permute-start(bf16[48,768]{1,0:T(8,128)(2,1)S(1)} %broadcast_select_fusion.40), channel_id=1, source_target_pairs={{0,16},{4,20},{8,24},{12,28},{16,0},{20,4},{24,8},{28,12},{1,17},{... | collective-permute-start | bytes 221192 | tf_op jit(solution)/shard_map/ppermute | solution.py:33
  605.5 10.8 %collective-permute-start.115 = (bf16[48,768]{1,0:T(8,128)(2,1)S(1)}, bf16[48,768]{1,0:T(8,128)(2,1)S(1)}, u32[]{:S(2)}, u32[]{:S(2)}) collective-permute-start(bf16[48,768]{1,0:T(8,128)(2,1)S(1)} %add_convert_fusion.16), channel_id=1, source_target_pairs={{0,16},{4,20},{8,24},{12,28},{16,0},{20,4},{24,8},{28,12},{1,17},{... | collective-permute-start | bytes 221192 | tf_op jit(solution)/shard_map/ppermute | solution.py:33
  605.6 18.1 %collective-permute-start.122 = (bf16[96,768]{1,0:T(8,128)(2,1)S(1)}, bf16[96,768]{1,0:T(8,128)(2,1)S(1)}, u32[]{:S(2)}, u32[]{:S(2)}) collective-permute-start(bf16[96,768]{1,0:T(8,128)(2,1)S(1)} %pad_maximum_fusion.26), channel_id=1, source_target_pairs={{0,16},{4,20},{8,24},{12,28},{16,0},{20,4},{24,8},{28,12},{1,17},{... | collective-permute-start | bytes 442376 | tf_op jit(solution)/shard_map/ppermute | solution.py:33
  616.3 12.9 %collective-permute-start.116 = (bf16[96,768]{1,0:T(8,128)(2,1)S(1)}, bf16[96,768]{1,0:T(8,128)(2,1)S(1)}, u32[]{:S(2)}, u32[]{:S(2)}) collective-permute-start(bf16[96,768]{1,0:T(8,128)(2,1)S(1)} %pad_maximum_fusion.25), channel_id=1, source_target_pairs={{0,8},{4,12},{8,0},{12,4},{16,24},{20,28},{24,16},{28,20},{1,9},{5... | collective-permute-start | bytes 442376 | tf_op jit(solution)/shard_map/ppermute | solution.py:33
  623.8 10.2 %collective-permute-start.123 = (bf16[192,768]{1,0:T(8,128)(2,1)S(1)}, bf16[192,768]{1,0:T(8,128)(2,1)S(1)}, u32[]{:S(2)}, u32[]{:S(2)}) collective-permute-start(bf16[192,768]{1,0:T(8,128)(2,1)S(1)} %pad_maximum_fusion.22), channel_id=1, source_target_pairs={{0,8},{4,12},{8,0},{12,4},{16,24},{20,28},{24,16},{28,20},{1,9},{5... | collective-permute-start | bytes 884744 | tf_op jit(solution)/shard_map/ppermute | solution.py:33
  (264 other events, 2224.7 us)
Sparse Core Ops, SparseCore 0:
  60.8 51.9 all-gather.14
  122.6 44.6 all-gather.6
  178.4 42.9 all-gather.8
  263.0 108.4 reduce-scatter.2
  383.9 50.4 all-gather.10
  438.5 98.5 reduce-scatter.4
  546.0 81.6 all-gather.12

commit v6 on v5

--- a/solution.py
+++ b/solution.py
@@ -620,16 +620,18 @@
         jnp.concatenate([query_weight[i].T, key_weight[i].T, value_weight[i].T], 0)
         for i in range(2)
     ]
-    pack, *pooled = tied(packs[0], *pooled)
+    cut = packs[0].shape[0] * 2 // 3
+    pack, *pooled = tied(packs[0][:cut], *pooled)
     other = exchange(pack, 0, 2)
     own_out, other = tied(out_weight[0], other)
     other_out = exchange(own_out, 0, 2)
     held = jnp.concatenate([packs[1], out_weight[1]], 0)
     held, other = tied(held, other)
-    first = ordered(pack.reshape(3, -1, model), other.reshape(3, -1, model), 1)
+    first = ordered(pack.reshape(2, -1, model), other.reshape(2, -1, model), 1)
     layers = [
         dict(
-            qkv=first.reshape(-1, model),
+            front=first.reshape(-1, model),
+            back=packs[0][cut:],
             out=ordered(own_out, other_out, 0).reshape(-1, model),
             up=up_weight[:1],
             down=down_weight[:1],
@@ -699,7 +701,12 @@
     x_full, pooled = joined
     if params["offload"]:
         weights["up"], *pooled = tied(weights["up"], *pooled)
-    pooled = jnp.concatenate(spread_row(item_total(pooled, layout).astype(LOW)), axis=0)
+    own_pooled = item_total(pooled, layout).astype(LOW)
+    if not params["offload"]:
+        back, own_pooled = tied(weights["back"], own_pooled)
+        back = ordered(back, exchange(back, 0, 2), 0).reshape(-1, model)
+        weights["qkv"] = jnp.concatenate([weights["front"], back], axis=0)
+    pooled = jnp.concatenate(spread_row(own_pooled), axis=0)
     pooled = pair_join(pooled, 1)
     bias_q, bias_v = params["q_bias"], params["v_bias"]
     no_bias = jnp.zeros_like(bias_q)

time: 660 us -> 666 us (level)
    ppermute x51 -> x52, waiting for transfers between devices: 71.1 us -> 92.1 us  [exchange(): lax.ppermute(values, 'head', [(i, i ^ head_mask) for i in range(count)])]
    ppermute x16, waiting for transfers between devices: 30.3 us -> 16.9 us  [exchange(): return lax.ppermute(values, ('seq', 'head'), route)]
    ppermute x51 -> x52, starting transfers between devices: 40.6 us -> 36 us  [exchange(): lax.ppermute(values, 'head', [(i, i ^ head_mask) for i in range(count)])]
    unnamed x383 -> x412, local copies, waits for them, and re-layouts: 32.3 us -> 35.8 us
  transfers between devices with their start and end apart: 137 -> 138, of which waited for: 62 -> 64; matrix products, arithmetic and copies ran while one was open for 17% -> 16% of each run, Pallas kernels for 14% -> 13%
where the time goes in v6:
time: 666 us; the launch traced here: 658 us
  waiting for transfers between devices  208 us (31%)
  starting transfers between devices  158 us (24%)
  Pallas kernels  92.4 us (14%)
  local copies, waits for them, and re-layouts  79.3 us (12%)
  other arithmetic  57.2 us (9%)
  matrix products  43.7 us (7%)
  between operations  19.7 us (3%)
    pallas_call x24, Pallas kernels, on_core(): pl.pallas_call(kernel, out_shape=shapes, in_specs=specs, out_specs=tuple(...  92.4 us
    ppermute x52, waiting for transfers between devices, exchange(): lax.ppermute(values, 'head', [(i, i ^ head_mask) for i in range(count)])  92.1 us
    ppermute x55, waiting for transfers between devices, exchange(): lax.ppermute(values, 'seq', [(i, i ^ seq_mask) for i in range(count)])  83 us
    ppermute x55, starting transfers between devices, exchange(): lax.ppermute(values, 'seq', [(i, i ^ seq_mask) for i in range(count)])  74.7 us
    ppermute x52, starting transfers between devices, exchange(): lax.ppermute(values, 'head', [(i, i ^ head_mask) for i in range(count)])  36 us
    unnamed x412, local copies, waits for them, and re-layouts  35.8 us
    ppermute x16, starting transfers between devices, exchange(): return lax.ppermute(values, ('seq', 'head'), route)  29 us
    dot_general x18, matrix products, dot(): return jnp.einsum(spec, one, two, preferred_element_type=jnp.float32)  25.2 us
  transfers between devices with their start and end apart: 138, of which 64 were waited for; matrix products, arithmetic and copies ran while one was open for 16% of the time, Pallas kernels for 13%

profile of v6, /device:TPU:0, one launch (start us, length us, event | category | flops | bytes accessed | tf_op | source)
XLA Modules:
  0.0 658.1 jit_solution(13271108295317019089)
XLA Ops:
  9.0 3.0 collective-permute-start.9
  26.3 2.8 collective-permute-done.3
  29.1 3.7 collective-permute-start.7
  35.1 2.7 collective-permute-done.6
  41.4 3.5 collective-permute-done.10
  49.6 5.8 collective-permute-done.8
  56.6 11.0 %collective-permute-done.4 = bf16[384,768]{1,0:T(8,128)(2,1)S(1)} collective-permute-done((bf16[384,768]{1,0:T(8,128)(2,1)S(1)}, bf16[384,768]{1,0:T(8,128)(2,1)S(1)}, u32[]{:S(2)}, u32[]{:S(2)}) %collective-permute-start.4) | collective-permute-done | bytes 589856 | tf_op jit(solution)/shard_map/ppermute | solution.py:30
  72.4 4.0 shard_map.323
  80.9 3.6 collective-permute-start.14
  91.1 5.0 shard_map.325
  101.7 3.7 collective-permute-start.24
  108.6 3.3 collective-permute-done.24.four.refs_3_
  113.1 3.2 shard_map.327
  119.3 3.8 copy.107
  129.5 9.0 %collective-permute-done.29 = bf16[4,64,768]{2,1,0:T(8,128)(2,1)S(1)} collective-permute-done((bf16[4,64,768]{2,1,0:T(8,128)(2,1)S(1)}, bf16[4,64,768]{2,1,0:T(8,128)(2,1)S(1)}, u32[]{:S(2)}, u32[]{:S(2)}) %collective-permute-start.29) | collective-permute-done | bytes 393248 | tf_op jit(solution)/shard_map/ppermute | solution.py:30
  147.8 19.0 %collective-permute-done.32 = bf16[4,64,768]{2,1,0:T(8,128)(2,1)S(1)} collective-permute-done((bf16[4,64,768]{2,1,0:T(8,128)(2,1)S(1)}, bf16[4,64,768]{2,1,0:T(8,128)(2,1)S(1)}, u32[]{:S(2)}, u32[]{:S(2)}) %collective-permute-start.32) | collective-permute-done | bytes 393248 | tf_op jit(solution)/shard_map/ppermute | solution.py:30
  180.0 2.7 collective-permute-start.37
  194.9 4.0 shard_map.329
  202.5 2.5 collective-permute-start.44
  209.1 4.4 collective-permute-start.51
  214.5 5.0 shard_map.331
  235.4 3.2 shard_map.333
  259.2 2.9 convert_reduce_fusion
  266.0 2.5 pad_maximum_fusion
  268.6 3.1 multiply_reduce_fusion.2
  276.5 6.1 shard_map.334
  295.4 3.4 collective-permute-start.68
  305.5 3.5 collective-permute-start.61
  313.3 3.1 collective-permute-start.71
  318.4 5.7 shard_map.335
  324.2 4.5 shard_map.337
  330.0 4.4 collective-permute-start.73
  335.6 5.4 collective-permute-done.73
  341.5 2.5 collective-permute-start.76
  345.6 13.0 %shard_map.338 = f32[64,768]{1,0:T(8,128)S(1)} custom-call(f32[64,384]{1,0:T(8,128)S(1)} %select_add_fusion.2.grads, f32[64,384]{1,0:T(8,128)S(1)} %copy-done.52, bf16[64,768]{1,0:T(8,128)(2,1)S(1)} %slice.704.land, f32[6,64,64]{2,1,0:T(8,128)S(1)} %copy-done.70, f32[42,64,64]{2,1,0:T(8,128)S(1)} %get-tuple-element.175.inverses, ...), custom_call_target="tpu_custom_call" | custom-call | flops 12999999488 | bytes 39000000 | tf_op jit(solution)/shard_map/pallas_call | solution.py:112
  367.5 2.7 fusion.125
  381.0 7.6 %collective-permute-done.91 = bf16[192,768]{1,0:T(8,128)(2,1)S(1)} collective-permute-done((bf16[192,768]{1,0:T(8,128)(2,1)S(1)}, bf16[192,768]{1,0:T(8,128)(2,1)S(1)}, u32[]{:S(2)}, u32[]{:S(2)}) %collective-permute-start.91) | collective-permute-done | bytes 294944 | tf_op jit(solution)/shard_map/ppermute | solution.py:30
  389.7 5.2 collective-permute-done.84
  394.9 2.7 convert_reduce_fusion.4
  414.0 6.4 collective-permute-done.87
  427.5 5.5 shard_map.340
  444.2 2.5 collective-permute-start.95
  446.7 2.6 convolution_bitcast_fusion
  453.7 3.0 collective-permute-start.100
  459.4 5.7 shard_map.341
  472.2 4.5 shard_map.343
  479.1 4.8 collective-permute-start.102
  484.5 13.0 %shard_map.344 = f32[64,768]{1,0:T(8,128)S(1)} custom-call(f32[64,384]{1,0:T(8,128)S(1)} %select_add_fusion.1.grads, f32[64,384]{1,0:T(8,128)S(1)} %copy-done.49, bf16[64,768]{1,0:T(8,128)(2,1)S(1)} %copy-done.6, f32[6,64,64]{2,1,0:T(8,128)S(1)} %copy-done.68, f32[42,64,64]{2,1,0:T(8,128)S(1)} %copy-done.8, f32[36,64,64]{2,1,0:T(8,128)S(1)} %copy-done.54, ...), custom_call_target="tpu_custom_call" | custom-call | flops 12999999488 | bytes 39000000 | tf_op jit(solution)/shard_map/pallas_call | solution.py:112
  510.2 4.0 collective-permute-start.110
  527.2 5.5 collective-permute-done.112
  532.9 9.8 %reduce-scatter.5.cloned.1.call-done = bf16[4,96,768]{2,1,0:T(8,128)(2,1)} async-done(((bf16[4,768,768]{2,1,0:T(8,128)(2,1)}), bf16[4,96,768]{2,1,0:T(8,128)(2,1)}) %reduce-scatter.5.cloned.1.call-update) | async-done | bytes 589840 | tf_op jit(solution)/shard_map/reduce_scatter | solution.py:963
  551.5 2.5 fusion.45
  555.0 3.2 collective-permute-done.128
  562.6 7.4 %collective-permute-done.129 = f32[12288]{0:T(1024)S(1)} collective-permute-done((f32[12288]{0:T(1024)S(1)}, f32[12288]{0:T(1024)S(1)}, u32[]{:S(2)}, u32[]{:S(2)}) %collective-permute-start.129) | collective-permute-done | bytes 49184 | tf_op jit(solution)/shard_map/ppermute | solution.py:33
  580.3 6.0 collective-permute-done.113
  589.3 9.0 %collective-permute-done.114 = bf16[96,768]{1,0:T(8,128)(2,1)S(1)} collective-permute-done((bf16[96,768]{1,0:T(8,128)(2,1)S(1)}, bf16[96,768]{1,0:T(8,128)(2,1)S(1)}, u32[]{:S(2)}, u32[]{:S(2)}) %collective-permute-start.114) | collective-permute-done | bytes 147488 | tf_op jit(solution)/shard_map/ppermute | solution.py:33
  598.4 12.2 %collective-permute-done.115 = bf16[48,768]{1,0:T(8,128)(2,1)S(1)} collective-permute-done((bf16[48,768]{1,0:T(8,128)(2,1)S(1)}, bf16[48,768]{1,0:T(8,128)(2,1)S(1)}, u32[]{:S(2)}, u32[]{:S(2)}) %collective-permute-start.115) | collective-permute-done | bytes 73760 | tf_op jit(solution)/shard_map/ppermute | solution.py:33
  610.8 2.9 collective-permute-start.123
  613.8 7.6 %collective-permute-done.116 = bf16[48,768]{1,0:T(8,128)(2,1)S(1)} collective-permute-done((bf16[48,768]{1,0:T(8,128)(2,1)S(1)}, bf16[48,768]{1,0:T(8,128)(2,1)S(1)}, u32[]{:S(2)}, u32[]{:S(2)}) %collective-permute-start.116) | collective-permute-done | bytes 73760 | tf_op jit(solution)/shard_map/ppermute | solution.py:33
  621.5 7.4 %collective-permute-done.123 = bf16[96,768]{1,0:T(8,128)(2,1)S(1)} collective-permute-done((bf16[96,768]{1,0:T(8,128)(2,1)S(1)}, bf16[96,768]{1,0:T(8,128)(2,1)S(1)}, u32[]{:S(2)}, u32[]{:S(2)}) %collective-permute-start.123) | collective-permute-done | bytes 147488 | tf_op jit(solution)/shard_map/ppermute | solution.py:33
  629.1 5.1 collective-permute-done.117
  636.1 2.9 collective-permute-done.124
  643.6 2.5 maximum_convert_fusion.1
  646.1 2.5 maximum_convert_fusion
  (978 shorter events, 312.5 us)
Async XLA Ops:
  7.2 112.0 %all-gather.15.cloned.1.call-start = ((), (), s32[]{:S(2)}) async-start(), calls=%async_computation.8 | async-start | bytes 3538944 | tf_op jit(solution)/shard_map/all_gather | solution.py:612
  9.0 12.1 %collective-permute-start.9 = (f32[2,1408]{1,0:T(2,128)S(1)}, f32[2,1408]{1,0:T(2,128)S(1)}, u32[]{:S(2)}, u32[]{:S(2)}) collective-permute-start(f32[2,1408]{1,0:T(2,128)S(1)} %pad.38), channel_id=1, source_target_pairs={{0,2},{1,3},{2,0},{3,1},{4,6},{5,7},{6,4},{7,5},{8,10},{9,11},{10,... | collective-permute-start | bytes 33800 | tf_op jit(solution)/shard_map/ppermute | solution.py:30
  12.0 9.2 %collective-permute-start = (bf16[4,64,768]{2,1,0:T(8,128)(2,1)}, bf16[4,64,768]{2,1,0:T(8,128)(2,1)S(1)}, u32[]{:S(2)}, u32[]{:S(2)}) collective-permute-start(bf16[4,64,768]{2,1,0:T(8,128)(2,1)} %own), channel_id=1, source_target_pairs={{0,1},{1,0},{2,3},{3,2},{4,5},{5,4},{6,7},{7,6},{8,9},{9,8},{10,11... | collective-permute-start | bytes 1179656 | tf_op jit(solution)/shard_map/ppermute | solution.py:30
  45.6 9.8 %collective-permute-start.8 = (bf16[192,768]{1,0:T(8,128)(2,1)S(1)}, bf16[192,768]{1,0:T(8,128)(2,1)S(1)}, u32[]{:S(2)}, u32[]{:S(2)}) collective-permute-start(bf16[192,768]{1,0:T(8,128)(2,1)S(1)} %get-tuple-element.145), channel_id=1, source_target_pairs={{0,2},{1,3},{2,0},{3,1},{4,6},{5,7},{6,4},{7,5},{8,10},{9,11},{10,... | collective-permute-start | bytes 884744 | tf_op jit(solution)/shard_map/ppermute | solution.py:30
  47.3 20.3 %collective-permute-start.4 = (bf16[384,768]{1,0:T(8,128)(2,1)S(1)}, bf16[384,768]{1,0:T(8,128)(2,1)S(1)}, u32[]{:S(2)}, u32[]{:S(2)}) collective-permute-start(bf16[384,768]{1,0:T(8,128)(2,1)S(1)} %pad_maximum_fusion.19), channel_id=1, source_target_pairs={{0,2},{1,3},{2,0},{3,1},{4,6},{5,7},{6,4},{7,5},{8,10},{9,11},{10,... | collective-permute-start | bytes 1769480 | tf_op jit(solution)/shard_map/ppermute | solution.py:30
  68.5 106.1 %all-gather.7.cloned.1.call-start = ((), (), s32[]{:S(2)}) async-start(), calls=%async_computation.2 | async-start | bytes 3538944 | tf_op jit(solution)/shard_map/all_gather | solution.py:612
  80.3 36.3 %collective-permute-start.25 = (bf16[192,768]{1,0:T(8,128)(2,1)}, bf16[192,768]{1,0:T(8,128)(2,1)}, u32[]{:S(2)}, u32[]{:S(2)}) collective-permute-start(bf16[192,768]{1,0:T(8,128)(2,1)} %get-tuple-element.156), channel_id=1, source_target_pairs={{0,2},{1,3},{2,0},{3,1},{4,6},{5,7},{6,4},{7,5},{8,10},{9,11},{10,... | collective-permute-start | bytes 884744 | tf_op jit(solution)/shard_map/ppermute | solution.py:30
  80.9 25.0 %collective-permute-start.14 = (bf16[384,128]{1,0:T(8,128)(2,1)S(1)}, bf16[384,128]{1,0:T(8,128)(2,1)S(1)}, u32[]{:S(2)}, u32[]{:S(2)}) collective-permute-start(bf16[384,128]{1,0:T(8,128)(2,1)S(1)} %get-tuple-element.148), channel_id=1, source_target_pairs={{0,2},{1,3},{2,4},{3,5},{4,6},{5,7},{6,8},{7,9},{8,10},{9,11},{10,... | collective-permute-start | bytes 294920 | tf_op jit(solution)/shard_map/ppermute | solution.py:53
  86.6 12.2 %collective-permute-start.21 = (bf16[64,512]{1,0:T(8,128)(2,1)S(1)}, bf16[64,512]{1,0:T(8,128)(2,1)S(1)}, u32[]{:S(2)}, u32[]{:S(2)}) collective-permute-start(bf16[64,512]{1,0:T(8,128)(2,1)S(1)} %shard_map.324.refs_0_), channel_id=1, source_target_pairs={{0,24},{4,28},{8,16},{12,20},{16,8},{20,12},{24,0},{28,4},{1,25},{... | collective-permute-start | bytes 196616 | tf_op jit(solution)/shard_map/ppermute | solution.py:33
  88.0 12.3 %collective-permute-start.20 = (bf16[64,512]{1,0:T(8,128)(2,1)S(1)}, bf16[64,512]{1,0:T(8,128)(2,1)S(1)}, u32[]{:S(2)}, u32[]{:S(2)}) collective-permute-start(bf16[64,512]{1,0:T(8,128)(2,1)S(1)} %shard_map.324.refs_0_), channel_id=1, source_target_pairs={{0,16},{4,20},{8,24},{12,28},{16,0},{20,4},{24,8},{28,12},{1,17},{... | collective-permute-start | bytes 196616 | tf_op jit(solution)/shard_map/ppermute | solution.py:33
  88.6 11.7 %collective-permute-start.19 = (bf16[64,512]{1,0:T(8,128)(2,1)S(1)}, bf16[64,512]{1,0:T(8,128)(2,1)S(1)}, u32[]{:S(2)}, u32[]{:S(2)}) collective-permute-start(bf16[64,512]{1,0:T(8,128)(2,1)S(1)} %shard_map.324.refs_0_), channel_id=1, source_target_pairs={{0,8},{4,12},{8,0},{12,4},{16,24},{20,28},{24,16},{28,20},{1,9},{5... | collective-permute-start | bytes 196616 | tf_op jit(solution)/shard_map/ppermute | solution.py:33
  98.9 9.7 %collective-permute-start.15 = (bf16[384,128]{1,0:T(8,128)(2,1)S(1)}, bf16[384,128]{1,0:T(8,128)(2,1)S(1)}, u32[]{:S(2)}, u32[]{:S(2)}) collective-permute-start(bf16[384,128]{1,0:T(8,128)(2,1)S(1)} %get-tuple-element.149), channel_id=1, source_target_pairs={{2,0},{3,1},{4,2},{5,3},{6,4},{7,5},{8,6},{9,7},{10,8},{11,9},{12,... | collective-permute-start | bytes 294920 | tf_op jit(solution)/shard_map/ppermute | solution.py:53
  101.7 10.2 %collective-permute-start.24 = (bf16[64,512]{1,0:T(8,128)(2,1)S(1)}, bf16[64,512]{1,0:T(8,128)(2,1)S(1)}, u32[]{:S(2)}, u32[]{:S(2)}) collective-permute-start(bf16[64,512]{1,0:T(8,128)(2,1)S(1)} %get-tuple-element.155.one.refs_0_), channel_id=1, source_target_pairs={{0,6},{1,7},{2,4},{3,5},{4,2},{5,3},{6,0},{7,1},{8,14},{9,15},{10,... | collective-permute-start | bytes 196616 | tf_op jit(solution)/shard_map/ppermute | solution.py:39
  127.3 11.2 %collective-permute-start.29 = (bf16[4,64,768]{2,1,0:T(8,128)(2,1)S(1)}, bf16[4,64,768]{2,1,0:T(8,128)(2,1)S(1)}, u32[]{:S(2)}, u32[]{:S(2)}) collective-permute-start(bf16[4,64,768]{2,1,0:T(8,128)(2,1)S(1)} %fusion.62), channel_id=1, source_target_pairs={{0,2},{1,3},{2,0},{3,1},{4,6},{5,7},{6,4},{7,5},{8,10},{9,11},{10,... | collective-permute-start | bytes 1179656 | tf_op jit(solution)/shard_map/ppermute | solution.py:30
  127.8 10.6 %collective-permute-start.27 = (bf16[4,64,768]{2,1,0:T(8,128)(2,1)S(1)}, bf16[4,64,768]{2,1,0:T(8,128)(2,1)S(1)}, u32[]{:S(2)}, u32[]{:S(2)}) collective-permute-start(bf16[4,64,768]{2,1,0:T(8,128)(2,1)S(1)} %fusion.62), channel_id=1, source_target_pairs={{0,1},{1,0},{2,3},{3,2},{4,5},{5,4},{6,7},{7,6},{8,9},{9,8},{10,11... | collective-permute-start | bytes 1179656 | tf_op jit(solution)/shard_map/ppermute | solution.py:30
  129.0 98.0 %all-gather.9.cloned.1.call-start = ((), (), s32[]{:S(2)}) async-start(), calls=%async_computation.3 | async-start | bytes 3538944 | tf_op jit(solution)/shard_map/all_gather | solution.py:612
  146.6 20.3 %collective-permute-start.32 = (bf16[4,64,768]{2,1,0:T(8,128)(2,1)S(1)}, bf16[4,64,768]{2,1,0:T(8,128)(2,1)S(1)}, u32[]{:S(2)}, u32[]{:S(2)}) collective-permute-start(bf16[4,64,768]{2,1,0:T(8,128)(2,1)S(1)} %add_convert_fusion.4), channel_id=1, source_target_pairs={{0,2},{1,3},{2,0},{3,1},{4,6},{5,7},{6,4},{7,5},{8,10},{9,11},{10,... | collective-permute-start | bytes 1179656 | tf_op jit(solution)/shard_map/ppermute | solution.py:30
  185.1 192.1 %reduce-scatter.3.cloned.1.call-start = ((), (), s32[]{:S(2)}) async-start(), calls=%async_computation.4 | async-start | bytes 5308416 | tf_op jit(solution)/shard_map/reduce_scatter | solution.py:963
  202.5 28.0 %collective-permute-start.44 = (bf16[384,128]{1,0:T(8,128)(2,1)S(1)}, bf16[384,128]{1,0:T(8,128)(2,1)S(1)}, u32[]{:S(2)}, u32[]{:S(2)}) collective-permute-start(bf16[384,128]{1,0:T(8,128)(2,1)S(1)} %get-tuple-element.169), channel_id=1, source_target_pairs={{0,2},{1,3},{2,4},{3,5},{4,6},{5,7},{6,8},{7,9},{8,10},{9,11},{10,... | collective-permute-start | bytes 294920 | tf_op jit(solution)/shard_map/ppermute | solution.py:53
  205.0 25.5 %collective-permute-start.45 = (bf16[384,128]{1,0:T(8,128)(2,1)S(1)}, bf16[384,128]{1,0:T(8,128)(2,1)S(1)}, u32[]{:S(2)}, u32[]{:S(2)}) collective-permute-start(bf16[384,128]{1,0:T(8,128)(2,1)S(1)} %get-tuple-element.170), channel_id=1, source_target_pairs={{2,0},{3,1},{4,2},{5,3},{6,4},{7,5},{8,6},{9,7},{10,8},{11,9},{12,... | collective-permute-start | bytes 294920 | tf_op jit(solution)/shard_map/ppermute | solution.py:53
  209.1 13.5 %collective-permute-start.51 = (bf16[64,512]{1,0:T(8,128)(2,1)S(1)}, bf16[64,512]{1,0:T(8,128)(2,1)S(1)}, u32[]{:S(2)}, u32[]{:S(2)}) collective-permute-start(bf16[64,512]{1,0:T(8,128)(2,1)S(1)} %shard_map.330.refs_0_), channel_id=1, source_target_pairs={{0,24},{4,28},{8,16},{12,20},{16,8},{20,12},{24,0},{28,4},{1,25},{... | collective-permute-start | bytes 196616 | tf_op jit(solution)/shard_map/ppermute | solution.py:33
  213.4 9.2 %collective-permute-start.50 = (bf16[64,512]{1,0:T(8,128)(2,1)S(1)}, bf16[64,512]{1,0:T(8,128)(2,1)S(1)}, u32[]{:S(2)}, u32[]{:S(2)}) collective-permute-start(bf16[64,512]{1,0:T(8,128)(2,1)S(1)} %shard_map.330.refs_0_), channel_id=1, source_target_pairs={{0,16},{4,20},{8,24},{12,28},{16,0},{20,4},{24,8},{28,12},{1,17},{... | collective-permute-start | bytes 196616 | tf_op jit(solution)/shard_map/ppermute | solution.py:33
  214.5 8.8 %collective-permute-start.49 = (bf16[64,512]{1,0:T(8,128)(2,1)S(1)}, bf16[64,512]{1,0:T(8,128)(2,1)S(1)}, u32[]{:S(2)}, u32[]{:S(2)}) collective-permute-start(bf16[64,512]{1,0:T(8,128)(2,1)S(1)} %shard_map.330.refs_0_), channel_id=1, source_target_pairs={{0,8},{4,12},{8,0},{12,4},{16,24},{20,28},{24,16},{28,20},{1,9},{5... | collective-permute-start | bytes 196616 | tf_op jit(solution)/shard_map/ppermute | solution.py:33
  268.5 198.8 %all-gather.11.cloned.1.call-start = ((), (), s32[]{:S(2)}) async-start(), calls=%async_computation.5 | async-start | bytes 2654208 | tf_op jit(solution)/shard_map/all_gather | solution.py:967
  295.4 15.3 %collective-permute-start.68 = (bf16[64,384]{1,0:T(8,128)(2,1)}, bf16[64,384]{1,0:T(8,128)(2,1)S(1)}, u32[]{:S(2)}, u32[]{:S(2)}) collective-permute-start(bf16[64,384]{1,0:T(8,128)(2,1)} %fusion.79), channel_id=1, source_target_pairs={{0,24},{4,28},{8,16},{12,20},{16,8},{20,12},{24,0},{28,4},{1,25},{... | collective-permute-start | bytes 147464 | tf_op jit(solution)/shard_map/ppermute | solution.py:33
  298.7 12.0 %collective-permute-start.67 = (bf16[64,384]{1,0:T(8,128)(2,1)}, bf16[64,384]{1,0:T(8,128)(2,1)}, u32[]{:S(2)}, u32[]{:S(2)}) collective-permute-start(bf16[64,384]{1,0:T(8,128)(2,1)} %fusion.79), channel_id=1, source_target_pairs={{0,16},{4,20},{8,24},{12,28},{16,0},{20,4},{24,8},{28,12},{1,17},{... | collective-permute-start | bytes 147464 | tf_op jit(solution)/shard_map/ppermute | solution.py:33
  298.7 12.0 %collective-permute-start.66 = (bf16[64,384]{1,0:T(8,128)(2,1)}, bf16[64,384]{1,0:T(8,128)(2,1)}, u32[]{:S(2)}, u32[]{:S(2)}) collective-permute-start(bf16[64,384]{1,0:T(8,128)(2,1)} %fusion.79), channel_id=1, source_target_pairs={{0,8},{4,12},{8,0},{12,4},{16,24},{20,28},{24,16},{28,20},{1,9},{5... | collective-permute-start | bytes 147464 | tf_op jit(solution)/shard_map/ppermute | solution.py:33
  305.5 12.9 %collective-permute-start.61 = (bf16[384,128]{1,0:T(8,128)(2,1)}, bf16[384,128]{1,0:T(8,128)(2,1)S(1)}, u32[]{:S(2)}, u32[]{:S(2)}) collective-permute-start(bf16[384,128]{1,0:T(8,128)(2,1)} %get-tuple-element.181), channel_id=1, source_target_pairs={{0,2},{1,3},{2,4},{3,5},{4,6},{5,7},{6,8},{7,9},{8,10},{9,11},{10,... | collective-permute-start | bytes 294920 | tf_op jit(solution)/shard_map/ppermute | solution.py:53
  309.0 9.4 %collective-permute-start.62 = (bf16[384,128]{1,0:T(8,128)(2,1)}, bf16[384,128]{1,0:T(8,128)(2,1)S(1)}, u32[]{:S(2)}, u32[]{:S(2)}) collective-permute-start(bf16[384,128]{1,0:T(8,128)(2,1)} %get-tuple-element.182), channel_id=1, source_target_pairs={{2,0},{3,1},{4,2},{5,3},{6,4},{7,5},{8,6},{9,7},{10,8},{11,9},{12,... | collective-permute-start | bytes 294920 | tf_op jit(solution)/shard_map/ppermute | solution.py:53
  313.3 10.8 %collective-permute-start.71 = (bf16[64,512]{1,0:T(8,128)(2,1)S(1)}, bf16[64,512]{1,0:T(8,128)(2,1)S(1)}, u32[]{:S(2)}, u32[]{:S(2)}) collective-permute-start(bf16[64,512]{1,0:T(8,128)(2,1)S(1)} %shard_map.336.refs_4_), channel_id=1, source_target_pairs={{0,6},{1,7},{2,4},{3,5},{4,2},{5,3},{6,0},{7,1},{8,14},{9,15},{10,... | collective-permute-start | bytes 196616 | tf_op jit(solution)/shard_map/ppermute | solution.py:39
  330.0 11.1 %collective-permute-start.73 = (bf16[64,768]{1,0:T(8,128)(2,1)S(1)}, bf16[64,768]{1,0:T(8,128)(2,1)S(1)}, u32[]{:S(2)}, u32[]{:S(2)}) collective-permute-start(bf16[64,768]{1,0:T(8,128)(2,1)S(1)} %get-tuple-element.201), channel_id=1, source_target_pairs={{0,4},{4,0},{8,12},{12,8},{16,20},{20,16},{24,28},{28,24},{1,5},{5... | collective-permute-start | bytes 294920 | tf_op jit(solution)/shard_map/ppermute | solution.py:33
  341.1 17.5 %collective-permute-start.77 = (bf16[64,768]{1,0:T(8,128)(2,1)S(1)}, bf16[64,768]{1,0:T(8,128)(2,1)S(1)}, u32[]{:S(2)}, u32[]{:S(2)}) collective-permute-start(bf16[64,768]{1,0:T(8,128)(2,1)S(1)} %fusion.76), channel_id=1, source_target_pairs={{0,24},{4,28},{8,16},{12,20},{16,8},{20,12},{24,0},{28,4},{1,25},{... | collective-permute-start | bytes 294920 | tf_op jit(solution)/shard_map/ppermute | solution.py:33
  341.5 17.1 %collective-permute-start.76 = (bf16[64,768]{1,0:T(8,128)(2,1)S(1)}, bf16[64,768]{1,0:T(8,128)(2,1)S(1)}, u32[]{:S(2)}, u32[]{:S(2)}) collective-permute-start(bf16[64,768]{1,0:T(8,128)(2,1)S(1)} %fusion.76), channel_id=1, source_target_pairs={{0,16},{4,20},{8,24},{12,28},{16,0},{20,4},{24,8},{28,12},{1,17},{... | collective-permute-start | bytes 294920 | tf_op jit(solution)/shard_map/ppermute | solution.py:33
  344.0 14.6 %collective-permute-start.75 = (bf16[64,768]{1,0:T(8,128)(2,1)S(1)}, bf16[64,768]{1,0:T(8,128)(2,1)S(1)}, u32[]{:S(2)}, u32[]{:S(2)}) collective-permute-start(bf16[64,768]{1,0:T(8,128)(2,1)S(1)} %fusion.76), channel_id=1, source_target_pairs={{0,8},{4,12},{8,0},{12,4},{16,24},{20,28},{24,16},{28,20},{1,9},{5... | collective-permute-start | bytes 294920 | tf_op jit(solution)/shard_map/ppermute | solution.py:33
  378.6 10.0 %collective-permute-start.91 = (bf16[192,768]{1,0:T(8,128)(2,1)S(1)}, bf16[192,768]{1,0:T(8,128)(2,1)S(1)}, u32[]{:S(2)}, u32[]{:S(2)}) collective-permute-start(bf16[192,768]{1,0:T(8,128)(2,1)S(1)} %select_bitcast_fusion), channel_id=1, source_target_pairs={{0,2},{1,3},{2,0},{3,1},{4,6},{5,7},{6,4},{7,5},{8,10},{9,11},{10,... | collective-permute-start | bytes 884744 | tf_op jit(solution)/shard_map/ppermute | solution.py:30
  380.6 14.2 %collective-permute-start.84 = (bf16[4,64,768]{2,1,0:T(8,128)(2,1)S(1)}, bf16[4,64,768]{2,1,0:T(8,128)(2,1)}, u32[]{:S(2)}, u32[]{:S(2)}) collective-permute-start(bf16[4,64,768]{2,1,0:T(8,128)(2,1)S(1)} %get-tuple-element.335), channel_id=1, source_target_pairs={{0,2},{1,3},{2,0},{3,1},{4,6},{5,7},{6,4},{7,5},{8,10},{9,11},{10,... | collective-permute-start | bytes 1179656 | tf_op jit(solution)/shard_map/ppermute | solution.py:30
  389.5 153.2 %reduce-scatter.5.cloned.1.call-start = ((), (), s32[]{:S(2)}) async-start(), calls=%async_computation.6 | async-start | bytes 5308416 | tf_op jit(solution)/shard_map/reduce_scatter | solution.py:963
  400.7 12.6 %collective-permute-start.83 = (bf16[4,64,768]{2,1,0:T(8,128)(2,1)}, bf16[4,64,768]{2,1,0:T(8,128)(2,1)S(1)}, u32[]{:S(2)}, u32[]{:S(2)}) collective-permute-start(bf16[4,64,768]{2,1,0:T(8,128)(2,1)} %select_convert_fusion.4), channel_id=1, source_target_pairs={{0,1},{1,0},{2,3},{3,2},{4,5},{5,4},{6,7},{7,6},{8,9},{9,8},{10,11... | collective-permute-start | bytes 1179656 | tf_op jit(solution)/shard_map/ppermute | solution.py:30
  408.8 11.6 %collective-permute-start.87 = (bf16[4,64,768]{2,1,0:T(8,128)(2,1)}, bf16[4,64,768]{2,1,0:T(8,128)(2,1)}, u32[]{:S(2)}, u32[]{:S(2)}) collective-permute-start(bf16[4,64,768]{2,1,0:T(8,128)(2,1)} %add_convert_fusion.2), channel_id=1, source_target_pairs={{0,2},{1,3},{2,0},{3,1},{4,6},{5,7},{6,4},{7,5},{8,10},{9,11},{10,... | collective-permute-start | bytes 1179656 | tf_op jit(solution)/shard_map/ppermute | solution.py:30
  413.0 228.2 %all-gather.13.cloned.1.call-start = ((), (), s32[]{:S(2)}) async-start(), calls=%async_computation.7 | async-start | bytes 3981312 | tf_op jit(solution)/shard_map/all_gather | solution.py:1131
  442.3 10.6 %collective-permute-start.97 = (bf16[64,384]{1,0:T(8,128)(2,1)S(1)}, bf16[64,384]{1,0:T(8,128)(2,1)S(1)}, u32[]{:S(2)}, u32[]{:S(2)}) collective-permute-start(bf16[64,384]{1,0:T(8,128)(2,1)S(1)} %fusion.80), channel_id=1, source_target_pairs={{0,24},{4,28},{8,16},{12,20},{16,8},{20,12},{24,0},{28,4},{1,25},{... | collective-permute-start | bytes 147464 | tf_op jit(solution)/shard_map/ppermute | solution.py:33
  449.4 10.0 %collective-permute-start.89 = (bf16[384,128]{1,0:T(8,128)(2,1)S(1)}, bf16[384,128]{1,0:T(8,128)(2,1)S(1)}, u32[]{:S(2)}, u32[]{:S(2)}) collective-permute-start(bf16[384,128]{1,0:T(8,128)(2,1)S(1)} %get-tuple-element.210), channel_id=1, source_target_pairs={{0,2},{1,3},{2,4},{3,5},{4,6},{5,7},{6,8},{7,9},{8,10},{9,11},{10,... | collective-permute-start | bytes 294920 | tf_op jit(solution)/shard_map/ppermute | solution.py:53
  453.7 13.5 %collective-permute-start.100 = (bf16[64,512]{1,0:T(8,128)(2,1)S(1)}, bf16[64,512]{1,0:T(8,128)(2,1)S(1)}, u32[]{:S(2)}, u32[]{:S(2)}) collective-permute-start(bf16[64,512]{1,0:T(8,128)(2,1)S(1)} %shard_map.342.refs_4_), channel_id=1, source_target_pairs={{0,6},{1,7},{2,4},{3,5},{4,2},{5,3},{6,0},{7,1},{8,14},{9,15},{10,... | collective-permute-start | bytes 196616 | tf_op jit(solution)/shard_map/ppermute | solution.py:39
  456.7 10.6 %collective-permute-start.99 = (bf16[64,512]{1,0:T(8,128)(2,1)S(1)}, bf16[64,512]{1,0:T(8,128)(2,1)S(1)}, u32[]{:S(2)}, u32[]{:S(2)}) collective-permute-start(bf16[64,512]{1,0:T(8,128)(2,1)S(1)} %shard_map.342.refs_4_), channel_id=1, source_target_pairs={{0,4},{4,0},{8,12},{12,8},{16,20},{20,16},{24,28},{28,24},{1,5},{5... | collective-permute-start | bytes 196616 | tf_op jit(solution)/shard_map/ppermute | solution.py:33
  458.0 9.3 %collective-permute-start.98 = (bf16[64,512]{1,0:T(8,128)(2,1)S(1)}, bf16[64,512]{1,0:T(8,128)(2,1)S(1)}, u32[]{:S(2)}, u32[]{:S(2)}) collective-permute-start(bf16[64,512]{1,0:T(8,128)(2,1)S(1)} %shard_map.342.refs_4_), channel_id=1, source_target_pairs={{0,2},{1,3},{2,0},{3,1},{4,6},{5,7},{6,4},{7,5},{8,10},{9,11},{10,... | collective-permute-start | bytes 196616 | tf_op jit(solution)/shard_map/ppermute | solution.py:30
  476.7 20.9 %collective-permute-start.101 = (bf16[64,768]{1,0:T(8,128)(2,1)S(1)}, bf16[64,768]{1,0:T(8,128)(2,1)S(1)}, u32[]{:S(2)}, u32[]{:S(2)}) collective-permute-start(bf16[64,768]{1,0:T(8,128)(2,1)S(1)} %get-tuple-element.234), channel_id=1, source_target_pairs={{0,2},{1,3},{2,0},{3,1},{4,6},{5,7},{6,4},{7,5},{8,10},{9,11},{10,... | collective-permute-start | bytes 294920 | tf_op jit(solution)/shard_map/ppermute | solution.py:30
  479.1 18.6 %collective-permute-start.102 = (bf16[64,768]{1,0:T(8,128)(2,1)S(1)}, bf16[64,768]{1,0:T(8,128)(2,1)S(1)}, u32[]{:S(2)}, u32[]{:S(2)}) collective-permute-start(bf16[64,768]{1,0:T(8,128)(2,1)S(1)} %get-tuple-element.235), channel_id=1, source_target_pairs={{0,4},{4,0},{8,12},{12,8},{16,20},{20,16},{24,28},{28,24},{1,5},{5... | collective-permute-start | bytes 294920 | tf_op jit(solution)/shard_map/ppermute | solution.py:33
  484.0 13.7 %collective-permute-start.103 = (bf16[64,768]{1,0:T(8,128)(2,1)S(1)}, bf16[64,768]{1,0:T(8,128)(2,1)S(1)}, u32[]{:S(2)}, u32[]{:S(2)}) collective-permute-start(bf16[64,768]{1,0:T(8,128)(2,1)S(1)} %get-tuple-element.236), channel_id=1, source_target_pairs={{0,6},{1,7},{2,4},{3,5},{4,2},{5,3},{6,0},{7,1},{8,14},{9,15},{10,... | collective-permute-start | bytes 294920 | tf_op jit(solution)/shard_map/ppermute | solution.py:39
  497.8 12.4 %collective-permute-start.104 = (bf16[384,768]{1,0:T(8,128)(2,1)S(1)}, bf16[384,768]{1,0:T(8,128)(2,1)S(1)}, u32[]{:S(2)}, u32[]{:S(2)}) collective-permute-start(bf16[384,768]{1,0:T(8,128)(2,1)S(1)} %bitcast.436), channel_id=1, source_target_pairs={{0,2},{1,3},{2,0},{3,1},{4,6},{5,7},{6,4},{7,5},{8,10},{9,11},{10,... | collective-permute-start | bytes 1769480 | tf_op jit(solution)/shard_map/ppermute | solution.py:30
  515.7 43.4 %collective-permute-start.119 = (bf16[192,768]{1,0:T(8,128)(2,1)}, bf16[192,768]{1,0:T(8,128)(2,1)}, u32[]{:S(2)}, u32[]{:S(2)}) collective-permute-start(bf16[192,768]{1,0:T(8,128)(2,1)} %broadcast_select_fusion.21), channel_id=1, source_target_pairs={{0,8},{4,12},{8,0},{12,4},{16,24},{20,28},{24,16},{28,20},{1,9},{5... | collective-permute-start | bytes 884744 | tf_op jit(solution)/shard_map/ppermute | solution.py:33
  522.8 9.9 %collective-permute-start.112 = (bf16[384,768]{1,0:T(8,128)(2,1)S(1)}, bf16[384,768]{1,0:T(8,128)(2,1)S(1)}, u32[]{:S(2)}, u32[]{:S(2)}) collective-permute-start(bf16[384,768]{1,0:T(8,128)(2,1)S(1)} %bitcast.437), channel_id=1, source_target_pairs={{0,2},{1,3},{2,0},{3,1},{4,6},{5,7},{6,4},{7,5},{8,10},{9,11},{10,... | collective-permute-start | bytes 1769480 | tf_op jit(solution)/shard_map/ppermute | solution.py:30
  524.1 21.1 %collective-permute-start.126 = (f32[12288]{0:T(1024)S(1)}, f32[12288]{0:T(1024)}, u32[]{:S(2)}, u32[]{:S(2)}) collective-permute-start(f32[12288]{0:T(1024)S(1)} %pad.47), channel_id=1, source_target_pairs={{0,2},{1,3},{2,0},{3,1},{4,6},{5,7},{6,4},{7,5},{8,10},{9,11},{10,... | collective-permute-start | bytes 147464 | tf_op jit(solution)/shard_map/ppermute | solution.py:30
  554.9 80.1 %collective-permute-start.111 = (bf16[4,64,768]{2,1,0:T(8,128)(2,1)S(1)}, bf16[4,64,768]{2,1,0:T(8,128)(2,1)S(1)}, u32[]{:S(2)}, u32[]{:S(2)}) collective-permute-start(bf16[4,64,768]{2,1,0:T(8,128)(2,1)S(1)} %select_convert_fusion.2), channel_id=1, source_target_pairs={{0,1},{1,0},{2,3},{3,2},{4,5},{5,4},{6,7},{7,6},{8,9},{9,8},{10,11... | collective-permute-start | bytes 1179656 | tf_op jit(solution)/shard_map/ppermute | solution.py:30
  558.2 11.8 %collective-permute-start.129 = (f32[12288]{0:T(1024)S(1)}, f32[12288]{0:T(1024)S(1)}, u32[]{:S(2)}, u32[]{:S(2)}) collective-permute-start(f32[12288]{0:T(1024)S(1)} %add.765), channel_id=1, source_target_pairs={{0,16},{4,20},{8,24},{12,28},{16,0},{20,4},{24,8},{28,12},{1,17},{... | collective-permute-start | bytes 147464 | tf_op jit(solution)/shard_map/ppermute | solution.py:33
  560.2 18.3 %collective-permute-start.120 = (bf16[96,768]{1,0:T(8,128)(2,1)S(1)}, bf16[96,768]{1,0:T(8,128)(2,1)S(1)}, u32[]{:S(2)}, u32[]{:S(2)}) collective-permute-start(bf16[96,768]{1,0:T(8,128)(2,1)S(1)} %broadcast_select_fusion.31), channel_id=1, source_target_pairs={{0,16},{4,20},{8,24},{12,28},{16,0},{20,4},{24,8},{28,12},{1,17},{... | collective-permute-start | bytes 442376 | tf_op jit(solution)/shard_map/ppermute | solution.py:33
  576.5 9.9 %collective-permute-start.113 = (bf16[192,768]{1,0:T(8,128)(2,1)S(1)}, bf16[192,768]{1,0:T(8,128)(2,1)S(1)}, u32[]{:S(2)}, u32[]{:S(2)}) collective-permute-start(bf16[192,768]{1,0:T(8,128)(2,1)S(1)} %broadcast_select_fusion.24), channel_id=1, source_target_pairs={{0,4},{4,0},{8,12},{12,8},{16,20},{20,16},{24,28},{28,24},{1,5},{5... | collective-permute-start | bytes 884744 | tf_op jit(solution)/shard_map/ppermute | solution.py:33
  578.6 9.0 %collective-permute-start.121 = (bf16[48,768]{1,0:T(8,128)(2,1)S(1)}, bf16[48,768]{1,0:T(8,128)(2,1)S(1)}, u32[]{:S(2)}, u32[]{:S(2)}) collective-permute-start(bf16[48,768]{1,0:T(8,128)(2,1)S(1)} %broadcast_select_fusion.37), channel_id=1, source_target_pairs={{0,4},{4,0},{8,12},{12,8},{16,20},{20,16},{24,28},{28,24},{1,5},{5... | collective-permute-start | bytes 221192 | tf_op jit(solution)/shard_map/ppermute | solution.py:33
  586.5 11.7 %collective-permute-start.114 = (bf16[96,768]{1,0:T(8,128)(2,1)S(1)}, bf16[96,768]{1,0:T(8,128)(2,1)S(1)}, u32[]{:S(2)}, u32[]{:S(2)}) collective-permute-start(bf16[96,768]{1,0:T(8,128)(2,1)S(1)} %broadcast_select_fusion.34), channel_id=1, source_target_pairs={{0,8},{4,12},{8,0},{12,4},{16,24},{20,28},{24,16},{28,20},{1,9},{5... | collective-permute-start | bytes 442376 | tf_op jit(solution)/shard_map/ppermute | solution.py:33
  587.6 10.8 %collective-permute-start.122 = (bf16[48,768]{1,0:T(8,128)(2,1)S(1)}, bf16[48,768]{1,0:T(8,128)(2,1)S(1)}, u32[]{:S(2)}, u32[]{:S(2)}) collective-permute-start(bf16[48,768]{1,0:T(8,128)(2,1)S(1)} %add_convert_fusion.15), channel_id=1, source_target_pairs={{0,4},{4,0},{8,12},{12,8},{16,20},{20,16},{24,28},{28,24},{1,5},{5... | collective-permute-start | bytes 221192 | tf_op jit(solution)/shard_map/ppermute | solution.py:33
  598.3 12.4 %collective-permute-start.115 = (bf16[48,768]{1,0:T(8,128)(2,1)S(1)}, bf16[48,768]{1,0:T(8,128)(2,1)S(1)}, u32[]{:S(2)}, u32[]{:S(2)}) collective-permute-start(bf16[48,768]{1,0:T(8,128)(2,1)S(1)} %broadcast_select_fusion.40), channel_id=1, source_target_pairs={{0,16},{4,20},{8,24},{12,28},{16,0},{20,4},{24,8},{28,12},{1,17},{... | collective-permute-start | bytes 221192 | tf_op jit(solution)/shard_map/ppermute | solution.py:33
  610.7 10.7 %collective-permute-start.116 = (bf16[48,768]{1,0:T(8,128)(2,1)S(1)}, bf16[48,768]{1,0:T(8,128)(2,1)S(1)}, u32[]{:S(2)}, u32[]{:S(2)}) collective-permute-start(bf16[48,768]{1,0:T(8,128)(2,1)S(1)} %add_convert_fusion.16), channel_id=1, source_target_pairs={{0,16},{4,20},{8,24},{12,28},{16,0},{20,4},{24,8},{28,12},{1,17},{... | collective-permute-start | bytes 221192 | tf_op jit(solution)/shard_map/ppermute | solution.py:33
  610.8 18.0 %collective-permute-start.123 = (bf16[96,768]{1,0:T(8,128)(2,1)S(1)}, bf16[96,768]{1,0:T(8,128)(2,1)S(1)}, u32[]{:S(2)}, u32[]{:S(2)}) collective-permute-start(bf16[96,768]{1,0:T(8,128)(2,1)S(1)} %pad_maximum_fusion.29), channel_id=1, source_target_pairs={{0,16},{4,20},{8,24},{12,28},{16,0},{20,4},{24,8},{28,12},{1,17},{... | collective-permute-start | bytes 442376 | tf_op jit(solution)/shard_map/ppermute | solution.py:33
  621.4 12.7 %collective-permute-start.117 = (bf16[96,768]{1,0:T(8,128)(2,1)S(1)}, bf16[96,768]{1,0:T(8,128)(2,1)S(1)}, u32[]{:S(2)}, u32[]{:S(2)}) collective-permute-start(bf16[96,768]{1,0:T(8,128)(2,1)S(1)} %pad_maximum_fusion.28), channel_id=1, source_target_pairs={{0,8},{4,12},{8,0},{12,4},{16,24},{20,28},{24,16},{28,20},{1,9},{5... | collective-permute-start | bytes 442376 | tf_op jit(solution)/shard_map/ppermute | solution.py:33
  629.0 10.0 %collective-permute-start.124 = (bf16[192,768]{1,0:T(8,128)(2,1)S(1)}, bf16[192,768]{1,0:T(8,128)(2,1)S(1)}, u32[]{:S(2)}, u32[]{:S(2)}) collective-permute-start(bf16[192,768]{1,0:T(8,128)(2,1)S(1)} %pad_maximum_fusion.26), channel_id=1, source_target_pairs={{0,8},{4,12},{8,0},{12,4},{16,24},{20,28},{24,16},{28,20},{1,9},{5... | collective-permute-start | bytes 884744 | tf_op jit(solution)/shard_map/ppermute | solution.py:33
  (278 other events, 2358.0 us)
Sparse Core Ops, SparseCore 0:
  68.7 50.0 all-gather.14
  129.1 43.7 all-gather.6
  185.2 41.7 all-gather.8
  268.6 108.4 reduce-scatter.2
  389.6 50.5 all-gather.10
  444.3 98.3 reduce-scatter.4
  551.6 81.0 all-gather.12
